TPU v7x, 32 devices: a whole 2x2x4 slice. The times are simulated.
32 devices in a mesh: fsdp: 8 (over z, y), tp: 4 (over x, core).
Axes of the slice: x: 2, y: 2, z: 4, core: 2. Of those that a mesh axis runs over, the one named last changes fastest.
Arguments:
- inputs: float32 [16, 2048, 1280], P('fsdp', 'tp'), may hold values from -6 to 6
- cotangent: float32 [16, 2048, 1280], P('fsdp', 'tp'), may hold values from -6 to 6
- w_qkv: bfloat16 [2, 3, 1280, 1280], P(None, None, 'fsdp', 'tp'), may hold values from -0.15625 to 0.15625
- w_out: bfloat16 [2, 1280, 1280], P(None, 'tp', 'fsdp'), may hold values from -2 to 2
- w_up: bfloat16 [2, 1280, 1280], P(None, 'fsdp', 'tp'), may hold values from -0.15625 to 0.15625
- w_down: bfloat16 [2, 1280, 1280], P(None, 'tp', 'fsdp'), may hold values from -0.15625 to 0.15625
- norm_gain: float32 [2, 2, 1280], replicated, may hold values from 0.1 to 1.9
- query_scale: float32 [2, 80], replicated, may hold values from -1 to 1
- prefix_len: int32 [16], P('fsdp'), may hold values from 204 to 1024
Outputs:
- outputs: float32 [16, 2048, 1280], P('fsdp', 'tp')
- input_grad: float32 [16, 2048, 1280], P('fsdp', 'tp')
- w_qkv_grad: float32 [2, 3, 1280, 1280], P(None, None, 'fsdp', 'tp')
- w_out_grad: float32 [2, 1280, 1280], P(None, 'tp', 'fsdp')
- w_up_grad: float32 [2, 1280, 1280], P(None, 'fsdp', 'tp')
- w_down_grad: float32 [2, 1280, 1280], P(None, 'tp', 'fsdp')
- attn_gain_grad: float32 [2, 1280], replicated
- mlp_gain_grad: float32 [2, 1280], replicated
- scale_grad: float32 [2, 80], replicated
All inputs are finite; a program needn't handle non-finite values.
Results may differ from a plain program's by a relative error of at most 0.04.
Values may be sent and summed in bfloat16 or wider, within the bound.
A program may use at most 384 MiB of HBM per device.

v0:
```python
import math

import jax
import jax.numpy as jnp
from jax import lax
from jax.sharding import PartitionSpec as P

EPSILON = 1e-06
SOFT_ONE = 1.442695041
MASKED = -1e30


def rms_forward(x_rows):
    inv_scale = lax.rsqrt(jnp.mean(x_rows * x_rows, axis=-1, keepdims=True) + EPSILON)
    return (x_rows * inv_scale, inv_scale)


def rms_backward(normed, inv_scale, gain_row, grad_output):
    grad_normed = grad_output * gain_row
    grad_input = inv_scale * (
        grad_normed - normed * jnp.mean(grad_normed * normed, axis=-1, keepdims=True)
    )
    return (grad_input, jnp.sum(grad_output * normed, axis=0))


def block_scores(query_block, key_low, row_start, prefix):
    block_len = query_block.shape[0]
    length = key_low.shape[0]
    scores = jnp.einsum("qhd,khd->hqk", query_block, key_low, preferred_element_type=jnp.float32)
    row_ids = row_start + lax.broadcasted_iota(jnp.int32, (block_len, length), 0)
    col_ids = lax.broadcasted_iota(jnp.int32, (block_len, length), 1)
    allowed = (col_ids <= row_ids) | (col_ids < prefix)
    return jnp.where(allowed[None], scores, MASKED)


def attend_forward(query_low, key_low, value_low, prefix, block_rows):
    length, heads_here, head_dim = query_low.shape
    nblocks = length // block_rows
    query_blocks = query_low.reshape(nblocks, block_rows, heads_here, head_dim)
    block_starts = jnp.arange(nblocks, dtype=jnp.int32) * block_rows

    def one_block(element):
        query_block, row_start = element
        scores = block_scores(query_block, key_low, row_start, prefix)
        row_max = jnp.max(scores, axis=-1, keepdims=True)
        unnormed = jnp.exp(scores - row_max)
        row_sum = jnp.sum(unnormed, axis=-1, keepdims=True)
        softmaxed = (unnormed / row_sum).astype(jnp.bfloat16)
        block_out = jnp.einsum(
            "hqk,khd->qhd", softmaxed, value_low, preferred_element_type=jnp.float32
        )
        return (block_out, (row_max + jnp.log(row_sum))[..., 0])

    block_outs, logsums = lax.map(one_block, (query_blocks, block_starts))
    return (block_outs.reshape(length, heads_here, head_dim), logsums)


def attend_backward(query_low, key_low, value_low, grad_att, logsums, prefix, block_rows):
    length, heads_here, head_dim = query_low.shape
    nblocks = length // block_rows
    query_blocks = query_low.reshape(nblocks, block_rows, heads_here, head_dim)
    grad_blocks = grad_att.reshape(nblocks, block_rows, heads_here, head_dim)
    block_starts = jnp.arange(nblocks, dtype=jnp.int32) * block_rows

    def one_block(running, element):
        key_grad, value_grad = running
        query_block, grad_block, logsum, row_start = element
        scores = block_scores(query_block, key_low, row_start, prefix)
        softmaxed = jnp.exp(scores - logsum[..., None])
        soft_low = softmaxed.astype(jnp.bfloat16)
        grad_probs = jnp.einsum(
            "qhd,khd->hqk", grad_block, value_low, preferred_element_type=jnp.float32
        )
        row_inner = jnp.sum(softmaxed * grad_probs, axis=-1, keepdims=True)
        grad_scores = (softmaxed * (grad_probs - row_inner)).astype(jnp.bfloat16)
        query_grad = jnp.einsum(
            "hqk,khd->qhd", grad_scores, key_low, preferred_element_type=jnp.float32
        )
        key_grad = key_grad + jnp.einsum(
            "hqk,qhd->khd", grad_scores, query_block, preferred_element_type=jnp.float32
        )
        value_grad = value_grad + jnp.einsum(
            "hqk,qhd->khd", soft_low, grad_block, preferred_element_type=jnp.float32
        )
        return ((key_grad, value_grad), query_grad)

    zero_acc = jnp.zeros((length, heads_here, head_dim), jnp.float32)
    (key_grad, value_grad), query_grads = lax.scan(
        one_block, (zero_acc, zero_acc), (query_blocks, grad_blocks, logsums, block_starts)
    )
    return (query_grads.reshape(length, heads_here, head_dim), key_grad, value_grad)


def layer_forward(x_rows, prefix, weights, gains, factor, block_rows):
    w_qkv, w_out, w_up, w_down = weights
    head_dim = factor.shape[0]
    normed_a, scale_a = rms_forward(x_rows)
    low_a = (normed_a * gains[0]).astype(jnp.bfloat16)
    whole_a = lax.all_gather(low_a, "tp", axis=0, tiled=True)
    length = whole_a.shape[0]
    projected = jnp.einsum("rd,cde->cre", whole_a, w_qkv, preferred_element_type=jnp.float32)
    head_shape = (length, w_qkv.shape[2] // head_dim, head_dim)
    query_raw = projected[0].reshape(head_shape)
    query_low = (query_raw * factor).astype(jnp.bfloat16)
    key_low = projected[1].reshape(head_shape).astype(jnp.bfloat16)
    value_low = projected[2].reshape(head_shape).astype(jnp.bfloat16)
    attended, logsums = attend_forward(query_low, key_low, value_low, prefix, block_rows)
    attended_low = attended.reshape(length, -1).astype(jnp.bfloat16)
    middle = x_rows + lax.psum_scatter(
        jnp.dot(attended_low, w_out, preferred_element_type=jnp.float32).astype(jnp.bfloat16),
        "tp",
        scatter_dimension=0,
        tiled=True,
    ).astype(jnp.float32)
    normed_m, scale_m = rms_forward(middle)
    low_m = (normed_m * gains[1]).astype(jnp.bfloat16)
    hidden_pre = jnp.dot(low_m, w_up, preferred_element_type=jnp.float32)
    hidden_low = jax.nn.silu(hidden_pre).astype(jnp.bfloat16)
    mlp_result = jnp.dot(hidden_low, w_down, preferred_element_type=jnp.float32)
    saved = (
        normed_a,
        scale_a,
        whole_a,
        query_raw,
        query_low,
        key_low,
        value_low,
        logsums,
        attended_low,
        normed_m,
        scale_m,
        low_m,
        hidden_pre,
        hidden_low,
    )
    return (middle + mlp_result, saved)


def layer_backward(grad_rows, saved, weights, gains, factor, prefix, block_rows):
    w_qkv, w_out, w_up, w_down = weights
    (
        normed_a,
        scale_a,
        whole_a,
        query_raw,
        query_low,
        key_low,
        value_low,
        logsums,
        attended_low,
        normed_m,
        scale_m,
        inputs_m,
        hidden_pre,
        hidden_low,
    ) = saved
    local_rows = grad_rows.shape[0]
    length = whole_a.shape[0]
    grad_low = grad_rows.astype(jnp.bfloat16)
    grad_hidden = jnp.einsum("rd,fd->rf", grad_low, w_down, preferred_element_type=jnp.float32)
    down_grad = jnp.einsum("rf,rd->fd", hidden_low, grad_low, preferred_element_type=jnp.float32)
    sigma = jax.nn.sigmoid(hidden_pre)
    grad_pre = (grad_hidden * sigma * (1.0 + hidden_pre * (1.0 - sigma))).astype(jnp.bfloat16)
    up_grad = jnp.einsum("rd,rf->df", inputs_m, grad_pre, preferred_element_type=jnp.float32)
    grad_norm_m = jnp.einsum("rf,df->rd", grad_pre, w_up, preferred_element_type=jnp.float32)
    back_m, gain_grad_m = rms_backward(normed_m, scale_m, gains[1], grad_norm_m)
    grad_middle = grad_rows + back_m
    grad_mid_low = grad_middle.astype(jnp.bfloat16)
    grad_whole = lax.all_gather(grad_mid_low, "tp", axis=0, tiled=True)
    out_grad = jnp.einsum("re,rd->ed", attended_low, grad_whole, preferred_element_type=jnp.float32)
    grad_att = jnp.einsum("rd,ed->re", grad_whole, w_out, preferred_element_type=jnp.float32)
    grad_att = grad_att.astype(jnp.bfloat16).reshape(query_low.shape)
    query_grad, key_grad, value_grad = attend_backward(
        query_low, key_low, value_low, grad_att, logsums, prefix, block_rows
    )
    factor_grad = jnp.sum(query_grad * query_raw, axis=(0, 1))
    stacked = jnp.stack(
        [
            (query_grad * factor).reshape(length, -1).astype(jnp.bfloat16),
            key_grad.reshape(length, -1).astype(jnp.bfloat16),
            value_grad.reshape(length, -1).astype(jnp.bfloat16),
        ]
    )
    qkv_grad = jnp.einsum("rd,cre->cde", whole_a, stacked, preferred_element_type=jnp.float32)
    section = lax.slice_in_dim(stacked, 0, lax.axis_size("tp") * local_rows, axis=1)
    grad_norm_a = lax.psum_scatter(
        jnp.einsum("cre,cde->rd", section, w_qkv, preferred_element_type=jnp.float32).astype(
            jnp.bfloat16
        ),
        "tp",
        scatter_dimension=0,
        tiled=True,
    ).astype(jnp.float32)
    back_a, gain_grad_a = rms_backward(normed_a, scale_a, gains[0], grad_norm_a)
    grads = (
        qkv_grad,
        out_grad,
        up_grad,
        down_grad,
        jnp.stack([gain_grad_a, gain_grad_m]),
        factor_grad,
    )
    return (grad_middle + back_a, grads)


def body(inputs, cotangent, w_qkv, w_out, w_up, w_down, norm_gain, query_scale, prefix_len):
    full_qkv, full_out, full_up, full_down = (
        lax.all_gather(w_qkv, "fsdp", axis=2, tiled=True),
        lax.all_gather(w_out, "fsdp", axis=2, tiled=True),
        lax.all_gather(w_up, "fsdp", axis=1, tiled=True),
        lax.all_gather(w_down, "fsdp", axis=2, tiled=True),
    )
    full_up, full_down = (
        lax.all_gather(full_up, "tp", axis=2, tiled=True),
        lax.all_gather(full_down, "tp", axis=1, tiled=True),
    )
    layer_count = w_qkv.shape[0]
    head_dim = query_scale.shape[1]
    factors = jax.nn.softplus(query_scale) * (SOFT_ONE / math.sqrt(head_dim))
    length = inputs.shape[1] * lax.axis_size("tp")
    block_rows = min(512, length)

    def one_sequence(totals, element):
        x_rows, grad_rows, prefix = element
        kept = []
        for layer_id in range(layer_count):
            weights = (
                full_qkv[layer_id],
                full_out[layer_id],
                full_up[layer_id],
                full_down[layer_id],
            )
            x_rows, saved = layer_forward(
                x_rows, prefix, weights, norm_gain[layer_id], factors[layer_id], block_rows
            )
            kept.append(saved)
        per_layer = [None] * layer_count
        for layer_id in reversed(range(layer_count)):
            weights = (
                full_qkv[layer_id],
                full_out[layer_id],
                full_up[layer_id],
                full_down[layer_id],
            )
            grad_rows, per_layer[layer_id] = layer_backward(
                grad_rows,
                kept[layer_id],
                weights,
                norm_gain[layer_id],
                factors[layer_id],
                prefix,
                block_rows,
            )
        stacked = tuple((jnp.stack([entry[index] for entry in per_layer]) for index in range(6)))
        totals = tuple((old + new for old, new in zip(totals, stacked)))
        return (totals, (x_rows, grad_rows))

    initial = (
        jnp.zeros(full_qkv.shape, jnp.float32),
        jnp.zeros(full_out.shape, jnp.float32),
        jnp.zeros(full_up.shape, jnp.float32),
        jnp.zeros(full_down.shape, jnp.float32),
        jnp.zeros(norm_gain.shape, jnp.float32),
        jnp.zeros(query_scale.shape, jnp.float32),
    )
    totals, (results, grads_in) = lax.scan(one_sequence, initial, (inputs, cotangent, prefix_len))
    qkv_total, out_total, up_total, down_total, gain_total, factor_total = totals
    up_total, down_total = (
        lax.psum_scatter(
            up_total.astype(jnp.bfloat16), "tp", scatter_dimension=2, tiled=True
        ).astype(jnp.float32),
        lax.psum_scatter(
            down_total.astype(jnp.bfloat16), "tp", scatter_dimension=1, tiled=True
        ).astype(jnp.float32),
    )
    qkv_total, out_total, up_total, down_total = (
        lax.psum_scatter(
            qkv_total.astype(jnp.bfloat16), "fsdp", scatter_dimension=2, tiled=True
        ).astype(jnp.float32),
        lax.psum_scatter(
            out_total.astype(jnp.bfloat16), "fsdp", scatter_dimension=2, tiled=True
        ).astype(jnp.float32),
        lax.psum_scatter(
            up_total.astype(jnp.bfloat16), "fsdp", scatter_dimension=1, tiled=True
        ).astype(jnp.float32),
        lax.psum_scatter(
            down_total.astype(jnp.bfloat16), "fsdp", scatter_dimension=2, tiled=True
        ).astype(jnp.float32),
    )
    scale_total = factor_total * jax.nn.sigmoid(query_scale) * (SOFT_ONE / math.sqrt(head_dim))
    gain_total, scale_total = lax.psum((gain_total, scale_total), ("fsdp", "tp"))
    return (
        results,
        grads_in,
        qkv_total,
        out_total,
        up_total,
        down_total,
        gain_total[:, 0],
        gain_total[:, 1],
        scale_total,
    )


def solution(mesh):
    placed = (
        P("fsdp", "tp", None),
        P("fsdp", "tp", None),
        P(None, None, "fsdp", "tp"),
        P(None, "tp", "fsdp"),
        P(None, "fsdp", "tp"),
        P(None, "tp", "fsdp"),
        P(),
        P(),
        P("fsdp"),
    )
    return jax.shard_map(
        body,
        mesh=mesh,
        in_specs=placed,
        out_specs=(
            P("fsdp", "tp", None),
            P("fsdp", "tp", None),
            P(None, None, "fsdp", "tp"),
            P(None, "tp", "fsdp"),
            P(None, "fsdp", "tp"),
            P(None, "tp", "fsdp"),
            P(),
            P(),
            P(),
        ),
        check_vma=False,
    )
```

profile of v0, /device:TPU:0, one launch (start us, length us, event | category | flops | bytes accessed | tf_op | source)
XLA Modules:
  0.0 3046.3 jit_solution(10894018422014340388)
XLA Ops:
  14.5 46.5 %all-gather.15.cloned.1.call-done = bf16[2,1280,320]{2,0,1:T(2,128)(2,1)} async-done(((bf16[2,160,320]{2,0,1:T(2,128)(2,1)}), bf16[2,1280,320]{2,0,1:T(2,128)(2,1)}) %all-gather.15.cloned.1.call-update) | async-done | bytes 1638416 | tf_op jit(solution)/shard_map/all_gather | solution.py:210
  68.5 41.9 %all-gather.19.cloned.1.call-done = bf16[2,320,1280]{1,0,2:T(2,128)(2,1)} async-done(((bf16[2,320,160]{1,0,2:T(2,128)(2,1)}), bf16[2,320,1280]{1,0,2:T(2,128)(2,1)}) %all-gather.19.cloned.1.call-update) | async-done | bytes 1638416 | tf_op jit(solution)/shard_map/all_gather | solution.py:211
  118.6 41.3 %all-gather.13.cloned.1.call-done = bf16[2,320,1280]{1,0,2:T(2,128)(2,1)} async-done(((bf16[2,320,160]{1,0,2:T(2,128)(2,1)}), bf16[2,320,1280]{1,0,2:T(2,128)(2,1)}) %all-gather.13.cloned.1.call-update) | async-done | bytes 1638416 | tf_op jit(solution)/shard_map/all_gather | solution.py:209
  166.4 89.4 %all-gather.11.cloned.1.call-done = bf16[2,3,1280,320]{3,0,1,2:T(2,128)(2,1)} async-done(((bf16[2,3,160,320]{3,0,1,2:T(2,128)(2,1)}), bf16[2,3,1280,320]{3,0,1,2:T(2,128)(2,1)}) %all-gather.11.cloned.1.call-update) | async-done | bytes 4915216 | tf_op jit(solution)/shard_map/all_gather | solution.py:208
  255.8 17.9 copy.136
  273.6 29.6 all-gather.17.cloned.1.call-done
  303.3 17.0 copy.138
  320.3 32.3 %all-gather.21.cloned.1.call-done = bf16[2,1280,1280]{2,0,1:T(2,128)(2,1)} async-done(((bf16[2,320,1280]{2,0,1:T(2,128)(2,1)}), bf16[2,1280,1280]{2,0,1:T(2,128)(2,1)}) %all-gather.21.cloned.1.call-update) | async-done | bytes 6553616 | tf_op jit(solution)/shard_map/all_gather | solution.py:215
  359.1 2213.7 %while.87 = (s32[]{:T(128)}, f32[2,3,1280,320]{2,3,1,0:T(8,128)}, f32[2,320,1280]{2,1,0:T(8,128)}, f32[2,1280,1280]{2,1,0:T(8,128)}, f32[2,1280,1280]{2,1,0:T(8,...) while((s32[]{:T(128)}, f32[2,3,1280,320]{2,3,1,0:T(8,128)}, ...), condition=%wide.region_33.34_spmd.clone, body=%wide.region_0.33_spmd.clone.sunk | while | flops 70137700352 | bytes 1964189312 | solution.py:266
  371.6 35.6 %all-gather.23.cloned.1.call-done = bf16[2048,1280]{1,0:T(8,128)(2,1)} async-done(((bf16[512,1280]{1,0:T(8,128)(2,1)}), bf16[2048,1280]{1,0:T(8,128)(2,1)}) %all-gather.23.cloned.1.call-update) | async-done | bytes 5242896 | tf_op jit(solution)/shard_map/while/body/eval_jaxpr/all_gather | solution.py:99
  424.3 64.7 %while.88 = (s32[]{:T(128)}, bf16[4,512,4,80]{1,3,2,0:T(8,128)(2,1)}, f32[4,4,512]{2,1,0:T(4,128)S(1)}, s32[4]{0:T(128)S(1)}, s32[]{:T(128)}, /*index=5*/bf16[4,...) while((s32[]{:T(128)}, ...), condition=%wide.region_5.5_spmd, body=%wide.region_2.4_spmd.sunk | while | flops 1382023680 | bytes 68690112 | solution.py:54
  498.6 51.5 %reduce-scatter.31.cloned.1.call-done = bf16[512,1280]{1,0:T(8,128)(2,1)} async-done(((bf16[2048,1280]{1,0:T(8,128)(2,1)}), bf16[512,1280]{1,0:T(8,128)(2,1)}) %reduce-scatter.31.cloned.1.call-update) | async-done | bytes 1310736 | tf_op jit(solution)/shard_map/while/body/eval_jaxpr/reduce_scatter | solution.py:109
  563.0 40.5 %all-gather.25.cloned.1.call-done = bf16[2048,1280]{1,0:T(8,128)(2,1)} async-done(((bf16[512,1280]{1,0:T(8,128)(2,1)}), bf16[2048,1280]{1,0:T(8,128)(2,1)}) %all-gather.25.cloned.1.call-update) | async-done | bytes 5242896 | tf_op jit(solution)/shard_map/while/body/eval_jaxpr/all_gather | solution.py:99
  620.8 65.4 %while.89 = (s32[]{:T(128)}, bf16[4,512,4,80]{1,3,2,0:T(8,128)(2,1)}, f32[4,4,512]{2,1,0:T(4,128)S(1)}, s32[4]{0:T(128)S(1)}, s32[]{:T(128)}, /*index=5*/bf16[4,...) while((s32[]{:T(128)}, ...), condition=%wide.region_12.12_spmd, body=%wide.region_9.11_spmd.sunk | while | flops 1382023680 | bytes 68690112 | solution.py:54
  694.9 51.5 %reduce-scatter.33.cloned.1.call-done = bf16[512,1280]{1,0:T(8,128)(2,1)} async-done(((bf16[2048,1280]{1,0:T(8,128)(2,1)}), bf16[512,1280]{1,0:T(8,128)(2,1)}) %reduce-scatter.33.cloned.1.call-update) | async-done | bytes 1310736 | tf_op jit(solution)/shard_map/while/body/eval_jaxpr/reduce_scatter | solution.py:109
  766.0 39.8 %all-gather.27.cloned.1.call-done = bf16[2048,1280]{1,0:T(8,128)(2,1)} async-done(((bf16[512,1280]{1,0:T(8,128)(2,1)}), bf16[2048,1280]{1,0:T(8,128)(2,1)}) %all-gather.27.cloned.1.call-update) | async-done | bytes 5242896 | tf_op jit(solution)/shard_map/while/body/eval_jaxpr/all_gather | solution.py:169
  820.1 203.0 %while.90 = (s32[]{:T(128)}, f32[2048,4,80]{0,2,1:T(8,128)}, f32[2048,4,80]{0,2,1:T(8,128)}, f32[4,512,4,80]{1,3,2,0:T(8,128)}, bf16[4,512,4,80]{1,3,2,0:T(8,128...) while((s32[]{:T(128)}, f32[2048,4,80]{0,2,1:T(8,128)}, ...), condition=%wide.region_18.18_spmd.clone, body=%wide.region_16.17_spmd.clone.sunk | while | flops 3410493952 | bytes 245039408 | solution.py:88
  839.2 12.4 multiply_reduce_fusion.27
  851.6 12.1 multiply_convert_fusion.48
  890.0 12.5 multiply_reduce_fusion.27
  902.4 12.1 multiply_convert_fusion.48
  940.8 12.4 multiply_reduce_fusion.27
  953.2 12.1 multiply_convert_fusion.48
  991.6 12.5 multiply_reduce_fusion.27
  1004.1 12.1 multiply_convert_fusion.48
  1046.5 51.5 %reduce-scatter.35.cloned.1.call-done = bf16[512,1280]{1,0:T(8,128)(2,1)} async-done(((bf16[2048,1280]{1,0:T(8,128)(2,1)}), bf16[512,1280]{1,0:T(8,128)(2,1)}) %reduce-scatter.35.cloned.1.call-update) | async-done | bytes 1310736 | tf_op jit(solution)/shard_map/while/body/eval_jaxpr/reduce_scatter | solution.py:186
  1163.0 205.6 %while.91 = (s32[]{:T(128)}, f32[2048,4,80]{0,2,1:T(8,128)}, f32[2048,4,80]{0,2,1:T(8,128)}, f32[4,512,4,80]{1,3,2,0:T(8,128)}, bf16[4,512,4,80]{1,3,2,0:T(8,128...) while((s32[]{:T(128)}, f32[2048,4,80]{0,2,1:T(8,128)}, ...), condition=%wide.region_24.24_spmd.clone, body=%wide.region_22.23_spmd.clone.sunk | while | flops 3410493952 | bytes 234553584 | solution.py:88
  1183.0 12.4 multiply_reduce_fusion.28
  1195.5 12.1 multiply_convert_fusion.49
  1234.6 12.5 multiply_reduce_fusion.28
  1247.0 12.1 multiply_convert_fusion.49
  1286.1 12.4 multiply_reduce_fusion.28
  1298.5 12.1 multiply_convert_fusion.49
  1337.5 12.4 multiply_reduce_fusion.28
  1408.4 16.9 maximum_add_fusion.13
  1469.0 35.7 %all-gather.23.cloned.1.call-done = bf16[2048,1280]{1,0:T(8,128)(2,1)} async-done(((bf16[512,1280]{1,0:T(8,128)(2,1)}), bf16[2048,1280]{1,0:T(8,128)(2,1)}) %all-gather.23.cloned.1.call-update) | async-done | bytes 5242896 | tf_op jit(solution)/shard_map/while/body/eval_jaxpr/all_gather | solution.py:99
  1521.8 64.3 %while.88 = (s32[]{:T(128)}, bf16[4,512,4,80]{1,3,2,0:T(8,128)(2,1)}, f32[4,4,512]{2,1,0:T(4,128)S(1)}, s32[4]{0:T(128)S(1)}, s32[]{:T(128)}, /*index=5*/bf16[4,...) while((s32[]{:T(128)}, ...), condition=%wide.region_5.5_spmd, body=%wide.region_2.4_spmd.sunk | while | flops 1382023680 | bytes 68690112 | solution.py:54
  1595.7 51.5 %reduce-scatter.31.cloned.1.call-done = bf16[512,1280]{1,0:T(8,128)(2,1)} async-done(((bf16[2048,1280]{1,0:T(8,128)(2,1)}), bf16[512,1280]{1,0:T(8,128)(2,1)}) %reduce-scatter.31.cloned.1.call-update) | async-done | bytes 1310736 | tf_op jit(solution)/shard_map/while/body/eval_jaxpr/reduce_scatter | solution.py:109
  1660.1 40.5 %all-gather.25.cloned.1.call-done = bf16[2048,1280]{1,0:T(8,128)(2,1)} async-done(((bf16[512,1280]{1,0:T(8,128)(2,1)}), bf16[2048,1280]{1,0:T(8,128)(2,1)}) %all-gather.25.cloned.1.call-update) | async-done | bytes 5242896 | tf_op jit(solution)/shard_map/while/body/eval_jaxpr/all_gather | solution.py:99
  1717.9 65.4 %while.89 = (s32[]{:T(128)}, bf16[4,512,4,80]{1,3,2,0:T(8,128)(2,1)}, f32[4,4,512]{2,1,0:T(4,128)S(1)}, s32[4]{0:T(128)S(1)}, s32[]{:T(128)}, /*index=5*/bf16[4,...) while((s32[]{:T(128)}, ...), condition=%wide.region_12.12_spmd, body=%wide.region_9.11_spmd.sunk | while | flops 1382023680 | bytes 68690112 | solution.py:54
  1792.0 51.5 %reduce-scatter.33.cloned.1.call-done = bf16[512,1280]{1,0:T(8,128)(2,1)} async-done(((bf16[2048,1280]{1,0:T(8,128)(2,1)}), bf16[512,1280]{1,0:T(8,128)(2,1)}) %reduce-scatter.33.cloned.1.call-update) | async-done | bytes 1310736 | tf_op jit(solution)/shard_map/while/body/eval_jaxpr/reduce_scatter | solution.py:109
  1863.2 39.8 %all-gather.27.cloned.1.call-done = bf16[2048,1280]{1,0:T(8,128)(2,1)} async-done(((bf16[512,1280]{1,0:T(8,128)(2,1)}), bf16[2048,1280]{1,0:T(8,128)(2,1)}) %all-gather.27.cloned.1.call-update) | async-done | bytes 5242896 | tf_op jit(solution)/shard_map/while/body/eval_jaxpr/all_gather | solution.py:169
  1917.3 203.0 %while.90 = (s32[]{:T(128)}, f32[2048,4,80]{0,2,1:T(8,128)}, f32[2048,4,80]{0,2,1:T(8,128)}, f32[4,512,4,80]{1,3,2,0:T(8,128)}, bf16[4,512,4,80]{1,3,2,0:T(8,128...) while((s32[]{:T(128)}, f32[2048,4,80]{0,2,1:T(8,128)}, ...), condition=%wide.region_18.18_spmd.clone, body=%wide.region_16.17_spmd.clone.sunk | while | flops 3410493952 | bytes 245039408 | solution.py:88
  1936.4 12.4 multiply_reduce_fusion.27
  1987.2 12.5 multiply_reduce_fusion.27
  2038.0 12.4 multiply_reduce_fusion.27
  2088.8 12.5 multiply_reduce_fusion.27
  2143.7 51.5 %reduce-scatter.35.cloned.1.call-done = bf16[512,1280]{1,0:T(8,128)(2,1)} async-done(((bf16[2048,1280]{1,0:T(8,128)(2,1)}), bf16[512,1280]{1,0:T(8,128)(2,1)}) %reduce-scatter.35.cloned.1.call-update) | async-done | bytes 1310736 | tf_op jit(solution)/shard_map/while/body/eval_jaxpr/reduce_scatter | solution.py:186
  2260.2 205.6 %while.91 = (s32[]{:T(128)}, f32[2048,4,80]{0,2,1:T(8,128)}, f32[2048,4,80]{0,2,1:T(8,128)}, f32[4,512,4,80]{1,3,2,0:T(8,128)}, bf16[4,512,4,80]{1,3,2,0:T(8,128...) while((s32[]{:T(128)}, f32[2048,4,80]{0,2,1:T(8,128)}, ...), condition=%wide.region_24.24_spmd.clone, body=%wide.region_22.23_spmd.clone.sunk | while | flops 3410493952 | bytes 234553584 | solution.py:88
  2280.2 12.4 multiply_reduce_fusion.28
  2331.7 12.5 multiply_reduce_fusion.28
  2383.2 12.4 multiply_reduce_fusion.28
  2434.7 12.4 multiply_reduce_fusion.28
  2505.6 26.1 maximum_add_fusion.13
  2580.9 17.0 copy.148
  2616.6 17.1 copy.150
  2659.3 12.6 copy.144
  2671.9 15.5 reshape.415
  2696.3 31.2 %reduce-scatter.29.cloned.1.call-done = bf16[320,2560]{1,0:T(8,128)(2,1)} async-done(((bf16[1280,2560]{1,0:T(8,128)(2,1)}), bf16[320,2560]{1,0:T(8,128)(2,1)}) %reduce-scatter.29.cloned.1.call-update) | async-done | bytes 1638416
  2736.1 40.3 %all-reduce = (f32[2,2,1280]{2,0,1:T(2,128)S(1)}, f32[2,80]{1,0:T(2,128)}) all-reduce(f32[2,2,1280]{2,0,1:T(2,128)S(1)} %copy.141, f32[2,80]{1,0:T(2,128)S(1)} %fusion.176), channel_id=1, replica_groups=mesh['fsdp'=8,'tp'=4] {'fsdp','tp'}, use_global_device_ids=true, to_apply=%region_40.41 | all-reduce | flops 5280 | bytes 42240 | tf_op jit(solution)/shard_map/psum | solution.py:291
  2777.0 19.4 reduce-scatter.25.cloned.1.call-done
  2798.8 99.3 %reduce-scatter.23.cloned.1.call-done = bf16[160,1920]{1,0:T(8,128)(2,1)} async-done(((bf16[1280,1920]{1,0:T(8,128)(2,1)}), bf16[160,1920]{1,0:T(8,128)(2,1)}) %reduce-scatter.23.cloned.1.call-update) | async-done | bytes 614416
  2902.7 65.2 %reduce-scatter.19.cloned.1.call-done = bf16[2,160,320]{2,1,0:T(8,128)(2,1)} async-done(((bf16[2,1280,320]{2,1,0:T(8,128)(2,1)}), bf16[2,160,320]{2,1,0:T(8,128)(2,1)}) %reduce-scatter.19.cloned.1.call-update) | async-done | bytes 204816 | tf_op jit(solution)/shard_map/reduce_scatter | solution.py:283
  2969.7 67.7 %reduce-scatter.21.cloned.1.call-done = bf16[2,320,160]{1,2,0:T(8,128)(2,1)} async-done(((bf16[2,320,1280]{1,2,0:T(8,128)(2,1)}), bf16[2,320,160]{1,2,0:T(8,128)(2,1)}) %reduce-scatter.21.cloned.1.call-update) | async-done | bytes 204816 | tf_op jit(solution)/shard_map/reduce_scatter | solution.py:286
  (1232 shorter events, 1445.9 us)
Async XLA Ops:
  7.2 53.8 %all-gather.15.cloned.1.call-start = ((), (), s32[]{:S(2)}) async-start(), calls=%async_computation.12 | async-start | bytes 2211840 | tf_op jit(solution)/shard_map/all_gather | solution.py:210
  9.1 101.3 %all-gather.19.cloned.1.call-start = ((), (), s32[]{:S(2)}) async-start(), calls=%async_computation.14 | async-start | bytes 2211840 | tf_op jit(solution)/shard_map/all_gather | solution.py:211
  11.1 148.8 %all-gather.13.cloned.1.call-start = ((), (), s32[]{:S(2)}) async-start(), calls=%async_computation.11 | async-start | bytes 2211840 | tf_op jit(solution)/shard_map/all_gather | solution.py:209
  13.0 242.8 %all-gather.11.cloned.1.call-start = ((), (), s32[]{:S(2)}) async-start(), calls=%async_computation.10 | async-start | bytes 6635520 | tf_op jit(solution)/shard_map/all_gather | solution.py:208
  14.5 288.8 %all-gather.17.cloned.1.call-start = ((), (), s32[]{:S(2)}) async-start(), calls=%async_computation.13 | async-start | bytes 8192000 | tf_op jit(solution)/shard_map/all_gather | solution.py:214
  68.5 49.5 %copy-start.94 = (f32[2,80]{1,0:T(2,128)S(1)}, f32[2,80]{1,0:T(2,128)}, u32[]{:S(2)}) copy-start(f32[2,80]{1,0:T(2,128)} %param.26) | copy-start | bytes 1924
  68.5 284.1 %all-gather.21.cloned.1.call-start = ((), (), s32[]{:S(2)}) async-start(), calls=%async_computation.15 | async-start | bytes 8192000 | tf_op jit(solution)/shard_map/all_gather | solution.py:215
  359.4 47.8 %all-gather.23.cloned.1.call-start = ((), (), s32[]{:S(2)}) async-start(), calls=%async_computation.22 | async-start | bytes 6553600 | tf_op jit(solution)/shard_map/while/body/eval_jaxpr/all_gather | solution.py:99
  366.6 183.5 %reduce-scatter.31.cloned.1.call-start = ((), (), s32[]{:S(2)}) async-start(), calls=%async_computation.23 | async-start | bytes 6553600 | tf_op jit(solution)/shard_map/while/body/eval_jaxpr/reduce_scatter | solution.py:109
  371.6 50.4 %copy-start.87 = (f32[80]{0:T(128)}, f32[80]{0:T(128)S(1)}, u32[]{:S(2)}) copy-start(f32[80]{0:T(128)S(1)} %get-tuple-element.1302) | copy-start | bytes 964 | tf_op jit(solution)/shard_map/while
  498.6 54.3 %copy-start.67 = (f32[1280]{0:T(1024)S(1)}, f32[1280]{0:T(1024)}, u32[]{:S(2)}) copy-start(f32[1280]{0:T(1024)} %get-tuple-element.1309) | copy-start | bytes 15364 | tf_op jit(solution)/shard_map/while
  498.6 105.0 %all-gather.25.cloned.1.call-start = ((), (), s32[]{:S(2)}) async-start(), calls=%async_computation.24 | async-start | bytes 6553600 | tf_op jit(solution)/shard_map/while/body/eval_jaxpr/all_gather | solution.py:99
  563.0 183.4 %reduce-scatter.33.cloned.1.call-start = ((), (), s32[]{:S(2)}) async-start(), calls=%async_computation.25 | async-start | bytes 6553600 | tf_op jit(solution)/shard_map/while/body/eval_jaxpr/reduce_scatter | solution.py:109
  694.8 54.2 %copy-start.70 = (f32[1280]{0:T(1024)S(1)}, f32[1280]{0:T(1024)}, u32[]{:S(2)}) copy-start(f32[1280]{0:T(1024)} %get-tuple-element.1323) | copy-start | bytes 15364 | tf_op jit(solution)/shard_map/while
  694.8 111.0 %all-gather.27.cloned.1.call-start = ((), (), s32[]{:S(2)}) async-start(), calls=%async_computation.26 | async-start | bytes 6553600 | tf_op jit(solution)/shard_map/while/body/eval_jaxpr/all_gather | solution.py:169
  749.0 13.6 copy-start.30
  749.0 13.6 copy-start.83
  765.2 332.8 %reduce-scatter.35.cloned.1.call-start = ((), (), s32[]{:S(2)}) async-start(), calls=%async_computation.27 | async-start | bytes 6553600 | tf_op jit(solution)/shard_map/while/body/eval_jaxpr/reduce_scatter | solution.py:186
  851.6 12.1 copy-start.6
  902.4 12.1 copy-start.6
  953.2 12.1 copy-start.6
  1004.1 12.1 copy-start.6
  1046.4 51.6 %copy-start.14 = (f32[512,1280]{1,0:T(8,128)S(1)}, f32[512,1280]{1,0:T(8,128)}, u32[]{:S(2)}) copy-start(f32[512,1280]{1,0:T(8,128)} %copy-done.13) | copy-start | bytes 7864324 | tf_op jit(solution)/shard_map/while
  1046.4 51.6 %copy-start.60 = (f32[1280]{0:T(1024)S(1)}, f32[1280]{0:T(1024)}, u32[]{:S(2)}) copy-start(f32[1280]{0:T(1024)} %get-tuple-element.1312) | copy-start | bytes 15364 | tf_op jit(solution)/shard_map/while
  1046.4 51.6 %copy-start.66 = (f32[512]{0:T(512)S(1)}, f32[512]{0:T(512)}, u32[]{:S(2)}) copy-start(f32[512]{0:T(512)} %copy-done.65) | copy-start | bytes 6148 | tf_op jit(solution)/shard_map/while
  1046.5 107.8 %all-gather.29.cloned.1.call-start = ((), (), s32[]{:S(2)}) async-start(), calls=%async_computation.28 | async-start | bytes 6553600 | tf_op jit(solution)/shard_map/while/body/eval_jaxpr/all_gather | solution.py:169
  1113.6 335.6 %reduce-scatter.37.cloned.1.call-start = ((), (), s32[]{:S(2)}) async-start(), calls=%async_computation.29 | async-start | bytes 6553600 | tf_op jit(solution)/shard_map/while/body/eval_jaxpr/reduce_scatter | solution.py:186
  1115.1 13.6 slice-start.10
  1115.1 13.6 slice-start.18
  1195.5 12.1 copy-start.4
  1247.0 12.1 copy-start.4
  1298.5 12.1 copy-start.4
  1350.0 12.1 copy-start.4
  1408.4 16.9 copy-start.18
  1456.8 47.9 %all-gather.23.cloned.1.call-start = ((), (), s32[]{:S(2)}) async-start(), calls=%async_computation.22 | async-start | bytes 6553600 | tf_op jit(solution)/shard_map/while/body/eval_jaxpr/all_gather | solution.py:99
  1464.1 183.1 %reduce-scatter.31.cloned.1.call-start = ((), (), s32[]{:S(2)}) async-start(), calls=%async_computation.23 | async-start | bytes 6553600 | tf_op jit(solution)/shard_map/while/body/eval_jaxpr/reduce_scatter | solution.py:109
  1469.0 50.5 %copy-start.87 = (f32[80]{0:T(128)}, f32[80]{0:T(128)S(1)}, u32[]{:S(2)}) copy-start(f32[80]{0:T(128)S(1)} %get-tuple-element.1302) | copy-start | bytes 964 | tf_op jit(solution)/shard_map/while
  1595.6 54.3 %copy-start.67 = (f32[1280]{0:T(1024)S(1)}, f32[1280]{0:T(1024)}, u32[]{:S(2)}) copy-start(f32[1280]{0:T(1024)} %get-tuple-element.1309) | copy-start | bytes 15364 | tf_op jit(solution)/shard_map/while
  1595.6 105.0 %all-gather.25.cloned.1.call-start = ((), (), s32[]{:S(2)}) async-start(), calls=%async_computation.24 | async-start | bytes 6553600 | tf_op jit(solution)/shard_map/while/body/eval_jaxpr/all_gather | solution.py:99
  1660.0 183.5 %reduce-scatter.33.cloned.1.call-start = ((), (), s32[]{:S(2)}) async-start(), calls=%async_computation.25 | async-start | bytes 6553600 | tf_op jit(solution)/shard_map/while/body/eval_jaxpr/reduce_scatter | solution.py:109
  1792.0 54.3 %copy-start.70 = (f32[1280]{0:T(1024)S(1)}, f32[1280]{0:T(1024)}, u32[]{:S(2)}) copy-start(f32[1280]{0:T(1024)} %get-tuple-element.1323) | copy-start | bytes 15364 | tf_op jit(solution)/shard_map/while
  1792.0 111.0 %all-gather.27.cloned.1.call-start = ((), (), s32[]{:S(2)}) async-start(), calls=%async_computation.26 | async-start | bytes 6553600 | tf_op jit(solution)/shard_map/while/body/eval_jaxpr/all_gather | solution.py:169
  1846.2 13.6 copy-start.30
  1846.2 13.6 copy-start.83
  1862.4 332.8 %reduce-scatter.35.cloned.1.call-start = ((), (), s32[]{:S(2)}) async-start(), calls=%async_computation.27 | async-start | bytes 6553600 | tf_op jit(solution)/shard_map/while/body/eval_jaxpr/reduce_scatter | solution.py:186
  1948.8 12.1 copy-start.6
  1999.6 12.1 copy-start.6
  2050.4 12.1 copy-start.6
  2101.3 12.1 copy-start.6
  2143.6 51.6 %copy-start.14 = (f32[512,1280]{1,0:T(8,128)S(1)}, f32[512,1280]{1,0:T(8,128)}, u32[]{:S(2)}) copy-start(f32[512,1280]{1,0:T(8,128)} %copy-done.13) | copy-start | bytes 7864324 | tf_op jit(solution)/shard_map/while
  2143.6 51.6 %copy-start.60 = (f32[1280]{0:T(1024)S(1)}, f32[1280]{0:T(1024)}, u32[]{:S(2)}) copy-start(f32[1280]{0:T(1024)} %get-tuple-element.1312) | copy-start | bytes 15364 | tf_op jit(solution)/shard_map/while
  2143.7 51.6 %copy-start.66 = (f32[512]{0:T(512)S(1)}, f32[512]{0:T(512)}, u32[]{:S(2)}) copy-start(f32[512]{0:T(512)} %copy-done.65) | copy-start | bytes 6148 | tf_op jit(solution)/shard_map/while
  2143.7 107.7 %all-gather.29.cloned.1.call-start = ((), (), s32[]{:S(2)}) async-start(), calls=%async_computation.28 | async-start | bytes 6553600 | tf_op jit(solution)/shard_map/while/body/eval_jaxpr/all_gather | solution.py:169
  2210.8 347.6 %reduce-scatter.37.cloned.1.call-start = ((), (), s32[]{:S(2)}) async-start(), calls=%async_computation.29 | async-start | bytes 6553600 | tf_op jit(solution)/shard_map/while/body/eval_jaxpr/reduce_scatter | solution.py:186
  2212.3 13.6 slice-start.10
  2212.3 13.6 slice-start.18
  2395.7 12.1 copy-start.4
  2505.6 26.1 copy-start.18
  2572.8 114.7 %reduce-scatter.27.cloned.1.call-start = ((), (), s32[]{:S(2)}) async-start(), calls=%async_computation.20 | async-start | bytes 8192000
  2604.7 122.8 %reduce-scatter.29.cloned.1.call-start = ((), (), s32[]{:S(2)}) async-start(), calls=%async_computation.21 | async-start | bytes 8192000
  2640.5 155.9 %reduce-scatter.25.cloned.1.call-start = ((), (), s32[]{:S(2)}) async-start(), calls=%async_computation.19 | async-start | bytes 1843200
  2652.6 245.5 %reduce-scatter.23.cloned.1.call-start = ((), (), s32[]{:S(2)}) async-start(), calls=%async_computation.18 | async-start | bytes 5529600
  2687.4 280.6 %reduce-scatter.19.cloned.1.call-start = ((), (), s32[]{:S(2)}) async-start(), calls=%async_computation.16 | async-start | bytes 2211840 | tf_op jit(solution)/shard_map/reduce_scatter | solution.py:283
  2696.2 341.2 %reduce-scatter.21.cloned.1.call-start = ((), (), s32[]{:S(2)}) async-start(), calls=%async_computation.17 | async-start | bytes 2211840 | tf_op jit(solution)/shard_map/reduce_scatter | solution.py:286
  (280 other events, 1120.2 us)
Sparse Core Ops, SparseCore 0:
  10.8 50.2 all-gather.14
  63.8 46.5 all-gather.18
  113.2 46.5 all-gather.12
  162.4 93.3 all-gather.10
  257.2 46.0 all-gather.16
  304.7 47.8 all-gather.20
  366.8 40.4 all-gather.22
  498.7 51.3 reduce-scatter.30
  563.1 40.4 all-gather.24
  694.9 51.3 reduce-scatter.32
  765.3 40.4 all-gather.26
  1046.6 51.3 reduce-scatter.34
  1113.8 40.4 all-gather.28
  1394.2 51.3 reduce-scatter.36
  1464.2 40.4 all-gather.22
  1595.7 51.3 reduce-scatter.30
  1660.1 40.4 all-gather.24
  1792.1 51.3 reduce-scatter.32
  1862.5 40.4 all-gather.26
  2143.8 51.3 reduce-scatter.34
  2211.0 40.4 all-gather.28
  2491.4 51.3 reduce-scatter.36
  2604.8 59.9 reduce-scatter.26
  2667.3 60.0 reduce-scatter.28
  2730.9 65.4 reduce-scatter.24
  2800.4 97.6 reduce-scatter.22
  2901.4 66.5 reduce-scatter.18
  2971.8 65.5 reduce-scatter.20
where the time goes:
time: 3060 us; the launch traced here: 3050 us
  waiting for transfers between devices  1130 us (37%)
  matrix products  879 us (29%)
  other arithmetic  500 us (16%)
  local copies, waits for them, and re-layouts  467 us (15%)
  blocking collectives  40.3 us (1%)
    reduce_scatter x4, waiting for transfers between devices, layer_forward(): lax.psum_scatter(jnp.dot(attended_low, w_out, preferred_element_type=jnp....  206 us
    dot_general x16, matrix products, one_block(): jnp.einsum('qhd,khd->hqk', grad_block, value_low, preferred_element_type=...  199 us
    convert_element_type x16, other arithmetic, one_block(): grad_scores = (softmaxed * (grad_probs - row_inner)).astype(jnp.bfloat16)  194 us
    unnamed x38, local copies, waits for them, and re-layouts  166 us
    while x630, local copies, waits for them, and re-layouts  158 us
    all_gather x4, waiting for transfers between devices, layer_forward(): whole_a = lax.all_gather(low_a, 'tp', axis=0, tiled=True)  152 us
    unnamed x16, waiting for transfers between devices  150 us
    dot_general x16, matrix products, one_block(): jnp.einsum('hqk,qhd->khd', soft_low, grad_block, preferred_element_type=j...  123 us
  transfers between devices with their start and end apart: 28, of which 25 were waited for; matrix products, arithmetic and copies ran while one was open for 12% of the time, Pallas kernels for 0%

commit v1 on v0

v1 whole, which is shorter than its diff:
```python
import functools, math
import jax
import jax.numpy as jnp
from jax import lax
from jax.experimental import pallas as pl
from jax.experimental.pallas import tpu as pltpu
from jax.sharding import PartitionSpec as P

MASKED = -1e30
F32, BF16 = jnp.float32, jnp.bfloat16
EPSILON = 1e-06
SOFT_ONE = 1.442695041
LOG2E = math.log2(math.e)
VMEM_LIMIT = 60 * 2**20

def dot(a, b, dims=((1,), (0,))):
    return lax.dot_general(a, b, (dims, ((), ())), preferred_element_type=F32)

def key_range(row_start, rows, prefix, block):
    full = jnp.maximum(row_start + 1, prefix) // block
    stop = (jnp.maximum(row_start + rows, prefix) + block - 1) // block
    return full, stop

def forward_kernel(prefix_ref, q_ref, k_ref, v_ref, o_ref, lse_ref, key_rows, value_ext, *, pair, dh, bq, bk):
    length = q_ref.shape[1]
    prefix = prefix_ref[0]
    ext = value_ext.shape[1]
    for h in range(pair):
        key_rows[h] = k_ref[h * dh:(h + 1) * dh, :].T
        value_ext[h, :dh] = v_ref[h * dh:(h + 1) * dh, :]
        value_ext[h, dh:] = jnp.ones((ext - dh, length), BF16)

    def one_query(qi, carry):
        start = pl.multiple_of(qi * bq, bq)
        here = pl.ds(start, bq)
        queries = [q_ref[h * dh:(h + 1) * dh, here] for h in range(pair)]
        full, stop = key_range(start, bq, prefix, bk)

        def step(masked, ki, state):
            first = pl.multiple_of(ki * bk, bk)
            if masked:
                rows = first + lax.broadcasted_iota(jnp.int32, (bk, bq), 0)
                cols = start + lax.broadcasted_iota(jnp.int32, (bk, bq), 1)
                allowed = rows <= jnp.maximum(cols, prefix - 1)
            scores = [dot(key_rows[h, pl.ds(first, bk)], queries[h]) for h in range(pair)]
            fresh = []
            for h in range(pair):
                top, total = state[h]
                s = scores[h]
                if masked:
                    s = jnp.where(allowed, s, MASKED)
                new_top = jnp.maximum(top, jnp.max(s, axis=0, keepdims=True))
                p = jnp.exp2(s - new_top).astype(BF16)
                total = total * jnp.exp2(top - new_top) + dot(value_ext[h, :, pl.ds(first, bk)], p)
                fresh.append((new_top, total))
            return tuple(fresh)

        state = tuple((jnp.full((1, bq), MASKED, F32), jnp.zeros((ext, bq), F32)) for _ in range(pair))
        state = lax.fori_loop(0, full, functools.partial(step, False), state)
        state = lax.fori_loop(full, stop, functools.partial(step, True), state)
        for h in range(pair):
            top, total = state[h]
            norm = total[dh:dh + 1]
            o_ref[h * dh:(h + 1) * dh, here] = (total[:dh] / norm).astype(BF16)
            lse_ref[h, :, here] = top + jnp.log2(norm)
        return carry

    lax.fori_loop(0, length // bq, one_query, 0)

def attention_forward(q, k, v, prefix, dh, pair=2, bq=512, bk=512):
    width, length = q.shape
    heads = width // dh
    pair = min(pair, heads); bq = min(bq, length); bk = min(bk, length)
    ext = dh + 16
    spec = pl.BlockSpec((pair * dh, length), lambda i, p: (i, 0))
    return pl.pallas_call(
        functools.partial(forward_kernel, pair=pair, dh=dh, bq=bq, bk=bk),
        grid_spec=pltpu.PrefetchScalarGridSpec(
            num_scalar_prefetch=1, grid=(heads // pair,),
            in_specs=[spec, spec, spec],
            out_specs=[spec, pl.BlockSpec((pair, 1, length), lambda i, p: (i, 0, 0))],
            scratch_shapes=[pltpu.VMEM((pair, length, dh), BF16), pltpu.VMEM((pair, ext, length), BF16)],
        ),
        out_shape=[jax.ShapeDtypeStruct((width, length), BF16), jax.ShapeDtypeStruct((heads, 1, length), F32)],
        compiler_params=pltpu.CompilerParams(vmem_limit_bytes=VMEM_LIMIT),
        cost_estimate=pl.CostEstimate(flops=2 * 2 * 256 * length * length * heads * 2 // 3, bytes_accessed=8 * width * length, transcendentals=0),
        name="attention_forward",
    )(prefix, q, k, v)

def split3(x):
    a = x.astype(BF16)
    r = x - a.astype(F32)
    b = r.astype(BF16)
    c = (r - b.astype(F32)).astype(BF16)
    return a, b, c

def backward_kernel(prefix_ref, q_ref, k_ref, v_ref, o_ref, g_ref, lse_ref, scale_ref, dq_ref, dk_ref, dv_ref, fg_ref,
                    key_rows, key_ext, value_ext, query_ext, grad_ext, dk_acc, dv_acc, *, pair, dh, bq, bk):
    length = q_ref.shape[1]
    prefix = prefix_ref[0]
    ext = key_ext.shape[1]
    pad = ext - dh
    ones = (lax.broadcasted_iota(jnp.int32, (pad, length), 0) < 3).astype(F32).astype(BF16)
    fg_zero = pl.program_id(0) == 0
    @pl.when(fg_zero)
    def _():
        fg_ref[...] = jnp.zeros_like(fg_ref)
    for h in range(pair):
        rows = slice(h * dh, (h + 1) * dh)
        q, k, v, g = q_ref[rows, :], k_ref[rows, :], v_ref[rows, :], g_ref[rows, :]
        key_rows[h] = k.T
        key_ext[h, :dh] = k
        key_ext[h, dh:] = ones
        value_ext[h, :dh] = v
        value_ext[h, dh:] = ones
        delta = jnp.sum(o_ref[rows, :].astype(F32) * g.astype(F32), axis=0, keepdims=True)
        def stack(base, row):
            parts = split3(-row)
            idx = lax.broadcasted_iota(jnp.int32, (pad, length), 0)
            tail = jnp.where(idx == 0, parts[0].astype(F32), jnp.where(idx == 1, parts[1].astype(F32), jnp.where(idx == 2, parts[2].astype(F32), 0.0)))
            return jnp.concatenate([base, tail.astype(BF16)], axis=0).T
        query_ext[h] = stack(q, lse_ref[h])
        grad_ext[h] = stack(g, delta)
        dk_acc[h] = jnp.zeros((dh, length), F32)
        dv_acc[h] = jnp.zeros((dh, length), F32)

    def one_query(qi, carry):
        start = pl.multiple_of(qi * bq, bq)
        here = pl.ds(start, bq)
        full, stop = key_range(start, bq, prefix, bk)

        def step(masked, ki, state):
            first = pl.multiple_of(ki * bk, bk)
            there = pl.ds(first, bk)
            if masked:
                rows = start + lax.broadcasted_iota(jnp.int32, (bq, bk), 0)
                cols = first + lax.broadcasted_iota(jnp.int32, (bq, bk), 1)
                allowed = cols <= jnp.maximum(rows, prefix - 1)
            fresh = []
            s = [dot(query_ext[h, here], key_ext[h, :, there]) for h in range(pair)]
            gp = [dot(grad_ext[h, here], value_ext[h, :, there]) for h in range(pair)]
            for h in range(pair):
                x = jnp.where(allowed, s[h], MASKED) if masked else s[h]
                p = jnp.exp2(x)
                ds = (p * gp[h]).astype(BF16)
                rows = slice(h * dh, (h + 1) * dh)
                dv_acc[h, :, there] += dot(g_ref[rows, here], p.astype(BF16))
                dk_acc[h, :, there] += dot(q_ref[rows, here], ds)
                fresh.append(state[h] + dot(ds, key_rows[h, there]))
            return tuple(fresh)

        state = tuple(jnp.zeros((bq, dh), F32) for _ in range(pair))
        state = lax.fori_loop(0, full, functools.partial(step, False), state)
        state = lax.fori_loop(full, stop, functools.partial(step, True), state)
        for h in range(pair):
            rows = slice(h * dh, (h + 1) * dh)
            dq = state[h].T
            prod = dq * q_ref[rows, here].astype(F32)
            part = prod[:, :128]
            for c in range(1, bq // 128):
                part = part + prod[:, c * 128:(c + 1) * 128]
            fg_ref[...] += part
            dq_ref[rows, here] = (dq * scale_ref[...]).astype(BF16)
        return carry

    lax.fori_loop(0, length // bq, one_query, 0)
    for h in range(pair):
        rows = slice(h * dh, (h + 1) * dh)
        dk_ref[rows, :] = (dk_acc[h] * math.log(2.0)).astype(BF16)
        dv_ref[rows, :] = dv_acc[h].astype(BF16)

def attention_backward(q, k, v, o, g, lse, factor, prefix, dh, pair=2, bq=512, bk=512):
    width, length = q.shape
    heads = width // dh
    pair = min(pair, heads); bq = min(bq, length); bk = min(bk, length)
    ext = dh + 16
    spec = pl.BlockSpec((pair * dh, length), lambda i, p: (i, 0))
    wide = jax.ShapeDtypeStruct((width, length), BF16)
    return pl.pallas_call(
        functools.partial(backward_kernel, pair=pair, dh=dh, bq=bq, bk=bk),
        grid_spec=pltpu.PrefetchScalarGridSpec(
            num_scalar_prefetch=1, grid=(heads // pair,),
            in_specs=[spec] * 5 + [pl.BlockSpec((pair, 1, length), lambda i, p: (i, 0, 0)), pl.BlockSpec((dh, 1), lambda i, p: (0, 0))],
            out_specs=[spec] * 3 + [pl.BlockSpec((dh, 128), lambda i, p: (0, 0))],
            scratch_shapes=[
                pltpu.VMEM((pair, length, dh), BF16),
                pltpu.VMEM((pair, ext, length), BF16),
                pltpu.VMEM((pair, ext, length), BF16),
                pltpu.VMEM((pair, length, ext), BF16),
                pltpu.VMEM((pair, length, ext), BF16),
                pltpu.VMEM((pair, dh, length), F32),
                pltpu.VMEM((pair, dh, length), F32)],
        ),
        out_shape=[wide] * 3 + [jax.ShapeDtypeStruct((dh, 128), F32)],
        compiler_params=pltpu.CompilerParams(vmem_limit_bytes=VMEM_LIMIT),
        cost_estimate=pl.CostEstimate(flops=5 * 2 * 256 * length * length * heads * 2 // 3, bytes_accessed=16 * width * length, transcendentals=0),
        name="attention_backward",
    )(prefix, q, k, v, o, g, lse, factor.reshape(dh, 1))


def rms(x):
    inv = lax.rsqrt(jnp.mean(x * x, axis=-1, keepdims=True) + EPSILON)
    return x * inv, inv


def rms_back(normed, inv, gain, grad):
    scaled = grad * gain
    out = inv * (scaled - normed * jnp.mean(scaled * normed, axis=-1, keepdims=True))
    return out, jnp.sum(grad * normed, axis=0)


def ein(spec, *args):
    return jnp.einsum(spec, *args, preferred_element_type=F32)


class Plan:
    def __init__(self, seqs, tp):
        self.seqs, self.tp, self.ring = seqs, tp, tp // seqs
        self.same_member = [[s * self.ring + r for s in range(seqs)] for r in range(self.ring)]
        self.same_seq = [[s * self.ring + r for r in range(self.ring)] for s in range(seqs)]

    def swap(self, blocks):
        return lax.all_to_all(
            blocks, "tp", 0, 0, tiled=True, axis_index_groups=self.same_member
        )

    def whole(self, rows):
        got = lax.all_gather(rows, "tp", axis=1, axis_index_groups=self.same_seq)
        return got.reshape(-1, rows.shape[-1])

    def share(self, full, positions):
        cut = full.reshape(self.seqs, self.ring, positions, full.shape[-1])
        return lax.psum_scatter(
            cut, "tp", scatter_dimension=1, axis_index_groups=self.same_seq
        )


def gather_heads(plan, shards):
    rows = lax.all_gather(shards, "fsdp", axis=1, tiled=True)
    return lax.all_gather(rows, "tp", axis_index_groups=plan.same_member)


def gather_full(plan, shards):
    part = gather_heads(plan, shards)
    every = lax.all_gather(part, "tp", axis_index_groups=plan.same_seq)
    r, s, m, d, w = every.shape
    return every.transpose(2, 3, 0, 1, 4).reshape(m, d, r * s * w)


def scatter_heads(plan, grads):
    mine = lax.psum_scatter(
        grads.astype(BF16), "tp", scatter_dimension=0, axis_index_groups=plan.same_member
    )
    return lax.psum_scatter(mine, "fsdp", scatter_dimension=1, tiled=True).astype(F32)


def scatter_full(plan, grads):
    m, d, cols = grads.shape
    cut = grads.astype(BF16).reshape(m, d, plan.ring, plan.seqs, -1).transpose(2, 3, 0, 1, 4)
    mine = lax.psum_scatter(cut, "tp", scatter_dimension=0, axis_index_groups=plan.same_seq)
    return scatter_heads(plan, mine)


def layer_forward(plan, x, prefix, qkv, out_t, up, down_t, gains, factor, positions):
    dh = factor.shape[0]
    normed, inv = rms(x)
    low = (normed * gains[0]).astype(BF16)
    h = plan.whole(low.reshape(plan.seqs, positions, -1))
    seqs, _, d, w = qkv.shape
    raw = [ein("sdc,td->sct", qkv[:, c], h).reshape(seqs * w, -1) for c in range(3)]
    scale = jnp.tile(factor * LOG2E, seqs * w // dh)[:, None]
    q, k, v = (raw[0] * scale).astype(BF16), raw[1].astype(BF16), raw[2].astype(BF16)
    att, lse = attention_forward(q, k, v, prefix, dh)
    part = ein("sct,sdc->td", att.reshape(seqs, w, -1), out_t).astype(BF16)
    middle = x + plan.share(part, positions).reshape(x.shape).astype(F32)
    normed_m, inv_m = rms(middle)
    h_m = (normed_m * gains[1]).astype(BF16)
    pre = ein("td,df->tf", h_m, up)
    hidden = jax.nn.silu(pre).astype(BF16)
    result = middle + ein("tf,df->td", hidden, down_t)
    return result, (x, inv, h, q, k, v, att, lse, middle, inv_m, h_m, pre, hidden)


def layer_backward(plan, g, saved, prefix, qkv, out_t, up, down_t, gains, factor, positions):
    x, inv, h, q, k, v, att, lse, middle, inv_m, h_m, pre, hidden = saved
    dh = factor.shape[0]
    seqs, _, d, w = qkv.shape
    length = h.shape[0]
    g_low = g.astype(BF16)
    down_grad = ein("td,tf->df", g_low, hidden)
    g_hidden = ein("td,df->tf", g_low, down_t)
    sig = jax.nn.sigmoid(pre)
    g_pre = (g_hidden * sig * (1.0 + pre * (1.0 - sig))).astype(BF16)
    up_grad = ein("td,tf->df", h_m, g_pre)
    g_hm = ein("tf,df->td", g_pre, up)
    back_m, gain_m = rms_back(middle * inv_m, inv_m, gains[1], g_hm)
    g_mid = g + back_m
    g_all = plan.whole(g_mid.astype(BF16).reshape(plan.seqs, positions, -1))
    att3 = att.reshape(seqs, w, length)
    out_grad = ein("td,sct->sdc", g_all, att3)
    g_att = ein("td,sdc->sct", g_all, out_t).astype(BF16).reshape(seqs * w, length)
    dq, dk, dv, fg = attention_backward(q, k, v, att, g_att, lse, factor, prefix, dh)
    factor_grad = jnp.sum(fg, axis=1) / (factor * LOG2E)
    parts = [a.reshape(seqs, w, length) for a in (dq, dk, dv)]
    qkv_grad = jnp.stack([ein("td,sct->sdc", h, a) for a in parts], axis=1)
    g_ha = sum(ein("sct,sdc->td", a, qkv[:, c]) for c, a in enumerate(parts)).astype(BF16)
    g_ha = plan.share(g_ha, positions).reshape(x.shape).astype(F32)
    back_a, gain_a = rms_back(x * inv, inv, gains[0], g_ha)
    return g_mid + back_a, (qkv_grad, out_grad, up_grad, down_grad, gain_a, gain_m, factor_grad)


def body(inputs, cotangent, w_qkv, w_out, w_up, w_down, norm_gain, query_scale, prefix_len):
    seqs, positions, d = inputs.shape
    tp = lax.axis_size("tp")
    plan = Plan(seqs, tp)
    layers = w_qkv.shape[0]
    dh = query_scale.shape[1]
    unit = SOFT_ONE / math.sqrt(dh)
    factors = jax.nn.softplus(query_scale) * unit
    mine = lax.axis_index("tp") // plan.ring
    prefix = lax.dynamic_slice_in_dim(prefix_len, mine, 1)
    out_shard, down_shard = jnp.swapaxes(w_out, 1, 2), jnp.swapaxes(w_down, 1, 2)

    weights = []
    for l in range(layers):
        qkv = gather_heads(plan, w_qkv[l])
        out_t = gather_heads(plan, out_shard[l][None])[:, 0]
        up, down_t = gather_full(plan, jnp.stack([w_up[l], down_shard[l]]))
        weights.append((qkv, out_t, up, down_t))

    x = plan.swap(inputs.astype(BF16)).astype(F32).reshape(seqs * positions, d)
    g = plan.swap(cotangent.astype(BF16)).astype(F32).reshape(seqs * positions, d)
    kept = []
    for l in range(layers):
        x, saved = layer_forward(plan, x, prefix, *weights[l], norm_gain[l], factors[l], positions)
        kept.append(saved)
    outputs = plan.swap(x.astype(BF16).reshape(seqs, positions, d)).astype(F32)
    grads = [None] * layers
    for l in reversed(range(layers)):
        g, (qkv_g, out_g, up_g, down_g, gain_a, gain_m, f_g) = layer_backward(
            plan, g, kept[l], prefix, *weights[l], norm_gain[l], factors[l], positions
        )
        qkv_g = scatter_heads(plan, qkv_g)
        out_g = scatter_heads(plan, out_g[:, None])[0].T
        up_g, down_g = scatter_full(plan, jnp.stack([up_g, down_g]))
        grads[l] = (qkv_g, out_g, up_g, down_g.T, gain_a, gain_m, f_g)
    input_grad = plan.swap(g.astype(BF16).reshape(seqs, positions, d)).astype(F32)
    qkv_g, out_g, up_g, down_g, gain_a, gain_m, f_g = (jnp.stack(a) for a in zip(*grads))
    scale_g = f_g * jax.nn.sigmoid(query_scale) * unit
    gain_a, gain_m, scale_g = lax.psum((gain_a, gain_m, scale_g), ("fsdp", "tp"))
    return outputs, input_grad, qkv_g, out_g, up_g, down_g, gain_a, gain_m, scale_g


def solution(mesh):
    placed = (
        P("fsdp", "tp", None),
        P("fsdp", "tp", None),
        P(None, None, "fsdp", "tp"),
        P(None, "tp", "fsdp"),
        P(None, "fsdp", "tp"),
        P(None, "tp", "fsdp"),
        P(),
        P(),
        P("fsdp"),
    )
    return jax.shard_map(
        body,
        mesh=mesh,
        in_specs=placed,
        out_specs=placed[:6] + (P(), P(), P()),
        check_vma=False,
    )
```

time: 3060 us -> 1840 us (0.60)
  matrix products: 879 us -> 244 us
  other arithmetic: 500 us -> 84.2 us
  local copies, waits for them, and re-layouts: 467 us -> 175 us
  Pallas kernels: 0 us -> 248 us
  waiting for transfers between devices: 1130 us -> 928 us
  blocking collectives: 40.3 us -> 112 us
    dot_general x160 -> x36, matrix products: 879 us -> 244 us  [ein(): return jnp.einsum(spec, *args, preferred_element_type=F32)]
    reduce_scatter x10 -> x8, waiting for transfers between devices: 442 us -> 23.6 us  [the longest x4 23.5 us: share(): lax.psum_scatter(cut, 'tp', scatter_dimension=1, axis_index_groups=self.s...]
    unnamed x16 -> x38, waiting for transfers between devices: 150 us -> 544 us
    pallas_call x0 -> x4, Pallas kernels: none -> 248 us  [the longest x2 155 us: attention_backward(): pl.pallas_call(functools.partial(backward_kernel, pair=pair, dh=dh, bq=bq...]
    all_gather x14 -> x16, waiting for transfers between devices: 534 us -> 299 us  [the longest x6 141 us: gather_heads(): return lax.all_gather(rows, 'tp', axis_index_groups=plan.same_member)]
    convert_element_type x45 -> x14, other arithmetic: 262 us -> 39.4 us  [the longest x1 7.11 us: body(): g.astype(BF16).reshape(seqs, positions, d)]
    while x636 -> x0, local copies, waits for them, and re-layouts: 183 us -> none
    unnamed x38 -> x193, local copies, waits for them, and re-layouts: 166 us -> 68.6 us
  transfers between devices with their start and end apart: 28 -> 35, of which waited for: 25 -> 22; matrix products, arithmetic and copies ran while one was open for 12% -> 21% of each run, Pallas kernels for 0% -> 9%
where the time goes in v1:
time: 1840 us; the launch traced here: 1830 us
  waiting for transfers between devices  928 us (50%)
  Pallas kernels  248 us (13%)
  matrix products  244 us (13%)
  local copies, waits for them, and re-layouts  175 us (10%)
  blocking collectives  112 us (6%)
  other arithmetic  84.2 us (5%)
  starting transfers between devices  20.5 us (1%)
    unnamed x38, waiting for transfers between devices  544 us
    dot_general x36, matrix products, ein(): return jnp.einsum(spec, *args, preferred_element_type=F32)  244 us
    pallas_call x2, Pallas kernels, attention_backward(): pl.pallas_call(functools.partial(backward_kernel, pair=pair, dh=dh, bq=bq...  155 us
    all_gather x6, waiting for transfers between devices, gather_heads(): return lax.all_gather(rows, 'tp', axis_index_groups=plan.same_member)  141 us
    all_gather x4, waiting for transfers between devices, gather_heads(): rows = lax.all_gather(shards, 'fsdp', axis=1, tiled=True)  108 us
    pallas_call x2, Pallas kernels, attention_forward(): pl.pallas_call(functools.partial(forward_kernel, pair=pair, dh=dh, bq=bq,...  93.3 us
    unnamed x193, local copies, waits for them, and re-layouts  68.6 us
    all_gather x2, blocking collectives, gather_heads(): rows = lax.all_gather(shards, 'fsdp', axis=1, tiled=True)  67.3 us
  transfers between devices with their start and end apart: 35, of which 22 were waited for; matrix products, arithmetic and copies ran while one was open for 21% of the time, Pallas kernels for 9%

profile of v1, /device:TPU:0, one launch (start us, length us, event | category | flops | bytes accessed | tf_op | source)
XLA Modules:
  0.0 1829.4 jit_solution(3851534696632975851)
XLA Ops:
  13.4 48.2 %all-gather.28.cloned.1.call-done = bf16[2,1280,320]{2,0,1:T(2,128)(2,1)} async-done(((bf16[2,160,320]{2,0,1:T(2,128)(2,1)}), bf16[2,1280,320]{2,0,1:T(2,128)(2,1)}) %all-gather.28.cloned.1.call-update) | async-done | bytes 1638416 | tf_op jit(solution)/shard_map/all_gather | solution.py:239
  61.6 6.6 copy.88
  77.0 29.5 %all-to-all-done = bf16[2,512,1280]{2,1,0:T(8,128)(2,1)S(1)} async-done(((bf16[2,512,1280]{2,1,0:T(8,128)(2,1)}), bf16[2,512,1280]{2,1,0:T(8,128)(2,1)S(1)}, u32[]{:S(2)}, u32[]{:S(2)}) %all-to-all-start) | async-done | bytes 2621472 | tf_op jit(solution)/shard_map/all_to_all | solution.py:223
  110.2 11.6 all-gather.40.cloned.1.call-done
  127.2 34.7 %all_gather.82 = bf16[1,1280,320]{2,1,0:T(8,128)(2,1)} all-gather(bf16[1,160,320]{2,1,0:T(8,128)(2,1)S(1)} %get-tuple-element.106), channel_id=1, replica_groups=mesh['fsdp'=8,'tp'=4] {'fsdp'}, dimensions={1}, use_global_device_ids=true | all-gather | bytes 921600 | tf_op jit(solution)/shard_map/all_gather | solution.py:239
  174.5 11.8 all-gather.38.cloned.1.call-done
  186.3 67.5 %all-gather.42.cloned.1.call-done = bf16[2,3,1280,320]{2,3,0,1:T(8,128)(2,1)} async-done(((bf16[1,3,1280,320]{2,3,0,1:T(8,128)(2,1)}), bf16[2,3,1280,320]{2,3,0,1:T(8,128)(2,1)}) %all-gather.42.cloned.1.call-update) | async-done | bytes 4915216 | tf_op jit(solution)/shard_map/all_gather | solution.py:240
  253.7 6.5 fusion.39
  273.7 46.6 %attention_forward.2 = (bf16[640,2048]{1,0:T(8,128)(2,1)}, f32[8,1,2048]{2,1,0:T(1,128)}) custom-call(s32[1]{0:T(128)} %dynamic_slice.3.prefix_ref, bf16[640,2048]{1,0:T(8,128)(2,1)} %fusion.9.q_ref, bf16[640,2048]{1,0:T(8,128)(2,1)} %bitcast.511, bf16[640,2048]{1,0:T(8,128)(2,1)} %bitcast.509), custom_call_target="tpu_custom_call" | custom-call | flops 22906492928 | bytes 10485760 | tf_op jit(solution)/shard_map/attention_forward/pallas_call | solution.py:76
  320.4 6.5 bitcast_convert_fusion.1
  334.0 6.7 copy.95
  341.0 11.4 all-gather.48.cloned.1.call-done
  352.4 6.0 fusion.56
  358.4 11.3 reduce-scatter.33.cloned.1.call-done
  388.1 44.1 %all-gather.50.cloned.1.call-done = bf16[1,3,1280,320]{3,2,1,0:T(8,128)(2,1)} async-done(((bf16[1,3,160,320]{3,2,1,0:T(8,128)(2,1)}), bf16[1,3,1280,320]{3,2,1,0:T(8,128)(2,1)}) %all-gather.50.cloned.1.call-update) | async-done | bytes 2457616 | tf_op jit(solution)/shard_map/all_gather | solution.py:239
  437.6 32.7 %all_gather.94 = bf16[1,1280,320]{2,1,0:T(8,128)(2,1)S(1)} all-gather(bf16[1,160,320]{2,1,0:T(8,128)(2,1)S(1)} %get-tuple-element.105), channel_id=1, replica_groups=mesh['fsdp'=8,'tp'=4] {'fsdp'}, dimensions={1}, use_global_device_ids=true | all-gather | bytes 921600 | tf_op jit(solution)/shard_map/all_gather | solution.py:239
  471.6 7.3 all-gather.56.cloned.1.call-done
  483.3 12.9 all-gather.30.cloned.1.call-done
  501.4 62.5 %all-gather.52.cloned.1.call-done = bf16[2,3,1280,320]{2,3,0,1:T(8,128)(2,1)} async-done(((bf16[1,3,1280,320]{2,3,0,1:T(8,128)(2,1)}), bf16[2,3,1280,320]{2,3,0,1:T(8,128)(2,1)}) %all-gather.52.cloned.1.call-update) | async-done | bytes 4915216 | tf_op jit(solution)/shard_map/all_gather | solution.py:240
  563.9 6.7 fusion.42
  584.1 46.6 %attention_forward.3 = (bf16[640,2048]{1,0:T(8,128)(2,1)}, f32[8,1,2048]{2,1,0:T(1,128)}) custom-call(s32[1]{0:T(128)} %dynamic_slice.3.prefix_ref, bf16[640,2048]{1,0:T(8,128)(2,1)} %fusion.8.q_ref, bf16[640,2048]{1,0:T(8,128)(2,1)} %bitcast.525, bf16[640,2048]{1,0:T(8,128)(2,1)} %bitcast.523), custom_call_target="tpu_custom_call" | custom-call | flops 22906492928 | bytes 10485760 | tf_op jit(solution)/shard_map/attention_forward/pallas_call | solution.py:76
  630.7 6.5 bitcast_convert_fusion
  648.4 7.2 fusion.55
  662.0 5.6 fusion.52
  667.6 11.3 all-to-all-done.2
  678.9 7.4 fusion.23
  694.8 14.6 all-gather.34.cloned.1.call-done
  717.5 77.5 %attention_backward.2 = (bf16[640,2048]{1,0:T(8,128)(2,1)}, bf16[640,2048]{1,0:T(8,128)(2,1)}, bf16[640,2048]{1,0:T(8,128)(2,1)}, f32[80,128]{1,0:T(8,128)}) custom-call(s32[1]{0:T(128)} %dynamic_slice.3.prefix_ref, bf16[640,2048]{1,0:T(8,128)(2,1)} %fusion.8.q_ref, bf16[640,2048]{1,0:T(8,128)(2,1)} %bitcast.526, bf16[640,2048]{1,0:T(8,128)(2,1)} %bitcast.524, ...), custom_call_target="tpu_custom_call" | custom-call | flops 57266229248 | bytes 20971520 | tf_op jit(solution)/shard_map/attention_backward/pallas_call | solution.py:179
  794.9 10.6 fusion.41
  805.5 8.4 fusion.43
  813.9 10.2 fusion.1
  827.5 12.2 reduce-scatter.37.cloned.1.call-done
  839.8 5.5 fusion.7
  845.3 7.3 fusion.6
  852.6 10.0 fusion.15
  862.7 8.8 multiply_reduce_fusion.1
  874.9 7.2 convolution_convert_fusion.1
  882.1 6.9 convolution_convert_fusion
  897.2 6.2 fusion.28
  903.4 7.6 convolution_convert_fusion.2
  916.1 7.1 fusion.36
  936.5 8.1 fusion.33
  944.7 6.7 fusion.32
  957.9 7.4 convolution_convert_fusion.12
  965.3 77.7 %attention_backward.3 = (bf16[640,2048]{1,0:T(8,128)(2,1)}, bf16[640,2048]{1,0:T(8,128)(2,1)}, bf16[640,2048]{1,0:T(8,128)(2,1)}, f32[80,128]{1,0:T(8,128)}) custom-call(s32[1]{0:T(128)} %dynamic_slice.3.prefix_ref, bf16[640,2048]{1,0:T(8,128)(2,1)} %fusion.9.q_ref, bf16[640,2048]{1,0:T(8,128)(2,1)} %bitcast.512, bf16[640,2048]{1,0:T(8,128)(2,1)} %bitcast.510, ...), custom_call_target="tpu_custom_call" | custom-call | flops 57266229248 | bytes 20971520 | tf_op jit(solution)/shard_map/attention_backward/pallas_call | solution.py:179
  1043.0 7.0 fusion.30
  1050.1 6.2 fusion.29
  1067.4 10.6 fusion.38
  1078.0 8.3 fusion.40
  1086.3 9.8 fusion
  1110.7 6.7 copy.109
  1117.4 250.2 %all-reduce.17.cloned.1.call-done = (bf16[2,3,1280,320]{2,3,0,1:T(8,128)(2,1)}, bf16[2,3,1280,320]{2,3,0,1:T(8,128)(2,1)}, bf16[2,2,1280,320]{2,3,0,1:T(8,128)(2,1)}) async-done(((bf16[2,3,1280,320]{2,3,0,1:T(8,128)(2,1)}, bf16[2,3,1280,320]{2,3,0,1:T(8,128)(2,1)}, bf16[2,2,1280,320]{2,3,0,1:T(8,128)(2,1)}), (bf16[2,3,1280,320]{2,3,0,1:T(8,128)(2,1)}, bf16[2,3,1280,320]{2,3,0,1:T(8,128)(2,1)}, ...) | async-done | bytes 13107216
  1380.5 7.7 copy.121
  1388.2 8.3 reshape.355
  1396.6 6.0 copy.117
  1402.6 8.5 reshape.351
  1411.1 9.1 add_convert_fusion
  1429.6 7.1 fusion.21
  1436.7 20.2 %all-to-all-done.1 = bf16[2,512,1280]{2,1,0:T(8,128)(2,1)} async-done(((bf16[2,512,1280]{2,1,0:T(8,128)(2,1)}), bf16[2,512,1280]{2,1,0:T(8,128)(2,1)}, u32[]{:S(2)}, u32[]{:S(2)}) %all-to-all-start.1) | async-done | bytes 2621472 | tf_op jit(solution)/shard_map/all_to_all | solution.py:223
  1468.2 49.8 %reduce-scatter.53.cloned.1.call-done = bf16[160,320]{1,0:T(8,128)(2,1)} async-done(((bf16[1280,320]{1,0:T(8,128)(2,1)}), bf16[160,320]{1,0:T(8,128)(2,1)}) %reduce-scatter.53.cloned.1.call-update) | async-done | bytes 102416
  1522.0 44.7 %all-reduce.6 = (f32[2,1280]{1,0:T(2,128)}, f32[2,1280]{1,0:T(2,128)}, f32[2,80]{1,0:T(2,128)}) all-reduce(f32[2,1280]{1,0:T(2,128)S(1)} %get-tuple-element.127, f32[2,1280]{1,0:T(2,128)S(1)} %get-tuple-element.128, f32[2,80]{1,0:T(2,128)S(1)} %fusion.48), channel_id=1, replica_groups=mesh['fsdp'=8,'tp'=4] {'fsdp','tp'}, use_global_device_ids=true, to_apply=%region_28.29 | all-reduce | flops 5280 | bytes 42240 | tf_op jit(solution)/shard_map/psum | solution.py:350
  1569.4 102.4 %all-reduce.15.cloned.1.call-done = (bf16[2,1280,320]{2,0,1:T(2,128)(2,1)}, bf16[2,1280,320]{2,0,1:T(2,128)(2,1)}) async-done(((bf16[2,1280,320]{2,0,1:T(2,128)(2,1)}, bf16[2,1280,320]{2,0,1:T(2,128)(2,1)}), (bf16[2,1280,320]{2,0,1:T(2,128)(2,1)}, bf16[2,1280,320]{2,0,1:T(2,128)(2,1)})) %all-reduce.15.cloned.1.call-update) | async-done | bytes 3276816
  1675.4 69.7 %reduce-scatter.51.cloned.1.call-done = bf16[160,960]{1,0:T(8,128)(2,1)} async-done(((bf16[1280,960]{1,0:T(8,128)(2,1)}), bf16[160,960]{1,0:T(8,128)(2,1)}) %reduce-scatter.51.cloned.1.call-update) | async-done | bytes 307216
  1746.9 71.3 %reduce-scatter.49.cloned.1.call-done = bf16[160,960]{1,0:T(8,128)(2,1)} async-done(((bf16[1280,960]{1,0:T(8,128)(2,1)}), bf16[160,960]{1,0:T(8,128)(2,1)}) %reduce-scatter.49.cloned.1.call-update) | async-done | bytes 307216
  (363 shorter events, 253.3 us)
Async XLA Ops:
  7.2 54.4 %all-gather.28.cloned.1.call-start = ((), (), s32[]{:S(2)}) async-start(), calls=%async_computation.17 | async-start | bytes 2211840 | tf_op jit(solution)/shard_map/all_gather | solution.py:239
  11.2 110.6 %all-gather.40.cloned.1.call-start = ((), (), s32[]{:S(2)}) async-start(), calls=%async_computation.30 | async-start | bytes 3317760 | tf_op jit(solution)/shard_map/all_gather | solution.py:239
  13.3 155.7 %all-gather.46.cloned.1.call-start = ((), (), s32[]{:S(2)}) async-start(), calls=%async_computation.33 | async-start | bytes 4915200 | tf_op jit(solution)/shard_map/all_gather | solution.py:240
  72.5 34.1 %all-to-all-start = ((bf16[2,512,1280]{2,1,0:T(8,128)(2,1)}), bf16[2,512,1280]{2,1,0:T(8,128)(2,1)S(1)}, u32[]{:S(2)}, u32[]{:S(2)}) async-start(bf16[2,512,1280]{2,1,0:T(8,128)(2,1)} %convert_element_type.196), calls=%async_computation | async-start | bytes 5242880 | tf_op jit(solution)/shard_map/all_to_all | solution.py:223
  76.3 109.9 %all-gather.38.cloned.1.call-start = ((), (), s32[]{:S(2)}) async-start(), calls=%async_computation.29 | async-start | bytes 7864320 | tf_op jit(solution)/shard_map/all_gather | solution.py:228
  77.0 33.2 %copy-start.26 = (f32[1280]{0:T(1024)}, f32[1280]{0:T(1024)S(1)}, u32[]{:S(2)}) copy-start(f32[1280]{0:T(1024)S(1)} %get-tuple-element.79) | copy-start | bytes 15364
  77.0 296.8 %copy-start.28 = (f32[1280]{0:T(1024)}, f32[1280]{0:T(1024)S(1)}, u32[]{:S(2)}) copy-start(f32[1280]{0:T(1024)S(1)} %get-tuple-element.78) | copy-start | bytes 15364
  77.0 306.7 %copy-start.31 = (f32[1280]{0:T(1024)}, f32[1280]{0:T(1024)S(1)}, u32[]{:S(2)}) copy-start(f32[1280]{0:T(1024)S(1)} %get-tuple-element.80) | copy-start | bytes 15364
  106.5 267.3 %copy-start = (bf16[2,512,1280]{2,1,0:T(8,128)(2,1)}, bf16[2,512,1280]{2,1,0:T(8,128)(2,1)S(1)}, u32[]{:S(2)}) copy-start(bf16[2,512,1280]{2,1,0:T(8,128)(2,1)S(1)} %all-to-all-done) | copy-start | bytes 7864324
  108.0 19.1 %copy-start.38 = (f32[2,512]{1,0:T(2,128)}, f32[2,512]{1,0:T(2,128)S(1)}, u32[]{:S(2)}) copy-start(f32[2,512]{1,0:T(2,128)S(1)} %get-tuple-element.108) | copy-start | bytes 12292
  110.2 17.0 copy-start.25
  110.2 143.5 %all-gather.42.cloned.1.call-start = ((), (), s32[]{:S(2)}) async-start(), calls=%async_computation.31 | async-start | bytes 7372800 | tf_op jit(solution)/shard_map/all_gather | solution.py:240
  127.1 193.2 %all-gather.44.cloned.1.call-start = ((), (), s32[]{:S(2)}) async-start(), calls=%async_computation.32 | async-start | bytes 2457600 | tf_op jit(solution)/shard_map/all_gather | solution.py:240
  164.1 169.9 %all-gather.32.cloned.1.call-start = ((), (), s32[]{:S(2)}) async-start(), calls=%async_computation.20 | async-start | bytes 2211840 | tf_op jit(solution)/shard_map/all_gather | solution.py:239
  165.7 186.7 %all-gather.48.cloned.1.call-start = ((), (), s32[]{:S(2)}) async-start(), calls=%async_computation.34 | async-start | bytes 9830400 | tf_op jit(solution)/shard_map/all_gather | solution.py:245
  172.9 196.8 %reduce-scatter.33.cloned.1.call-start = ((), (), s32[]{:S(2)}) async-start(), calls=%async_computation.16 | async-start | bytes 7864320 | tf_op jit(solution)/shard_map/reduce_scatter | solution.py:233
  253.7 8.4 copy-start.57
  329.7 102.5 %all-gather.50.cloned.1.call-start = ((), (), s32[]{:S(2)}) async-start(), calls=%async_computation.35 | async-start | bytes 3317760 | tf_op jit(solution)/shard_map/all_gather | solution.py:239
  330.2 148.6 %all-gather.56.cloned.1.call-start = ((), (), s32[]{:S(2)}) async-start(), calls=%async_computation.38 | async-start | bytes 4915200 | tf_op jit(solution)/shard_map/all_gather | solution.py:240
  340.7 155.5 %all-gather.30.cloned.1.call-start = ((), (), s32[]{:S(2)}) async-start(), calls=%async_computation.18 | async-start | bytes 7864320 | tf_op jit(solution)/shard_map/all_gather | solution.py:228
  388.1 175.8 %all-gather.52.cloned.1.call-start = ((), (), s32[]{:S(2)}) async-start(), calls=%async_computation.36 | async-start | bytes 7372800 | tf_op jit(solution)/shard_map/all_gather | solution.py:240
  437.5 193.2 %all-gather.54.cloned.1.call-start = ((), (), s32[]{:S(2)}) async-start(), calls=%async_computation.37 | async-start | bytes 2457600 | tf_op jit(solution)/shard_map/all_gather | solution.py:240
  471.5 176.8 %all-gather.58.cloned.1.call-start = ((), (), s32[]{:S(2)}) async-start(), calls=%async_computation.39 | async-start | bytes 9830400 | tf_op jit(solution)/shard_map/all_gather | solution.py:245
  482.7 172.8 %reduce-scatter.35.cloned.1.call-start = ((), (), s32[]{:S(2)}) async-start(), calls=%async_computation.19 | async-start | bytes 7864320 | tf_op jit(solution)/shard_map/reduce_scatter | solution.py:233
  563.9 8.5 copy-start.58
  644.2 34.7 %all-to-all-start.2 = ((bf16[2,512,1280]{2,1,0:T(8,128)(2,1)}), bf16[2,512,1280]{2,1,0:T(8,128)(2,1)S(1)}, u32[]{:S(2)}, u32[]{:S(2)}) async-start(bf16[2,512,1280]{2,1,0:T(8,128)(2,1)} %convert_element_type.230), calls=%async_computation.4 | async-start | bytes 5242880 | tf_op jit(solution)/shard_map/all_to_all | solution.py:223
  648.1 61.2 %all-gather.34.cloned.1.call-start = ((), (), s32[]{:S(2)}) async-start(), calls=%async_computation.21 | async-start | bytes 7864320 | tf_op jit(solution)/shard_map/all_gather | solution.py:228
  694.0 145.8 %reduce-scatter.37.cloned.1.call-start = ((), (), s32[]{:S(2)}) async-start(), calls=%async_computation.22 | async-start | bytes 7864320 | tf_op jit(solution)/shard_map/reduce_scatter | solution.py:233
  794.9 10.6 copy-start.67
  805.5 8.4 copy-start.64
  826.9 12.9 copy-start.32
  826.9 12.9 copy-start.35
  826.9 96.5 %all-gather.36.cloned.1.call-start = ((), (), s32[]{:S(2)}) async-start(), calls=%async_computation.23 | async-start | bytes 7864320 | tf_op jit(solution)/shard_map/all_gather | solution.py:228
  827.5 44.0 %copy-start.40 = (f32[1,4,2,128]{3,1,2,0:T(4,128)}, f32[1,4,2,128]{3,1,2,0:T(4,128)S(1)}, u32[]{:S(2)}) copy-start(f32[1,4,2,128]{3,1,2,0:T(4,128)S(1)} %copy.137) | copy-start | bytes 12292
  852.6 18.9 %copy-start.9 = (f32[1024,1280]{1,0:T(8,128)}, f32[1024,1280]{1,0:T(8,128)S(1)}, u32[]{:S(2)}) copy-start(f32[1024,1280]{1,0:T(8,128)S(1)} %fusion.6) | copy-start | bytes 15728644
  852.6 10.1 copy-start.1
  852.6 10.1 copy-start.5
  852.6 10.1 copy-start.19
  852.6 10.1 copy-start.29
  874.7 83.1 %reduce-scatter.45.cloned.1.call-start = ((), (), s32[]{:S(2)}) async-start(), calls=%async_computation.27 | async-start | bytes 9830400 | tf_op jit(solution)/shard_map/reduce_scatter | solution.py:260
  892.3 170.3 %all-reduce.13.cloned.1.call-start = ((), (), s32[]{:S(2)}) async-start(), calls=%async_computation.44 | async-start | bytes 13107200
  892.6 10.8 slice-start
  914.4 184.4 %reduce-scatter.43.cloned.1.call-start = ((), (), s32[]{:S(2)}) async-start(), calls=%async_computation.26 | async-start | bytes 2457600 | tf_op jit(solution)/shard_map/reduce_scatter | solution.py:251
  923.3 181.2 %reduce-scatter.41.cloned.1.call-start = ((), (), s32[]{:S(2)}) async-start(), calls=%async_computation.25 | async-start | bytes 2457600 | tf_op jit(solution)/shard_map/reduce_scatter | solution.py:251
  934.7 176.0 %reduce-scatter.47.cloned.1.call-start = ((), (), s32[]{:S(2)}) async-start(), calls=%async_computation.28 | async-start | bytes 4915200 | tf_op jit(solution)/shard_map/reduce_scatter | solution.py:251
  936.5 14.9 slice-start.2
  957.8 409.7 %all-reduce.17.cloned.1.call-start = ((), (), s32[]{:S(2)}) async-start(), calls=%async_computation.46 | async-start | bytes 26214400
  1043.0 13.3 slice-start.4
  1067.1 358.5 %reduce-scatter.39.cloned.1.call-start = ((), (), s32[]{:S(2)}) async-start(), calls=%async_computation.24 | async-start | bytes 7864320 | tf_op jit(solution)/shard_map/reduce_scatter | solution.py:233
  1067.4 10.6 copy-start.69
  1098.8 368.0 %reduce-scatter.55.cloned.1.call-start = ((), (), s32[]{:S(2)}) async-start(), calls=%async_computation.43 | async-start | bytes 1105920
  1104.4 413.6 %reduce-scatter.53.cloned.1.call-start = ((), (), s32[]{:S(2)}) async-start(), calls=%async_computation.42 | async-start | bytes 1105920
  1110.1 561.8 %all-reduce.15.cloned.1.call-start = ((), (), s32[]{:S(2)}) async-start(), calls=%async_computation.45 | async-start | bytes 7864320
  1375.0 370.1 %reduce-scatter.51.cloned.1.call-start = ((), (), s32[]{:S(2)}) async-start(), calls=%async_computation.41 | async-start | bytes 2949120
  1388.2 8.3 copy-start.46
  1396.5 421.7 %reduce-scatter.49.cloned.1.call-start = ((), (), s32[]{:S(2)}) async-start(), calls=%async_computation.40 | async-start | bytes 2949120
  1402.6 8.5 copy-start.17
  1420.2 9.3 copy-start.30
  1420.2 9.3 copy-start.41
  1420.3 9.3 copy-start.43
  1420.3 36.7 %all-to-all-start.1 = ((bf16[2,512,1280]{2,1,0:T(8,128)(2,1)}), bf16[2,512,1280]{2,1,0:T(8,128)(2,1)}, u32[]{:S(2)}, u32[]{:S(2)}) async-start(bf16[2,512,1280]{2,1,0:T(8,128)(2,1)} %bitcast.482), calls=%async_computation.3 | async-start | bytes 5242880 | tf_op jit(solution)/shard_map/all_to_all | solution.py:223
  1436.7 24.1 %copy-start.71 = (u32[32]{0:T(128)S(1)}, u32[32]{0:T(128)}, u32[]{:S(2)}) copy-start(u32[32]{0:T(128)} %constant.67) | copy-start | bytes 388
  1436.7 25.4 %copy-start.50 = (f32[1280]{0:T(1024)S(1)}, f32[1280]{0:T(1024)}, u32[]{:S(2)}) copy-start(f32[1280]{0:T(1024)} %get-tuple-element.71) | copy-start | bytes 15364
  1456.9 109.7 %all-to-all-start.3 = ((bf16[2,512,1280]{2,1,0:T(8,128)(2,1)}), bf16[2,512,1280]{2,1,0:T(8,128)(2,1)S(1)}, u32[]{:S(2)}, u32[]{:S(2)}) async-start(bf16[2,512,1280]{2,1,0:T(8,128)(2,1)} %bitcast.440), calls=%async_computation.7 | async-start | bytes 5242880 | tf_op jit(solution)/shard_map/all_to_all | solution.py:223
  (53 other events, 270.7 us)
Sparse Core Ops, SparseCore 0:
  11.3 50.2 all-gather.27
  64.4 57.4 all-gather.39
  124.0 45.0 all-gather.45
  171.0 15.2 all-gather.37
  187.7 66.0 all-gather.41
  255.7 27.9 all-gather.43
  286.4 47.5 all-gather.31
  336.2 16.2 all-gather.47
  355.3 14.3 reduce-scatter.32
  372.6 59.5 all-gather.49
  433.8 45.0 all-gather.55
  480.9 15.2 all-gather.29
  497.8 66.0 all-gather.51
  565.9 27.9 all-gather.53
  595.4 17.1 all-gather.57
  640.1 12.9 reduce-scatter.34
  694.1 15.2 all-gather.33
  827.0 12.7 reduce-scatter.36
  874.8 16.4 all-gather.35
  893.6 15.9 reduce-scatter.44
  914.6 33.7 all-reduce.12
  950.7 27.9 reduce-scatter.42
  981.0 26.7 reduce-scatter.40
  1010.0 44.7 reduce-scatter.46
  1067.2 300.2 all-reduce.16
  1370.3 13.1 reduce-scatter.38
  1387.7 64.6 reduce-scatter.54
  1455.7 62.2 reduce-scatter.52
  1522.1 149.7 all-reduce.14
  1675.6 69.4 reduce-scatter.50
  1749.0 69.1 reduce-scatter.48

commit v2 on v1

v2 whole, which is shorter than its diff:
```python
import functools, math
import jax
import jax.numpy as jnp
from jax import lax
from jax.experimental import pallas as pl
from jax.experimental.pallas import tpu as pltpu
from jax.sharding import PartitionSpec as P

MASKED = -1e30
F32, BF16 = jnp.float32, jnp.bfloat16
EPSILON = 1e-06
SOFT_ONE = 1.442695041
LOG2E = math.log2(math.e)
MESH = pl.DeviceIdType.MESH
HINT = 1
VMEM_LIMIT = 60 * 2**20

def dot(a, b, dims=((1,), (0,))):
    return lax.dot_general(a, b, (dims, ((), ())), preferred_element_type=F32)

def key_range(row_start, rows, prefix, block):
    full = jnp.maximum(row_start + 1, prefix) // block
    stop = (jnp.maximum(row_start + rows, prefix) + block - 1) // block
    return full, stop

def forward_kernel(prefix_ref, order_ref, q_ref, k_ref, v_ref, o_ref, lse_ref, key_rows, value_ext, *, pair, dh, bq, bk):
    length = q_ref.shape[1]
    prefix = prefix_ref[0]
    ext = value_ext.shape[1]
    for h in range(pair):
        key_rows[h] = k_ref[h * dh:(h + 1) * dh, :].T
        value_ext[h, :dh] = v_ref[h * dh:(h + 1) * dh, :]
        value_ext[h, dh:] = jnp.ones((ext - dh, length), BF16)

    def one_query(qi, carry):
        start = qi * bq
        here = pl.ds(pl.multiple_of(order_ref[qi] * bq, bq), bq)
        queries = [q_ref[h * dh:(h + 1) * dh, here] for h in range(pair)]
        full, stop = key_range(start, bq, prefix, bk)

        def step(masked, ki, state):
            first = ki * bk
            there = pl.ds(pl.multiple_of(order_ref[ki] * bk, bk), bk)
            if masked:
                rows = first + lax.broadcasted_iota(jnp.int32, (bk, bq), 0)
                cols = start + lax.broadcasted_iota(jnp.int32, (bk, bq), 1)
                allowed = rows <= jnp.maximum(cols, prefix - 1)
            scores = [dot(key_rows[h, there], queries[h]) for h in range(pair)]
            fresh = []
            for h in range(pair):
                top, total = state[h]
                s = scores[h]
                if masked:
                    s = jnp.where(allowed, s, MASKED)
                new_top = jnp.maximum(top, jnp.max(s, axis=0, keepdims=True))
                p = jnp.exp2(s - new_top).astype(BF16)
                total = total * jnp.exp2(top - new_top) + dot(value_ext[h, :, there], p)
                fresh.append((new_top, total))
            return tuple(fresh)

        state = tuple((jnp.full((1, bq), MASKED, F32), jnp.zeros((ext, bq), F32)) for _ in range(pair))
        state = lax.fori_loop(0, full, functools.partial(step, False), state)
        state = lax.fori_loop(full, stop, functools.partial(step, True), state)
        for h in range(pair):
            top, total = state[h]
            norm = total[dh:dh + 1]
            o_ref[h * dh:(h + 1) * dh, here] = (total[:dh] / norm).astype(BF16)
            lse_ref[h, :, here] = top + jnp.log2(norm)
        return carry

    lax.fori_loop(0, length // bq, one_query, 0)

def attention_forward(q, k, v, prefix, order, dh, pair=4):
    width, length = q.shape
    heads = width // dh
    pair = min(pair, heads)
    bq = bk = length // order.shape[0]
    ext = dh + 16
    spec = pl.BlockSpec((pair * dh, length), lambda i, p, o: (i, 0))
    return pl.pallas_call(
        functools.partial(forward_kernel, pair=pair, dh=dh, bq=bq, bk=bk),
        grid_spec=pltpu.PrefetchScalarGridSpec(
            num_scalar_prefetch=2, grid=(heads // pair,),
            in_specs=[spec, spec, spec],
            out_specs=[spec, pl.BlockSpec((pair, 1, length), lambda i, p, o: (i, 0, 0))],
            scratch_shapes=[pltpu.VMEM((pair, length, dh), BF16), pltpu.VMEM((pair, ext, length), BF16)],
        ),
        out_shape=[jax.ShapeDtypeStruct((width, length), BF16), jax.ShapeDtypeStruct((heads, 1, length), F32)],
        compiler_params=pltpu.CompilerParams(vmem_limit_bytes=VMEM_LIMIT),
        cost_estimate=pl.CostEstimate(flops=int(HINT * 600 * length * length * heads), bytes_accessed=int(HINT * 8 * width * length), transcendentals=0),
        name="attention_forward",
    )(prefix, order, q, k, v)

def split3(x):
    a = x.astype(BF16)
    r = x - a.astype(F32)
    b = r.astype(BF16)
    c = (r - b.astype(F32)).astype(BF16)
    return a, b, c

def backward_kernel(prefix_ref, order_ref, q_ref, k_ref, v_ref, o_ref, g_ref, lse_ref, scale_ref, dq_ref, dk_ref, dv_ref, fg_ref,
                    key_rows, key_ext, value_ext, query_ext, grad_ext, dk_acc, dv_acc, *, pair, dh, bq, bk):
    length = q_ref.shape[1]
    prefix = prefix_ref[0]
    ext = key_ext.shape[1]
    pad = ext - dh
    ones = (lax.broadcasted_iota(jnp.int32, (pad, length), 0) < 3).astype(F32).astype(BF16)
    fg_zero = pl.program_id(0) == 0
    @pl.when(fg_zero)
    def _():
        fg_ref[...] = jnp.zeros_like(fg_ref)
    for h in range(pair):
        rows = slice(h * dh, (h + 1) * dh)
        q, k, v, g = q_ref[rows, :], k_ref[rows, :], v_ref[rows, :], g_ref[rows, :]
        key_rows[h] = k.T
        key_ext[h, :dh] = k
        key_ext[h, dh:] = ones
        value_ext[h, :dh] = v
        value_ext[h, dh:] = ones
        delta = jnp.sum(o_ref[rows, :].astype(F32) * g.astype(F32), axis=0, keepdims=True)
        def stack(base, row):
            parts = split3(-row)
            idx = lax.broadcasted_iota(jnp.int32, (pad, length), 0)
            tail = jnp.where(idx == 0, parts[0].astype(F32), jnp.where(idx == 1, parts[1].astype(F32), jnp.where(idx == 2, parts[2].astype(F32), 0.0)))
            return jnp.concatenate([base, tail.astype(BF16)], axis=0).T
        query_ext[h] = stack(q, lse_ref[h])
        grad_ext[h] = stack(g, delta)
        dk_acc[h] = jnp.zeros((dh, length), F32)
        dv_acc[h] = jnp.zeros((dh, length), F32)

    def one_query(qi, carry):
        start = qi * bq
        here = pl.ds(pl.multiple_of(order_ref[qi] * bq, bq), bq)
        full, stop = key_range(start, bq, prefix, bk)

        def step(masked, ki, state):
            first = ki * bk
            there = pl.ds(pl.multiple_of(order_ref[ki] * bk, bk), bk)
            if masked:
                rows = start + lax.broadcasted_iota(jnp.int32, (bq, bk), 0)
                cols = first + lax.broadcasted_iota(jnp.int32, (bq, bk), 1)
                allowed = cols <= jnp.maximum(rows, prefix - 1)
            fresh = []
            s = [dot(query_ext[h, here], key_ext[h, :, there]) for h in range(pair)]
            gp = [dot(grad_ext[h, here], value_ext[h, :, there]) for h in range(pair)]
            for h in range(pair):
                x = jnp.where(allowed, s[h], MASKED) if masked else s[h]
                p = jnp.exp2(x)
                ds = (p * gp[h]).astype(BF16)
                rows = slice(h * dh, (h + 1) * dh)
                dv_acc[h, :, there] += dot(g_ref[rows, here], p.astype(BF16))
                dk_acc[h, :, there] += dot(q_ref[rows, here], ds)
                fresh.append(state[h] + dot(ds, key_rows[h, there]))
            return tuple(fresh)

        state = tuple(jnp.zeros((bq, dh), F32) for _ in range(pair))
        state = lax.fori_loop(0, full, functools.partial(step, False), state)
        state = lax.fori_loop(full, stop, functools.partial(step, True), state)
        for h in range(pair):
            rows = slice(h * dh, (h + 1) * dh)
            dq = state[h].T
            prod = dq * q_ref[rows, here].astype(F32)
            part = prod[:, :128]
            for c in range(1, bq // 128):
                part = part + prod[:, c * 128:(c + 1) * 128]
            fg_ref[...] += part
            dq_ref[rows, here] = (dq * scale_ref[...]).astype(BF16)
        return carry

    lax.fori_loop(0, length // bq, one_query, 0)
    for h in range(pair):
        rows = slice(h * dh, (h + 1) * dh)
        dk_ref[rows, :] = (dk_acc[h] * math.log(2.0)).astype(BF16)
        dv_ref[rows, :] = dv_acc[h].astype(BF16)

def attention_backward(q, k, v, o, g, lse, factor, prefix, order, dh, base=0, width=None, pair=2):
    full, length = q.shape
    width = width or full
    heads = width // dh
    pair = min(pair, heads)
    bq = bk = length // order.shape[0]
    ext = dh + 16
    spec = pl.BlockSpec((pair * dh, length), lambda i, p, o: (i, 0))
    skip = base // (pair * dh)
    source = pl.BlockSpec((pair * dh, length), lambda i, p, o: (i + skip, 0))
    wide = jax.ShapeDtypeStruct((width, length), BF16)
    return pl.pallas_call(
        functools.partial(backward_kernel, pair=pair, dh=dh, bq=bq, bk=bk),
        grid_spec=pltpu.PrefetchScalarGridSpec(
            num_scalar_prefetch=2, grid=(heads // pair,),
            in_specs=[source] * 5 + [pl.BlockSpec((pair, 1, length), lambda i, p, o: (i + skip, 0, 0)), pl.BlockSpec((dh, 1), lambda i, p, o: (0, 0))],
            out_specs=[spec] * 3 + [pl.BlockSpec((dh, 128), lambda i, p, o: (0, 0))],
            scratch_shapes=[
                pltpu.VMEM((pair, length, dh), BF16),
                pltpu.VMEM((pair, ext, length), BF16),
                pltpu.VMEM((pair, ext, length), BF16),
                pltpu.VMEM((pair, length, ext), BF16),
                pltpu.VMEM((pair, length, ext), BF16),
                pltpu.VMEM((pair, dh, length), F32),
                pltpu.VMEM((pair, dh, length), F32)],
        ),
        out_shape=[wide] * 3 + [jax.ShapeDtypeStruct((dh, 128), F32)],
        compiler_params=pltpu.CompilerParams(vmem_limit_bytes=VMEM_LIMIT),
        cost_estimate=pl.CostEstimate(flops=int(HINT * 1600 * length * length * heads), bytes_accessed=int(HINT * 16 * width * length), transcendentals=0),
        name="attention_backward",
    )(prefix, order, q, k, v, o, g, lse, factor.reshape(dh, 1))


def rms(x):
    inv = lax.rsqrt(jnp.mean(x * x, axis=-1, keepdims=True) + EPSILON)
    return x * inv, inv


def rms_back(normed, inv, gain, grad):
    scaled = grad * gain
    out = inv * (scaled - normed * jnp.mean(scaled * normed, axis=-1, keepdims=True))
    return out, jnp.sum(grad * normed, axis=0)


def ein(spec, *args):
    return jnp.einsum(spec, *args, preferred_element_type=F32)


def gather_kernel(pieces, pairs, outer, ring, shard_ref, block_ref, *refs):
    outs = [refs[2 * m:2 * m + 2] for m in range(pairs)]
    got_ref = refs[2 * pairs]
    send, recv, local = refs[2 * pairs + 1:]
    f, t = lax.axis_index("fsdp"), lax.axis_index("tp")
    zz, yy = f // 2, f % 2
    across = {"tp": lax.rem(t + ring, 2 * ring)}
    beside = {"fsdp": zz * 2 + 1 - yy}
    along = [{"fsdp": lax.rem(zz + k, outer) * 2 + yy} for k in range(1, outer)]
    peers = along + [across, beside]
    barrier = pltpu.get_barrier_semaphore()
    for peer in peers:
        pl.semaphore_signal(barrier, inc=1, device_id=peer, device_id_type=MESH)
    pl.semaphore_wait(barrier, len(peers))
    used = [0]

    def copy(src, dst, peer):
        slot = used[0]
        used[0] += 1
        return pltpu.make_async_remote_copy(
            src_ref=src, dst_ref=dst, send_sem=send.at[slot], recv_sem=recv.at[slot],
            device_id=peer, device_id_type=MESH,
        )

    count = len(pieces)
    chunks = 4
    step = block_ref.shape[0] // chunks
    blocks = [
        copy(block_ref.at[pl.ds(i * step, step)], got_ref.at[pl.ds(i * step, step)], across)
        for i in range(chunks)
    ]
    own, first, second, third = [], [], [], []
    for i, (m, low, rows, route) in enumerate(pieces):
        part = pl.ds(low, rows)
        w = [out.at[:, :, part] for out in outs[m]]
        src = shard_ref.at[m, part]
        own.append(pltpu.make_async_copy(src, w[0].at[zz, yy], local.at[i]))
        first.append([copy(src, w[0].at[zz, yy], peer) for peer in along])
        if route:
            second.append([copy(w[0].at[:, yy], w[0].at[:, yy], beside)])
            third.append([copy(w[0], w[1], across)])
        else:
            second.append([copy(w[0].at[:, yy], w[1].at[:, yy], across)])
            third.append([copy(w[s].at[:, yy], w[s].at[:, yy], beside) for s in range(2)])

    def begin(i):
        own[i].start()
        for c in first[i]:
            c.start()

    ahead = 3
    for i in range(min(ahead, count)):
        begin(i)
    started = 0
    for b in blocks[:2]:
        b.start()
    started = 2
    for i in range(count + 2):
        if i < count:
            own[i].wait()
            for c in first[i]:
                c.wait_recv()
            for c in second[i]:
                c.start()
            if i + ahead < count:
                begin(i + ahead)
            if started < chunks:
                blocks[started].start()
                started += 1
        if 0 <= i - 1 < count:
            for c in second[i - 1]:
                c.wait_recv()
            for c in third[i - 1]:
                c.start()
        if 0 <= i - 2 < count:
            for c in third[i - 2]:
                c.wait_recv()
    for b in blocks[started:]:
        b.start()
    for i in range(count):
        for c in first[i] + second[i] + third[i]:
            c.wait_send()
    for b in blocks:
        b.wait()


def pieces_of(pairs, rows):
    half = rows // 32 * 16
    return tuple(
        (m, low, size, m_part) for m in range(pairs) for m_part, (low, size) in enumerate(((0, half), (half, rows - half)))
    )


def gather_call(shards, block, pieces, fsdp, ring):
    pairs, rows, w = shards.shape
    outer = fsdp // 2
    slots = 4 + len(pieces) * (outer + 2)
    any_spec = pl.BlockSpec(memory_space=pl.ANY)
    got = pl.pallas_call(
        functools.partial(gather_kernel, pieces, pairs, outer, ring),
        out_shape=[jax.ShapeDtypeStruct((outer, 2, rows, w), BF16)] * (2 * pairs)
        + [jax.ShapeDtypeStruct(block.shape, block.dtype)],
        in_specs=[any_spec] * 2,
        out_specs=[any_spec] * (2 * pairs + 1),
        scratch_shapes=[
            pltpu.SemaphoreType.DMA((slots,)),
            pltpu.SemaphoreType.DMA((slots,)),
            pltpu.SemaphoreType.DMA((len(pieces),)),
        ],
        compiler_params=pltpu.CompilerParams(collective_id=0, has_side_effects=True),
        name="gather_weights",
    )(shards, block)
    return [a.reshape(outer * 2 * rows, w) for a in got[:-1]], got[-1]


class Plan:
    def __init__(self, seqs, tp, fsdp, rows):
        self.seqs, self.tp, self.ring, self.fsdp = seqs, tp, tp // seqs, fsdp
        self.same_member = [[s * self.ring + r for s in range(seqs)] for r in range(self.ring)]
        self.same_seq = [[s * self.ring + r for r in range(self.ring)] for s in range(seqs)]
        self.fast = seqs == 2 and self.ring == 2 and fsdp % 2 == 0 and rows % 32 == 0
        t = lax.axis_index("tp")
        self.seq, self.member = t // self.ring, lax.rem(t, self.ring)

    def across(self, a):
        n = self.tp
        return lax.ppermute(a, "tp", [(t, (t + self.ring) % n) for t in range(n)])

    def core(self, a):
        return lax.ppermute(a, "tp", [(t, t ^ 1) for t in range(self.tp)])

    def pick(self, blocks, index):
        return lax.dynamic_index_in_dim(blocks, index, 0, keepdims=False)

    def order(self, own, other):
        first = self.seq == 0
        return jnp.concatenate([jnp.where(first, own, other), jnp.where(first, other, own)])

    def swap(self, blocks):
        if self.seqs == 2:
            other = self.across(self.pick(blocks, 1 - self.seq).astype(BF16))
            return self.order(self.pick(blocks, self.seq), other.astype(F32))
        got = lax.all_to_all(
            blocks.astype(BF16), "tp", 0, 0, tiled=True, axis_index_groups=self.same_member
        )
        return got.reshape(-1, got.shape[-1]).astype(F32)

    def unswap(self, rows):
        blocks = rows.reshape(self.seqs, -1, rows.shape[-1])
        return self.swap(blocks).reshape(blocks.shape)

    def whole(self, rows):
        if self.fast:
            return jnp.concatenate([rows, self.core(rows)])
        cut = rows.reshape(self.seqs, -1, rows.shape[-1])
        got = lax.all_gather(cut, "tp", axis=1, axis_index_groups=self.same_seq)
        return got.reshape(-1, rows.shape[-1])

    def share(self, full):
        if self.fast:
            own = full.shape[0] // 2
            return full[:own].astype(F32) + self.core(full[own:].astype(BF16)).astype(F32)
        cut = full.astype(BF16).reshape(self.seqs, self.ring, -1, full.shape[-1])
        got = lax.psum_scatter(cut, "tp", scatter_dimension=1, axis_index_groups=self.same_seq)
        return got.reshape(-1, full.shape[-1]).astype(F32)

    def blocks(self, length):
        if self.fast:
            j = jnp.arange(self.tp, dtype=jnp.int32)
            apart = (j % self.ring != self.member).astype(jnp.int32)
            return apart * self.seqs + j // self.ring
        return jnp.arange(max(1, length // 512), dtype=jnp.int32)

    def gather_heads(self, shards):
        rows = lax.all_gather(shards, "fsdp", axis=1, tiled=True)
        if self.fast:
            return jnp.stack([rows, self.across(rows)])
        return lax.all_gather(rows, "tp", axis_index_groups=self.same_member)

    def join(self, every):
        r, s, m, d, w = every.shape
        return every.transpose(2, 3, 0, 1, 4).reshape(m, d, r * s * w)

    def gather_full(self, shards):
        part = self.gather_heads(shards)
        if self.fast:
            return self.join(jnp.stack([part, self.core(part)]))
        return self.join(lax.all_gather(part, "tp", axis_index_groups=self.same_seq))

    def scatter_heads(self, grads):
        if self.fast:
            other = self.across(grads[1].astype(BF16))
            mine = (grads[0].astype(F32) + other.astype(F32)).astype(BF16)
        else:
            mine = lax.psum_scatter(
                grads.astype(BF16), "tp", scatter_dimension=0, axis_index_groups=self.same_member
            )
        return lax.psum_scatter(mine, "fsdp", scatter_dimension=1, tiled=True).astype(F32)

    def scatter_full(self, grads):
        m, d, cols = grads.shape
        if self.fast:
            half = cols // 2
            other = self.core(grads[:, :, half:].astype(BF16))
            mine = grads[:, :, :half].astype(F32) + other.astype(F32)
            mine = mine.astype(BF16).reshape(m, d, self.seqs, -1).transpose(2, 0, 1, 3)
        else:
            cut = grads.astype(BF16).reshape(m, d, self.ring, self.seqs, -1).transpose(2, 3, 0, 1, 4)
            mine = lax.psum_scatter(cut, "tp", scatter_dimension=0, axis_index_groups=self.same_seq)
        return self.scatter_heads(mine)


def layer_forward(plan, x, prefix, order, qkv, out_t, up, down_t, gains, factor):
    dh = factor.shape[0]
    normed, inv = rms(x)
    h = plan.whole((normed * gains[0]).astype(BF16))
    seqs, d, w = out_t.shape
    raw = [ein("sdc,td->sct", qkv[c], h).reshape(seqs * w, -1) for c in range(3)]
    scale = jnp.tile(factor * LOG2E, seqs * w // dh)[:, None]
    q, k, v = (raw[0] * scale).astype(BF16), raw[1].astype(BF16), raw[2].astype(BF16)
    att, lse = attention_forward(q, k, v, prefix, order, dh)
    middle = x + plan.share(ein("sct,sdc->td", att.reshape(seqs, w, -1), out_t))
    normed_m, inv_m = rms(middle)
    h_m = (normed_m * gains[1]).astype(BF16)
    pre = ein("td,df->tf", h_m, up)
    hidden = jax.nn.silu(pre).astype(BF16)
    result = middle + ein("tf,df->td", hidden, down_t)
    return result, (x, inv, h, q, k, v, att, lse, middle, inv_m, h_m, pre, hidden)


def layer_backward(plan, g, saved, prefix, order, qkv, out_t, up, down_t, gains, factor):
    x, inv, h, q, k, v, att, lse, middle, inv_m, h_m, pre, hidden = saved
    dh = factor.shape[0]
    seqs, d, w = out_t.shape
    length = h.shape[0]
    g_low = g.astype(BF16)
    down_grad = ein("td,tf->df", g_low, hidden)
    g_hidden = ein("td,df->tf", g_low, down_t)
    sig = jax.nn.sigmoid(pre)
    g_pre = (g_hidden * sig * (1.0 + pre * (1.0 - sig))).astype(BF16)
    up_grad = ein("td,tf->df", h_m, g_pre)
    mlp_grads = plan.scatter_full(jnp.stack([up_grad, down_grad]))
    g_hm = ein("tf,df->td", g_pre, up)
    back_m, gain_m = rms_back(middle * inv_m, inv_m, gains[1], g_hm)
    g_mid = g + back_m
    g_all = plan.whole(g_mid.astype(BF16))
    att3 = att.reshape(seqs, w, length)
    out_grad = plan.scatter_heads(ein("td,sct->sdc", g_all, att3)[:, None])[0]
    g_att = ein("td,sdc->sct", g_all, out_t).astype(BF16).reshape(seqs * w, length)
    dq, dk, dv, fg = attention_backward(q, k, v, att, g_att, lse, factor, prefix, order, dh)
    factor_grad = jnp.sum(fg, axis=1) / (factor * LOG2E)
    parts = [a.reshape(seqs, w, length) for a in (dq, dk, dv)]
    qkv_grad = plan.scatter_heads(jnp.stack([ein("td,sct->sdc", h, a) for a in parts], axis=1))
    g_ha = plan.share(sum(ein("sct,sdc->td", a, b) for a, b in zip(parts, qkv)))
    back_a, gain_a = rms_back(x * inv, inv, gains[0], g_ha)
    return g_mid + back_a, (qkv_grad, out_grad.T, mlp_grads[0], mlp_grads[1].T, gain_a, gain_m, factor_grad)


TN, NT, TT = ((0,), (0,)), ((1,), (1,)), ((0,), (1,))
ONE = pl.Buffered(1)


def cost(flops, nbytes):
    return pl.CostEstimate(flops=int(flops * HINT), bytes_accessed=int(nbytes * HINT), transcendentals=0)


def params():
    return pltpu.CompilerParams(vmem_limit_bytes=VMEM_LIMIT)


def fixed(shape):
    return pl.BlockSpec(shape, lambda *a: (0,) * len(shape), pipeline_mode=ONE)


def shape_of(shape, dtype=BF16):
    return jax.ShapeDtypeStruct(shape, dtype)


def inverse_rms(x):
    return lax.rsqrt(jnp.mean(x * x, axis=-1, keepdims=True) + EPSILON)


def eight(x):
    return jnp.sum(x.reshape(-1, 8, x.shape[-1]), axis=0)


def join_lanes(dst, refs, low, high):
    width = high - low
    for i, ref in enumerate(refs):
        dst[:, i * width:(i + 1) * width] = ref[:, low:high]


def project_kernel(w, h_ref, qk0, qk1, vo0, vo1, scale_ref, *refs):
    q_ref, k_ref, v_ref = refs[-3:]
    h = h_ref[...]
    for s, (qk, vo) in enumerate(((qk0, vo0), (qk1, vo1))):
        rows = slice(s * w, (s + 1) * w)
        both = dot(qk[...], h, TT)
        q_ref[rows] = (both[:w] * scale_ref[rows]).astype(BF16)
        k_ref[rows] = both[w:].astype(BF16)
        v_ref[rows] = dot(vo[:, :w], h, TT).astype(BF16)


def project(h, qk, vo, scale, base, bufs=None):
    rows, d = h.shape
    w = qk[0].shape[1] // 2
    bt = 512
    steps = rows // bt
    out = pl.BlockSpec((2 * w, bt), lambda i: (0, i + base * steps))
    whole = fixed((d, 2 * w))
    extra = [] if bufs is None else list(bufs)
    return pl.pallas_call(
        functools.partial(project_kernel, w),
        grid=(steps,),
        in_specs=[pl.BlockSpec((bt, d), lambda i: (i, 0))] + [whole] * 4 + [fixed((2 * w, 1))]
        + [pl.BlockSpec(memory_space=pl.ANY)] * len(extra),
        out_specs=[out] * 3,
        out_shape=[shape_of((2 * w, 2 * rows))] * 3,
        input_output_aliases={6 + i: i for i in range(len(extra))},
        compiler_params=params(),
        cost_estimate=cost(2 * rows * d * 6 * w, 4 * rows * d),
        name="project",
    )(h, *qk, *vo, scale, *extra)


def out_kernel(w, att_ref, vo0, vo1, part_ref, mat):
    @pl.when(pl.program_id(0) == 0)
    def _():
        join_lanes(mat, (vo0, vo1), w, 2 * w)

    part_ref[...] = dot(att_ref[...], mat[...], TT).astype(BF16)


def out_project(att, vo, base):
    d, w2 = vo[0].shape
    rows = att.shape[1] // 2
    bt = 512
    steps = rows // bt
    return pl.pallas_call(
        functools.partial(out_kernel, w2 // 2),
        grid=(steps,),
        in_specs=[pl.BlockSpec((w2, bt), lambda i: (0, i + base * steps)), fixed((d, w2)), fixed((d, w2))],
        out_specs=pl.BlockSpec((bt, d), lambda i: (i, 0)),
        out_shape=shape_of((rows, d)),
        scratch_shapes=[pltpu.VMEM((d, w2), BF16)],
        compiler_params=params(),
        cost_estimate=cost(2 * rows * d * w2, 4 * rows * d),
        name="out_project",
    )(att, *vo)


def middle_kernel(w, x_ref, att_ref, got_ref, gm_ref, ga_ref, vo0, vo1, un0, un1, un2, un3,
                  mid_ref, pre_ref, res_ref, h_ref, out_mat, up_mat, down_mat):
    @pl.when(pl.program_id(0) == 0)
    def _():
        join_lanes(out_mat, (vo0, vo1), w, 2 * w)
        join_lanes(up_mat, (un0, un1, un2, un3), 0, w)
        join_lanes(down_mat, (un0, un1, un2, un3), w, 2 * w)

    mid = x_ref[...] + got_ref[...].astype(F32) + dot(att_ref[...], out_mat[...], TT)
    mid_ref[...] = mid
    h_m = (mid * inverse_rms(mid) * gm_ref[...]).astype(BF16)
    pre = dot(h_m, up_mat[...])
    pre_ref[...] = pre
    hidden = (pre / (1.0 + jnp.exp(-pre))).astype(BF16)
    res = mid + dot(hidden, down_mat[...], NT)
    res_ref[...] = res
    h_ref[...] = (res * inverse_rms(res) * ga_ref[...]).astype(BF16)


def middle_call(x, att, got, gain_m, gain_a, vo, un):
    rows, d = x.shape
    w2 = vo[0].shape[1]
    ff = 2 * w2
    bt = 256
    row = pl.BlockSpec((bt, d), lambda i: (i, 0))
    wide = pl.BlockSpec((bt, ff), lambda i: (i, 0))
    return pl.pallas_call(
        functools.partial(middle_kernel, w2 // 2),
        grid=(rows // bt,),
        in_specs=[row, pl.BlockSpec((w2, bt), lambda i: (0, i)), row] + [fixed((1, d))] * 2 + [fixed((d, w2))] * 6,
        out_specs=[row, wide, row, row],
        out_shape=[shape_of((rows, d), F32), shape_of((rows, ff), F32), shape_of((rows, d), F32), shape_of((rows, d))],
        scratch_shapes=[pltpu.VMEM((d, w2), BF16), pltpu.VMEM((d, ff), BF16), pltpu.VMEM((d, ff), BF16)],
        compiler_params=params(),
        cost_estimate=cost(2 * rows * d * (w2 + 2 * ff), 30 * rows * d),
        name="middle",
    )(x, att, got, gain_m, gain_a, *vo, *un)


def mlp_back_kernel(w, g_ref, mid_ref, pre_ref, gm_ref, un0, un1, un2, un3,
                    g_mid_ref, low_ref, gain_ref, o0, o1, o2, o3,
                    up_mat, down_mat, g_all, hid_all, hm_all, gpre_all):
    i = pl.program_id(0)
    bt = g_ref.shape[0]

    @pl.when(i == 0)
    def _():
        join_lanes(up_mat, (un0, un1, un2, un3), 0, w)
        join_lanes(down_mat, (un0, un1, un2, un3), w, 2 * w)
        gain_ref[...] = jnp.zeros_like(gain_ref)

    here = pl.ds(pl.multiple_of(i * bt, bt), bt)
    g = g_ref[...]
    g_low = g.astype(BF16)
    g_all[here] = g_low
    pre = pre_ref[...]
    sig = 1.0 / (1.0 + jnp.exp(-pre))
    hid_all[here] = (pre * sig).astype(BF16)
    g_hidden = dot(g_low, down_mat[...])
    g_pre = (g_hidden * sig * (1.0 + pre * (1.0 - sig))).astype(BF16)
    gpre_all[here] = g_pre
    mid = mid_ref[...]
    inv = inverse_rms(mid)
    normed = mid * inv
    gain = gm_ref[...]
    hm_all[here] = (normed * gain).astype(BF16)
    g_hm = dot(g_pre, up_mat[...], NT)
    gain_ref[...] += eight(g_hm * normed)
    scaled = g_hm * gain
    g_mid = g + inv * (scaled - normed * jnp.mean(scaled * normed, axis=-1, keepdims=True))
    g_mid_ref[...] = g_mid
    low_ref[...] = g_mid.astype(BF16)

    @pl.when(i == pl.num_programs(0) - 1)
    def _():
        d = up_mat.shape[0]
        step = 256

        def chunk(c, carry):
            cols = pl.ds(pl.multiple_of(c * step, step), step)
            up = dot(hm_all[:, cols], gpre_all[...], TN).astype(BF16)
            down = dot(g_all[:, cols], hid_all[...], TN).astype(BF16)
            for b, out in enumerate((o0, o1, o2, o3)):
                out[cols, 0:w] = up[:, b * w:(b + 1) * w]
                out[cols, w:2 * w] = down[:, b * w:(b + 1) * w]
            return carry

        lax.fori_loop(0, d // step, chunk, 0)


def mlp_back(g, mid, pre, gain, un):
    rows, d = g.shape
    ff = pre.shape[1]
    w2 = un[0].shape[1]
    bt = 256
    row = pl.BlockSpec((bt, d), lambda i: (i, 0))
    wide = pl.BlockSpec((bt, ff), lambda i: (i, 0))
    return pl.pallas_call(
        functools.partial(mlp_back_kernel, w2 // 2),
        grid=(rows // bt,),
        in_specs=[row, row, wide, fixed((1, d))] + [fixed((d, w2))] * 4,
        out_specs=[row, row, fixed((8, d))] + [fixed((d, w2))] * 4,
        out_shape=[shape_of((rows, d), F32), shape_of((rows, d)), shape_of((8, d), F32)] + [shape_of((d, w2))] * 4,
        scratch_shapes=[pltpu.VMEM((d, ff), BF16)] * 2
        + [pltpu.VMEM((rows, d), BF16), pltpu.VMEM((rows, ff), BF16), pltpu.VMEM((rows, d), BF16), pltpu.VMEM((rows, ff), BF16)],
        compiler_params=params(),
        cost_estimate=cost(8 * rows * d * ff, 30 * rows * d),
        name="mlp_back",
    )(g, mid, pre, gain, *un)


def grad_att_kernel(w, g_ref, vo0, vo1, *refs):
    out_ref, mat = refs[-2:]

    @pl.when(pl.program_id(0) == 0)
    def _():
        join_lanes(mat, (vo0, vo1), w, 2 * w)

    out_ref[...] = dot(mat[...], g_ref[...], TT).astype(BF16)


def grad_att(g, vo, base, buf=None):
    rows, d = g.shape
    w2 = vo[0].shape[1]
    bt = 512
    steps = rows // bt
    extra = [] if buf is None else [buf]
    return pl.pallas_call(
        functools.partial(grad_att_kernel, w2 // 2),
        grid=(steps,),
        in_specs=[pl.BlockSpec((bt, d), lambda i: (i, 0)), fixed((d, w2)), fixed((d, w2))]
        + [pl.BlockSpec(memory_space=pl.ANY)] * len(extra),
        out_specs=pl.BlockSpec((w2, bt), lambda i: (0, i + base * steps)),
        out_shape=shape_of((w2, 2 * rows)),
        scratch_shapes=[pltpu.VMEM((d, w2), BF16)],
        input_output_aliases={3: 0} if extra else {},
        compiler_params=params(),
        cost_estimate=cost(2 * rows * d * w2, 4 * rows * d),
        name="grad_att",
    )(g, *vo, *extra)


def out_grad_kernel(w, own_ref, other_ref, att_ref, o0, o1):
    half = own_ref.shape[0]
    att = att_ref[...]
    grad = dot(own_ref[...], att[:, :half], TT) + dot(other_ref[...], att[:, half:], TT)
    grad = grad.astype(BF16)
    o0[...] = grad[:, :w]
    o1[...] = grad[:, w:]


def out_grad_call(own, other, att):
    rows, d = own.shape
    w2 = att.shape[0]
    bd = 256
    col = pl.BlockSpec((rows, bd), lambda i: (0, i))
    out = pl.BlockSpec((bd, w2 // 2), lambda i: (i, 0))
    return pl.pallas_call(
        functools.partial(out_grad_kernel, w2 // 2),
        grid=(d // bd,),
        in_specs=[col, col, fixed(att.shape)],
        out_specs=[out] * 2,
        out_shape=[shape_of((d, w2 // 2))] * 2,
        compiler_params=params(),
        cost_estimate=cost(4 * rows * d * w2, 8 * rows * d),
        name="out_grad",
    )(own, other, att)


def weight_grad_kernel(w, own_ref, other_ref, dq_ref, dk_ref, dv_ref, out, stacked):
    half = own_ref.shape[0]

    @pl.when(pl.program_id(0) == 0)
    def _():
        for j, ref in enumerate((dq_ref, dk_ref, dv_ref)):
            stacked[j * w:(j + 1) * w, :] = ref[...]

    grad = dot(own_ref[...], stacked[:, :half], TT) + dot(other_ref[...], stacked[:, half:], TT)
    out[:, :3 * w] = grad.astype(BF16)
    out[:, 3 * w:] = jnp.zeros((out.shape[0], out.shape[1] - 3 * w), BF16)


def weight_grad(own, other, dq, dk, dv, width):
    rows, d = own.shape
    w = dq.shape[0]
    bd = 256
    col = pl.BlockSpec((rows, bd), lambda i: (0, i))
    return pl.pallas_call(
        functools.partial(weight_grad_kernel, w),
        grid=(d // bd,),
        in_specs=[col, col] + [fixed(dq.shape)] * 3,
        out_specs=pl.BlockSpec((bd, width), lambda i: (i, 0)),
        out_shape=shape_of((d, width)),
        scratch_shapes=[pltpu.VMEM((3 * w, 2 * rows), BF16)],
        compiler_params=params(),
        cost_estimate=cost(12 * rows * d * w, 12 * rows * d),
        name="weight_grad",
    )(own, other, dq, dk, dv)


def input_sum(w, grads, qk, vo):
    total = None
    for s in range(2):
        dq, dk, dv = grads[3 * s:3 * s + 3]
        both = jnp.concatenate([dq[...], dk[...]], axis=0)
        part = dot(both, qk[s][...], TT) + dot(dv[...], vo[s][:, :w], TT)
        total = part if total is None else total + part
    return total


def input_other_kernel(w, *refs):
    refs, out_ref = refs[:-1], refs[-1]
    out_ref[...] = input_sum(w, refs[:6], refs[6:8], refs[8:10]).astype(BF16)


def input_other(grads, qk, vo):
    w, length = grads[0].shape
    d, w2 = qk[0].shape
    bt = 512
    steps = length // 2 // bt
    col = pl.BlockSpec((w, bt), lambda i: (0, i + steps))
    return pl.pallas_call(
        functools.partial(input_other_kernel, w),
        grid=(steps,),
        in_specs=[col] * 6 + [fixed((d, w2))] * 4,
        out_specs=pl.BlockSpec((bt, d), lambda i: (i, 0)),
        out_shape=shape_of((length // 2, d)),
        compiler_params=params(),
        cost_estimate=cost(3 * length * d * w2, 4 * length * d),
        name="input_other",
    )(*grads, *qk, *vo)


def input_own_kernel(w, *refs):
    grads, refs = refs[:6], refs[6:]
    got_ref, x_ref, g_ref, gain_ref, qk0, qk1, vo0, vo1, out_ref, sum_ref = refs

    @pl.when(pl.program_id(0) == 0)
    def _():
        sum_ref[...] = jnp.zeros_like(sum_ref)

    g_ha = input_sum(w, grads, (qk0, qk1), (vo0, vo1)) + got_ref[...].astype(F32)
    x = x_ref[...]
    inv = inverse_rms(x)
    normed = x * inv
    sum_ref[...] += eight(g_ha * normed)
    scaled = g_ha * gain_ref[...]
    out_ref[...] = g_ref[...] + inv * (scaled - normed * jnp.mean(scaled * normed, axis=-1, keepdims=True))


def input_own(grads, got, x, g, gain, qk, vo):
    w = grads[0].shape[0]
    rows, d = x.shape
    w2 = 2 * w
    bt = 256
    col = pl.BlockSpec((w, bt), lambda i: (0, i))
    row = pl.BlockSpec((bt, d), lambda i: (i, 0))
    return pl.pallas_call(
        functools.partial(input_own_kernel, w),
        grid=(rows // bt,),
        in_specs=[col] * 6 + [row] * 3 + [fixed((1, d))] + [fixed((d, w2))] * 4,
        out_specs=[row, fixed((8, d))],
        out_shape=[shape_of((rows, d), F32), shape_of((8, d), F32)],
        compiler_params=params(),
        cost_estimate=cost(6 * rows * d * w2, 24 * rows * d),
        name="input_own",
    )(*grads, got, x, g, gain, *qk, *vo)


def total_over_all(plan, a):
    n, f = plan.tp, plan.fsdp
    hop = 1
    while hop < n:
        a = a + lax.ppermute(a, "tp", [(t, t ^ hop) for t in range(n)])
        hop *= 2
    hop = 1
    while hop < f:
        a = a + lax.ppermute(a, "fsdp", [(t, t ^ hop) for t in range(f)])
        hop *= 2
    return a


def add_low(own, got):
    return (own.astype(F32) + got.astype(F32)).astype(BF16)


def scatter_rows(mine):
    return lax.psum_scatter(mine, "fsdp", scatter_dimension=0, tiled=True).astype(F32)


def after(*arrays):
    return lax.optimization_barrier(arrays)


def fast_body(plan, inputs, cotangent, w_qkv, w_out, w_up, w_down, norm_gain, query_scale, prefix_len):
    seqs, positions, d = inputs.shape
    layers, w = w_qkv.shape[0], w_qkv.shape[3]
    dh = query_scale.shape[1]
    unit = SOFT_ONE / math.sqrt(dh)
    factors = jax.nn.softplus(query_scale) * unit
    prefix = lax.dynamic_slice_in_dim(prefix_len, plan.seq, 1)
    order = plan.blocks(positions * plan.tp)
    out_shard, down_shard = jnp.swapaxes(w_out, 1, 2), jnp.swapaxes(w_down, 1, 2)
    pairs = jnp.concatenate(
        [
            jnp.concatenate([w_qkv[:, 0], w_qkv[:, 1]], axis=2)[:, None],
            jnp.concatenate([w_qkv[:, 2], out_shard], axis=2)[:, None],
            jnp.concatenate([w_up, down_shard], axis=2)[:, None],
        ],
        axis=1,
    )

    block = plan.pick(inputs, 1 - plan.seq).astype(BF16)
    got, other = gather_call(pairs[0, :2], block, pieces_of(2, pairs.shape[2]), plan.fsdp, plan.ring)
    qk0, vo0 = got[0:2], got[2:4]

    def along(l, m):
        return lax.all_gather(pairs[l, m], "fsdp", axis=0, tiled=True)

    def both(rows):
        return rows, plan.across(rows)

    def four(pair):
        return (*pair, plan.core(pair[0]), plan.core(pair[1]))

    un0_rows, qk1_rows, vo1_rows, un1_rows = along(0, 2), along(1, 0), along(1, 1), along(1, 2)
    x = plan.order(plan.pick(inputs, plan.seq), other.astype(F32))
    h = (x * inverse_rms(x) * norm_gain[0, 0]).astype(BF16)
    h, un0_rows, qk1_rows, cotangent = after(h, un0_rows, qk1_rows, cotangent)
    un0, qk1 = both(un0_rows), both(qk1_rows)
    cot_block = plan.pick(cotangent, 1 - plan.seq).astype(BF16)
    kept, weights = [], []
    for l in range(layers):
        qk, vo = (qk0, vo0) if l == 0 else (qk1, vo1)
        scale = jnp.tile(factors[l] * LOG2E, 2 * w // dh)[:, None]
        h_other = plan.core(h)
        qkv = project(h, qk, vo, scale, 0)
        q, k, v = project(h_other, qk, vo, scale, 1, qkv)
        att, lse = attention_forward(q, k, v, prefix, order, dh)
        if l == 0:
            att, un0_got, qk1_got, vo1_rows = after(att, un0[1], qk1[1], vo1_rows)
            un, qk1 = four((un0[0], un0_got)), (qk1[0], qk1_got)
            vo1 = both(vo1_rows)
        else:
            att, un1_got, cot_got = after(att, un1[1], cot_got)
            un = four((un1[0], un1_got))
        part = plan.core(out_project(att, vo, 1))
        next_gain = norm_gain[(l + 1) % layers, 0][None]
        mid, pre, res, h_next = middle_call(x, att, part, norm_gain[l, 1][None], next_gain, vo, un)
        kept.append((x, h, h_other, q, k, v, att, lse, mid, pre))
        weights.append((qk, vo, un))
        x, h = res, h_next
        if l == 0:
            h, un1_rows, cot_block = after(h, un1_rows, cot_block)
            un1, cot_got = both(un1_rows), plan.across(cot_block)
    g = plan.order(plan.pick(cotangent, plan.seq), cot_got.astype(F32))
    out_blocks = x.reshape(seqs, positions, d)
    out_send = plan.pick(out_blocks, 1 - plan.seq).astype(BF16)
    g, out_send = after(g, out_send)
    out_got = plan.across(out_send)
    outputs = None
    width = -(-3 * w // 128) * 128
    grads = [None] * layers
    for l in reversed(range(layers)):
        qk, vo, un = weights[l]
        x, h, h_other, q, k, v, att, lse, mid, pre = kept[l]
        g_mid, low, gain_m, u0, u1, u2, u3 = mlp_back(g, mid, pre, norm_gain[l, 1][None], un)
        if outputs is None:
            low, out_got = after(low, out_got)
            outputs = plan.order(plan.pick(out_blocks, plan.seq), out_got.astype(F32)).reshape(out_blocks.shape)
        low_other = plan.core(low)
        g_att = grad_att(low, vo, 0)
        g_att = grad_att(low_other, vo, 1, g_att)
        o0, o1 = out_grad_call(low, low_other, att)
        pad = jnp.zeros((d, width - 3 * w), BF16)
        early = []
        for a, c, o in ((u1, plan.core(u3), o1), (u0, plan.core(u2), o0)):
            early.append(jnp.concatenate([(a.astype(F32) + c.astype(F32)).astype(BF16), o, pad], axis=1))
        g_att, *early = after(g_att, *early)
        early_got = plan.across(early[0])
        dgrads, fgs, pieces = [None] * 6, [], [None] * 2
        for s in (1, 0):
            dq, dk, dv, fg = attention_backward(
                q, k, v, att, g_att, lse, factors[l], prefix, order, dh, s * w, w
            )
            pieces[s] = weight_grad(h, h_other, dq, dk, dv, width)
            if s == 1:
                g_att, pieces[1], early_got = after(g_att, pieces[1], early_got)
                late_got = plan.across(pieces[1])
                mine, g_att = after(add_low(early[1], early_got), g_att)
                early = scatter_rows(mine)
            dgrads[3 * s:3 * s + 3] = [dq, dk, dv]
            fgs.append(fg)
        fg = fgs[0] + fgs[1]
        dgrads[0], pieces[0], late_got = after(dgrads[0], pieces[0], late_got)
        mine, dgrads[0] = after(add_low(pieces[0], late_got), dgrads[0])
        late = scatter_rows(mine)
        part = plan.core(input_other(dgrads, qk, vo))
        g, gain_a = input_own(dgrads, part, x, g_mid, norm_gain[l, 0][None], qk, vo)
        if l > 0:
            g, early = after(g, early)
        factor_grad = jnp.sum(fg, axis=1) / (factors[l] * LOG2E)
        small = jnp.concatenate([jnp.sum(gain_a, axis=0), jnp.sum(gain_m, axis=0), factor_grad])
        grads[l] = (early, late, small)
    input_grad = plan.unswap(g)
    small = jnp.stack([entry[2] for entry in grads])
    small = total_over_all(plan, small)
    early, late = jnp.stack([e[0] for e in grads]), jnp.stack([e[1] for e in grads])
    qkv_g = jnp.stack([late[:, :, c * w:(c + 1) * w] for c in range(3)], axis=1)
    up_g, down_g, out_g = (early[:, :, c * w:(c + 1) * w] for c in range(3))
    scale_g = small[:, 2 * d:] * jax.nn.sigmoid(query_scale) * unit
    return (
        outputs, input_grad, qkv_g, jnp.swapaxes(out_g, 1, 2), up_g, jnp.swapaxes(down_g, 1, 2),
        small[:, :d], small[:, d:2 * d], scale_g,
    )


def body(inputs, cotangent, w_qkv, w_out, w_up, w_down, norm_gain, query_scale, prefix_len):
    seqs, positions, d = inputs.shape
    fsdp, tp = lax.axis_size("fsdp"), lax.axis_size("tp")
    layers = w_qkv.shape[0]
    plan = Plan(seqs, tp, fsdp, w_qkv.shape[2])
    if plan.fast:
        return fast_body(
            plan, inputs, cotangent, w_qkv, w_out, w_up, w_down, norm_gain, query_scale, prefix_len
        )
    dh = query_scale.shape[1]
    unit = SOFT_ONE / math.sqrt(dh)
    factors = jax.nn.softplus(query_scale) * unit
    prefix = lax.dynamic_slice_in_dim(prefix_len, plan.seq, 1)
    order = plan.blocks(positions * tp)
    out_shard, down_shard = jnp.swapaxes(w_out, 1, 2), jnp.swapaxes(w_down, 1, 2)

    weights = []
    for l in range(layers):
        qkv = plan.gather_heads(w_qkv[l])
        out_t = plan.gather_heads(out_shard[l][None])[:, 0]
        up, down_t = plan.gather_full(jnp.stack([w_up[l], down_shard[l]]))
        weights.append(([qkv[:, c] for c in range(3)], out_t, up, down_t))

    x = plan.swap(inputs)
    g = plan.swap(cotangent)
    kept = []
    for l in range(layers):
        x, saved = layer_forward(plan, x, prefix, order, *weights[l], norm_gain[l], factors[l])
        kept.append(saved)
    outputs = plan.unswap(x)
    grads = [None] * layers
    for l in reversed(range(layers)):
        g, grads[l] = layer_backward(
            plan, g, kept[l], prefix, order, *weights[l], norm_gain[l], factors[l]
        )
    input_grad = plan.unswap(g)
    qkv_g, out_g, up_g, down_g, gain_a, gain_m, f_g = (jnp.stack(a) for a in zip(*grads))
    scale_g = f_g * jax.nn.sigmoid(query_scale) * unit
    gain_a, gain_m, scale_g = lax.psum((gain_a, gain_m, scale_g), ("fsdp", "tp"))
    return outputs, input_grad, qkv_g, out_g, up_g, down_g, gain_a, gain_m, scale_g


def solution(mesh):
    placed = (
        P("fsdp", "tp", None),
        P("fsdp", "tp", None),
        P(None, None, "fsdp", "tp"),
        P(None, "tp", "fsdp"),
        P(None, "fsdp", "tp"),
        P(None, "tp", "fsdp"),
        P(),
        P(),
        P("fsdp"),
    )
    return jax.shard_map(
        body,
        mesh=mesh,
        in_specs=placed,
        out_specs=placed[:6] + (P(), P(), P()),
        check_vma=False,
    )
```

time: 1840 us -> 999 us (0.54)
  waiting for transfers between devices: 928 us -> 212 us
  Pallas kernels: 248 us -> 636 us
  matrix products: 244 us -> 0 us
  local copies, waits for them, and re-layouts: 175 us -> 30.2 us
  blocking collectives: 112 us -> 0 us
    unnamed x38 -> x8, waiting for transfers between devices: 544 us -> 0.81 us
    pallas_call x0 -> x25, Pallas kernels: none -> 400 us  [the longest x1 104 us: gather_call(): pl.pallas_call(functools.partial(gather_kernel, pieces, pairs, outer, rin...]
    all_gather x16 -> x4, waiting for transfers between devices: 299 us -> 17.9 us  [along(): return lax.all_gather(pairs[l, m], 'fsdp', axis=0, tiled=True)]
    dot_general x36 -> x0, matrix products: 244 us -> none  [ein(): return jnp.einsum(spec, *args, preferred_element_type=F32)]
    ppermute x0 -> x32, waiting for transfers between devices: none -> 120 us  [the longest x11 96.6 us: across(): return lax.ppermute(a, 'tp', [(t, (t + self.ring) % n) for t in range(n)])]
    all_gather x2 -> x0, blocking collectives: 67.3 us -> none  [gather_heads(): rows = lax.all_gather(shards, 'fsdp', axis=1, tiled=True)]
    all_to_all x4 -> x0, waiting for transfers between devices: 61 us -> none  [swap(): lax.all_to_all(blocks, 'tp', 0, 0, tiled=True, axis_index_groups=self.sam...]
    unnamed x193 -> x61, local copies, waits for them, and re-layouts: 68.6 us -> 13.9 us
  transfers between devices with their start and end apart: 35 -> 40, of which waited for: 22 -> 22; matrix products, arithmetic and copies ran while one was open for 21% -> 7% of each run, Pallas kernels for 9% -> 54%
where the time goes in v2:
time: 999 us; the launch traced here: 994 us
  Pallas kernels  636 us (64%)
  waiting for transfers between devices  212 us (21%)
  other arithmetic  74.4 us (7%)
  local copies, waits for them, and re-layouts  30.2 us (3%)
  starting transfers between devices  26.1 us (3%)
  between operations  14.9 us (1%)
    pallas_call x4, Pallas kernels, attention_backward(): pl.pallas_call(functools.partial(backward_kernel, pair=pair, dh=dh, bq=bq...  155 us
    pallas_call x1, Pallas kernels, gather_call(): pl.pallas_call(functools.partial(gather_kernel, pieces, pairs, outer, rin...  104 us
    ppermute x11, waiting for transfers between devices, across(): return lax.ppermute(a, 'tp', [(t, (t + self.ring) % n) for t in range(n)])  96.6 us
    pallas_call x2, Pallas kernels, attention_forward(): pl.pallas_call(functools.partial(forward_kernel, pair=pair, dh=dh, bq=bq,...  81.4 us
    reduce_scatter x4, waiting for transfers between devices, scatter_rows(): lax.psum_scatter(mine, 'fsdp', scatter_dimension=0, tiled=True).astype(F32)  73.8 us
    pallas_call x2, Pallas kernels, mlp_back(): pl.pallas_call(functools.partial(mlp_back_kernel, w2 // 2), grid=(rows //...  67.5 us
    pallas_call x4, Pallas kernels, weight_grad(): pl.pallas_call(functools.partial(weight_grad_kernel, w), grid=(d // bd,),...  41.1 us
    pallas_call x2, Pallas kernels, middle_call(): pl.pallas_call(functools.partial(middle_kernel, w2 // 2), grid=(rows // b...  40.1 us
  transfers between devices with their start and end apart: 40, of which 22 were waited for; matrix products, arithmetic and copies ran while one was open for 7% of the time, Pallas kernels for 54%

profile of v2, /device:TPU:0, one launch (start us, length us, event | category | flops | bytes accessed | tf_op | source)
XLA Modules:
  0.0 994.0 jit_solution(5768147155803072439)
XLA Ops:
  12.6 2.9 fusion.block_ref
  15.5 103.6 %gather_weights.1 = (bf16[4,2,160,640]{3,2,1,0:T(8,128)(2,1)}, bf16[4,2,160,640]{3,2,1,0:T(8,128)(2,1)}, bf16[4,2,160,640]{3,2,1,0:T(8,128)(2,1)}, bf16[4,2,160,640]{3,2,1,0:T(8,128)(2,1)}, bf16[512,1280]{1,0:T(8,128)(2,1)}) custom-call(bf16[2,160,640]{2,1,0:T(8,128)(2,1)} %fusion.10.shard_ref, bf16[512,1280]{1,0:T(8,128)(2,1)} %fusion.block_ref), custom_call_target="tpu_custom_call" | custom-call | tf_op jit(solution)/shard_map/gather_weights/pallas_call | solution.py:322
  119.1 2.5 convert_select_fusion.7
  123.0 3.1 multiply_convert_fusion
  126.1 2.8 all-gather.9.cloned.1.call-done
  132.7 2.6 collective-permute-start.1
  135.3 9.7 project.4
  145.0 9.8 project.5
  154.9 40.5 %attention_forward.2 = (bf16[640,2048]{1,0:T(8,128)(2,1)}, f32[8,1,2048]{2,1,0:T(1,128)}) custom-call(s32[1]{0:T(128)} %dynamic_slice.30.prefix_ref, s32[4]{0:T(128)} %fusion.16.order_ref, bf16[640,2048]{1,0:T(8,128)(2,1)} %get-tuple-element.130.q_ref, bf16[640,2048]{1,0:T(8,128)(2,1)} %get-tuple-element.131.k_ref, bf16[640,2048]{1,0:T(8,128)(2,1)} %get-tuple-element.132.v_ref), custom_call_target="tpu_custom_call" | custom-call | flops 20132659200 | bytes 10485760 | tf_op jit(solution)/shard_map/attention_forward/pallas_call | solution.py:80
  195.4 11.8 %collective-permute-done.2.qk1.refs_7_.refs_11_ = bf16[1280,640]{1,0:T(8,128)(2,1)} collective-permute-done((bf16[1280,640]{1,0:T(8,128)(2,1)}, bf16[1280,640]{1,0:T(8,128)(2,1)}, u32[]{:S(2)}, u32[]{:S(2)}) %collective-permute-start.2) | collective-permute-done | bytes 1638432 | tf_op jit(solution)/shard_map/ppermute | solution.py:350
  207.2 6.1 out_project.2
  214.2 2.9 fusion.1
  217.1 3.6 collective-permute-done.4.un2
  225.1 20.1 %middle.2 = (f32[1024,1280]{1,0:T(8,128)}, f32[1024,1280]{1,0:T(8,128)}, f32[1024,1280]{1,0:T(8,128)}, bf16[1024,1280]{1,0:T(8,128)(2,1)}) custom-call(f32[1024,1280]{1,0:T(8,128)} %get-tuple-element.260.x_ref.refs_7_, bf16[640,2048]{1,0:T(8,128)(2,1)} %get-tuple-element.136.att_ref.o_ref, bf16[1024,1280]{1,0:T(8,128)(2,1)} %copy-done.23, ...), custom_call_target="tpu_custom_call" | custom-call | flops 8388608000 | bytes 39321600 | tf_op jit(solution)/shard_map/middle/pallas_call | solution.py:601
  245.1 15.0 %all-gather.15.cloned.1.call-done = bf16[1,1280,640]{2,1,0:T(8,128)(2,1)} async-done(((bf16[1,160,640]{2,1,0:T(8,128)(2,1)}), bf16[1,1280,640]{2,1,0:T(8,128)(2,1)}) %all-gather.15.cloned.1.call-update) | async-done | bytes 1638416 | tf_op jit(solution)/shard_map/all_gather | solution.py:892
  264.6 34.2 %collective-permute-done.7.vo1.refs_9_.refs_13_ = bf16[1280,640]{1,0:T(8,128)(2,1)S(1)} collective-permute-done((bf16[1280,640]{1,0:T(8,128)(2,1)S(1)}, bf16[1280,640]{1,0:T(8,128)(2,1)S(1)}, u32[]{:S(2)}, u32[]{:S(2)}) %collective-permute-start.7) | collective-permute-done | bytes 1638432 | tf_op jit(solution)/shard_map/ppermute | solution.py:350
  300.0 9.8 project.6
  309.7 9.8 project.7
  319.6 40.9 %attention_forward.3 = (bf16[640,2048]{1,0:T(8,128)(2,1)}, f32[8,1,2048]{2,1,0:T(1,128)}) custom-call(s32[1]{0:T(128)} %dynamic_slice.30.prefix_ref, s32[4]{0:T(128)} %fusion.16.order_ref, bf16[640,2048]{1,0:T(8,128)(2,1)} %get-tuple-element.147.q_ref, bf16[640,2048]{1,0:T(8,128)(2,1)} %get-tuple-element.148.k_ref, bf16[640,2048]{1,0:T(8,128)(2,1)} %get-tuple-element.149.v_ref), custom_call_target="tpu_custom_call" | custom-call | flops 20132659200 | bytes 10485760 | tf_op jit(solution)/shard_map/attention_forward/pallas_call | solution.py:80
  361.7 6.1 out_project.3
  370.8 2.7 pad_maximum_fusion.1.g_ref
  379.7 20.0 %middle.3 = (f32[1024,1280]{1,0:T(8,128)}, f32[1024,1280]{1,0:T(8,128)}, f32[1024,1280]{1,0:T(8,128)}, bf16[1024,1280]{1,0:T(8,128)(2,1)}) custom-call(f32[1024,1280]{1,0:T(8,128)} %get-tuple-element.138.x_ref.refs_7_, bf16[640,2048]{1,0:T(8,128)(2,1)} %get-tuple-element.153.att_ref.o_ref, bf16[1024,1280]{1,0:T(8,128)(2,1)} %copy-done.24, ...), custom_call_target="tpu_custom_call" | custom-call | flops 8388608000 | bytes 39321600 | tf_op jit(solution)/shard_map/middle/pallas_call | solution.py:601
  401.6 3.5 collective-permute-start.13
  405.1 27.8 %mlp_back.2 = (f32[1024,1280]{1,0:T(8,128)}, bf16[1024,1280]{1,0:T(8,128)(2,1)}, f32[8,1280]{1,0:T(8,128)}, bf16[1280,640]{1,0:T(8,128)(2,1)}, bf16[1280,640]{1,...) custom-call(f32[1024,1280]{1,0:T(8,128)} %pad_maximum_fusion.1.g_ref, ...), custom_call_target="tpu_custom_call" | custom-call | flops 13421772800 | bytes 39321600 | tf_op jit(solution)/shard_map/mlp_back/pallas_call | solution.py:672
  436.5 5.8 grad_att.4.refs_0_
  442.3 3.7 add_convert_fusion.7
  446.0 3.0 add_convert_fusion.6
  450.7 8.6 out_grad.2
  459.3 4.3 maximum_maximum_fusion.1
  463.6 5.8 grad_att.5.g_ref
  471.1 38.9 %attention_backward.4 = (bf16[320,2048]{1,0:T(8,128)(2,1)}, bf16[320,2048]{1,0:T(8,128)(2,1)}, bf16[320,2048]{1,0:T(8,128)(2,1)}, f32[80,128]{1,0:T(8,128)}) custom-call(s32[1]{0:T(128)} %dynamic_slice.30.prefix_ref, s32[4]{0:T(128)} %fusion.16.order_ref, bf16[640,2048]{1,0:T(8,128)(2,1)} %get-tuple-element.147.q_ref, ...), custom_call_target="tpu_custom_call" | custom-call | flops 26843545600 | bytes 10485760 | tf_op jit(solution)/shard_map/attention_backward/pallas_call | solution.py:187
  510.0 10.3 %weight_grad.4 = bf16[1280,1024]{1,0:T(8,128)(2,1)} custom-call(bf16[1024,1280]{1,0:T(8,128)(2,1)} %get-tuple-element.141.h_ref.own_ref, bf16[1024,1280]{1,0:T(8,128)(2,1)} %collective-permute-done.6.h_ref.other_ref, bf16[320,2048]{1,0:T(8,128)(2,1)} %get-tuple-element.173.dq_ref.refs_3_, bf16[320,2048]{1,0:T(8,128)(2,1)} %get-tuple-element.174.dk_ref.refs_4_, ...), custom_call_target="tpu_custom_call" | custom-call | flops 5033164800 | bytes 15728640 | tf_op jit(solution)/shard_map/weight_grad/pallas_call | solution.py:762
  520.2 8.2 collective-permute-done.17
  528.5 4.6 add_convert_fusion.3
  534.9 38.9 %attention_backward.5 = (bf16[320,2048]{1,0:T(8,128)(2,1)}, bf16[320,2048]{1,0:T(8,128)(2,1)}, bf16[320,2048]{1,0:T(8,128)(2,1)}, f32[80,128]{1,0:T(8,128)}) custom-call(s32[1]{0:T(128)} %dynamic_slice.30.prefix_ref, s32[4]{0:T(128)} %fusion.16.order_ref, bf16[640,2048]{1,0:T(8,128)(2,1)} %get-tuple-element.147.q_ref, ...), custom_call_target="tpu_custom_call" | custom-call | flops 26843545600 | bytes 10485760 | tf_op jit(solution)/shard_map/attention_backward/pallas_call | solution.py:187
  573.8 10.3 %weight_grad.5 = bf16[1280,1024]{1,0:T(8,128)(2,1)} custom-call(bf16[1024,1280]{1,0:T(8,128)(2,1)} %get-tuple-element.141.h_ref.own_ref, bf16[1024,1280]{1,0:T(8,128)(2,1)} %collective-permute-done.6.h_ref.other_ref, bf16[320,2048]{1,0:T(8,128)(2,1)} %get-tuple-element.187.dq_ref.refs_0_, bf16[320,2048]{1,0:T(8,128)(2,1)} %get-tuple-element.181.dk_ref.refs_1_, ...), custom_call_target="tpu_custom_call" | custom-call | flops 5033164800 | bytes 15728640 | tf_op jit(solution)/shard_map/weight_grad/pallas_call | solution.py:762
  584.1 7.1 collective-permute-done.18
  591.2 4.4 add_convert_fusion.2
  595.7 12.1 %input_other.2 = bf16[1024,1280]{1,0:T(8,128)(2,1)} custom-call(bf16[320,2048]{1,0:T(8,128)(2,1)} %get-tuple-element.187.dq_ref.refs_0_, bf16[320,2048]{1,0:T(8,128)(2,1)} %get-tuple-element.181.dk_ref.refs_1_, bf16[320,2048]{1,0:T(8,128)(2,1)} %get-tuple-element.182.dv_ref.refs_2_, bf16[320,2048]{1,0:T(8,128)(2,1)} %get-tuple-element.173.dq_ref.refs_3_, ...), custom_call_target="tpu_custom_call" | custom-call | flops 5033164800 | bytes 10485760 | tf_op jit(solution)/shard_map/input_other/pallas_call | solution.py:796
  607.8 5.1 collective-permute-done.19.refs_6_
  614.4 15.4 %input_own.2 = (f32[1024,1280]{1,0:T(8,128)}, f32[8,1280]{1,0:T(8,128)}) custom-call(bf16[320,2048]{1,0:T(8,128)(2,1)} %get-tuple-element.187.dq_ref.refs_0_, bf16[320,2048]{1,0:T(8,128)(2,1)} %get-tuple-element.181.dk_ref.refs_1_, bf16[320,2048]{1,0:T(8,128)(2,1)} %get-tuple-element.182.dv_ref.refs_2_, bf16[320,2048]{1,0:T(8,128)(2,1)} %get-tuple-element.173.dq_ref.refs_3_, ...), custom_call_target="tpu_custom_call" | custom-call | flops 5033164800 | bytes 31457280 | tf_op jit(solution)/shard_map/input_own/pallas_call | solution.py:832
  630.8 39.7 %mlp_back.3 = (f32[1024,1280]{1,0:T(8,128)}, bf16[1024,1280]{1,0:T(8,128)(2,1)}, f32[8,1280]{1,0:T(8,128)}, bf16[1280,640]{1,0:T(8,128)(2,1)}, bf16[1280,640]{1,...) custom-call(f32[1024,1280]{1,0:T(8,128)} %get-tuple-element.191.g_ref, ...), custom_call_target="tpu_custom_call" | custom-call | flops 13421772800 | bytes 39321600 | tf_op jit(solution)/shard_map/mlp_back/pallas_call | solution.py:672
  672.0 5.8 grad_att.6.refs_0_
  677.8 3.7 add_convert_fusion.5
  681.5 3.0 add_convert_fusion.4
  686.1 8.6 out_grad.3
  694.7 4.3 maximum_maximum_fusion.3
  699.0 5.8 grad_att.7.g_ref
  706.6 38.6 %attention_backward.6 = (bf16[320,2048]{1,0:T(8,128)(2,1)}, bf16[320,2048]{1,0:T(8,128)(2,1)}, bf16[320,2048]{1,0:T(8,128)(2,1)}, f32[80,128]{1,0:T(8,128)}) custom-call(s32[1]{0:T(128)} %dynamic_slice.30.prefix_ref, s32[4]{0:T(128)} %fusion.16.order_ref, bf16[640,2048]{1,0:T(8,128)(2,1)} %get-tuple-element.130.q_ref, ...), custom_call_target="tpu_custom_call" | custom-call | flops 26843545600 | bytes 10485760 | tf_op jit(solution)/shard_map/attention_backward/pallas_call | solution.py:187
  745.2 10.2 %weight_grad.6 = bf16[1280,1024]{1,0:T(8,128)(2,1)} custom-call(bf16[1024,1280]{1,0:T(8,128)(2,1)} %copy-done.4, bf16[1024,1280]{1,0:T(8,128)(2,1)} %collective-permute-done.h_ref.other_ref, bf16[320,2048]{1,0:T(8,128)(2,1)} %get-tuple-element.204.dq_ref.refs_3_, bf16[320,2048]{1,0:T(8,128)(2,1)} %get-tuple-element.205.dk_ref.refs_4_, ...), custom_call_target="tpu_custom_call" | custom-call | flops 5033164800 | bytes 15728640 | tf_op jit(solution)/shard_map/weight_grad/pallas_call | solution.py:762
  755.5 8.8 collective-permute-done.23
  764.3 4.5 add_convert_fusion.1
  771.4 38.9 %attention_backward.7 = (bf16[320,2048]{1,0:T(8,128)(2,1)}, bf16[320,2048]{1,0:T(8,128)(2,1)}, bf16[320,2048]{1,0:T(8,128)(2,1)}, f32[80,128]{1,0:T(8,128)}) custom-call(s32[1]{0:T(128)} %dynamic_slice.30.prefix_ref, s32[4]{0:T(128)} %fusion.16.order_ref, bf16[640,2048]{1,0:T(8,128)(2,1)} %get-tuple-element.130.q_ref, ...), custom_call_target="tpu_custom_call" | custom-call | flops 26843545600 | bytes 10485760 | tf_op jit(solution)/shard_map/attention_backward/pallas_call | solution.py:187
  810.3 10.3 %weight_grad.7 = bf16[1280,1024]{1,0:T(8,128)(2,1)} custom-call(bf16[1024,1280]{1,0:T(8,128)(2,1)} %copy-done.4, bf16[1024,1280]{1,0:T(8,128)(2,1)} %collective-permute-done.h_ref.other_ref, bf16[320,2048]{1,0:T(8,128)(2,1)} %get-tuple-element.218.dq_ref.refs_0_, bf16[320,2048]{1,0:T(8,128)(2,1)} %get-tuple-element.212.dk_ref.refs_1_, ...), custom_call_target="tpu_custom_call" | custom-call | flops 5033164800 | bytes 15728640 | tf_op jit(solution)/shard_map/weight_grad/pallas_call | solution.py:762
  820.6 7.7 collective-permute-done.24
  828.3 4.5 add_convert_fusion
  832.9 12.2 %input_other.3 = bf16[1024,1280]{1,0:T(8,128)(2,1)} custom-call(bf16[320,2048]{1,0:T(8,128)(2,1)} %get-tuple-element.218.dq_ref.refs_0_, bf16[320,2048]{1,0:T(8,128)(2,1)} %get-tuple-element.212.dk_ref.refs_1_, bf16[320,2048]{1,0:T(8,128)(2,1)} %get-tuple-element.213.dv_ref.refs_2_, bf16[320,2048]{1,0:T(8,128)(2,1)} %get-tuple-element.204.dq_ref.refs_3_, ...), custom_call_target="tpu_custom_call" | custom-call | flops 5033164800 | bytes 10485760 | tf_op jit(solution)/shard_map/input_other/pallas_call | solution.py:796
  846.3 3.9 collective-permute-done.25.refs_6_
  851.7 15.8 %input_own.3 = (f32[1024,1280]{1,0:T(8,128)}, f32[8,1280]{1,0:T(8,128)}) custom-call(bf16[320,2048]{1,0:T(8,128)(2,1)} %get-tuple-element.218.dq_ref.refs_0_, bf16[320,2048]{1,0:T(8,128)(2,1)} %get-tuple-element.212.dk_ref.refs_1_, bf16[320,2048]{1,0:T(8,128)(2,1)} %get-tuple-element.213.dv_ref.refs_2_, bf16[320,2048]{1,0:T(8,128)(2,1)} %get-tuple-element.204.dq_ref.refs_3_, ...), custom_call_target="tpu_custom_call" | custom-call | flops 5033164800 | bytes 31457280 | tf_op jit(solution)/shard_map/input_own/pallas_call | solution.py:832
  868.6 2.6 convert_select_fusion.3
  875.4 2.7 pad_maximum_fusion.2
  889.2 16.4 %collective-permute-done.26 = bf16[512,1280]{1,0:T(8,128)(2,1)S(1)} collective-permute-done((bf16[512,1280]{1,0:T(8,128)(2,1)S(1)}, bf16[512,1280]{1,0:T(8,128)(2,1)S(1)}, u32[]{:S(2)}, u32[]{:S(2)}) %collective-permute-start.26) | collective-permute-done | bytes 1310752 | tf_op jit(solution)/shard_map/ppermute | solution.py:350
  907.8 2.7 pad_maximum_fusion.3
  911.4 72.8 %reduce-scatter.7.cloned.1.call-done = bf16[160,1024]{1,0:T(8,128)(2,1)} async-done(((bf16[1280,1024]{1,0:T(8,128)(2,1)}), bf16[160,1024]{1,0:T(8,128)(2,1)}) %reduce-scatter.7.cloned.1.call-update) | async-done | bytes 327696 | tf_op jit(solution)/shard_map/reduce_scatter | solution.py:862
  (184 shorter events, 76.8 us)
Async XLA Ops:
  7.2 4.3 copy-start.10
  7.2 118.9 %all-gather.11.cloned.1.call-start = ((), (), s32[]{:S(2)}) async-start(), calls=%async_computation.9 | async-start | bytes 1843200 | tf_op jit(solution)/shard_map/all_gather | solution.py:892
  9.4 119.6 %all-gather.9.cloned.1.call-start = ((), (), s32[]{:S(2)}) async-start(), calls=%async_computation.8 | async-start | bytes 1843200 | tf_op jit(solution)/shard_map/all_gather | solution.py:892
  11.4 184.0 %all-gather.13.cloned.1.call-start = ((), (), s32[]{:S(2)}) async-start(), calls=%async_computation.10 | async-start | bytes 1843200 | tf_op jit(solution)/shard_map/all_gather | solution.py:892
  123.0 6.9 copy-start.20
  123.0 9.0 copy-start.29
  126.1 9.2 copy-start.4
  128.9 16.1 %collective-permute-start = (bf16[1024,1280]{1,0:T(8,128)(2,1)S(1)}, bf16[1024,1280]{1,0:T(8,128)(2,1)}, u32[]{:S(2)}, u32[]{:S(2)}) collective-permute-start(bf16[1024,1280]{1,0:T(8,128)(2,1)S(1)} %get-tuple-element.122.h_ref.own_ref), channel_id=1, source_target_pairs={{0,1},{1,0},{2,3},{3,2},{4,5},{5,4},{6,7},{7,6},{8,9},{9,8},{10,11... | collective-permute-start | bytes 7864328 | tf_op jit(solution)/shard_map/ppermute | solution.py:353
  129.7 130.4 %all-gather.15.cloned.1.call-start = ((), (), s32[]{:S(2)}) async-start(), calls=%async_computation.11 | async-start | bytes 1843200 | tf_op jit(solution)/shard_map/all_gather | solution.py:892
  132.7 62.7 %collective-permute-start.1 = (bf16[1280,640]{1,0:T(8,128)(2,1)}, bf16[1280,640]{1,0:T(8,128)(2,1)}, u32[]{:S(2)}, u32[]{:S(2)}) collective-permute-start(bf16[1280,640]{1,0:T(8,128)(2,1)} %bitcast.138), channel_id=1, source_target_pairs={{0,2},{1,3},{2,0},{3,1},{4,6},{5,7},{6,4},{7,5},{8,10},{9,11},{10,... | collective-permute-start | bytes 4915208 | tf_op jit(solution)/shard_map/ppermute | solution.py:350
  135.3 71.9 %collective-permute-start.2 = (bf16[1280,640]{1,0:T(8,128)(2,1)}, bf16[1280,640]{1,0:T(8,128)(2,1)}, u32[]{:S(2)}, u32[]{:S(2)}) collective-permute-start(bf16[1280,640]{1,0:T(8,128)(2,1)} %bitcast.128), channel_id=1, source_target_pairs={{0,2},{1,3},{2,0},{3,1},{4,6},{5,7},{6,4},{7,5},{8,10},{9,11},{10,... | collective-permute-start | bytes 4915208 | tf_op jit(solution)/shard_map/ppermute | solution.py:350
  213.3 9.8 collective-permute-start.3
  213.3 416.5 %reduce-scatter.5.cloned.1.call-start = ((), (), s32[]{:S(2)}) async-start(), calls=%async_computation.4 | async-start | bytes 2949120 | tf_op jit(solution)/shard_map/reduce_scatter | solution.py:862
  213.5 7.2 collective-permute-start.4
  214.1 8.9 collective-permute-start.5
  220.7 2.4 copy-start.25
  223.1 2.0 copy-start.23
  225.1 35.1 %copy-start = (bf16[1,1280,640]{2,1,0:T(8,128)(2,1)S(1)}, bf16[1,1280,640]{2,1,0:T(8,128)(2,1)}, u32[]{:S(2)}) copy-start(bf16[1,1280,640]{2,1,0:T(8,128)(2,1)} %all-gather.13.cloned.1.call-done) | copy-start | bytes 4915204
  260.2 49.6 %collective-permute-start.6 = (bf16[1024,1280]{1,0:T(8,128)(2,1)}, bf16[1024,1280]{1,0:T(8,128)(2,1)}, u32[]{:S(2)}, u32[]{:S(2)}) collective-permute-start(bf16[1024,1280]{1,0:T(8,128)(2,1)} %get-tuple-element.141.h_ref.own_ref), channel_id=1, source_target_pairs={{0,1},{1,0},{2,3},{3,2},{4,5},{5,4},{6,7},{7,6},{8,9},{9,8},{10,11... | collective-permute-start | bytes 7864328 | tf_op jit(solution)/shard_map/ppermute | solution.py:353
  260.2 38.6 %collective-permute-start.7 = (bf16[1280,640]{1,0:T(8,128)(2,1)S(1)}, bf16[1280,640]{1,0:T(8,128)(2,1)S(1)}, u32[]{:S(2)}, u32[]{:S(2)}) collective-permute-start(bf16[1280,640]{1,0:T(8,128)(2,1)S(1)} %bitcast.112), channel_id=1, source_target_pairs={{0,2},{1,3},{2,0},{3,1},{4,6},{5,7},{6,4},{7,5},{8,10},{9,11},{10,... | collective-permute-start | bytes 4915208 | tf_op jit(solution)/shard_map/ppermute | solution.py:350
  262.5 99.2 %collective-permute-start.8 = (bf16[1280,640]{1,0:T(8,128)(2,1)}, bf16[1280,640]{1,0:T(8,128)(2,1)}, u32[]{:S(2)}, u32[]{:S(2)}) collective-permute-start(bf16[1280,640]{1,0:T(8,128)(2,1)} %bitcast.142), channel_id=1, source_target_pairs={{0,2},{1,3},{2,0},{3,1},{4,6},{5,7},{6,4},{7,5},{8,10},{9,11},{10,... | collective-permute-start | bytes 4915208 | tf_op jit(solution)/shard_map/ppermute | solution.py:350
  263.1 98.6 %collective-permute-start.9 = (bf16[512,1280]{1,0:T(8,128)(2,1)}, bf16[512,1280]{1,0:T(8,128)(2,1)}, u32[]{:S(2)}, u32[]{:S(2)}) collective-permute-start(bf16[512,1280]{1,0:T(8,128)(2,1)} %fusion.1), channel_id=1, source_target_pairs={{0,2},{1,3},{2,0},{3,1},{4,6},{5,7},{6,4},{7,5},{8,10},{9,11},{10,... | collective-permute-start | bytes 3932168 | tf_op jit(solution)/shard_map/ppermute | solution.py:350
  367.8 9.8 collective-permute-start.10
  367.8 7.5 collective-permute-start.11
  368.3 9.3 collective-permute-start.12
  375.3 2.4 copy-start.27
  377.6 2.1 copy-start.24
  401.6 32.6 %collective-permute-start.13 = (bf16[512,1280]{1,0:T(8,128)(2,1)S(1)}, bf16[512,1280]{1,0:T(8,128)(2,1)S(1)}, u32[]{:S(2)}, u32[]{:S(2)}) collective-permute-start(bf16[512,1280]{1,0:T(8,128)(2,1)S(1)} %fusion.2), channel_id=1, source_target_pairs={{0,2},{1,3},{2,0},{3,1},{4,6},{5,7},{6,4},{7,5},{8,10},{9,11},{10,... | collective-permute-start | bytes 3932168 | tf_op jit(solution)/shard_map/ppermute | solution.py:350
  432.9 9.4 collective-permute-start.15
  435.2 13.9 %collective-permute-start.14 = (bf16[1024,1280]{1,0:T(8,128)(2,1)}, bf16[1024,1280]{1,0:T(8,128)(2,1)S(1)}, u32[]{:S(2)}, u32[]{:S(2)}) collective-permute-start(bf16[1024,1280]{1,0:T(8,128)(2,1)} %get-tuple-element.163.g_ref.own_ref), channel_id=1, source_target_pairs={{0,1},{1,0},{2,3},{3,2},{4,5},{5,4},{6,7},{7,6},{8,9},{9,8},{10,11... | collective-permute-start | bytes 7864328 | tf_op jit(solution)/shard_map/ppermute | solution.py:353
  435.2 10.8 %collective-permute-start.16 = (bf16[1280,640]{1,0:T(8,128)(2,1)}, bf16[1280,640]{1,0:T(8,128)(2,1)}, u32[]{:S(2)}, u32[]{:S(2)}) collective-permute-start(bf16[1280,640]{1,0:T(8,128)(2,1)} %get-tuple-element.168), channel_id=1, source_target_pairs={{0,1},{1,0},{2,3},{3,2},{4,5},{5,4},{6,7},{7,6},{8,9},{9,8},{10,11... | collective-permute-start | bytes 4915208 | tf_op jit(solution)/shard_map/ppermute | solution.py:353
  442.3 3.7 copy-start.7
  449.1 1.6 copy-start.5
  469.3 59.1 %collective-permute-start.17 = (bf16[1280,1024]{1,0:T(8,128)(2,1)}, bf16[1280,1024]{1,0:T(8,128)(2,1)}, u32[]{:S(2)}, u32[]{:S(2)}) collective-permute-start(bf16[1280,1024]{1,0:T(8,128)(2,1)} %get-tuple-element.176), channel_id=1, source_target_pairs={{0,2},{1,3},{2,0},{3,1},{4,6},{5,7},{6,4},{7,5},{8,10},{9,11},{10,... | collective-permute-start | bytes 7864328 | tf_op jit(solution)/shard_map/ppermute | solution.py:350
  533.0 58.2 %collective-permute-start.18 = (bf16[1280,1024]{1,0:T(8,128)(2,1)}, bf16[1280,1024]{1,0:T(8,128)(2,1)S(1)}, u32[]{:S(2)}, u32[]{:S(2)}) collective-permute-start(bf16[1280,1024]{1,0:T(8,128)(2,1)} %weight_grad.4), channel_id=1, source_target_pairs={{0,2},{1,3},{2,0},{3,1},{4,6},{5,7},{6,4},{7,5},{8,10},{9,11},{10,... | collective-permute-start | bytes 7864328 | tf_op jit(solution)/shard_map/ppermute | solution.py:350
  534.8 346.6 %reduce-scatter.11.cloned.1.call-start = ((), (), s32[]{:S(2)}) async-start(), calls=%async_computation.7 | async-start | bytes 2949120 | tf_op jit(solution)/shard_map/reduce_scatter | solution.py:862
  607.8 5.1 collective-permute-start.19
  612.9 1.5 copy-start.3
  630.8 40.5 %copy-start.22 = (f32[80,1]{0,1:T(1,128)S(1)}, f32[80,1]{0,1:T(1,128)}, u32[]{:S(2)}) copy-start(f32[80,1]{0,1:T(1,128)} %get-tuple-element.285) | copy-start | bytes 964
  670.6 7.3 collective-permute-start.21
  670.8 13.8 %collective-permute-start.20 = (bf16[1024,1280]{1,0:T(8,128)(2,1)}, bf16[1024,1280]{1,0:T(8,128)(2,1)S(1)}, u32[]{:S(2)}, u32[]{:S(2)}) collective-permute-start(bf16[1024,1280]{1,0:T(8,128)(2,1)} %get-tuple-element.194.g_ref.own_ref), channel_id=1, source_target_pairs={{0,1},{1,0},{2,3},{3,2},{4,5},{5,4},{6,7},{7,6},{8,9},{9,8},{10,11... | collective-permute-start | bytes 7864328 | tf_op jit(solution)/shard_map/ppermute | solution.py:353
  671.1 10.4 %collective-permute-start.22 = (bf16[1280,640]{1,0:T(8,128)(2,1)}, bf16[1280,640]{1,0:T(8,128)(2,1)}, u32[]{:S(2)}, u32[]{:S(2)}) collective-permute-start(bf16[1280,640]{1,0:T(8,128)(2,1)} %get-tuple-element.199), channel_id=1, source_target_pairs={{0,1},{1,0},{2,3},{3,2},{4,5},{5,4},{6,7},{7,6},{8,9},{9,8},{10,11... | collective-permute-start | bytes 4915208 | tf_op jit(solution)/shard_map/ppermute | solution.py:353
  677.8 3.7 copy-start.8
  684.6 1.5 copy-start.6
  704.8 59.5 %collective-permute-start.23 = (bf16[1280,1024]{1,0:T(8,128)(2,1)}, bf16[1280,1024]{1,0:T(8,128)(2,1)}, u32[]{:S(2)}, u32[]{:S(2)}) collective-permute-start(bf16[1280,1024]{1,0:T(8,128)(2,1)} %get-tuple-element.207), channel_id=1, source_target_pairs={{0,2},{1,3},{2,0},{3,1},{4,6},{5,7},{6,4},{7,5},{8,10},{9,11},{10,... | collective-permute-start | bytes 7864328 | tf_op jit(solution)/shard_map/ppermute | solution.py:350
  768.8 142.6 %reduce-scatter.9.cloned.1.call-start = ((), (), s32[]{:S(2)}) async-start(), calls=%async_computation.6 | async-start | bytes 2949120 | tf_op jit(solution)/shard_map/reduce_scatter | solution.py:862
  769.6 214.7 %reduce-scatter.7.cloned.1.call-start = ((), (), s32[]{:S(2)}) async-start(), calls=%async_computation.5 | async-start | bytes 2949120 | tf_op jit(solution)/shard_map/reduce_scatter | solution.py:862
  769.6 58.7 %collective-permute-start.24 = (bf16[1280,1024]{1,0:T(8,128)(2,1)}, bf16[1280,1024]{1,0:T(8,128)(2,1)S(1)}, u32[]{:S(2)}, u32[]{:S(2)}) collective-permute-start(bf16[1280,1024]{1,0:T(8,128)(2,1)} %weight_grad.6), channel_id=1, source_target_pairs={{0,2},{1,3},{2,0},{3,1},{4,6},{5,7},{6,4},{7,5},{8,10},{9,11},{10,... | collective-permute-start | bytes 7864328 | tf_op jit(solution)/shard_map/ppermute | solution.py:350
  832.8 12.3 %copy-start.15 = (f32[8,1280]{1,0:T(8,128)S(1)}, f32[8,1280]{1,0:T(8,128)}, u32[]{:S(2)}) copy-start(f32[8,1280]{1,0:T(8,128)} %get-tuple-element.230) | copy-start | bytes 122884
  832.8 12.3 %copy-start.11 = (f32[80,128]{1,0:T(8,128)S(1)}, f32[80,128]{1,0:T(8,128)}, u32[]{:S(2)}) copy-start(f32[80,128]{1,0:T(8,128)} %get-tuple-element.231) | copy-start | bytes 122884
  832.8 12.3 %copy-start.12 = (f32[80,128]{1,0:T(8,128)S(1)}, f32[80,128]{1,0:T(8,128)}, u32[]{:S(2)}) copy-start(f32[80,128]{1,0:T(8,128)} %get-tuple-element.232) | copy-start | bytes 122884
  832.8 12.4 %copy-start.16 = (f32[8,1280]{1,0:T(8,128)S(1)}, f32[8,1280]{1,0:T(8,128)}, u32[]{:S(2)}) copy-start(f32[8,1280]{1,0:T(8,128)} %get-tuple-element.229) | copy-start | bytes 122884
  832.8 13.2 %copy-start.13 = (f32[80,128]{1,0:T(8,128)S(1)}, f32[80,128]{1,0:T(8,128)}, u32[]{:S(2)}) copy-start(f32[80,128]{1,0:T(8,128)} %get-tuple-element.227) | copy-start | bytes 122884
  832.8 13.2 %copy-start.14 = (f32[80,128]{1,0:T(8,128)S(1)}, f32[80,128]{1,0:T(8,128)}, u32[]{:S(2)}) copy-start(f32[80,128]{1,0:T(8,128)} %get-tuple-element.228) | copy-start | bytes 122884
  832.8 13.3 %copy-start.19 = (f32[2,80]{1,0:T(2,128)S(1)}, f32[2,80]{1,0:T(2,128)}, u32[]{:S(2)}) copy-start(f32[2,80]{1,0:T(2,128)} %copy-done.18) | copy-start | bytes 1924
  845.1 5.1 collective-permute-start.25
  850.2 1.5 copy-start.2
  868.4 2.8 collective-permute-start.27
  871.2 4.1 collective-permute-start.28
  874.9 30.7 %collective-permute-start.26 = (bf16[512,1280]{1,0:T(8,128)(2,1)S(1)}, bf16[512,1280]{1,0:T(8,128)(2,1)S(1)}, u32[]{:S(2)}, u32[]{:S(2)}) collective-permute-start(bf16[512,1280]{1,0:T(8,128)(2,1)S(1)} %fusion.3), channel_id=1, source_target_pairs={{0,2},{1,3},{2,0},{3,1},{4,6},{5,7},{6,4},{7,5},{8,10},{9,11},{10,... | collective-permute-start | bytes 3932168 | tf_op jit(solution)/shard_map/ppermute | solution.py:350
  875.3 3.9 collective-permute-start.29
  878.1 9.9 copy-start.21
  879.2 4.0 collective-permute-start.30
  883.2 4.8 collective-permute-start.31
  (6 other events, 6.6 us)
Sparse Core Ops, SparseCore 0:
  10.8 65.7 all-gather.10
  79.3 49.5 all-gather.8
  131.7 47.2 all-gather.12
  213.4 46.7 all-gather.14
  534.9 68.4 reduce-scatter.4
  768.9 69.3 reduce-scatter.10
  841.8 69.5 reduce-scatter.8
  914.9 69.2 reduce-scatter.6

commit v3 on v2

--- a/solution.py
+++ b/solution.py
@@ -487,8 +487,8 @@
     return pl.CostEstimate(flops=int(flops * HINT), bytes_accessed=int(nbytes * HINT), transcendentals=0)
 
 
-def params():
-    return pltpu.CompilerParams(vmem_limit_bytes=VMEM_LIMIT)
+def params(mib=60):
+    return pltpu.CompilerParams(vmem_limit_bytes=mib * 2**20)
 
 
 def fixed(shape):
@@ -714,34 +714,38 @@
     )(g, *vo, *extra)
 
 
-def out_grad_kernel(w, own_ref, other_ref, att_ref, o0, o1):
+def out_grad_kernel(w, own_ref, other_ref, att_ref, u0, u1, got0, got1, o0, o1):
     half = own_ref.shape[0]
     att = att_ref[...]
     grad = dot(own_ref[...], att[:, :half], TT) + dot(other_ref[...], att[:, half:], TT)
     grad = grad.astype(BF16)
-    o0[...] = grad[:, :w]
-    o1[...] = grad[:, w:]
-
-
-def out_grad_call(own, other, att):
+    for s, (u, got, out) in enumerate(((u0, got0, o0), (u1, got1, o1))):
+        out[:, :2 * w] = (u[...].astype(F32) + got[...].astype(F32)).astype(BF16)
+        out[:, 2 * w:3 * w] = grad[:, s * w:(s + 1) * w]
+        out[:, 3 * w:] = jnp.zeros((out.shape[0], out.shape[1] - 3 * w), BF16)
+
+
+def out_grad_call(own, other, att, mlp, got, width):
     rows, d = own.shape
     w2 = att.shape[0]
     bd = 256
     col = pl.BlockSpec((rows, bd), lambda i: (0, i))
-    out = pl.BlockSpec((bd, w2 // 2), lambda i: (i, 0))
+    flat = pl.BlockSpec((bd, w2), lambda i: (i, 0))
+    out = pl.BlockSpec((bd, width), lambda i: (i, 0))
     return pl.pallas_call(
         functools.partial(out_grad_kernel, w2 // 2),
         grid=(d // bd,),
-        in_specs=[col, col, fixed(att.shape)],
+        in_specs=[col, col, fixed(att.shape)] + [flat] * 4,
         out_specs=[out] * 2,
-        out_shape=[shape_of((d, w2 // 2))] * 2,
+        out_shape=[shape_of((d, width))] * 2,
         compiler_params=params(),
         cost_estimate=cost(4 * rows * d * w2, 8 * rows * d),
         name="out_grad",
-    )(own, other, att)
-
-
-def weight_grad_kernel(w, own_ref, other_ref, dq_ref, dk_ref, dv_ref, out, stacked):
+    )(own, other, att, *mlp, *got)
+
+
+def weight_grad_kernel(w, own_ref, other_ref, dq_ref, dk_ref, dv_ref, *refs):
+    out, stacked = refs[-2:]
     half = own_ref.shape[0]
 
     @pl.when(pl.program_id(0) == 0)
@@ -750,26 +754,30 @@
             stacked[j * w:(j + 1) * w, :] = ref[...]
 
     grad = dot(own_ref[...], stacked[:, :half], TT) + dot(other_ref[...], stacked[:, half:], TT)
+    if len(refs) == 3:
+        grad = grad + refs[0][:, :3 * w].astype(F32)
     out[:, :3 * w] = grad.astype(BF16)
     out[:, 3 * w:] = jnp.zeros((out.shape[0], out.shape[1] - 3 * w), BF16)
 
 
-def weight_grad(own, other, dq, dk, dv, width):
+def weight_grad(own, other, dq, dk, dv, width, got=None):
     rows, d = own.shape
     w = dq.shape[0]
     bd = 256
     col = pl.BlockSpec((rows, bd), lambda i: (0, i))
+    flat = pl.BlockSpec((bd, width), lambda i: (i, 0))
+    extra = [] if got is None else [got]
     return pl.pallas_call(
         functools.partial(weight_grad_kernel, w),
         grid=(d // bd,),
-        in_specs=[col, col] + [fixed(dq.shape)] * 3,
-        out_specs=pl.BlockSpec((bd, width), lambda i: (i, 0)),
+        in_specs=[col, col] + [fixed(dq.shape)] * 3 + [flat] * len(extra),
+        out_specs=flat,
         out_shape=shape_of((d, width)),
         scratch_shapes=[pltpu.VMEM((3 * w, 2 * rows), BF16)],
         compiler_params=params(),
         cost_estimate=cost(12 * rows * d * w, 12 * rows * d),
         name="weight_grad",
-    )(own, other, dq, dk, dv)
+    )(own, other, dq, dk, dv, *extra)
 
 
 def input_sum(w, grads, qk, vo):
@@ -910,6 +918,9 @@
         h_other = plan.core(h)
         qkv = project(h, qk, vo, scale, 0)
         q, k, v = project(h_other, qk, vo, scale, 1, qkv)
+        if l == 1:
+            q, un1_rows = after(q, un1_rows)
+            un1 = both(un1_rows)
         att, lse = attention_forward(q, k, v, prefix, order, dh)
         if l == 0:
             att, un0_got, qk1_got, vo1_rows = after(att, un0[1], qk1[1], vo1_rows)
@@ -919,14 +930,17 @@
             att, un1_got, cot_got = after(att, un1[1], cot_got)
             un = four((un1[0], un1_got))
         part = plan.core(out_project(att, vo, 1))
+        if l == 0:
+            part, un1_rows = after(part, un1_rows)
         next_gain = norm_gain[(l + 1) % layers, 0][None]
         mid, pre, res, h_next = middle_call(x, att, part, norm_gain[l, 1][None], next_gain, vo, un)
+        if l == 0:
+            h_next, vo1_got, cot_block = after(h_next, vo1[1], cot_block)
+            vo1 = (vo1[0], vo1_got)
+            cot_got = plan.across(cot_block)
         kept.append((x, h, h_other, q, k, v, att, lse, mid, pre))
         weights.append((qk, vo, un))
         x, h = res, h_next
-        if l == 0:
-            h, un1_rows, cot_block = after(h, un1_rows, cot_block)
-            un1, cot_got = both(un1_rows), plan.across(cot_block)
     g = plan.order(plan.pick(cotangent, plan.seq), cot_got.astype(F32))
     out_blocks = x.reshape(seqs, positions, d)
     out_send = plan.pick(out_blocks, 1 - plan.seq).astype(BF16)
@@ -944,21 +958,21 @@
             outputs = plan.order(plan.pick(out_blocks, plan.seq), out_got.astype(F32)).reshape(out_blocks.shape)
         low_other = plan.core(low)
         g_att = grad_att(low, vo, 0)
+        early = out_grad_call(low, low_other, att, (u0, u1), (plan.core(u2), plan.core(u3)), width)
+        early = [early[1], early[0]]
+        low_other, *early = after(low_other, *early)
+        early_got = plan.across(early[0])
         g_att = grad_att(low_other, vo, 1, g_att)
-        o0, o1 = out_grad_call(low, low_other, att)
-        pad = jnp.zeros((d, width - 3 * w), BF16)
-        early = []
-        for a, c, o in ((u1, plan.core(u3), o1), (u0, plan.core(u2), o0)):
-            early.append(jnp.concatenate([(a.astype(F32) + c.astype(F32)).astype(BF16), o, pad], axis=1))
-        g_att, *early = after(g_att, *early)
-        early_got = plan.across(early[0])
         dgrads, fgs, pieces = [None] * 6, [], [None] * 2
         for s in (1, 0):
             dq, dk, dv, fg = attention_backward(
                 q, k, v, att, g_att, lse, factors[l], prefix, order, dh, s * w, w
             )
-            pieces[s] = weight_grad(h, h_other, dq, dk, dv, width)
+            if s == 0 and l + 1 < layers:
+                dq, upper = after(dq, grads[l + 1][1])
+                grads[l + 1] = (grads[l + 1][0], upper, grads[l + 1][2])
             if s == 1:
+                pieces[1] = weight_grad(h, h_other, dq, dk, dv, width)
                 g_att, pieces[1], early_got = after(g_att, pieces[1], early_got)
                 late_got = plan.across(pieces[1])
                 mine, g_att = after(add_low(early[1], early_got), g_att)
@@ -966,10 +980,11 @@
             dgrads[3 * s:3 * s + 3] = [dq, dk, dv]
             fgs.append(fg)
         fg = fgs[0] + fgs[1]
-        dgrads[0], pieces[0], late_got = after(dgrads[0], pieces[0], late_got)
-        mine, dgrads[0] = after(add_low(pieces[0], late_got), dgrads[0])
+        part = input_other(dgrads, qk, vo)
+        part, dgrads[0], late_got = after(part, dgrads[0], late_got)
+        part = plan.core(part)
+        mine, dgrads[1] = after(weight_grad(h, h_other, *dgrads[:3], width, late_got), dgrads[1])
         late = scatter_rows(mine)
-        part = plan.core(input_other(dgrads, qk, vo))
         g, gain_a = input_own(dgrads, part, x, g_mid, norm_gain[l, 0][None], qk, vo)
         if l > 0:
             g, early = after(g, early)

time: 999 us -> 859 us (0.86)
  waiting for transfers between devices: 212 us -> 93.6 us
  other arithmetic: 74.4 us -> 44.7 us
  Pallas kernels: 636 us -> 650 us
    ppermute x11, waiting for transfers between devices: 96.6 us -> 39.4 us  [across(): return lax.ppermute(a, 'tp', [(t, (t + self.ring) % n) for t in range(n)])]
    reduce_scatter x4, waiting for transfers between devices: 73.8 us -> 33.9 us  [scatter_rows(): lax.psum_scatter(mine, 'fsdp', scatter_dimension=0, tiled=True).astype(F32)]
    convert_element_type x4 -> x0, other arithmetic: 13.5 us -> none  [fast_body(): (a.astype(F32) + c.astype(F32)).astype(BF16)]
    ppermute x16, waiting for transfers between devices: 19 us -> 6.89 us  [core(): return lax.ppermute(a, 'tp', [(t, t ^ 1) for t in range(self.tp)])]
    pallas_call x2, Pallas kernels: 67.5 us -> 55.9 us  [mlp_back(): pl.pallas_call(functools.partial(mlp_back_kernel, w2 // 2), grid=(rows //...]
    pallas_call x4, Pallas kernels: 155 us -> 167 us  [attention_backward(): pl.pallas_call(functools.partial(backward_kernel, pair=pair, dh=dh, bq=bq...]
  transfers between devices with their start and end apart: 40 -> 40, of which waited for: 22 -> 17; matrix products, arithmetic and copies ran while one was open for 7% -> 5% of each run, Pallas kernels for 54% -> 70%
where the time goes in v3:
time: 859 us; the launch traced here: 855 us
  Pallas kernels  650 us (76%)
  waiting for transfers between devices  93.6 us (11%)
  other arithmetic  44.7 us (5%)
  local copies, waits for them, and re-layouts  28.8 us (3%)
  starting transfers between devices  23.1 us (3%)
  between operations  14.9 us (2%)
    pallas_call x4, Pallas kernels, attention_backward(): pl.pallas_call(functools.partial(backward_kernel, pair=pair, dh=dh, bq=bq...  167 us
    pallas_call x1, Pallas kernels, gather_call(): pl.pallas_call(functools.partial(gather_kernel, pieces, pairs, outer, rin...  104 us
    pallas_call x2, Pallas kernels, attention_forward(): pl.pallas_call(functools.partial(forward_kernel, pair=pair, dh=dh, bq=bq,...  87.4 us
    pallas_call x2, Pallas kernels, mlp_back(): pl.pallas_call(functools.partial(mlp_back_kernel, w2 // 2), grid=(rows //...  55.9 us
    pallas_call x4, Pallas kernels, weight_grad(): pl.pallas_call(functools.partial(weight_grad_kernel, w), grid=(d // bd,),...  42.7 us
    pallas_call x2, Pallas kernels, middle_call(): pl.pallas_call(functools.partial(middle_kernel, w2 // 2), grid=(rows // b...  40.1 us
    ppermute x11, waiting for transfers between devices, across(): return lax.ppermute(a, 'tp', [(t, (t + self.ring) % n) for t in range(n)])  39.4 us
    pallas_call x4, Pallas kernels, project(): pl.pallas_call(functools.partial(project_kernel, w), grid=(steps,), in_sp...  39.3 us
  transfers between devices with their start and end apart: 40, of which 17 were waited for; matrix products, arithmetic and copies ran while one was open for 5% of the time, Pallas kernels for 70%

profile of v3, /device:TPU:0, one launch (start us, length us, event | category | flops | bytes accessed | tf_op | source)
XLA Modules:
  0.0 854.7 jit_solution(10317212964344197687)
XLA Ops:
  9.4 2.0 pad_maximum_fusion.10
  12.6 2.9 fusion.block_ref
  16.4 103.8 %gather_weights.1 = (bf16[4,2,160,640]{3,2,1,0:T(8,128)(2,1)}, bf16[4,2,160,640]{3,2,1,0:T(8,128)(2,1)}, bf16[4,2,160,640]{3,2,1,0:T(8,128)(2,1)}, bf16[4,2,160,640]{3,2,1,0:T(8,128)(2,1)}, bf16[512,1280]{1,0:T(8,128)(2,1)}) custom-call(bf16[2,160,640]{2,1,0:T(8,128)(2,1)} %fusion.15.shard_ref, bf16[512,1280]{1,0:T(8,128)(2,1)} %fusion.block_ref), custom_call_target="tpu_custom_call" | custom-call | tf_op jit(solution)/shard_map/gather_weights/pallas_call | solution.py:322
  120.2 2.5 convert_select_fusion.7
  124.1 3.1 multiply_convert_fusion
  127.1 2.5 all-gather.9.cloned.1.call-done
  133.0 2.6 collective-permute-start.1
  135.7 9.7 %project.4 = (bf16[640,2048]{1,0:T(8,128)(2,1)}, bf16[640,2048]{1,0:T(8,128)(2,1)}, bf16[640,2048]{1,0:T(8,128)(2,1)}) custom-call(bf16[1024,1280]{1,0:T(8,128)(2,1)} %copy-done.6, bf16[1280,640]{1,0:T(8,128)(2,1)} %bitcast.123, bf16[1280,640]{1,0:T(8,128)(2,1)} %bitcast.127, bf16[1280,640]{1,0:T(8,128)(2,1)} %bitcast.90, bf16[1280,640]{1,0:T(8,128)(2,1)} %bitcast.98, ...), custom_call_target="tpu_custom_call" | custom-call | flops 5033164800 | bytes 5242880 | tf_op jit(solution)/shard_map/project/pallas_call | solution.py:535
  145.4 9.8 %project.5 = (bf16[640,2048]{1,0:T(8,128)(2,1)}, bf16[640,2048]{1,0:T(8,128)(2,1)}, bf16[640,2048]{1,0:T(8,128)(2,1)}) custom-call(bf16[1024,1280]{1,0:T(8,128)(2,1)} %collective-permute-done.h_ref.other_ref, bf16[1280,640]{1,0:T(8,128)(2,1)} %bitcast.124, bf16[1280,640]{1,0:T(8,128)(2,1)} %bitcast.128, ...), custom_call_target="tpu_custom_call", output_to_operand_aliasing={{0}: (6, {}), {1}: (7, {}), {2}: (8, {})} | custom-call | flops 5033164800 | bytes 5242880 | tf_op jit(solution)/shard_map/project/pallas_call | solution.py:535
  155.2 43.6 %attention_forward.2 = (bf16[640,2048]{1,0:T(8,128)(2,1)}, f32[8,1,2048]{2,1,0:T(1,128)}) custom-call(s32[1]{0:T(128)} %dynamic_slice.30.prefix_ref, s32[4]{0:T(128)} %fusion.21.order_ref, bf16[640,2048]{1,0:T(8,128)(2,1)} %get-tuple-element.136.q_ref, bf16[640,2048]{1,0:T(8,128)(2,1)} %get-tuple-element.137.k_ref, bf16[640,2048]{1,0:T(8,128)(2,1)} %get-tuple-element.138.v_ref), custom_call_target="tpu_custom_call" | custom-call | flops 20132659200 | bytes 10485760 | tf_op jit(solution)/shard_map/attention_forward/pallas_call | solution.py:80
  198.8 8.7 %collective-permute-done.2.qk1.refs_7_.refs_11_ = bf16[1280,640]{1,0:T(8,128)(2,1)} collective-permute-done((bf16[1280,640]{1,0:T(8,128)(2,1)}, bf16[1280,640]{1,0:T(8,128)(2,1)}, u32[]{:S(2)}, u32[]{:S(2)}) %collective-permute-start.2) | collective-permute-done | bytes 1638432 | tf_op jit(solution)/shard_map/ppermute | solution.py:350
  207.6 6.2 out_project.2
  214.3 1.7 collective-permute-start.6
  216.0 2.9 fusion.1
  219.0 6.4 all-gather.15.cloned.1.call-done
  225.4 20.1 %middle.2 = (f32[1024,1280]{1,0:T(8,128)}, f32[1024,1280]{1,0:T(8,128)}, f32[1024,1280]{1,0:T(8,128)}, bf16[1024,1280]{1,0:T(8,128)(2,1)}) custom-call(f32[1024,1280]{1,0:T(8,128)} %get-tuple-element.272.x_ref.refs_7_, bf16[640,2048]{1,0:T(8,128)(2,1)} %get-tuple-element.142.att_ref.o_ref, bf16[1024,1280]{1,0:T(8,128)(2,1)} %collective-permute-done.3.got_ref, ...), custom_call_target="tpu_custom_call" | custom-call | flops 8388608000 | bytes 39321600 | tf_op jit(solution)/shard_map/middle/pallas_call | solution.py:601
  245.5 7.0 collective-permute-done.6.vo1.refs_9_.refs_13_
  253.5 1.8 collective-permute-start.9
  255.3 9.8 %project.6 = (bf16[640,2048]{1,0:T(8,128)(2,1)}, bf16[640,2048]{1,0:T(8,128)(2,1)}, bf16[640,2048]{1,0:T(8,128)(2,1)}) custom-call(bf16[1024,1280]{1,0:T(8,128)(2,1)} %get-tuple-element.149.h_ref.own_ref, bf16[1280,640]{1,0:T(8,128)(2,1)} %bitcast.132, bf16[1280,640]{1,0:T(8,128)(2,1)} %collective-permute-done.2.qk1.refs_7_.refs_11_, ...), custom_call_target="tpu_custom_call" | custom-call | flops 5033164800 | bytes 5242880 | tf_op jit(solution)/shard_map/project/pallas_call | solution.py:535
  265.1 10.0 %project.7 = (bf16[640,2048]{1,0:T(8,128)(2,1)}, bf16[640,2048]{1,0:T(8,128)(2,1)}, bf16[640,2048]{1,0:T(8,128)(2,1)}) custom-call(bf16[1024,1280]{1,0:T(8,128)(2,1)} %collective-permute-done.7.h_ref.other_ref, bf16[1280,640]{1,0:T(8,128)(2,1)} %bitcast.133, ...), custom_call_target="tpu_custom_call", output_to_operand_aliasing={{0}: (6, {}), {1}: (7, {}), {2}: (8, {})} | custom-call | flops 5033164800 | bytes 5242880 | tf_op jit(solution)/shard_map/project/pallas_call | solution.py:535
  275.3 43.8 %attention_forward.3 = (bf16[640,2048]{1,0:T(8,128)(2,1)}, f32[8,1,2048]{2,1,0:T(1,128)}) custom-call(s32[1]{0:T(128)} %dynamic_slice.30.prefix_ref, s32[4]{0:T(128)} %fusion.21.order_ref, bf16[640,2048]{1,0:T(8,128)(2,1)} %get-tuple-element.157.q_ref, bf16[640,2048]{1,0:T(8,128)(2,1)} %get-tuple-element.158.k_ref, bf16[640,2048]{1,0:T(8,128)(2,1)} %get-tuple-element.159.v_ref), custom_call_target="tpu_custom_call" | custom-call | flops 20132659200 | bytes 10485760 | tf_op jit(solution)/shard_map/attention_forward/pallas_call | solution.py:80
  320.0 6.1 out_project.3
  326.6 2.1 convert_select_fusion.5
  328.7 2.7 pad_maximum_fusion.1.g_ref
  331.4 3.9 collective-permute-done.11.un2
  337.7 20.0 %middle.3 = (f32[1024,1280]{1,0:T(8,128)}, f32[1024,1280]{1,0:T(8,128)}, f32[1024,1280]{1,0:T(8,128)}, bf16[1024,1280]{1,0:T(8,128)(2,1)}) custom-call(f32[1024,1280]{1,0:T(8,128)} %get-tuple-element.145.x_ref.refs_7_, bf16[640,2048]{1,0:T(8,128)(2,1)} %get-tuple-element.163.att_ref.o_ref, bf16[1024,1280]{1,0:T(8,128)(2,1)} %collective-permute-done.10.got_ref, ...), custom_call_target="tpu_custom_call" | custom-call | flops 8388608000 | bytes 39321600 | tf_op jit(solution)/shard_map/middle/pallas_call | solution.py:601
  357.6 1.9 fusion.2
  359.5 1.8 collective-permute-start.13
  361.3 28.0 %mlp_back.2 = (f32[1024,1280]{1,0:T(8,128)}, bf16[1024,1280]{1,0:T(8,128)(2,1)}, f32[8,1280]{1,0:T(8,128)}, bf16[1280,640]{1,0:T(8,128)(2,1)}, bf16[1280,640]{1,...) custom-call(f32[1024,1280]{1,0:T(8,128)} %pad_maximum_fusion.1.g_ref, ...), custom_call_target="tpu_custom_call" | custom-call | flops 13421772800 | bytes 39321600 | tf_op jit(solution)/shard_map/mlp_back/pallas_call | solution.py:672
  392.9 5.8 grad_att.4.refs_0_
  398.9 2.7 collective-permute-done.16.got1
  403.1 11.4 %out_grad.2 = (bf16[1280,1024]{1,0:T(8,128)(2,1)}, bf16[1280,1024]{1,0:T(8,128)(2,1)}) custom-call(bf16[1024,1280]{1,0:T(8,128)(2,1)} %get-tuple-element.173.own_ref.g_ref, bf16[1024,1280]{1,0:T(8,128)(2,1)} %copy-done.3, bf16[640,2048]{1,0:T(8,128)(2,1)} %get-tuple-element.163.att_ref.o_ref, bf16[1280,640]{1,0:T(8,128)(2,1)} %get-tuple-element.174.u0, ...), custom_call_target="tpu_custom_call" | custom-call | flops 3355443200 | bytes 10485760 | tf_op jit(solution)/shard_map/out_grad/pallas_call | solution.py:735
  416.3 5.7 grad_att.5.g_ref
  422.0 41.6 %attention_backward.4 = (bf16[320,2048]{1,0:T(8,128)(2,1)}, bf16[320,2048]{1,0:T(8,128)(2,1)}, bf16[320,2048]{1,0:T(8,128)(2,1)}, f32[80,128]{1,0:T(8,128)}) custom-call(s32[1]{0:T(128)} %dynamic_slice.30.prefix_ref, s32[4]{0:T(128)} %fusion.21.order_ref, bf16[640,2048]{1,0:T(8,128)(2,1)} %get-tuple-element.157.q_ref, ...), custom_call_target="tpu_custom_call" | custom-call | flops 26843545600 | bytes 10485760 | tf_op jit(solution)/shard_map/attention_backward/pallas_call | solution.py:187
  463.6 10.4 %weight_grad.4 = bf16[1280,1024]{1,0:T(8,128)(2,1)} custom-call(bf16[1024,1280]{1,0:T(8,128)(2,1)} %get-tuple-element.149.h_ref.own_ref, bf16[1024,1280]{1,0:T(8,128)(2,1)} %collective-permute-done.7.h_ref.other_ref, bf16[320,2048]{1,0:T(8,128)(2,1)} %get-tuple-element.183.dq_ref.refs_3_, bf16[320,2048]{1,0:T(8,128)(2,1)} %get-tuple-element.184.dk_ref.refs_4_, ...), custom_call_target="tpu_custom_call" | custom-call | flops 5033164800 | bytes 15728640 | tf_op jit(solution)/shard_map/weight_grad/pallas_call | solution.py:770
  474.0 4.5 add_convert_fusion.1
  481.7 41.6 %attention_backward.5 = (bf16[320,2048]{1,0:T(8,128)(2,1)}, bf16[320,2048]{1,0:T(8,128)(2,1)}, bf16[320,2048]{1,0:T(8,128)(2,1)}, f32[80,128]{1,0:T(8,128)}) custom-call(s32[1]{0:T(128)} %dynamic_slice.30.prefix_ref, s32[4]{0:T(128)} %fusion.21.order_ref, bf16[640,2048]{1,0:T(8,128)(2,1)} %get-tuple-element.157.q_ref, ...), custom_call_target="tpu_custom_call" | custom-call | flops 26843545600 | bytes 10485760 | tf_op jit(solution)/shard_map/attention_backward/pallas_call | solution.py:187
  523.3 12.1 %input_other.2 = bf16[1024,1280]{1,0:T(8,128)(2,1)} custom-call(bf16[320,2048]{1,0:T(8,128)(2,1)} %get-tuple-element.194.refs_0_.dq_ref, bf16[320,2048]{1,0:T(8,128)(2,1)} %get-tuple-element.196.refs_1_.dk_ref, bf16[320,2048]{1,0:T(8,128)(2,1)} %get-tuple-element.192.refs_2_.dv_ref, bf16[320,2048]{1,0:T(8,128)(2,1)} %get-tuple-element.183.dq_ref.refs_3_, ...), custom_call_target="tpu_custom_call" | custom-call | flops 5033164800 | bytes 10485760 | tf_op jit(solution)/shard_map/input_other/pallas_call | solution.py:804
  535.4 3.5 collective-permute-done.18.refs_0_
  538.9 11.0 %weight_grad.5 = bf16[1280,1024]{1,0:T(8,128)(2,1)} custom-call(bf16[1024,1280]{1,0:T(8,128)(2,1)} %get-tuple-element.149.h_ref.own_ref, bf16[1024,1280]{1,0:T(8,128)(2,1)} %collective-permute-done.7.h_ref.other_ref, bf16[320,2048]{1,0:T(8,128)(2,1)} %get-tuple-element.194.refs_0_.dq_ref, bf16[320,2048]{1,0:T(8,128)(2,1)} %get-tuple-element.196.refs_1_.dk_ref, ...), custom_call_target="tpu_custom_call" | custom-call | flops 5033164800 | bytes 15728640 | tf_op jit(solution)/shard_map/weight_grad/pallas_call | solution.py:770
  553.4 15.6 %input_own.2 = (f32[1024,1280]{1,0:T(8,128)}, f32[8,1280]{1,0:T(8,128)}) custom-call(bf16[320,2048]{1,0:T(8,128)(2,1)} %get-tuple-element.194.refs_0_.dq_ref, bf16[320,2048]{1,0:T(8,128)(2,1)} %get-tuple-element.196.refs_1_.dk_ref, bf16[320,2048]{1,0:T(8,128)(2,1)} %get-tuple-element.192.refs_2_.dv_ref, bf16[320,2048]{1,0:T(8,128)(2,1)} %get-tuple-element.183.dq_ref.refs_3_, ...), custom_call_target="tpu_custom_call" | custom-call | flops 5033164800 | bytes 31457280 | tf_op jit(solution)/shard_map/input_own/pallas_call | solution.py:840
  569.0 27.9 %mlp_back.3 = (f32[1024,1280]{1,0:T(8,128)}, bf16[1024,1280]{1,0:T(8,128)(2,1)}, f32[8,1280]{1,0:T(8,128)}, bf16[1280,640]{1,0:T(8,128)(2,1)}, bf16[1280,640]{1,...) custom-call(f32[1024,1280]{1,0:T(8,128)} %get-tuple-element.201.g_ref, ...), custom_call_target="tpu_custom_call" | custom-call | flops 13421772800 | bytes 39321600 | tf_op jit(solution)/shard_map/mlp_back/pallas_call | solution.py:672
  598.2 5.8 grad_att.6.refs_0_
  604.0 19.5 %reduce-scatter.7.cloned.1.call-done = bf16[160,1024]{1,0:T(8,128)(2,1)} async-done(((bf16[1280,1024]{1,0:T(8,128)(2,1)}), bf16[160,1024]{1,0:T(8,128)(2,1)}) %reduce-scatter.7.cloned.1.call-update) | async-done | bytes 327696 | tf_op jit(solution)/shard_map/reduce_scatter | solution.py:870
  623.5 1.9 convert_element_type.82
  626.9 11.4 %out_grad.3 = (bf16[1280,1024]{1,0:T(8,128)(2,1)}, bf16[1280,1024]{1,0:T(8,128)(2,1)}) custom-call(bf16[1024,1280]{1,0:T(8,128)(2,1)} %get-tuple-element.204.own_ref.g_ref, bf16[1024,1280]{1,0:T(8,128)(2,1)} %copy-done.2, bf16[640,2048]{1,0:T(8,128)(2,1)} %get-tuple-element.142.att_ref.o_ref, bf16[1280,640]{1,0:T(8,128)(2,1)} %get-tuple-element.205.u0, ...), custom_call_target="tpu_custom_call" | custom-call | flops 3355443200 | bytes 10485760 | tf_op jit(solution)/shard_map/out_grad/pallas_call | solution.py:735
  639.9 5.8 grad_att.7.g_ref
  645.6 41.9 %attention_backward.6 = (bf16[320,2048]{1,0:T(8,128)(2,1)}, bf16[320,2048]{1,0:T(8,128)(2,1)}, bf16[320,2048]{1,0:T(8,128)(2,1)}, f32[80,128]{1,0:T(8,128)}) custom-call(s32[1]{0:T(128)} %dynamic_slice.30.prefix_ref, s32[4]{0:T(128)} %fusion.21.order_ref, bf16[640,2048]{1,0:T(8,128)(2,1)} %get-tuple-element.136.q_ref, ...), custom_call_target="tpu_custom_call" | custom-call | flops 26843545600 | bytes 10485760 | tf_op jit(solution)/shard_map/attention_backward/pallas_call | solution.py:187
  687.6 10.4 %weight_grad.6 = bf16[1280,1024]{1,0:T(8,128)(2,1)} custom-call(bf16[1024,1280]{1,0:T(8,128)(2,1)} %copy-done.6, bf16[1024,1280]{1,0:T(8,128)(2,1)} %collective-permute-done.h_ref.other_ref, bf16[320,2048]{1,0:T(8,128)(2,1)} %get-tuple-element.214.dq_ref.refs_3_, bf16[320,2048]{1,0:T(8,128)(2,1)} %get-tuple-element.215.dk_ref.refs_4_, ...), custom_call_target="tpu_custom_call" | custom-call | flops 5033164800 | bytes 15728640 | tf_op jit(solution)/shard_map/weight_grad/pallas_call | solution.py:770
  697.9 4.5 add_convert_fusion
  703.1 41.6 %attention_backward.7 = (bf16[320,2048]{1,0:T(8,128)(2,1)}, bf16[320,2048]{1,0:T(8,128)(2,1)}, bf16[320,2048]{1,0:T(8,128)(2,1)}, f32[80,128]{1,0:T(8,128)}) custom-call(s32[1]{0:T(128)} %dynamic_slice.30.prefix_ref, s32[4]{0:T(128)} %fusion.21.order_ref, bf16[640,2048]{1,0:T(8,128)(2,1)} %get-tuple-element.136.q_ref, ...), custom_call_target="tpu_custom_call" | custom-call | flops 26843545600 | bytes 10485760 | tf_op jit(solution)/shard_map/attention_backward/pallas_call | solution.py:187
  744.8 12.1 %input_other.3 = bf16[1024,1280]{1,0:T(8,128)(2,1)} custom-call(bf16[320,2048]{1,0:T(8,128)(2,1)} %get-tuple-element.227.refs_0_.dq_ref, bf16[320,2048]{1,0:T(8,128)(2,1)} %get-tuple-element.229.refs_1_.dk_ref, bf16[320,2048]{1,0:T(8,128)(2,1)} %get-tuple-element.225.refs_2_.dv_ref, bf16[320,2048]{1,0:T(8,128)(2,1)} %get-tuple-element.214.dq_ref.refs_3_, ...), custom_call_target="tpu_custom_call" | custom-call | flops 5033164800 | bytes 10485760 | tf_op jit(solution)/shard_map/input_other/pallas_call | solution.py:804
  756.9 3.2 collective-permute-done.24.refs_0_
  761.3 11.0 %weight_grad.7 = bf16[1280,1024]{1,0:T(8,128)(2,1)} custom-call(bf16[1024,1280]{1,0:T(8,128)(2,1)} %copy-done.6, bf16[1024,1280]{1,0:T(8,128)(2,1)} %collective-permute-done.h_ref.other_ref, bf16[320,2048]{1,0:T(8,128)(2,1)} %get-tuple-element.227.refs_0_.dq_ref, bf16[320,2048]{1,0:T(8,128)(2,1)} %get-tuple-element.229.refs_1_.dk_ref, ...), custom_call_target="tpu_custom_call" | custom-call | flops 5033164800 | bytes 15728640 | tf_op jit(solution)/shard_map/weight_grad/pallas_call | solution.py:770
  773.8 15.6 %input_own.3 = (f32[1024,1280]{1,0:T(8,128)}, f32[8,1280]{1,0:T(8,128)}) custom-call(bf16[320,2048]{1,0:T(8,128)(2,1)} %get-tuple-element.227.refs_0_.dq_ref, bf16[320,2048]{1,0:T(8,128)(2,1)} %get-tuple-element.229.refs_1_.dk_ref, bf16[320,2048]{1,0:T(8,128)(2,1)} %get-tuple-element.225.refs_2_.dv_ref, bf16[320,2048]{1,0:T(8,128)(2,1)} %get-tuple-element.214.dq_ref.refs_3_, ...), custom_call_target="tpu_custom_call" | custom-call | flops 5033164800 | bytes 31457280 | tf_op jit(solution)/shard_map/input_own/pallas_call | solution.py:840
  790.8 2.6 convert_select_fusion.3
  794.3 1.9 fusion.3
  799.0 2.7 pad_maximum_fusion.2
  803.7 2.1 collective-permute-done.30
  808.5 2.2 collective-permute-done.31
  811.9 14.9 %collective-permute-done.26 = bf16[512,1280]{1,0:T(8,128)(2,1)S(1)} collective-permute-done((bf16[512,1280]{1,0:T(8,128)(2,1)S(1)}, bf16[512,1280]{1,0:T(8,128)(2,1)S(1)}, u32[]{:S(2)}, u32[]{:S(2)}) %collective-permute-start.26) | collective-permute-done | bytes 1310752 | tf_op jit(solution)/shard_map/ppermute | solution.py:350
  826.7 2.1 convert_select_fusion.1
  828.8 2.7 pad_maximum_fusion.3
  831.5 13.6 %reduce-scatter.9.cloned.1.call-done = bf16[160,1024]{1,0:T(8,128)(2,1)} async-done(((bf16[1280,1024]{1,0:T(8,128)(2,1)}), bf16[160,1024]{1,0:T(8,128)(2,1)}) %reduce-scatter.9.cloned.1.call-update) | async-done | bytes 327696 | tf_op jit(solution)/shard_map/reduce_scatter | solution.py:870
  (173 shorter events, 49.0 us)
Async XLA Ops:
  7.2 4.3 copy-start.11
  7.2 120.0 %all-gather.11.cloned.1.call-start = ((), (), s32[]{:S(2)}) async-start(), calls=%async_computation.9 | async-start | bytes 1843200 | tf_op jit(solution)/shard_map/all_gather | solution.py:900
  9.4 120.3 %all-gather.9.cloned.1.call-start = ((), (), s32[]{:S(2)}) async-start(), calls=%async_computation.8 | async-start | bytes 1843200 | tf_op jit(solution)/shard_map/all_gather | solution.py:900
  11.4 187.4 %all-gather.13.cloned.1.call-start = ((), (), s32[]{:S(2)}) async-start(), calls=%async_computation.10 | async-start | bytes 1843200 | tf_op jit(solution)/shard_map/all_gather | solution.py:900
  12.3 213.1 %all-gather.15.cloned.1.call-start = ((), (), s32[]{:S(2)}) async-start(), calls=%async_computation.11 | async-start | bytes 1843200 | tf_op jit(solution)/shard_map/all_gather | solution.py:900
  124.1 6.2 copy-start.21
  124.1 7.7 copy-start.28
  127.1 8.6 %copy-start.6 = (bf16[1024,1280]{1,0:T(8,128)(2,1)}, bf16[1024,1280]{1,0:T(8,128)(2,1)S(1)}, u32[]{:S(2)}) copy-start(bf16[1024,1280]{1,0:T(8,128)(2,1)S(1)} %get-tuple-element.128.h_ref.own_ref) | copy-start | bytes 7864324
  129.7 15.8 %collective-permute-start = (bf16[1024,1280]{1,0:T(8,128)(2,1)S(1)}, bf16[1024,1280]{1,0:T(8,128)(2,1)}, u32[]{:S(2)}, u32[]{:S(2)}) collective-permute-start(bf16[1024,1280]{1,0:T(8,128)(2,1)S(1)} %get-tuple-element.128.h_ref.own_ref), channel_id=1, source_target_pairs={{0,1},{1,0},{2,3},{3,2},{4,5},{5,4},{6,7},{7,6},{8,9},{9,8},{10,11... | collective-permute-start | bytes 7864328 | tf_op jit(solution)/shard_map/ppermute | solution.py:353
  129.7 421.2 %reduce-scatter.5.cloned.1.call-start = ((), (), s32[]{:S(2)}) async-start(), calls=%async_computation.4 | async-start | bytes 2949120 | tf_op jit(solution)/shard_map/reduce_scatter | solution.py:870
  133.0 65.8 %collective-permute-start.1 = (bf16[1280,640]{1,0:T(8,128)(2,1)}, bf16[1280,640]{1,0:T(8,128)(2,1)}, u32[]{:S(2)}, u32[]{:S(2)}) collective-permute-start(bf16[1280,640]{1,0:T(8,128)(2,1)} %bitcast.10.un0), channel_id=1, source_target_pairs={{0,2},{1,3},{2,0},{3,1},{4,6},{5,7},{6,4},{7,5},{8,10},{9,11},{10,... | collective-permute-start | bytes 4915208 | tf_op jit(solution)/shard_map/ppermute | solution.py:350
  135.7 71.9 %collective-permute-start.2 = (bf16[1280,640]{1,0:T(8,128)(2,1)}, bf16[1280,640]{1,0:T(8,128)(2,1)}, u32[]{:S(2)}, u32[]{:S(2)}) collective-permute-start(bf16[1280,640]{1,0:T(8,128)(2,1)} %bitcast.131), channel_id=1, source_target_pairs={{0,2},{1,3},{2,0},{3,1},{4,6},{5,7},{6,4},{7,5},{8,10},{9,11},{10,... | collective-permute-start | bytes 4915208 | tf_op jit(solution)/shard_map/ppermute | solution.py:350
  207.5 6.7 copy-start
  213.8 11.6 %collective-permute-start.3 = (bf16[1024,1280]{1,0:T(8,128)(2,1)}, bf16[1024,1280]{1,0:T(8,128)(2,1)}, u32[]{:S(2)}, u32[]{:S(2)}) collective-permute-start(bf16[1024,1280]{1,0:T(8,128)(2,1)} %out_project.2), channel_id=1, source_target_pairs={{0,1},{1,0},{2,3},{3,2},{4,5},{5,4},{6,7},{7,6},{8,9},{9,8},{10,11... | collective-permute-start | bytes 7864328 | tf_op jit(solution)/shard_map/ppermute | solution.py:353
  213.8 11.6 %collective-permute-start.4 = (bf16[1280,640]{1,0:T(8,128)(2,1)}, bf16[1280,640]{1,0:T(8,128)(2,1)}, u32[]{:S(2)}, u32[]{:S(2)}) collective-permute-start(bf16[1280,640]{1,0:T(8,128)(2,1)} %bitcast.10.un0), channel_id=1, source_target_pairs={{0,1},{1,0},{2,3},{3,2},{4,5},{5,4},{6,7},{7,6},{8,9},{9,8},{10,11... | collective-permute-start | bytes 4915208 | tf_op jit(solution)/shard_map/ppermute | solution.py:353
  214.3 11.1 %collective-permute-start.5 = (bf16[1280,640]{1,0:T(8,128)(2,1)}, bf16[1280,640]{1,0:T(8,128)(2,1)}, u32[]{:S(2)}, u32[]{:S(2)}) collective-permute-start(bf16[1280,640]{1,0:T(8,128)(2,1)} %collective-permute-done.1.un1), channel_id=1, source_target_pairs={{0,1},{1,0},{2,3},{3,2},{4,5},{5,4},{6,7},{7,6},{8,9},{9,8},{10,11... | collective-permute-start | bytes 4915208 | tf_op jit(solution)/shard_map/ppermute | solution.py:353
  214.3 38.2 %collective-permute-start.6 = (bf16[1280,640]{1,0:T(8,128)(2,1)S(1)}, bf16[1280,640]{1,0:T(8,128)(2,1)S(1)}, u32[]{:S(2)}, u32[]{:S(2)}) collective-permute-start(bf16[1280,640]{1,0:T(8,128)(2,1)S(1)} %bitcast.114), channel_id=1, source_target_pairs={{0,2},{1,3},{2,0},{3,1},{4,6},{5,7},{6,4},{7,5},{8,10},{9,11},{10,... | collective-permute-start | bytes 4915208 | tf_op jit(solution)/shard_map/ppermute | solution.py:350
  252.5 2.8 copy-start.1
  252.5 12.6 %collective-permute-start.7 = (bf16[1024,1280]{1,0:T(8,128)(2,1)}, bf16[1024,1280]{1,0:T(8,128)(2,1)}, u32[]{:S(2)}, u32[]{:S(2)}) collective-permute-start(bf16[1024,1280]{1,0:T(8,128)(2,1)} %get-tuple-element.149.h_ref.own_ref), channel_id=1, source_target_pairs={{0,1},{1,0},{2,3},{3,2},{4,5},{5,4},{6,7},{7,6},{8,9},{9,8},{10,11... | collective-permute-start | bytes 7864328 | tf_op jit(solution)/shard_map/ppermute | solution.py:353
  253.5 65.6 %collective-permute-start.9 = (bf16[512,1280]{1,0:T(8,128)(2,1)}, bf16[512,1280]{1,0:T(8,128)(2,1)S(1)}, u32[]{:S(2)}, u32[]{:S(2)}) collective-permute-start(bf16[512,1280]{1,0:T(8,128)(2,1)} %fusion.1), channel_id=1, source_target_pairs={{0,2},{1,3},{2,0},{3,1},{4,6},{5,7},{6,4},{7,5},{8,10},{9,11},{10,... | collective-permute-start | bytes 3932168 | tf_op jit(solution)/shard_map/ppermute | solution.py:350
  265.1 10.0 %copy-start.25 = (bf16[1,1280,640]{2,1,0:T(8,128)(2,1)S(1)}, bf16[1,1280,640]{2,1,0:T(8,128)(2,1)}, u32[]{:S(2)}) copy-start(bf16[1,1280,640]{2,1,0:T(8,128)(2,1)} %all-gather.15.cloned.1.call-done) | copy-start | bytes 4915204
  275.0 45.0 %collective-permute-start.8 = (bf16[1280,640]{1,0:T(8,128)(2,1)S(1)}, bf16[1280,640]{1,0:T(8,128)(2,1)}, u32[]{:S(2)}, u32[]{:S(2)}) collective-permute-start(bf16[1280,640]{1,0:T(8,128)(2,1)S(1)} %bitcast.141), channel_id=1, source_target_pairs={{0,2},{1,3},{2,0},{3,1},{4,6},{5,7},{6,4},{7,5},{8,10},{9,11},{10,... | collective-permute-start | bytes 4915208 | tf_op jit(solution)/shard_map/ppermute | solution.py:350
  326.1 11.6 %collective-permute-start.10 = (bf16[1024,1280]{1,0:T(8,128)(2,1)}, bf16[1024,1280]{1,0:T(8,128)(2,1)}, u32[]{:S(2)}, u32[]{:S(2)}) collective-permute-start(bf16[1024,1280]{1,0:T(8,128)(2,1)} %out_project.3), channel_id=1, source_target_pairs={{0,1},{1,0},{2,3},{3,2},{4,5},{5,4},{6,7},{7,6},{8,9},{9,8},{10,11... | collective-permute-start | bytes 7864328 | tf_op jit(solution)/shard_map/ppermute | solution.py:353
  326.1 9.2 %collective-permute-start.11 = (bf16[1280,640]{1,0:T(8,128)(2,1)S(1)}, bf16[1280,640]{1,0:T(8,128)(2,1)S(1)}, u32[]{:S(2)}, u32[]{:S(2)}) collective-permute-start(bf16[1280,640]{1,0:T(8,128)(2,1)S(1)} %bitcast.142), channel_id=1, source_target_pairs={{0,1},{1,0},{2,3},{3,2},{4,5},{5,4},{6,7},{7,6},{8,9},{9,8},{10,11... | collective-permute-start | bytes 4915208 | tf_op jit(solution)/shard_map/ppermute | solution.py:353
  326.6 9.9 %collective-permute-start.12 = (bf16[1280,640]{1,0:T(8,128)(2,1)}, bf16[1280,640]{1,0:T(8,128)(2,1)S(1)}, u32[]{:S(2)}, u32[]{:S(2)}) collective-permute-start(bf16[1280,640]{1,0:T(8,128)(2,1)} %collective-permute-done.8.un1), channel_id=1, source_target_pairs={{0,1},{1,0},{2,3},{3,2},{4,5},{5,4},{6,7},{7,6},{8,9},{9,8},{10,11... | collective-permute-start | bytes 4915208 | tf_op jit(solution)/shard_map/ppermute | solution.py:353
  359.5 31.1 %collective-permute-start.13 = (bf16[512,1280]{1,0:T(8,128)(2,1)S(1)}, bf16[512,1280]{1,0:T(8,128)(2,1)S(1)}, u32[]{:S(2)}, u32[]{:S(2)}) collective-permute-start(bf16[512,1280]{1,0:T(8,128)(2,1)S(1)} %fusion.2), channel_id=1, source_target_pairs={{0,2},{1,3},{2,0},{3,1},{4,6},{5,7},{6,4},{7,5},{8,10},{9,11},{10,... | collective-permute-start | bytes 3932168 | tf_op jit(solution)/shard_map/ppermute | solution.py:350
  391.7 9.9 %collective-permute-start.14 = (bf16[1024,1280]{1,0:T(8,128)(2,1)}, bf16[1024,1280]{1,0:T(8,128)(2,1)S(1)}, u32[]{:S(2)}, u32[]{:S(2)}) collective-permute-start(bf16[1024,1280]{1,0:T(8,128)(2,1)} %get-tuple-element.173.own_ref.g_ref), channel_id=1, source_target_pairs={{0,1},{1,0},{2,3},{3,2},{4,5},{5,4},{6,7},{7,6},{8,9},{9,8},{10,11... | collective-permute-start | bytes 7864328 | tf_op jit(solution)/shard_map/ppermute | solution.py:353
  391.7 7.2 collective-permute-start.15
  392.2 9.4 %collective-permute-start.16 = (bf16[1280,640]{1,0:T(8,128)(2,1)}, bf16[1280,640]{1,0:T(8,128)(2,1)}, u32[]{:S(2)}, u32[]{:S(2)}) collective-permute-start(bf16[1280,640]{1,0:T(8,128)(2,1)} %get-tuple-element.177), channel_id=1, source_target_pairs={{0,1},{1,0},{2,3},{3,2},{4,5},{5,4},{6,7},{7,6},{8,9},{9,8},{10,11... | collective-permute-start | bytes 4915208 | tf_op jit(solution)/shard_map/ppermute | solution.py:353
  401.6 1.5 copy-start.3
  414.5 59.5 %collective-permute-start.17 = (bf16[1280,1024]{1,0:T(8,128)(2,1)}, bf16[1280,1024]{1,0:T(8,128)(2,1)}, u32[]{:S(2)}, u32[]{:S(2)}) collective-permute-start(bf16[1280,1024]{1,0:T(8,128)(2,1)} %get-tuple-element.186), channel_id=1, source_target_pairs={{0,2},{1,3},{2,0},{3,1},{4,6},{5,7},{6,4},{7,5},{8,10},{9,11},{10,... | collective-permute-start | bytes 7864328 | tf_op jit(solution)/shard_map/ppermute | solution.py:350
  463.6 10.4 %copy-start.7 = (bf16[1280,1024]{1,0:T(8,128)(2,1)S(1)}, bf16[1280,1024]{1,0:T(8,128)(2,1)}, u32[]{:S(2)}) copy-start(bf16[1280,1024]{1,0:T(8,128)(2,1)} %get-tuple-element.180) | copy-start | bytes 7864324
  478.4 1.7 copy-start.24
  478.5 145.1 %reduce-scatter.7.cloned.1.call-start = ((), (), s32[]{:S(2)}) async-start(), calls=%async_computation.5 | async-start | bytes 2949120 | tf_op jit(solution)/shard_map/reduce_scatter | solution.py:870
  480.2 58.8 %collective-permute-start.18 = (bf16[1280,1024]{1,0:T(8,128)(2,1)S(1)}, bf16[1280,1024]{1,0:T(8,128)(2,1)}, u32[]{:S(2)}, u32[]{:S(2)}) collective-permute-start(bf16[1280,1024]{1,0:T(8,128)(2,1)S(1)} %copy-done.24), channel_id=1, source_target_pairs={{0,2},{1,3},{2,0},{3,1},{4,6},{5,7},{6,4},{7,5},{8,10},{9,11},{10,... | collective-permute-start | bytes 7864328 | tf_op jit(solution)/shard_map/ppermute | solution.py:350
  538.9 13.0 %collective-permute-start.19 = (bf16[1024,1280]{1,0:T(8,128)(2,1)}, bf16[1024,1280]{1,0:T(8,128)(2,1)S(1)}, u32[]{:S(2)}, u32[]{:S(2)}) collective-permute-start(bf16[1024,1280]{1,0:T(8,128)(2,1)} %input_other.2), channel_id=1, source_target_pairs={{0,1},{1,0},{2,3},{3,2},{4,5},{5,4},{6,7},{7,6},{8,9},{9,8},{10,11... | collective-permute-start | bytes 7864328 | tf_op jit(solution)/shard_map/ppermute | solution.py:353
  550.0 252.7 %reduce-scatter.11.cloned.1.call-start = ((), (), s32[]{:S(2)}) async-start(), calls=%async_computation.7 | async-start | bytes 2949120 | tf_op jit(solution)/shard_map/reduce_scatter | solution.py:870
  551.9 1.5 copy-start.5
  569.0 28.5 %copy-start.23 = (f32[80,1]{0,1:T(1,128)S(1)}, f32[80,1]{0,1:T(1,128)}, u32[]{:S(2)}) copy-start(f32[80,1]{0,1:T(1,128)} %get-tuple-element.293) | copy-start | bytes 964
  596.9 28.6 %collective-permute-start.20 = (bf16[1024,1280]{1,0:T(8,128)(2,1)}, bf16[1024,1280]{1,0:T(8,128)(2,1)S(1)}, u32[]{:S(2)}, u32[]{:S(2)}) collective-permute-start(bf16[1024,1280]{1,0:T(8,128)(2,1)} %get-tuple-element.204.own_ref.g_ref), channel_id=1, source_target_pairs={{0,1},{1,0},{2,3},{3,2},{4,5},{5,4},{6,7},{7,6},{8,9},{9,8},{10,11... | collective-permute-start | bytes 7864328 | tf_op jit(solution)/shard_map/ppermute | solution.py:353
  596.9 28.5 %collective-permute-start.21 = (bf16[1280,640]{1,0:T(8,128)(2,1)}, bf16[1280,640]{1,0:T(8,128)(2,1)}, u32[]{:S(2)}, u32[]{:S(2)}) collective-permute-start(bf16[1280,640]{1,0:T(8,128)(2,1)} %get-tuple-element.207), channel_id=1, source_target_pairs={{0,1},{1,0},{2,3},{3,2},{4,5},{5,4},{6,7},{7,6},{8,9},{9,8},{10,11... | collective-permute-start | bytes 4915208 | tf_op jit(solution)/shard_map/ppermute | solution.py:353
  597.4 28.0 %collective-permute-start.22 = (bf16[1280,640]{1,0:T(8,128)(2,1)}, bf16[1280,640]{1,0:T(8,128)(2,1)}, u32[]{:S(2)}, u32[]{:S(2)}) collective-permute-start(bf16[1280,640]{1,0:T(8,128)(2,1)} %get-tuple-element.208), channel_id=1, source_target_pairs={{0,1},{1,0},{2,3},{3,2},{4,5},{5,4},{6,7},{7,6},{8,9},{9,8},{10,11... | collective-permute-start | bytes 4915208 | tf_op jit(solution)/shard_map/ppermute | solution.py:353
  625.4 1.5 copy-start.2
  638.4 59.5 %collective-permute-start.23 = (bf16[1280,1024]{1,0:T(8,128)(2,1)}, bf16[1280,1024]{1,0:T(8,128)(2,1)}, u32[]{:S(2)}, u32[]{:S(2)}) collective-permute-start(bf16[1280,1024]{1,0:T(8,128)(2,1)} %get-tuple-element.217), channel_id=1, source_target_pairs={{0,2},{1,3},{2,0},{3,1},{4,6},{5,7},{6,4},{7,5},{8,10},{9,11},{10,... | collective-permute-start | bytes 7864328 | tf_op jit(solution)/shard_map/ppermute | solution.py:350
  687.6 10.4 %copy-start.8 = (bf16[1280,1024]{1,0:T(8,128)(2,1)S(1)}, bf16[1280,1024]{1,0:T(8,128)(2,1)}, u32[]{:S(2)}) copy-start(bf16[1280,1024]{1,0:T(8,128)(2,1)} %get-tuple-element.211) | copy-start | bytes 7864324
  702.4 57.6 %collective-permute-start.24 = (bf16[1280,1024]{1,0:T(8,128)(2,1)}, bf16[1280,1024]{1,0:T(8,128)(2,1)}, u32[]{:S(2)}, u32[]{:S(2)}) collective-permute-start(bf16[1280,1024]{1,0:T(8,128)(2,1)} %weight_grad.6), channel_id=1, source_target_pairs={{0,2},{1,3},{2,0},{3,1},{4,6},{5,7},{6,4},{7,5},{8,10},{9,11},{10,... | collective-permute-start | bytes 7864328 | tf_op jit(solution)/shard_map/ppermute | solution.py:350
  703.0 142.1 %reduce-scatter.9.cloned.1.call-start = ((), (), s32[]{:S(2)}) async-start(), calls=%async_computation.6 | async-start | bytes 2949120 | tf_op jit(solution)/shard_map/reduce_scatter | solution.py:870
  744.7 15.4 %copy-start.16 = (f32[8,1280]{1,0:T(8,128)S(1)}, f32[8,1280]{1,0:T(8,128)}, u32[]{:S(2)}) copy-start(f32[8,1280]{1,0:T(8,128)} %get-tuple-element.242) | copy-start | bytes 122884
  744.7 15.4 %copy-start.12 = (f32[80,128]{1,0:T(8,128)S(1)}, f32[80,128]{1,0:T(8,128)}, u32[]{:S(2)}) copy-start(f32[80,128]{1,0:T(8,128)} %get-tuple-element.243) | copy-start | bytes 122884
  744.7 15.4 %copy-start.13 = (f32[80,128]{1,0:T(8,128)S(1)}, f32[80,128]{1,0:T(8,128)}, u32[]{:S(2)}) copy-start(f32[80,128]{1,0:T(8,128)} %get-tuple-element.244) | copy-start | bytes 122884
  744.7 16.3 %copy-start.17 = (f32[8,1280]{1,0:T(8,128)S(1)}, f32[8,1280]{1,0:T(8,128)}, u32[]{:S(2)}) copy-start(f32[8,1280]{1,0:T(8,128)} %get-tuple-element.241) | copy-start | bytes 122884
  744.7 16.3 %copy-start.14 = (f32[80,128]{1,0:T(8,128)S(1)}, f32[80,128]{1,0:T(8,128)}, u32[]{:S(2)}) copy-start(f32[80,128]{1,0:T(8,128)} %get-tuple-element.239) | copy-start | bytes 122884
  744.8 16.3 %copy-start.15 = (f32[80,128]{1,0:T(8,128)S(1)}, f32[80,128]{1,0:T(8,128)}, u32[]{:S(2)}) copy-start(f32[80,128]{1,0:T(8,128)} %get-tuple-element.240) | copy-start | bytes 122884
  744.8 16.4 %copy-start.20 = (f32[2,80]{1,0:T(2,128)S(1)}, f32[2,80]{1,0:T(2,128)}, u32[]{:S(2)}) copy-start(f32[2,80]{1,0:T(2,128)} %copy-done.19) | copy-start | bytes 1924
  760.1 12.2 %collective-permute-start.25 = (bf16[1024,1280]{1,0:T(8,128)(2,1)}, bf16[1024,1280]{1,0:T(8,128)(2,1)S(1)}, u32[]{:S(2)}, u32[]{:S(2)}) collective-permute-start(bf16[1024,1280]{1,0:T(8,128)(2,1)} %input_other.3), channel_id=1, source_target_pairs={{0,1},{1,0},{2,3},{3,2},{4,5},{5,4},{6,7},{7,6},{8,9},{9,8},{10,11... | collective-permute-start | bytes 7864328 | tf_op jit(solution)/shard_map/ppermute | solution.py:353
  772.3 1.5 copy-start.4
  790.2 3.1 collective-permute-start.27
  793.4 4.1 collective-permute-start.28
  796.2 30.5 %collective-permute-start.26 = (bf16[512,1280]{1,0:T(8,128)(2,1)S(1)}, bf16[512,1280]{1,0:T(8,128)(2,1)S(1)}, u32[]{:S(2)}, u32[]{:S(2)}) collective-permute-start(bf16[512,1280]{1,0:T(8,128)(2,1)S(1)} %fusion.3), channel_id=1, source_target_pairs={{0,2},{1,3},{2,0},{3,1},{4,6},{5,7},{6,4},{7,5},{8,10},{9,11},{10,... | collective-permute-start | bytes 3932168 | tf_op jit(solution)/shard_map/ppermute | solution.py:350
  797.6 4.2 collective-permute-start.29
  801.7 8.9 %copy-start.22 = (f32[2,80]{1,0:T(2,128)S(1)}, f32[2,80]{1,0:T(2,128)}, u32[]{:S(2)}) copy-start(f32[2,80]{1,0:T(2,128)} %param.16) | copy-start | bytes 1924
  801.8 4.1 collective-permute-start.30
  805.9 4.8 collective-permute-start.31
  828.8 17.3 %copy-start.9 = (f32[160,1024]{1,0:T(8,128)S(1)}, f32[160,1024]{1,0:T(8,128)}, u32[]{:S(2)}) copy-start(f32[160,1024]{1,0:T(8,128)} %convert_element_type.82) | copy-start | bytes 1966084
  (5 other events, 4.7 us)
Sparse Core Ops, SparseCore 0:
  10.8 66.4 all-gather.10
  80.0 49.5 all-gather.8
  131.9 47.4 all-gather.12
  181.9 43.3 all-gather.14
  478.6 72.2 reduce-scatter.4
  554.2 69.2 reduce-scatter.6
  703.1 68.7 reduce-scatter.10
  775.4 69.6 reduce-scatter.8

commit v4 on v3

--- a/solution.py
+++ b/solution.py
@@ -27,12 +27,16 @@
     length = q_ref.shape[1]
     prefix = prefix_ref[0]
     ext = value_ext.shape[1]
+    bound = 0.0
     for h in range(pair):
-        key_rows[h] = k_ref[h * dh:(h + 1) * dh, :].T
-        value_ext[h, :dh] = v_ref[h * dh:(h + 1) * dh, :]
+        rows = slice(h * dh, (h + 1) * dh)
+        q, k = q_ref[rows, :].astype(F32), k_ref[rows, :].astype(F32)
+        bound = jnp.maximum(bound, jnp.max(jnp.sum(q * q, axis=0)) * jnp.max(jnp.sum(k * k, axis=0)))
+        key_rows[h] = k_ref[rows, :].T
+        value_ext[h, :dh] = v_ref[rows, :]
         value_ext[h, dh:] = jnp.ones((ext - dh, length), BF16)
 
-    def one_query(qi, carry):
+    def one_query(shifted, qi, carry):
         start = qi * bq
         here = pl.ds(pl.multiple_of(order_ref[qi] * bq, bq), bq)
         queries = [q_ref[h * dh:(h + 1) * dh, here] for h in range(pair)]
@@ -48,27 +52,38 @@
             scores = [dot(key_rows[h, there], queries[h]) for h in range(pair)]
             fresh = []
             for h in range(pair):
-                top, total = state[h]
-                s = scores[h]
-                if masked:
-                    s = jnp.where(allowed, s, MASKED)
-                new_top = jnp.maximum(top, jnp.max(s, axis=0, keepdims=True))
-                p = jnp.exp2(s - new_top).astype(BF16)
-                total = total * jnp.exp2(top - new_top) + dot(value_ext[h, :, there], p)
-                fresh.append((new_top, total))
+                s = jnp.where(allowed, scores[h], MASKED) if masked else scores[h]
+                if shifted:
+                    top, total = state[h]
+                    new_top = jnp.maximum(top, jnp.max(s, axis=0, keepdims=True))
+                    p = jnp.exp2(s - new_top).astype(BF16)
+                    total = total * jnp.exp2(top - new_top) + dot(value_ext[h, :, there], p)
+                    fresh.append((new_top, total))
+                else:
+                    fresh.append(state[h] + dot(value_ext[h, :, there], jnp.exp2(s).astype(BF16)))
             return tuple(fresh)
 
-        state = tuple((jnp.full((1, bq), MASKED, F32), jnp.zeros((ext, bq), F32)) for _ in range(pair))
+        zero = jnp.zeros((ext, bq), F32)
+        state = tuple((jnp.full((1, bq), MASKED, F32), zero) if shifted else zero for _ in range(pair))
         state = lax.fori_loop(0, full, functools.partial(step, False), state)
         state = lax.fori_loop(full, stop, functools.partial(step, True), state)
         for h in range(pair):
-            top, total = state[h]
+            top, total = state[h] if shifted else (0.0, state[h])
             norm = total[dh:dh + 1]
             o_ref[h * dh:(h + 1) * dh, here] = (total[:dh] / norm).astype(BF16)
             lse_ref[h, :, here] = top + jnp.log2(norm)
         return carry
 
-    lax.fori_loop(0, length // bq, one_query, 0)
+    small = bound <= 3600.0
+
+    @pl.when(small)
+    def _():
+        lax.fori_loop(0, length // bq, functools.partial(one_query, False), 0)
+
+    @pl.when(jnp.logical_not(small))
+    def _():
+        lax.fori_loop(0, length // bq, functools.partial(one_query, True), 0)
+
 
 def attention_forward(q, k, v, prefix, order, dh, pair=4):
     width, length = q.shape
@@ -99,32 +114,34 @@
     return a, b, c
 
 def backward_kernel(prefix_ref, order_ref, q_ref, k_ref, v_ref, o_ref, g_ref, lse_ref, scale_ref, dq_ref, dk_ref, dv_ref, fg_ref,
-                    key_rows, key_ext, value_ext, query_ext, grad_ext, dk_acc, dv_acc, *, pair, dh, bq, bk):
+                    key_ext, value_ext, query_ext, grad_ext, dk_acc, dv_acc, *, pair, dh, bq, bk):
     length = q_ref.shape[1]
     prefix = prefix_ref[0]
-    ext = key_ext.shape[1]
-    pad = ext - dh
-    ones = (lax.broadcasted_iota(jnp.int32, (pad, length), 0) < 3).astype(F32).astype(BF16)
-    fg_zero = pl.program_id(0) == 0
-    @pl.when(fg_zero)
+    pad = key_ext.shape[1] - dh
+    index = lax.broadcasted_iota(jnp.int32, (pad, length), 0)
+    ones = (index < 3).astype(F32).astype(BF16)
+
+    @pl.when(pl.program_id(0) == 0)
     def _():
         fg_ref[...] = jnp.zeros_like(fg_ref)
+
+    def tail(row):
+        high, mid, low = (part.astype(F32) for part in split3(-row))
+        rest = jnp.where(index == 1, mid, jnp.where(index == 2, low, 0.0))
+        return jnp.where(index == 0, high, rest).astype(BF16)
+
     for h in range(pair):
         rows = slice(h * dh, (h + 1) * dh)
-        q, k, v, g = q_ref[rows, :], k_ref[rows, :], v_ref[rows, :], g_ref[rows, :]
-        key_rows[h] = k.T
-        key_ext[h, :dh] = k
+        g = g_ref[rows, :]
+        key_ext[h, :dh] = k_ref[rows, :]
         key_ext[h, dh:] = ones
-        value_ext[h, :dh] = v
+        value_ext[h, :dh] = v_ref[rows, :]
         value_ext[h, dh:] = ones
         delta = jnp.sum(o_ref[rows, :].astype(F32) * g.astype(F32), axis=0, keepdims=True)
-        def stack(base, row):
-            parts = split3(-row)
-            idx = lax.broadcasted_iota(jnp.int32, (pad, length), 0)
-            tail = jnp.where(idx == 0, parts[0].astype(F32), jnp.where(idx == 1, parts[1].astype(F32), jnp.where(idx == 2, parts[2].astype(F32), 0.0)))
-            return jnp.concatenate([base, tail.astype(BF16)], axis=0).T
-        query_ext[h] = stack(q, lse_ref[h])
-        grad_ext[h] = stack(g, delta)
+        query_ext[h, :dh] = q_ref[rows, :]
+        query_ext[h, dh:] = tail(lse_ref[h])
+        grad_ext[h, :dh] = g
+        grad_ext[h, dh:] = tail(delta)
         dk_acc[h] = jnp.zeros((dh, length), F32)
         dv_acc[h] = jnp.zeros((dh, length), F32)
 
@@ -141,8 +158,8 @@
                 cols = first + lax.broadcasted_iota(jnp.int32, (bq, bk), 1)
                 allowed = cols <= jnp.maximum(rows, prefix - 1)
             fresh = []
-            s = [dot(query_ext[h, here], key_ext[h, :, there]) for h in range(pair)]
-            gp = [dot(grad_ext[h, here], value_ext[h, :, there]) for h in range(pair)]
+            s = [dot(query_ext[h, :, here], key_ext[h, :, there], ((0,), (0,))) for h in range(pair)]
+            gp = [dot(grad_ext[h, :, here], value_ext[h, :, there], ((0,), (0,))) for h in range(pair)]
             for h in range(pair):
                 x = jnp.where(allowed, s[h], MASKED) if masked else s[h]
                 p = jnp.exp2(x)
@@ -150,7 +167,7 @@
                 rows = slice(h * dh, (h + 1) * dh)
                 dv_acc[h, :, there] += dot(g_ref[rows, here], p.astype(BF16))
                 dk_acc[h, :, there] += dot(q_ref[rows, here], ds)
-                fresh.append(state[h] + dot(ds, key_rows[h, there]))
+                fresh.append(state[h] + dot(ds, k_ref[rows, there], ((1,), (1,))))
             return tuple(fresh)
 
         state = tuple(jnp.zeros((bq, dh), F32) for _ in range(pair))
@@ -172,6 +189,7 @@
         rows = slice(h * dh, (h + 1) * dh)
         dk_ref[rows, :] = (dk_acc[h] * math.log(2.0)).astype(BF16)
         dv_ref[rows, :] = dv_acc[h].astype(BF16)
+
 
 def attention_backward(q, k, v, o, g, lse, factor, prefix, order, dh, base=0, width=None, pair=2):
     full, length = q.shape
@@ -191,11 +209,10 @@
             in_specs=[source] * 5 + [pl.BlockSpec((pair, 1, length), lambda i, p, o: (i + skip, 0, 0)), pl.BlockSpec((dh, 1), lambda i, p, o: (0, 0))],
             out_specs=[spec] * 3 + [pl.BlockSpec((dh, 128), lambda i, p, o: (0, 0))],
             scratch_shapes=[
-                pltpu.VMEM((pair, length, dh), BF16),
                 pltpu.VMEM((pair, ext, length), BF16),
                 pltpu.VMEM((pair, ext, length), BF16),
-                pltpu.VMEM((pair, length, ext), BF16),
-                pltpu.VMEM((pair, length, ext), BF16),
+                pltpu.VMEM((pair, ext, length), BF16),
+                pltpu.VMEM((pair, ext, length), BF16),
                 pltpu.VMEM((pair, dh, length), F32),
                 pltpu.VMEM((pair, dh, length), F32)],
         ),
@@ -495,6 +512,18 @@
     return pl.BlockSpec(shape, lambda *a: (0,) * len(shape), pipeline_mode=ONE)
 
 
+def weight(w, lanes=None):
+    stack, index = w if isinstance(w, tuple) else (w, None)
+    shape = (stack.shape[-2], lanes or stack.shape[-1])
+    if index is None:
+        return fixed(shape)
+    return pl.BlockSpec((None,) + shape, lambda *a: (index, 0, 0), pipeline_mode=ONE)
+
+
+def plain(weights):
+    return [w[0] if isinstance(w, tuple) else w for w in weights]
+
+
 def shape_of(shape, dtype=BF16):
     return jax.ShapeDtypeStruct(shape, dtype)
 
@@ -526,16 +555,15 @@
 
 def project(h, qk, vo, scale, base, bufs=None):
     rows, d = h.shape
-    w = qk[0].shape[1] // 2
+    w = plain(qk)[0].shape[-1] // 2
     bt = 512
     steps = rows // bt
     out = pl.BlockSpec((2 * w, bt), lambda i: (0, i + base * steps))
-    whole = fixed((d, 2 * w))
     extra = [] if bufs is None else list(bufs)
     return pl.pallas_call(
         functools.partial(project_kernel, w),
         grid=(steps,),
-        in_specs=[pl.BlockSpec((bt, d), lambda i: (i, 0))] + [whole] * 4 + [fixed((2 * w, 1))]
+        in_specs=[pl.BlockSpec((bt, d), lambda i: (i, 0))] + [weight(a) for a in (*qk, *vo)] + [fixed((2 * w, 1))]
         + [pl.BlockSpec(memory_space=pl.ANY)] * len(extra),
         out_specs=[out] * 3,
         out_shape=[shape_of((2 * w, 2 * rows))] * 3,
@@ -543,7 +571,7 @@
         compiler_params=params(),
         cost_estimate=cost(2 * rows * d * 6 * w, 4 * rows * d),
         name="project",
-    )(h, *qk, *vo, scale, *extra)
+    )(h, *plain(qk), *plain(vo), scale, *extra)
 
 
 def out_kernel(w, att_ref, vo0, vo1, part_ref, mat):
@@ -555,21 +583,21 @@
 
 
 def out_project(att, vo, base):
-    d, w2 = vo[0].shape
+    d, w2 = plain(vo)[0].shape[-2:]
     rows = att.shape[1] // 2
     bt = 512
     steps = rows // bt
     return pl.pallas_call(
         functools.partial(out_kernel, w2 // 2),
         grid=(steps,),
-        in_specs=[pl.BlockSpec((w2, bt), lambda i: (0, i + base * steps)), fixed((d, w2)), fixed((d, w2))],
+        in_specs=[pl.BlockSpec((w2, bt), lambda i: (0, i + base * steps))] + [weight(a) for a in vo],
         out_specs=pl.BlockSpec((bt, d), lambda i: (i, 0)),
         out_shape=shape_of((rows, d)),
         scratch_shapes=[pltpu.VMEM((d, w2), BF16)],
         compiler_params=params(),
         cost_estimate=cost(2 * rows * d * w2, 4 * rows * d),
         name="out_project",
-    )(att, *vo)
+    )(att, *plain(vo))
 
 
 def middle_kernel(w, x_ref, att_ref, got_ref, gm_ref, ga_ref, vo0, vo1, un0, un1, un2, un3,
@@ -593,7 +621,7 @@
 
 def middle_call(x, att, got, gain_m, gain_a, vo, un):
     rows, d = x.shape
-    w2 = vo[0].shape[1]
+    w2 = plain(vo)[0].shape[-1]
     ff = 2 * w2
     bt = 256
     row = pl.BlockSpec((bt, d), lambda i: (i, 0))
@@ -601,147 +629,190 @@
     return pl.pallas_call(
         functools.partial(middle_kernel, w2 // 2),
         grid=(rows // bt,),
-        in_specs=[row, pl.BlockSpec((w2, bt), lambda i: (0, i)), row] + [fixed((1, d))] * 2 + [fixed((d, w2))] * 6,
+        in_specs=[row, pl.BlockSpec((w2, bt), lambda i: (0, i)), row] + [fixed((1, d))] * 2
+        + [weight(a) for a in (*vo, *un)],
         out_specs=[row, wide, row, row],
         out_shape=[shape_of((rows, d), F32), shape_of((rows, ff), F32), shape_of((rows, d), F32), shape_of((rows, d))],
         scratch_shapes=[pltpu.VMEM((d, w2), BF16), pltpu.VMEM((d, ff), BF16), pltpu.VMEM((d, ff), BF16)],
         compiler_params=params(),
         cost_estimate=cost(2 * rows * d * (w2 + 2 * ff), 30 * rows * d),
         name="middle",
-    )(x, att, got, gain_m, gain_a, *vo, *un)
-
-
-def mlp_back_kernel(w, g_ref, mid_ref, pre_ref, gm_ref, un0, un1, un2, un3,
-                    g_mid_ref, low_ref, gain_ref, o0, o1, o2, o3,
-                    up_mat, down_mat, g_all, hid_all, hm_all, gpre_all):
+    )(x, att, got, gain_m, gain_a, *plain(vo), *plain(un))
+
+
+def mlp_back_kernel(w, sides, steps, index, g_ref, mid_ref, pre_ref, gm_ref, att_any, *refs):
+    weights, refs = refs[:6], refs[6:]
+    g_mid_ref, gain_ref, g_att_ref, o0, o1 = refs[:5]
+    (up_mat, down_mat, out_mat, g_all, hid_all, hm_all, gpre_all, low_own, low_other, blocks, got, vo_side, att,
+     load, send, recv) = refs[5:]
     i = pl.program_id(0)
-    bt = g_ref.shape[0]
+    rows_steps, grad_steps, att_steps, _ = steps
+    bt, bd, ba = g_ref.shape[0], o0.shape[0], g_att_ref.shape[1]
+    t = lax.axis_index("tp")
+    core = {"tp": t + 1 - 2 * lax.rem(t, 2)}
+    low_lane = sides[0]
+
+    def loads():
+        pairs = [(weights[2 + b], blocks.at[b]) for b in range(4)]
+        for s in range(2):
+            pairs.append((weights[s], vo_side.at[s]))
+        views = []
+        for n, ((ref, dst), k) in enumerate(zip(pairs, index[2:] + index[:2])):
+            src = ref if k is None else ref.at[k]
+            if n >= 4:
+                src = src.at[:, pl.ds(low_lane, vo_side.shape[2])]
+            views.append(pltpu.make_async_copy(src, dst, load.at[n]))
+        views.append(pltpu.make_async_copy(att_any, att, load.at[6]))
+        return views
+
+    def push(src, dst, slot):
+        return pltpu.make_async_remote_copy(
+            src_ref=src, dst_ref=dst, send_sem=send.at[slot], recv_sem=recv.at[slot],
+            device_id=core, device_id_type=MESH,
+        )
+
+    def push_rows(k):
+        part = pl.ds(pl.multiple_of(k * bt, bt), bt)
+        return push(low_own.at[part], low_other.at[part], k)
+
+    def push_block(c, s):
+        part = pl.ds(pl.multiple_of(c * bd, bd), bd)
+        return push(blocks.at[2 + s, part], got.at[s, part], rows_steps + 2 * c + s)
 
     @pl.when(i == 0)
     def _():
-        join_lanes(up_mat, (un0, un1, un2, un3), 0, w)
-        join_lanes(down_mat, (un0, un1, un2, un3), w, 2 * w)
+        copies = loads()
+        for c in copies:
+            c.start()
+        barrier = pltpu.get_barrier_semaphore()
+        pl.semaphore_signal(barrier, inc=1, device_id=core, device_id_type=MESH)
         gain_ref[...] = jnp.zeros_like(gain_ref)
-
-    here = pl.ds(pl.multiple_of(i * bt, bt), bt)
-    g = g_ref[...]
-    g_low = g.astype(BF16)
-    g_all[here] = g_low
-    pre = pre_ref[...]
-    sig = 1.0 / (1.0 + jnp.exp(-pre))
-    hid_all[here] = (pre * sig).astype(BF16)
-    g_hidden = dot(g_low, down_mat[...])
-    g_pre = (g_hidden * sig * (1.0 + pre * (1.0 - sig))).astype(BF16)
-    gpre_all[here] = g_pre
-    mid = mid_ref[...]
-    inv = inverse_rms(mid)
-    normed = mid * inv
-    gain = gm_ref[...]
-    hm_all[here] = (normed * gain).astype(BF16)
-    g_hm = dot(g_pre, up_mat[...], NT)
-    gain_ref[...] += eight(g_hm * normed)
-    scaled = g_hm * gain
-    g_mid = g + inv * (scaled - normed * jnp.mean(scaled * normed, axis=-1, keepdims=True))
-    g_mid_ref[...] = g_mid
-    low_ref[...] = g_mid.astype(BF16)
-
-    @pl.when(i == pl.num_programs(0) - 1)
-    def _():
-        d = up_mat.shape[0]
-        step = 256
-
-        def chunk(c, carry):
-            cols = pl.ds(pl.multiple_of(c * step, step), step)
-            up = dot(hm_all[:, cols], gpre_all[...], TN).astype(BF16)
-            down = dot(g_all[:, cols], hid_all[...], TN).astype(BF16)
-            for b, out in enumerate((o0, o1, o2, o3)):
-                out[cols, 0:w] = up[:, b * w:(b + 1) * w]
-                out[cols, w:2 * w] = down[:, b * w:(b + 1) * w]
-            return carry
-
-        lax.fori_loop(0, d // step, chunk, 0)
-
-
-def mlp_back(g, mid, pre, gain, un):
+        for b in range(4):
+            copies[b].wait()
+            up_mat[:, b * w:(b + 1) * w] = blocks[b, :, 0:w]
+            down_mat[:, b * w:(b + 1) * w] = blocks[b, :, w:2 * w]
+        pl.semaphore_wait(barrier, 1)
+
+    @pl.when(i < rows_steps)
+    def _():
+        here = pl.ds(pl.multiple_of(i * bt, bt), bt)
+        g = g_ref[...]
+        g_low = g.astype(BF16)
+        g_all[here] = g_low
+        pre = pre_ref[...]
+        sig = 1.0 / (1.0 + jnp.exp(-pre))
+        hid_all[here] = (pre * sig).astype(BF16)
+        g_hidden = dot(g_low, down_mat[...])
+        g_pre = (g_hidden * sig * (1.0 + pre * (1.0 - sig))).astype(BF16)
+        gpre_all[here] = g_pre
+        mid = mid_ref[...]
+        inv = inverse_rms(mid)
+        normed = mid * inv
+        gain = gm_ref[...]
+        hm_all[here] = (normed * gain).astype(BF16)
+        g_hm = dot(g_pre, up_mat[...], NT)
+        gain_ref[...] += eight(g_hm * normed)
+        scaled = g_hm * gain
+        g_mid = g + inv * (scaled - normed * jnp.mean(scaled * normed, axis=-1, keepdims=True))
+        g_mid_ref[...] = g_mid
+        low_own[here] = g_mid.astype(BF16)
+        push_rows(i).start()
+
+    at = i - rows_steps
+
+    @pl.when((at >= 0) & (at < grad_steps))
+    def _():
+        cols = pl.ds(pl.multiple_of(at * bd, bd), bd)
+        up = dot(hm_all[:, cols], gpre_all[...], TN).astype(BF16)
+        down = dot(g_all[:, cols], hid_all[...], TN).astype(BF16)
+        for b in range(4):
+            blocks[b, cols, 0:w] = up[:, b * w:(b + 1) * w]
+            blocks[b, cols, w:2 * w] = down[:, b * w:(b + 1) * w]
+        for s in range(2):
+            push_block(at, s).start()
+
+    to = at - grad_steps
+
+    @pl.when(to == 0)
+    def _():
+        copies = loads()
+        for s in range(2):
+            copies[4 + s].wait()
+            out_mat[:, s * w:(s + 1) * w] = vo_side[s, :, sides[1]:sides[1] + w]
+
+    half = att_steps // 2
+
+    @pl.when((to >= 0) & (to < half))
+    def _():
+        here = pl.ds(pl.multiple_of(to * ba, ba), ba)
+        g_att_ref[...] = dot(out_mat[...], low_own[here], TT).astype(BF16)
+
+    @pl.when(to == half)
+    def _():
+        for k in range(rows_steps):
+            push_rows(k).wait()
+
+    @pl.when((to >= half) & (to < att_steps))
+    def _():
+        here = pl.ds(pl.multiple_of((to - half) * ba, ba), ba)
+        g_att_ref[...] = dot(out_mat[...], low_other[here], TT).astype(BF16)
+
+    last = to - att_steps
+
+    @pl.when(last == 0)
+    def _():
+        loads()[6].wait()
+
+    @pl.when(last >= 0)
+    def _():
+        cols = pl.ds(pl.multiple_of(last * bd, bd), bd)
+        rows = low_own.shape[0]
+        grad = dot(low_own[:, cols], att[:, :rows], TT) + dot(low_other[:, cols], att[:, rows:], TT)
+        grad = grad.astype(BF16)
+        for s, out in enumerate((o0, o1)):
+            push_block(last, s).wait()
+            out[:, :2 * w] = (blocks[s, cols].astype(F32) + got[s, cols].astype(F32)).astype(BF16)
+            out[:, 2 * w:3 * w] = grad[:, s * w:(s + 1) * w]
+            out[:, 3 * w:] = jnp.zeros((bd, out.shape[1] - 3 * w), BF16)
+
+
+def mlp_back(g, mid, pre, gain, att, vo, un, width, call):
     rows, d = g.shape
     ff = pre.shape[1]
-    w2 = un[0].shape[1]
-    bt = 256
-    row = pl.BlockSpec((bt, d), lambda i: (i, 0))
-    wide = pl.BlockSpec((bt, ff), lambda i: (i, 0))
+    w2 = plain(un)[0].shape[-1]
+    w = w2 // 2
+    bt, bd, ba = 256, 256, 512
+    steps = (rows // bt, d // bd, 2 * rows // ba, d // bd)
+    starts = [sum(steps[:n]) for n in range(4)]
+    low = w // 128 * 128
+    sides = (low, w - low)
+
+    def at(n, make):
+        return lambda i: make(jnp.clip(i - starts[n], 0, steps[n] - 1))
+
+    row = pl.BlockSpec((bt, d), at(0, lambda k: (k, 0)))
+    wide = pl.BlockSpec((bt, ff), at(0, lambda k: (k, 0)))
+    block = pl.BlockSpec((bd, width), at(3, lambda k: (k, 0)))
+    any_spec = pl.BlockSpec(memory_space=pl.ANY)
+    index = tuple(a[1] if isinstance(a, tuple) else None for a in (*vo, *un))
+    slots = steps[0] + 2 * steps[1]
     return pl.pallas_call(
-        functools.partial(mlp_back_kernel, w2 // 2),
-        grid=(rows // bt,),
-        in_specs=[row, row, wide, fixed((1, d))] + [fixed((d, w2))] * 4,
-        out_specs=[row, row, fixed((8, d))] + [fixed((d, w2))] * 4,
-        out_shape=[shape_of((rows, d), F32), shape_of((rows, d)), shape_of((8, d), F32)] + [shape_of((d, w2))] * 4,
+        functools.partial(mlp_back_kernel, w, sides, steps, index),
+        grid=(sum(steps),),
+        in_specs=[row, row, wide, fixed((1, d))] + [any_spec] * 7,
+        out_specs=[row, fixed((8, d)), pl.BlockSpec((w2, ba), at(2, lambda k: (0, k))), block, block],
+        out_shape=[shape_of((rows, d), F32), shape_of((8, d), F32), shape_of((w2, 2 * rows))] + [shape_of((d, width))] * 2,
         scratch_shapes=[pltpu.VMEM((d, ff), BF16)] * 2
-        + [pltpu.VMEM((rows, d), BF16), pltpu.VMEM((rows, ff), BF16), pltpu.VMEM((rows, d), BF16), pltpu.VMEM((rows, ff), BF16)],
-        compiler_params=params(),
-        cost_estimate=cost(8 * rows * d * ff, 30 * rows * d),
+        + [pltpu.VMEM((d, w2), BF16)]
+        + [pltpu.VMEM((rows, d), BF16), pltpu.VMEM((rows, ff), BF16)] * 2
+        + [pltpu.VMEM((rows, d), BF16)] * 2
+        + [pltpu.VMEM((4, d, w2), BF16), pltpu.VMEM((2, d, w2), BF16), pltpu.VMEM((2, d, w2 - low), BF16)]
+        + [pltpu.VMEM(att.shape, BF16)]
+        + [pltpu.SemaphoreType.DMA((7,)), pltpu.SemaphoreType.DMA((slots,)), pltpu.SemaphoreType.DMA((slots,))],
+        compiler_params=pltpu.CompilerParams(vmem_limit_bytes=62 * 2**20, collective_id=call, has_side_effects=True),
+        cost_estimate=cost(8 * rows * d * ff + 8 * rows * d * w2, 40 * rows * d),
         name="mlp_back",
-    )(g, mid, pre, gain, *un)
-
-
-def grad_att_kernel(w, g_ref, vo0, vo1, *refs):
-    out_ref, mat = refs[-2:]
-
-    @pl.when(pl.program_id(0) == 0)
-    def _():
-        join_lanes(mat, (vo0, vo1), w, 2 * w)
-
-    out_ref[...] = dot(mat[...], g_ref[...], TT).astype(BF16)
-
-
-def grad_att(g, vo, base, buf=None):
-    rows, d = g.shape
-    w2 = vo[0].shape[1]
-    bt = 512
-    steps = rows // bt
-    extra = [] if buf is None else [buf]
-    return pl.pallas_call(
-        functools.partial(grad_att_kernel, w2 // 2),
-        grid=(steps,),
-        in_specs=[pl.BlockSpec((bt, d), lambda i: (i, 0)), fixed((d, w2)), fixed((d, w2))]
-        + [pl.BlockSpec(memory_space=pl.ANY)] * len(extra),
-        out_specs=pl.BlockSpec((w2, bt), lambda i: (0, i + base * steps)),
-        out_shape=shape_of((w2, 2 * rows)),
-        scratch_shapes=[pltpu.VMEM((d, w2), BF16)],
-        input_output_aliases={3: 0} if extra else {},
-        compiler_params=params(),
-        cost_estimate=cost(2 * rows * d * w2, 4 * rows * d),
-        name="grad_att",
-    )(g, *vo, *extra)
-
-
-def out_grad_kernel(w, own_ref, other_ref, att_ref, u0, u1, got0, got1, o0, o1):
-    half = own_ref.shape[0]
-    att = att_ref[...]
-    grad = dot(own_ref[...], att[:, :half], TT) + dot(other_ref[...], att[:, half:], TT)
-    grad = grad.astype(BF16)
-    for s, (u, got, out) in enumerate(((u0, got0, o0), (u1, got1, o1))):
-        out[:, :2 * w] = (u[...].astype(F32) + got[...].astype(F32)).astype(BF16)
-        out[:, 2 * w:3 * w] = grad[:, s * w:(s + 1) * w]
-        out[:, 3 * w:] = jnp.zeros((out.shape[0], out.shape[1] - 3 * w), BF16)
-
-
-def out_grad_call(own, other, att, mlp, got, width):
-    rows, d = own.shape
-    w2 = att.shape[0]
-    bd = 256
-    col = pl.BlockSpec((rows, bd), lambda i: (0, i))
-    flat = pl.BlockSpec((bd, w2), lambda i: (i, 0))
-    out = pl.BlockSpec((bd, width), lambda i: (i, 0))
-    return pl.pallas_call(
-        functools.partial(out_grad_kernel, w2 // 2),
-        grid=(d // bd,),
-        in_specs=[col, col, fixed(att.shape)] + [flat] * 4,
-        out_specs=[out] * 2,
-        out_shape=[shape_of((d, width))] * 2,
-        compiler_params=params(),
-        cost_estimate=cost(4 * rows * d * w2, 8 * rows * d),
-        name="out_grad",
-    )(own, other, att, *mlp, *got)
+    )(g, mid, pre, gain, att, *plain(vo), *plain(un))
 
 
 def weight_grad_kernel(w, own_ref, other_ref, dq_ref, dk_ref, dv_ref, *refs):
@@ -797,20 +868,20 @@
 
 def input_other(grads, qk, vo):
     w, length = grads[0].shape
-    d, w2 = qk[0].shape
+    d, w2 = plain(qk)[0].shape[-2:]
     bt = 512
     steps = length // 2 // bt
     col = pl.BlockSpec((w, bt), lambda i: (0, i + steps))
     return pl.pallas_call(
         functools.partial(input_other_kernel, w),
         grid=(steps,),
-        in_specs=[col] * 6 + [fixed((d, w2))] * 4,
+        in_specs=[col] * 6 + [weight(a) for a in (*qk, *vo)],
         out_specs=pl.BlockSpec((bt, d), lambda i: (i, 0)),
         out_shape=shape_of((length // 2, d)),
         compiler_params=params(),
         cost_estimate=cost(3 * length * d * w2, 4 * length * d),
         name="input_other",
-    )(*grads, *qk, *vo)
+    )(*grads, *plain(qk), *plain(vo))
 
 
 def input_own_kernel(w, *refs):
@@ -840,13 +911,14 @@
     return pl.pallas_call(
         functools.partial(input_own_kernel, w),
         grid=(rows // bt,),
-        in_specs=[col] * 6 + [row] * 3 + [fixed((1, d))] + [fixed((d, w2))] * 4,
+        in_specs=[col] * 6 + [row] * 3 + [fixed((1, d))]
+        + [weight(a) for a in (*qk, *vo)],
         out_specs=[row, fixed((8, d))],
         out_shape=[shape_of((rows, d), F32), shape_of((8, d), F32)],
         compiler_params=params(),
         cost_estimate=cost(6 * rows * d * w2, 24 * rows * d),
         name="input_own",
-    )(*grads, got, x, g, gain, *qk, *vo)
+    )(*grads, got, x, g, gain, *plain(qk), *plain(vo))
 
 
 def total_over_all(plan, a):
@@ -905,11 +977,16 @@
     def four(pair):
         return (*pair, plan.core(pair[0]), plan.core(pair[1]))
 
-    un0_rows, qk1_rows, vo1_rows, un1_rows = along(0, 2), along(1, 0), along(1, 1), along(1, 2)
+    def stacked(rows):
+        return (rows, 0), (rows, 1)
+
+    shards = jnp.stack([pairs[1, 1:], plan.across(pairs[1, 1:])], axis=1)
+    un0_rows, qk1_rows = along(0, 2), along(1, 0)
+    vo1_rows, un1_rows = (lax.all_gather(shards[m], "fsdp", axis=1, tiled=True) for m in range(2))
     x = plan.order(plan.pick(inputs, plan.seq), other.astype(F32))
     h = (x * inverse_rms(x) * norm_gain[0, 0]).astype(BF16)
     h, un0_rows, qk1_rows, cotangent = after(h, un0_rows, qk1_rows, cotangent)
-    un0, qk1 = both(un0_rows), both(qk1_rows)
+    un0 = both(un0_rows)
     cot_block = plan.pick(cotangent, 1 - plan.seq).astype(BF16)
     kept, weights = [], []
     for l in range(layers):
@@ -918,25 +995,19 @@
         h_other = plan.core(h)
         qkv = project(h, qk, vo, scale, 0)
         q, k, v = project(h_other, qk, vo, scale, 1, qkv)
-        if l == 1:
-            q, un1_rows = after(q, un1_rows)
-            un1 = both(un1_rows)
         att, lse = attention_forward(q, k, v, prefix, order, dh)
         if l == 0:
-            att, un0_got, qk1_got, vo1_rows = after(att, un0[1], qk1[1], vo1_rows)
-            un, qk1 = four((un0[0], un0_got)), (qk1[0], qk1_got)
-            vo1 = both(vo1_rows)
+            att, un0_got, qk1_rows = after(att, un0[1], qk1_rows)
+            un, qk1 = four((un0[0], un0_got)), both(qk1_rows)
         else:
-            att, un1_got, cot_got = after(att, un1[1], cot_got)
-            un = four((un1[0], un1_got))
+            att, un1_rows, cot_got = after(att, un1_rows, cot_got)
+            un = (*stacked(un1_rows), *stacked(plan.core(un1_rows)))
         part = plan.core(out_project(att, vo, 1))
-        if l == 0:
-            part, un1_rows = after(part, un1_rows)
         next_gain = norm_gain[(l + 1) % layers, 0][None]
         mid, pre, res, h_next = middle_call(x, att, part, norm_gain[l, 1][None], next_gain, vo, un)
         if l == 0:
-            h_next, vo1_got, cot_block = after(h_next, vo1[1], cot_block)
-            vo1 = (vo1[0], vo1_got)
+            h_next, qk1_got, vo1_rows, cot_block = after(h_next, qk1[1], vo1_rows, cot_block)
+            qk1, vo1 = (qk1[0], qk1_got), stacked(vo1_rows)
             cot_got = plan.across(cot_block)
         kept.append((x, h, h_other, q, k, v, att, lse, mid, pre))
         weights.append((qk, vo, un))
@@ -952,17 +1023,13 @@
     for l in reversed(range(layers)):
         qk, vo, un = weights[l]
         x, h, h_other, q, k, v, att, lse, mid, pre = kept[l]
-        g_mid, low, gain_m, u0, u1, u2, u3 = mlp_back(g, mid, pre, norm_gain[l, 1][None], un)
+        g_mid, gain_m, g_att, *early = mlp_back(g, mid, pre, norm_gain[l, 1][None], att, vo, un, width, 1 + l)
+        early = [early[1], early[0]]
         if outputs is None:
-            low, out_got = after(low, out_got)
+            g_att, out_got = after(g_att, out_got)
             outputs = plan.order(plan.pick(out_blocks, plan.seq), out_got.astype(F32)).reshape(out_blocks.shape)
-        low_other = plan.core(low)
-        g_att = grad_att(low, vo, 0)
-        early = out_grad_call(low, low_other, att, (u0, u1), (plan.core(u2), plan.core(u3)), width)
-        early = [early[1], early[0]]
-        low_other, *early = after(low_other, *early)
         early_got = plan.across(early[0])
-        g_att = grad_att(low_other, vo, 1, g_att)
+        g_att, early[1] = after(g_att, early[1])
         dgrads, fgs, pieces = [None] * 6, [], [None] * 2
         for s in (1, 0):
             dq, dk, dv, fg = attention_backward(

time: 859 us -> 804 us (0.936)
  Pallas kernels: 650 us -> 608 us
  waiting for transfers between devices: 93.6 us -> 82.6 us
    pallas_call x8 -> x2, Pallas kernels: 102 us -> 79.6 us  [mlp_back(): pl.pallas_call(functools.partial(mlp_back_kernel, w, sides, steps, index)...]
    reduce_scatter x4, waiting for transfers between devices: 33.9 us -> 12.2 us  [scatter_rows(): lax.psum_scatter(mine, 'fsdp', scatter_dimension=0, tiled=True).astype(F32)]
    ppermute x11 -> x10, waiting for transfers between devices: 39.4 us -> 56 us  [across(): return lax.ppermute(a, 'tp', [(t, (t + self.ring) % n) for t in range(n)])]
    pallas_call x2, Pallas kernels: 87.4 us -> 72.4 us  [attention_forward(): pl.pallas_call(functools.partial(forward_kernel, pair=pair, dh=dh, bq=bq,...]
  transfers between devices with their start and end apart: 40 -> 32, of which waited for: 17 -> 14; matrix products, arithmetic and copies ran while one was open for 5% -> 6% of each run, Pallas kernels for 70% -> 74%
where the time goes in v4:
time: 804 us; the launch traced here: 796 us
  Pallas kernels  608 us (76%)
  waiting for transfers between devices  82.6 us (10%)
  other arithmetic  45.3 us (6%)
  local copies, waits for them, and re-layouts  25.9 us (3%)
  starting transfers between devices  19.5 us (2%)
  between operations  15 us (2%)
    pallas_call x4, Pallas kernels, attention_backward(): pl.pallas_call(functools.partial(backward_kernel, pair=pair, dh=dh, bq=bq...  161 us
    pallas_call x1, Pallas kernels, gather_call(): pl.pallas_call(functools.partial(gather_kernel, pieces, pairs, outer, rin...  104 us
    pallas_call x2, Pallas kernels, mlp_back(): pl.pallas_call(functools.partial(mlp_back_kernel, w, sides, steps, index)...  79.6 us
    pallas_call x2, Pallas kernels, attention_forward(): pl.pallas_call(functools.partial(forward_kernel, pair=pair, dh=dh, bq=bq,...  72.4 us
    ppermute x10, waiting for transfers between devices, across(): return lax.ppermute(a, 'tp', [(t, (t + self.ring) % n) for t in range(n)])  56 us
    pallas_call x4, Pallas kernels, weight_grad(): pl.pallas_call(functools.partial(weight_grad_kernel, w), grid=(d // bd,),...  42.9 us
    pallas_call x2, Pallas kernels, middle_call(): pl.pallas_call(functools.partial(middle_kernel, w2 // 2), grid=(rows // b...  40.1 us
    pallas_call x4, Pallas kernels, project(): pl.pallas_call(functools.partial(project_kernel, w), grid=(steps,), in_sp...  39.3 us
  transfers between devices with their start and end apart: 32, of which 14 were waited for; matrix products, arithmetic and copies ran while one was open for 6% of the time, Pallas kernels for 74%

profile of v4, /device:TPU:0, one launch (start us, length us, event | category | flops | bytes accessed | tf_op | source)
XLA Modules:
  0.0 795.9 jit_solution(4647806890552056076)
XLA Ops:
  9.5 1.7 fusion.17
  12.6 2.9 fusion.block_ref
  15.6 103.7 %gather_weights.1 = (bf16[4,2,160,640]{3,2,1,0:T(8,128)(2,1)}, bf16[4,2,160,640]{3,2,1,0:T(8,128)(2,1)}, bf16[4,2,160,640]{3,2,1,0:T(8,128)(2,1)}, bf16[4,2,160,640]{3,2,1,0:T(8,128)(2,1)}, bf16[512,1280]{1,0:T(8,128)(2,1)}) custom-call(bf16[2,160,640]{2,1,0:T(8,128)(2,1)} %get-tuple-element.258.shard_ref, bf16[512,1280]{1,0:T(8,128)(2,1)} %fusion.block_ref), custom_call_target="tpu_custom_call" | custom-call | tf_op jit(solution)/shard_map/gather_weights/pallas_call | solution.py:339
  119.2 2.5 convert_select_fusion.7
  123.1 3.1 multiply_convert_fusion
  126.2 2.6 all-gather.9.cloned.1.call-done
  128.8 2.7 collective-permute-start.6
  131.5 10.1 %collective-permute-done.6 = bf16[2,160,640]{2,1,0:T(8,128)(2,1)S(1)} collective-permute-done((bf16[2,160,640]{2,1,0:T(8,128)(2,1)S(1)}, bf16[2,160,640]{2,1,0:T(8,128)(2,1)S(1)}, u32[]{:S(2)}, u32[]{:S(2)}) %collective-permute-start.6) | collective-permute-done | bytes 409632 | tf_op jit(solution)/shard_map/ppermute | solution.py:367
  146.0 1.7 collective-permute-start.1
  147.7 9.8 %project.4 = (bf16[640,2048]{1,0:T(8,128)(2,1)}, bf16[640,2048]{1,0:T(8,128)(2,1)}, bf16[640,2048]{1,0:T(8,128)(2,1)}) custom-call(bf16[1024,1280]{1,0:T(8,128)(2,1)} %copy-done.4, bf16[1280,640]{1,0:T(8,128)(2,1)} %bitcast.138, bf16[1280,640]{1,0:T(8,128)(2,1)} %bitcast.142, bf16[1280,640]{1,0:T(8,128)(2,1)} %bitcast.116, bf16[1280,640]{1,0:T(8,128)(2,1)} %bitcast.123, ...), custom_call_target="tpu_custom_call" | custom-call | flops 5033164800 | bytes 5242880 | tf_op jit(solution)/shard_map/project/pallas_call | solution.py:563
  157.5 9.8 %project.5 = (bf16[640,2048]{1,0:T(8,128)(2,1)}, bf16[640,2048]{1,0:T(8,128)(2,1)}, bf16[640,2048]{1,0:T(8,128)(2,1)}) custom-call(bf16[1024,1280]{1,0:T(8,128)(2,1)} %collective-permute-done.h_ref.other_ref, bf16[1280,640]{1,0:T(8,128)(2,1)} %bitcast.139, bf16[1280,640]{1,0:T(8,128)(2,1)} %bitcast.143, ...), custom_call_target="tpu_custom_call", output_to_operand_aliasing={{0}: (6, {}), {1}: (7, {}), {2}: (8, {})} | custom-call | flops 5033164800 | bytes 5242880 | tf_op jit(solution)/shard_map/project/pallas_call | solution.py:563
  167.3 33.3 %attention_forward.2 = (bf16[640,2048]{1,0:T(8,128)(2,1)}, f32[8,1,2048]{2,1,0:T(1,128)}) custom-call(s32[1]{0:T(128)} %dynamic_slice.30.prefix_ref, s32[4]{0:T(128)} %fusion.23.order_ref, bf16[640,2048]{1,0:T(8,128)(2,1)} %get-tuple-element.122.q_ref, bf16[640,2048]{1,0:T(8,128)(2,1)} %get-tuple-element.123.k_ref, bf16[640,2048]{1,0:T(8,128)(2,1)} %get-tuple-element.124.v_ref), custom_call_target="tpu_custom_call" | custom-call | flops 20132659200 | bytes 10485760 | tf_op jit(solution)/shard_map/attention_forward/pallas_call | solution.py:95
  200.6 6.4 out_project.2
  207.6 2.9 fusion.1
  210.6 4.1 collective-permute-done.3.un2.refs_4_
  214.6 2.3 collective-permute-done.4.un3.refs_5_
  217.0 20.1 %middle.2 = (f32[1024,1280]{1,0:T(8,128)}, f32[1024,1280]{1,0:T(8,128)}, f32[1024,1280]{1,0:T(8,128)}, bf16[1024,1280]{1,0:T(8,128)(2,1)}) custom-call(f32[1024,1280]{1,0:T(8,128)} %get-tuple-element.244.x_ref.refs_7_, bf16[640,2048]{1,0:T(8,128)(2,1)} %get-tuple-element.128.att_ref.att_any.o_ref, bf16[1024,1280]{1,0:T(8,128)(2,1)} %collective-permute-done.2.got_ref, ...), custom_call_target="tpu_custom_call" | custom-call | flops 8388608000 | bytes 39321600 | tf_op jit(solution)/shard_map/middle/pallas_call | solution.py:629
  237.1 8.7 %collective-permute-done.5.qk1.refs_7_.refs_11_ = bf16[1280,640]{1,0:T(8,128)(2,1)} collective-permute-done((bf16[1280,640]{1,0:T(8,128)(2,1)S(1)}, bf16[1280,640]{1,0:T(8,128)(2,1)}, u32[]{:S(2)}, u32[]{:S(2)}) %collective-permute-start.5) | collective-permute-done | bytes 1638432 | tf_op jit(solution)/shard_map/ppermute | solution.py:367
  247.0 9.9 %project.6 = (bf16[640,2048]{1,0:T(8,128)(2,1)}, bf16[640,2048]{1,0:T(8,128)(2,1)}, bf16[640,2048]{1,0:T(8,128)(2,1)}) custom-call(bf16[1024,1280]{1,0:T(8,128)(2,1)} %get-tuple-element.134.h_ref.own_ref, bf16[1280,640]{1,0:T(8,128)(2,1)} %bitcast.111, bf16[1280,640]{1,0:T(8,128)(2,1)} %collective-permute-done.5.qk1.refs_7_.refs_11_, ...), custom_call_target="tpu_custom_call" | custom-call | flops 5033164800 | bytes 5242880 | tf_op jit(solution)/shard_map/project/pallas_call | solution.py:563
  257.0 1.5 copy-done.2
  258.5 9.8 %project.7 = (bf16[640,2048]{1,0:T(8,128)(2,1)}, bf16[640,2048]{1,0:T(8,128)(2,1)}, bf16[640,2048]{1,0:T(8,128)(2,1)}) custom-call(bf16[1024,1280]{1,0:T(8,128)(2,1)} %copy-done.2, bf16[1280,640]{1,0:T(8,128)(2,1)} %bitcast.112, ...), custom_call_target="tpu_custom_call", output_to_operand_aliasing={{0}: (6, {}), {1}: (7, {}), {2}: (8, {})} | custom-call | flops 5033164800 | bytes 5242880 | tf_op jit(solution)/shard_map/project/pallas_call | solution.py:563
  268.3 39.1 %attention_forward.3 = (bf16[640,2048]{1,0:T(8,128)(2,1)}, f32[8,1,2048]{2,1,0:T(1,128)}) custom-call(s32[1]{0:T(128)} %dynamic_slice.30.prefix_ref, s32[4]{0:T(128)} %fusion.23.order_ref, bf16[640,2048]{1,0:T(8,128)(2,1)} %get-tuple-element.140.q_ref, bf16[640,2048]{1,0:T(8,128)(2,1)} %get-tuple-element.141.k_ref, bf16[640,2048]{1,0:T(8,128)(2,1)} %get-tuple-element.142.v_ref), custom_call_target="tpu_custom_call" | custom-call | flops 20132659200 | bytes 10485760 | tf_op jit(solution)/shard_map/attention_forward/pallas_call | solution.py:95
  307.5 6.1 out_project.3
  314.8 2.5 convert_select_fusion.5
  317.3 2.7 pad_maximum_fusion.1.g_ref
  320.0 1.5 copy-done.24
  321.5 19.9 %middle.3 = (f32[1024,1280]{1,0:T(8,128)}, f32[1024,1280]{1,0:T(8,128)}, f32[1024,1280]{1,0:T(8,128)}, bf16[1024,1280]{1,0:T(8,128)(2,1)}) custom-call(f32[1024,1280]{1,0:T(8,128)} %get-tuple-element.130.x_ref.refs_7_, bf16[640,2048]{1,0:T(8,128)(2,1)} %get-tuple-element.145.att_ref.att_any.o_ref, bf16[1024,1280]{1,0:T(8,128)(2,1)} %copy-done.24, ...), custom_call_target="tpu_custom_call" | custom-call | flops 8388608000 | bytes 39321600 | tf_op jit(solution)/shard_map/middle/pallas_call | solution.py:629
  341.5 2.9 fusion.2
  344.4 39.8 %mlp_back.2 = (f32[1024,1280]{1,0:T(8,128)}, f32[8,1280]{1,0:T(8,128)}, bf16[640,2048]{1,0:T(8,128)(2,1)}, bf16[1280,1024]{1,0:T(8,128)(2,1)}, bf16[1280,1024]{1,0:T(8,128)(2,1)}) custom-call(f32[1024,1280]{1,0:T(8,128)} %pad_maximum_fusion.1.g_ref, f32[1024,1280]{1,0:T(8,128)} %get-tuple-element.150.mid_ref, f32[1024,1280]{1,0:T(8,128)} %get-tuple-element.151.pre_ref, ...), custom_call_target="tpu_custom_call" | custom-call | flops 20132659200 | bytes 52428800 | tf_op jit(solution)/shard_map/mlp_back/pallas_call | solution.py:799
  384.2 2.1 collective-permute-start.12
  386.3 40.2 %attention_backward.4 = (bf16[320,2048]{1,0:T(8,128)(2,1)}, bf16[320,2048]{1,0:T(8,128)(2,1)}, bf16[320,2048]{1,0:T(8,128)(2,1)}, f32[80,128]{1,0:T(8,128)}) custom-call(s32[1]{0:T(128)} %dynamic_slice.30.prefix_ref, s32[4]{0:T(128)} %fusion.23.order_ref, bf16[640,2048]{1,0:T(8,128)(2,1)} %get-tuple-element.140.q_ref, ...), custom_call_target="tpu_custom_call" | custom-call | flops 26843545600 | bytes 10485760 | tf_op jit(solution)/shard_map/attention_backward/pallas_call | solution.py:205
  426.5 10.6 %weight_grad.4 = bf16[1280,1024]{1,0:T(8,128)(2,1)} custom-call(bf16[1024,1280]{1,0:T(8,128)(2,1)} %get-tuple-element.134.h_ref.own_ref, bf16[1024,1280]{1,0:T(8,128)(2,1)} %copy-done.2, bf16[320,2048]{1,0:T(8,128)(2,1)} %get-tuple-element.160.dq_ref.refs_3_, bf16[320,2048]{1,0:T(8,128)(2,1)} %get-tuple-element.161.dk_ref.refs_4_, ...), custom_call_target="tpu_custom_call" | custom-call | flops 5033164800 | bytes 15728640 | tf_op jit(solution)/shard_map/weight_grad/pallas_call | solution.py:841
  437.1 6.3 collective-permute-done.12
  443.4 4.5 add_convert_fusion.1
  447.9 1.7 collective-permute-start.13
  449.7 40.2 %attention_backward.5 = (bf16[320,2048]{1,0:T(8,128)(2,1)}, bf16[320,2048]{1,0:T(8,128)(2,1)}, bf16[320,2048]{1,0:T(8,128)(2,1)}, f32[80,128]{1,0:T(8,128)}) custom-call(s32[1]{0:T(128)} %dynamic_slice.30.prefix_ref, s32[4]{0:T(128)} %fusion.23.order_ref, bf16[640,2048]{1,0:T(8,128)(2,1)} %get-tuple-element.140.q_ref, ...), custom_call_target="tpu_custom_call" | custom-call | flops 26843545600 | bytes 10485760 | tf_op jit(solution)/shard_map/attention_backward/pallas_call | solution.py:205
  489.8 12.2 %input_other.2 = bf16[1024,1280]{1,0:T(8,128)(2,1)} custom-call(bf16[320,2048]{1,0:T(8,128)(2,1)} %get-tuple-element.171.refs_0_.dq_ref, bf16[320,2048]{1,0:T(8,128)(2,1)} %get-tuple-element.173.refs_1_.dk_ref, bf16[320,2048]{1,0:T(8,128)(2,1)} %get-tuple-element.169.refs_2_.dv_ref, bf16[320,2048]{1,0:T(8,128)(2,1)} %get-tuple-element.160.dq_ref.refs_3_, ...), custom_call_target="tpu_custom_call" | custom-call | flops 5033164800 | bytes 10485760 | tf_op jit(solution)/shard_map/input_other/pallas_call | solution.py:875
  502.0 4.1 collective-permute-done.13.refs_0_
  506.9 10.9 %weight_grad.5 = bf16[1280,1024]{1,0:T(8,128)(2,1)} custom-call(bf16[1024,1280]{1,0:T(8,128)(2,1)} %get-tuple-element.134.h_ref.own_ref, bf16[1024,1280]{1,0:T(8,128)(2,1)} %copy-done.2, bf16[320,2048]{1,0:T(8,128)(2,1)} %get-tuple-element.171.refs_0_.dq_ref, bf16[320,2048]{1,0:T(8,128)(2,1)} %get-tuple-element.173.refs_1_.dk_ref, ...), custom_call_target="tpu_custom_call" | custom-call | flops 5033164800 | bytes 15728640 | tf_op jit(solution)/shard_map/weight_grad/pallas_call | solution.py:841
  517.9 1.5 copy-done.1
  519.4 15.9 %input_own.2 = (f32[1024,1280]{1,0:T(8,128)}, f32[8,1280]{1,0:T(8,128)}) custom-call(bf16[320,2048]{1,0:T(8,128)(2,1)} %get-tuple-element.171.refs_0_.dq_ref, bf16[320,2048]{1,0:T(8,128)(2,1)} %get-tuple-element.173.refs_1_.dk_ref, bf16[320,2048]{1,0:T(8,128)(2,1)} %get-tuple-element.169.refs_2_.dv_ref, bf16[320,2048]{1,0:T(8,128)(2,1)} %get-tuple-element.160.dq_ref.refs_3_, ...), custom_call_target="tpu_custom_call" | custom-call | flops 5033164800 | bytes 31457280 | tf_op jit(solution)/shard_map/input_own/pallas_call | solution.py:911
  535.4 2.0 convert_element_type.78
  537.4 39.8 %mlp_back.3 = (f32[1024,1280]{1,0:T(8,128)}, f32[8,1280]{1,0:T(8,128)}, bf16[640,2048]{1,0:T(8,128)(2,1)}, bf16[1280,1024]{1,0:T(8,128)(2,1)}, bf16[1280,1024]{1,0:T(8,128)(2,1)}) custom-call(f32[1024,1280]{1,0:T(8,128)} %get-tuple-element.178.g_ref, f32[1024,1280]{1,0:T(8,128)} %get-tuple-element.179.mid_ref, f32[1024,1280]{1,0:T(8,128)} %get-tuple-element.180.pre_ref, ...), custom_call_target="tpu_custom_call" | custom-call | flops 20132659200 | bytes 52428800 | tf_op jit(solution)/shard_map/mlp_back/pallas_call | solution.py:799
  578.5 40.3 %attention_backward.6 = (bf16[320,2048]{1,0:T(8,128)(2,1)}, bf16[320,2048]{1,0:T(8,128)(2,1)}, bf16[320,2048]{1,0:T(8,128)(2,1)}, f32[80,128]{1,0:T(8,128)}) custom-call(s32[1]{0:T(128)} %dynamic_slice.30.prefix_ref, s32[4]{0:T(128)} %fusion.23.order_ref, bf16[640,2048]{1,0:T(8,128)(2,1)} %get-tuple-element.122.q_ref, ...), custom_call_target="tpu_custom_call" | custom-call | flops 26843545600 | bytes 10485760 | tf_op jit(solution)/shard_map/attention_backward/pallas_call | solution.py:205
  618.8 10.4 %weight_grad.6 = bf16[1280,1024]{1,0:T(8,128)(2,1)} custom-call(bf16[1024,1280]{1,0:T(8,128)(2,1)} %copy-done.4, bf16[1024,1280]{1,0:T(8,128)(2,1)} %collective-permute-done.h_ref.other_ref, bf16[320,2048]{1,0:T(8,128)(2,1)} %get-tuple-element.186.dq_ref.refs_3_, bf16[320,2048]{1,0:T(8,128)(2,1)} %get-tuple-element.187.dk_ref.refs_4_, ...), custom_call_target="tpu_custom_call" | custom-call | flops 5033164800 | bytes 15728640 | tf_op jit(solution)/shard_map/weight_grad/pallas_call | solution.py:841
  630.2 6.8 collective-permute-done.15
  637.0 4.5 add_convert_fusion
  641.5 1.4 collective-permute-start.16
  643.0 40.4 %attention_backward.7 = (bf16[320,2048]{1,0:T(8,128)(2,1)}, bf16[320,2048]{1,0:T(8,128)(2,1)}, bf16[320,2048]{1,0:T(8,128)(2,1)}, f32[80,128]{1,0:T(8,128)}) custom-call(s32[1]{0:T(128)} %dynamic_slice.30.prefix_ref, s32[4]{0:T(128)} %fusion.23.order_ref, bf16[640,2048]{1,0:T(8,128)(2,1)} %get-tuple-element.122.q_ref, ...), custom_call_target="tpu_custom_call" | custom-call | flops 26843545600 | bytes 10485760 | tf_op jit(solution)/shard_map/attention_backward/pallas_call | solution.py:205
  683.4 12.2 %input_other.3 = bf16[1024,1280]{1,0:T(8,128)(2,1)} custom-call(bf16[320,2048]{1,0:T(8,128)(2,1)} %get-tuple-element.199.refs_0_.dq_ref, bf16[320,2048]{1,0:T(8,128)(2,1)} %get-tuple-element.201.refs_1_.dk_ref, bf16[320,2048]{1,0:T(8,128)(2,1)} %get-tuple-element.197.refs_2_.dv_ref, bf16[320,2048]{1,0:T(8,128)(2,1)} %get-tuple-element.186.dq_ref.refs_3_, ...), custom_call_target="tpu_custom_call" | custom-call | flops 5033164800 | bytes 10485760 | tf_op jit(solution)/shard_map/input_other/pallas_call | solution.py:875
  695.7 4.7 collective-permute-done.16.refs_0_
  701.6 11.0 %weight_grad.7 = bf16[1280,1024]{1,0:T(8,128)(2,1)} custom-call(bf16[1024,1280]{1,0:T(8,128)(2,1)} %copy-done.4, bf16[1024,1280]{1,0:T(8,128)(2,1)} %collective-permute-done.h_ref.other_ref, bf16[320,2048]{1,0:T(8,128)(2,1)} %get-tuple-element.199.refs_0_.dq_ref, bf16[320,2048]{1,0:T(8,128)(2,1)} %get-tuple-element.201.refs_1_.dk_ref, ...), custom_call_target="tpu_custom_call" | custom-call | flops 5033164800 | bytes 15728640 | tf_op jit(solution)/shard_map/weight_grad/pallas_call | solution.py:841
  712.6 1.5 copy-done.3
  714.1 15.8 %input_own.3 = (f32[1024,1280]{1,0:T(8,128)}, f32[8,1280]{1,0:T(8,128)}) custom-call(bf16[320,2048]{1,0:T(8,128)(2,1)} %get-tuple-element.199.refs_0_.dq_ref, bf16[320,2048]{1,0:T(8,128)(2,1)} %get-tuple-element.201.refs_1_.dk_ref, bf16[320,2048]{1,0:T(8,128)(2,1)} %get-tuple-element.197.refs_2_.dv_ref, bf16[320,2048]{1,0:T(8,128)(2,1)} %get-tuple-element.186.dq_ref.refs_3_, ...), custom_call_target="tpu_custom_call" | custom-call | flops 5033164800 | bytes 31457280 | tf_op jit(solution)/shard_map/input_own/pallas_call | solution.py:911
  731.3 2.6 convert_select_fusion.3
  733.9 1.7 collective-permute-start.20
  735.6 3.0 fusion.3
  739.1 2.7 pad_maximum_fusion.2
  742.9 3.5 collective-permute-start.22
  749.5 3.4 collective-permute-done.23
  754.1 15.2 %collective-permute-done.18 = bf16[512,1280]{1,0:T(8,128)(2,1)S(1)} collective-permute-done((bf16[512,1280]{1,0:T(8,128)(2,1)}, bf16[512,1280]{1,0:T(8,128)(2,1)S(1)}, u32[]{:S(2)}, u32[]{:S(2)}) %collective-permute-start.18) | collective-permute-done | bytes 1310752 | tf_op jit(solution)/shard_map/ppermute | solution.py:367
  769.3 2.1 convert_select_fusion.1
  771.4 2.7 pad_maximum_fusion.3
  774.1 12.1 %reduce-scatter.9.cloned.1.call-done = bf16[160,1024]{1,0:T(8,128)(2,1)} async-done(((bf16[1280,1024]{1,0:T(8,128)(2,1)}), bf16[160,1024]{1,0:T(8,128)(2,1)}) %reduce-scatter.9.cloned.1.call-update) | async-done | bytes 327696 | tf_op jit(solution)/shard_map/reduce_scatter | solution.py:942
  (146 shorter events, 26.5 us)
Async XLA Ops:
  7.2 4.2 copy-start.9
  7.2 4.2 copy-start.10
  7.2 4.3 copy-start.11
  7.2 119.0 %all-gather.11.cloned.1.call-start = ((), (), s32[]{:S(2)}) async-start(), calls=%async_computation.9 | async-start | bytes 1843200 | tf_op jit(solution)/shard_map/all_gather | solution.py:972
  9.4 119.3 %all-gather.9.cloned.1.call-start = ((), (), s32[]{:S(2)}) async-start(), calls=%async_computation.8 | async-start | bytes 1843200 | tf_op jit(solution)/shard_map/all_gather | solution.py:972
  11.3 225.9 %all-gather.13.cloned.1.call-start = ((), (), s32[]{:S(2)}) async-start(), calls=%async_computation.10 | async-start | bytes 3686400 | tf_op jit(solution)/shard_map/all_gather | solution.py:985
  121.8 0.7 copy-start.18
  123.1 20.2 %copy-start.21 = (f32[2,80]{1,0:T(2,128)S(1)}, f32[2,80]{1,0:T(2,128)}, u32[]{:S(2)}) copy-start(f32[2,80]{1,0:T(2,128)} %param.16) | copy-start | bytes 1924
  123.1 21.6 %copy-start.25 = (s32[2]{0:T(128)S(1)}, s32[2]{0:T(128)}, u32[]{:S(2)}) copy-start(s32[2]{0:T(128)} %param.17) | copy-start | bytes 28
  126.2 21.5 %copy-start.4 = (bf16[1024,1280]{1,0:T(8,128)(2,1)}, bf16[1024,1280]{1,0:T(8,128)(2,1)S(1)}, u32[]{:S(2)}) copy-start(bf16[1024,1280]{1,0:T(8,128)(2,1)S(1)} %get-tuple-element.114.h_ref.own_ref) | copy-start | bytes 7864324
  128.8 28.7 %collective-permute-start = (bf16[1024,1280]{1,0:T(8,128)(2,1)S(1)}, bf16[1024,1280]{1,0:T(8,128)(2,1)}, u32[]{:S(2)}, u32[]{:S(2)}) collective-permute-start(bf16[1024,1280]{1,0:T(8,128)(2,1)S(1)} %get-tuple-element.114.h_ref.own_ref), channel_id=1, source_target_pairs={{0,1},{1,0},{2,3},{3,2},{4,5},{5,4},{6,7},{7,6},{8,9},{9,8},{10,11... | collective-permute-start | bytes 7864328 | tf_op jit(solution)/shard_map/ppermute | solution.py:370
  128.8 12.9 %collective-permute-start.6 = (bf16[2,160,640]{2,1,0:T(8,128)(2,1)S(1)}, bf16[2,160,640]{2,1,0:T(8,128)(2,1)S(1)}, u32[]{:S(2)}, u32[]{:S(2)}) collective-permute-start(bf16[2,160,640]{2,1,0:T(8,128)(2,1)S(1)} %get-tuple-element.253), channel_id=1, source_target_pairs={{0,2},{1,3},{2,0},{3,1},{4,6},{5,7},{6,4},{7,5},{8,10},{9,11},{10,... | collective-permute-start | bytes 1228808 | tf_op jit(solution)/shard_map/ppermute | solution.py:367
  142.7 164.7 %all-gather.15.cloned.1.call-start = ((), (), s32[]{:S(2)}) async-start(), calls=%async_computation.11 | async-start | bytes 3686400 | tf_op jit(solution)/shard_map/all_gather | solution.py:985
  143.3 0.6 copy-start.19
  146.0 54.7 %collective-permute-start.1 = (bf16[1280,640]{1,0:T(8,128)(2,1)}, bf16[1280,640]{1,0:T(8,128)(2,1)}, u32[]{:S(2)}, u32[]{:S(2)}) collective-permute-start(bf16[1280,640]{1,0:T(8,128)(2,1)} %bitcast.155), channel_id=1, source_target_pairs={{0,2},{1,3},{2,0},{3,1},{4,6},{5,7},{6,4},{7,5},{8,10},{9,11},{10,... | collective-permute-start | bytes 4915208 | tf_op jit(solution)/shard_map/ppermute | solution.py:367
  200.6 6.9 copy-start
  207.0 9.9 %collective-permute-start.2 = (bf16[1024,1280]{1,0:T(8,128)(2,1)}, bf16[1024,1280]{1,0:T(8,128)(2,1)}, u32[]{:S(2)}, u32[]{:S(2)}) collective-permute-start(bf16[1024,1280]{1,0:T(8,128)(2,1)} %out_project.2), channel_id=1, source_target_pairs={{0,1},{1,0},{2,3},{3,2},{4,5},{5,4},{6,7},{7,6},{8,9},{9,8},{10,11... | collective-permute-start | bytes 7864328 | tf_op jit(solution)/shard_map/ppermute | solution.py:370
  207.0 7.6 collective-permute-start.3
  207.6 9.4 %collective-permute-start.4 = (bf16[1280,640]{1,0:T(8,128)(2,1)}, bf16[1280,640]{1,0:T(8,128)(2,1)}, u32[]{:S(2)}, u32[]{:S(2)}) collective-permute-start(bf16[1280,640]{1,0:T(8,128)(2,1)} %collective-permute-done.1.un1.refs_3_), channel_id=1, source_target_pairs={{0,1},{1,0},{2,3},{3,2},{4,5},{5,4},{6,7},{7,6},{8,9},{9,8},{10,11... | collective-permute-start | bytes 4915208 | tf_op jit(solution)/shard_map/ppermute | solution.py:370
  207.6 38.3 %collective-permute-start.5 = (bf16[1280,640]{1,0:T(8,128)(2,1)S(1)}, bf16[1280,640]{1,0:T(8,128)(2,1)}, u32[]{:S(2)}, u32[]{:S(2)}) collective-permute-start(bf16[1280,640]{1,0:T(8,128)(2,1)S(1)} %bitcast.115), channel_id=1, source_target_pairs={{0,2},{1,3},{2,0},{3,1},{4,6},{5,7},{6,4},{7,5},{8,10},{9,11},{10,... | collective-permute-start | bytes 4915208 | tf_op jit(solution)/shard_map/ppermute | solution.py:367
  207.6 327.8 %reduce-scatter.5.cloned.1.call-start = ((), (), s32[]{:S(2)}) async-start(), calls=%async_computation.4 | async-start | bytes 2949120 | tf_op jit(solution)/shard_map/reduce_scatter | solution.py:942
  245.9 11.1 %collective-permute-start.7 = (bf16[1024,1280]{1,0:T(8,128)(2,1)}, bf16[1024,1280]{1,0:T(8,128)(2,1)S(1)}, u32[]{:S(2)}, u32[]{:S(2)}) collective-permute-start(bf16[1024,1280]{1,0:T(8,128)(2,1)} %get-tuple-element.134.h_ref.own_ref), channel_id=1, source_target_pairs={{0,1},{1,0},{2,3},{3,2},{4,5},{5,4},{6,7},{7,6},{8,9},{9,8},{10,11... | collective-permute-start | bytes 7864328 | tf_op jit(solution)/shard_map/ppermute | solution.py:370
  246.8 60.6 %collective-permute-start.8 = (bf16[512,1280]{1,0:T(8,128)(2,1)}, bf16[512,1280]{1,0:T(8,128)(2,1)}, u32[]{:S(2)}, u32[]{:S(2)}) collective-permute-start(bf16[512,1280]{1,0:T(8,128)(2,1)} %fusion.1), channel_id=1, source_target_pairs={{0,2},{1,3},{2,0},{3,1},{4,6},{5,7},{6,4},{7,5},{8,10},{9,11},{10,... | collective-permute-start | bytes 3932168 | tf_op jit(solution)/shard_map/ppermute | solution.py:367
  256.9 1.5 copy-start.2
  307.4 12.6 %collective-permute-start.10 = (bf16[2,1280,640]{2,1,0:T(8,128)(2,1)}, bf16[2,1280,640]{2,1,0:T(8,128)(2,1)}, u32[]{:S(2)}, u32[]{:S(2)}) collective-permute-start(bf16[2,1280,640]{2,1,0:T(8,128)(2,1)} %bitcast.150), channel_id=1, source_target_pairs={{0,1},{1,0},{2,3},{3,2},{4,5},{5,4},{6,7},{7,6},{8,9},{9,8},{10,11... | collective-permute-start | bytes 9830408 | tf_op jit(solution)/shard_map/ppermute | solution.py:370
  313.6 6.4 collective-permute-start.9
  320.0 1.5 copy-start.24
  344.4 41.9 %collective-permute-start.11 = (bf16[512,1280]{1,0:T(8,128)(2,1)}, bf16[512,1280]{1,0:T(8,128)(2,1)S(1)}, u32[]{:S(2)}, u32[]{:S(2)}) collective-permute-start(bf16[512,1280]{1,0:T(8,128)(2,1)} %fusion.2), channel_id=1, source_target_pairs={{0,2},{1,3},{2,0},{3,1},{4,6},{5,7},{6,4},{7,5},{8,10},{9,11},{10,... | collective-permute-start | bytes 3932168 | tf_op jit(solution)/shard_map/ppermute | solution.py:367
  384.2 59.2 %collective-permute-start.12 = (bf16[1280,1024]{1,0:T(8,128)(2,1)}, bf16[1280,1024]{1,0:T(8,128)(2,1)}, u32[]{:S(2)}, u32[]{:S(2)}) collective-permute-start(bf16[1280,1024]{1,0:T(8,128)(2,1)} %get-tuple-element.163), channel_id=1, source_target_pairs={{0,2},{1,3},{2,0},{3,1},{4,6},{5,7},{6,4},{7,5},{8,10},{9,11},{10,... | collective-permute-start | bytes 7864328 | tf_op jit(solution)/shard_map/ppermute | solution.py:367
  386.3 40.2 %copy-start.8 = (bf16[512,1280]{1,0:T(8,128)(2,1)}, bf16[512,1280]{1,0:T(8,128)(2,1)S(1)}, u32[]{:S(2)}) copy-start(bf16[512,1280]{1,0:T(8,128)(2,1)S(1)} %collective-permute-done.11) | copy-start | bytes 3932164
  426.5 17.0 %copy-start.6 = (bf16[1280,1024]{1,0:T(8,128)(2,1)S(1)}, bf16[1280,1024]{1,0:T(8,128)(2,1)}, u32[]{:S(2)}) copy-start(bf16[1280,1024]{1,0:T(8,128)(2,1)} %get-tuple-element.157) | copy-start | bytes 7864324
  447.9 58.3 %collective-permute-start.13 = (bf16[1280,1024]{1,0:T(8,128)(2,1)}, bf16[1280,1024]{1,0:T(8,128)(2,1)}, u32[]{:S(2)}, u32[]{:S(2)}) collective-permute-start(bf16[1280,1024]{1,0:T(8,128)(2,1)} %weight_grad.4), channel_id=1, source_target_pairs={{0,2},{1,3},{2,0},{3,1},{4,6},{5,7},{6,4},{7,5},{8,10},{9,11},{10,... | collective-permute-start | bytes 7864328 | tf_op jit(solution)/shard_map/ppermute | solution.py:367
  449.6 179.6 %reduce-scatter.7.cloned.1.call-start = ((), (), s32[]{:S(2)}) async-start(), calls=%async_computation.5 | async-start | bytes 2949120 | tf_op jit(solution)/shard_map/reduce_scatter | solution.py:942
  489.8 16.3 %copy-start.23 = (f32[80,1]{0,1:T(1,128)S(1)}, f32[80,1]{0,1:T(1,128)}, u32[]{:S(2)}) copy-start(f32[80,1]{0,1:T(1,128)} %get-tuple-element.268) | copy-start | bytes 964
  506.1 11.7 %collective-permute-start.14 = (bf16[1024,1280]{1,0:T(8,128)(2,1)}, bf16[1024,1280]{1,0:T(8,128)(2,1)S(1)}, u32[]{:S(2)}, u32[]{:S(2)}) collective-permute-start(bf16[1024,1280]{1,0:T(8,128)(2,1)} %input_other.2), channel_id=1, source_target_pairs={{0,1},{1,0},{2,3},{3,2},{4,5},{5,4},{6,7},{7,6},{8,9},{9,8},{10,11... | collective-permute-start | bytes 7864328 | tf_op jit(solution)/shard_map/ppermute | solution.py:370
  517.8 228.5 %reduce-scatter.11.cloned.1.call-start = ((), (), s32[]{:S(2)}) async-start(), calls=%async_computation.7 | async-start | bytes 2949120 | tf_op jit(solution)/shard_map/reduce_scatter | solution.py:942
  517.9 1.5 copy-start.1
  577.1 59.8 %collective-permute-start.15 = (bf16[1280,1024]{1,0:T(8,128)(2,1)}, bf16[1280,1024]{1,0:T(8,128)(2,1)}, u32[]{:S(2)}, u32[]{:S(2)}) collective-permute-start(bf16[1280,1024]{1,0:T(8,128)(2,1)} %get-tuple-element.189), channel_id=1, source_target_pairs={{0,2},{1,3},{2,0},{3,1},{4,6},{5,7},{6,4},{7,5},{8,10},{9,11},{10,... | collective-permute-start | bytes 7864328 | tf_op jit(solution)/shard_map/ppermute | solution.py:367
  618.8 18.2 %copy-start.5 = (bf16[1280,1024]{1,0:T(8,128)(2,1)S(1)}, bf16[1280,1024]{1,0:T(8,128)(2,1)}, u32[]{:S(2)}) copy-start(bf16[1280,1024]{1,0:T(8,128)(2,1)} %get-tuple-element.183) | copy-start | bytes 7864324
  641.5 58.9 %collective-permute-start.16 = (bf16[1280,1024]{1,0:T(8,128)(2,1)}, bf16[1280,1024]{1,0:T(8,128)(2,1)}, u32[]{:S(2)}, u32[]{:S(2)}) collective-permute-start(bf16[1280,1024]{1,0:T(8,128)(2,1)} %weight_grad.6), channel_id=1, source_target_pairs={{0,2},{1,3},{2,0},{3,1},{4,6},{5,7},{6,4},{7,5},{8,10},{9,11},{10,... | collective-permute-start | bytes 7864328 | tf_op jit(solution)/shard_map/ppermute | solution.py:367
  642.9 143.3 %reduce-scatter.9.cloned.1.call-start = ((), (), s32[]{:S(2)}) async-start(), calls=%async_computation.6 | async-start | bytes 2949120 | tf_op jit(solution)/shard_map/reduce_scatter | solution.py:942
  683.4 17.0 %copy-start.16 = (f32[8,1280]{1,0:T(8,128)S(1)}, f32[8,1280]{1,0:T(8,128)}, u32[]{:S(2)}) copy-start(f32[8,1280]{1,0:T(8,128)} %get-tuple-element.214) | copy-start | bytes 122884
  683.4 17.0 %copy-start.12 = (f32[80,128]{1,0:T(8,128)S(1)}, f32[80,128]{1,0:T(8,128)}, u32[]{:S(2)}) copy-start(f32[80,128]{1,0:T(8,128)} %get-tuple-element.215) | copy-start | bytes 122884
  683.4 17.0 %copy-start.13 = (f32[80,128]{1,0:T(8,128)S(1)}, f32[80,128]{1,0:T(8,128)}, u32[]{:S(2)}) copy-start(f32[80,128]{1,0:T(8,128)} %get-tuple-element.216) | copy-start | bytes 122884
  683.4 17.1 %copy-start.17 = (f32[8,1280]{1,0:T(8,128)S(1)}, f32[8,1280]{1,0:T(8,128)}, u32[]{:S(2)}) copy-start(f32[8,1280]{1,0:T(8,128)} %get-tuple-element.213) | copy-start | bytes 122884
  683.4 18.0 %copy-start.14 = (f32[80,128]{1,0:T(8,128)S(1)}, f32[80,128]{1,0:T(8,128)}, u32[]{:S(2)}) copy-start(f32[80,128]{1,0:T(8,128)} %get-tuple-element.211) | copy-start | bytes 122884
  683.4 18.0 %copy-start.15 = (f32[80,128]{1,0:T(8,128)S(1)}, f32[80,128]{1,0:T(8,128)}, u32[]{:S(2)}) copy-start(f32[80,128]{1,0:T(8,128)} %get-tuple-element.212) | copy-start | bytes 122884
  683.4 18.1 %copy-start.20 = (f32[2,80]{1,0:T(2,128)S(1)}, f32[2,80]{1,0:T(2,128)}, u32[]{:S(2)}) copy-start(f32[2,80]{1,0:T(2,128)} %copy-done.19) | copy-start | bytes 1924
  700.4 12.2 %collective-permute-start.17 = (bf16[1024,1280]{1,0:T(8,128)(2,1)}, bf16[1024,1280]{1,0:T(8,128)(2,1)S(1)}, u32[]{:S(2)}, u32[]{:S(2)}) collective-permute-start(bf16[1024,1280]{1,0:T(8,128)(2,1)} %input_other.3), channel_id=1, source_target_pairs={{0,1},{1,0},{2,3},{3,2},{4,5},{5,4},{6,7},{7,6},{8,9},{9,8},{10,11... | collective-permute-start | bytes 7864328 | tf_op jit(solution)/shard_map/ppermute | solution.py:370
  712.6 1.5 copy-start.3
  730.7 3.1 collective-permute-start.19
  733.9 5.0 collective-permute-start.20
  738.6 30.7 %collective-permute-start.18 = (bf16[512,1280]{1,0:T(8,128)(2,1)}, bf16[512,1280]{1,0:T(8,128)(2,1)S(1)}, u32[]{:S(2)}, u32[]{:S(2)}) collective-permute-start(bf16[512,1280]{1,0:T(8,128)(2,1)} %fusion.3), channel_id=1, source_target_pairs={{0,2},{1,3},{2,0},{3,1},{4,6},{5,7},{6,4},{7,5},{8,10},{9,11},{10,... | collective-permute-start | bytes 3932168 | tf_op jit(solution)/shard_map/ppermute | solution.py:367
  739.0 3.9 collective-permute-start.21
  739.1 9.1 %copy-start.7 = (f32[160,1024]{1,0:T(8,128)S(1)}, f32[160,1024]{1,0:T(8,128)}, u32[]{:S(2)}) copy-start(f32[160,1024]{1,0:T(8,128)} %convert_element_type.78) | copy-start | bytes 1966084
  741.8 11.1 %copy-start.22 = (f32[2,80]{1,0:T(2,128)S(1)}, f32[2,80]{1,0:T(2,128)}, u32[]{:S(2)}) copy-start(f32[2,80]{1,0:T(2,128)} %param.16) | copy-start | bytes 1924
  742.9 5.2 collective-permute-start.22
  748.1 4.8 collective-permute-start.23
Sparse Core Ops, SparseCore 0:
  10.8 65.6 all-gather.10
  79.2 49.4 all-gather.8
  142.8 64.0 all-gather.12
  209.5 66.1 all-gather.14
  449.7 69.9 reduce-scatter.4
  523.1 69.2 reduce-scatter.6
  643.1 70.2 reduce-scatter.10
  716.9 69.3 reduce-scatter.8

commit v5 on v4

--- a/solution.py
+++ b/solution.py
@@ -542,135 +542,272 @@
         dst[:, i * width:(i + 1) * width] = ref[:, low:high]
 
 
-def project_kernel(w, h_ref, qk0, qk1, vo0, vo1, scale_ref, *refs):
-    q_ref, k_ref, v_ref = refs[-3:]
-    h = h_ref[...]
-    for s, (qk, vo) in enumerate(((qk0, vo0), (qk1, vo1))):
-        rows = slice(s * w, (s + 1) * w)
-        both = dot(qk[...], h, TT)
-        q_ref[rows] = (both[:w] * scale_ref[rows]).astype(BF16)
-        k_ref[rows] = both[w:].astype(BF16)
-        v_ref[rows] = dot(vo[:, :w], h, TT).astype(BF16)
-
-
-def project(h, qk, vo, scale, base, bufs=None):
-    rows, d = h.shape
-    w = plain(qk)[0].shape[-1] // 2
-    bt = 512
-    steps = rows // bt
-    out = pl.BlockSpec((2 * w, bt), lambda i: (0, i + base * steps))
-    extra = [] if bufs is None else list(bufs)
-    return pl.pallas_call(
-        functools.partial(project_kernel, w),
-        grid=(steps,),
-        in_specs=[pl.BlockSpec((bt, d), lambda i: (i, 0))] + [weight(a) for a in (*qk, *vo)] + [fixed((2 * w, 1))]
-        + [pl.BlockSpec(memory_space=pl.ANY)] * len(extra),
-        out_specs=[out] * 3,
-        out_shape=[shape_of((2 * w, 2 * rows))] * 3,
-        input_output_aliases={6 + i: i for i in range(len(extra))},
-        compiler_params=params(),
-        cost_estimate=cost(2 * rows * d * 6 * w, 4 * rows * d),
-        name="project",
-    )(h, *plain(qk), *plain(vo), scale, *extra)
-
-
-def out_kernel(w, att_ref, vo0, vo1, part_ref, mat):
-    @pl.when(pl.program_id(0) == 0)
-    def _():
-        join_lanes(mat, (vo0, vo1), w, 2 * w)
-
-    part_ref[...] = dot(att_ref[...], mat[...], TT).astype(BF16)
-
-
-def out_project(att, vo, base):
-    d, w2 = plain(vo)[0].shape[-2:]
-    rows = att.shape[1] // 2
-    bt = 512
-    steps = rows // bt
-    return pl.pallas_call(
-        functools.partial(out_kernel, w2 // 2),
-        grid=(steps,),
-        in_specs=[pl.BlockSpec((w2, bt), lambda i: (0, i + base * steps))] + [weight(a) for a in vo],
-        out_specs=pl.BlockSpec((bt, d), lambda i: (i, 0)),
-        out_shape=shape_of((rows, d)),
-        scratch_shapes=[pltpu.VMEM((d, w2), BF16)],
-        compiler_params=params(),
-        cost_estimate=cost(2 * rows * d * w2, 4 * rows * d),
-        name="out_project",
-    )(att, *plain(vo))
-
-
-def middle_kernel(w, x_ref, att_ref, got_ref, gm_ref, ga_ref, vo0, vo1, un0, un1, un2, un3,
-                  mid_ref, pre_ref, res_ref, h_ref, out_mat, up_mat, down_mat):
-    @pl.when(pl.program_id(0) == 0)
-    def _():
-        join_lanes(out_mat, (vo0, vo1), w, 2 * w)
-        join_lanes(up_mat, (un0, un1, un2, un3), 0, w)
-        join_lanes(down_mat, (un0, un1, un2, un3), w, 2 * w)
-
-    mid = x_ref[...] + got_ref[...].astype(F32) + dot(att_ref[...], out_mat[...], TT)
-    mid_ref[...] = mid
-    h_m = (mid * inverse_rms(mid) * gm_ref[...]).astype(BF16)
-    pre = dot(h_m, up_mat[...])
-    pre_ref[...] = pre
-    hidden = (pre / (1.0 + jnp.exp(-pre))).astype(BF16)
-    res = mid + dot(hidden, down_mat[...], NT)
-    res_ref[...] = res
-    h_ref[...] = (res * inverse_rms(res) * ga_ref[...]).astype(BF16)
-
-
-def middle_call(x, att, got, gain_m, gain_a, vo, un):
-    rows, d = x.shape
-    w2 = plain(vo)[0].shape[-1]
-    ff = 2 * w2
-    bt = 256
-    row = pl.BlockSpec((bt, d), lambda i: (i, 0))
-    wide = pl.BlockSpec((bt, ff), lambda i: (i, 0))
-    return pl.pallas_call(
-        functools.partial(middle_kernel, w2 // 2),
-        grid=(rows // bt,),
-        in_specs=[row, pl.BlockSpec((w2, bt), lambda i: (0, i)), row] + [fixed((1, d))] * 2
-        + [weight(a) for a in (*vo, *un)],
-        out_specs=[row, wide, row, row],
-        out_shape=[shape_of((rows, d), F32), shape_of((rows, ff), F32), shape_of((rows, d), F32), shape_of((rows, d))],
-        scratch_shapes=[pltpu.VMEM((d, w2), BF16), pltpu.VMEM((d, ff), BF16), pltpu.VMEM((d, ff), BF16)],
-        compiler_params=params(),
-        cost_estimate=cost(2 * rows * d * (w2 + 2 * ff), 30 * rows * d),
-        name="middle",
-    )(x, att, got, gain_m, gain_a, *plain(vo), *plain(un))
-
-
-def mlp_back_kernel(w, sides, steps, index, g_ref, mid_ref, pre_ref, gm_ref, att_any, *refs):
-    weights, refs = refs[:6], refs[6:]
-    g_mid_ref, gain_ref, g_att_ref, o0, o1 = refs[:5]
-    (up_mat, down_mat, out_mat, g_all, hid_all, hm_all, gpre_all, low_own, low_other, blocks, got, vo_side, att,
-     load, send, recv) = refs[5:]
-    i = pl.program_id(0)
-    rows_steps, grad_steps, att_steps, _ = steps
-    bt, bd, ba = g_ref.shape[0], o0.shape[0], g_att_ref.shape[1]
+def core_of():
     t = lax.axis_index("tp")
-    core = {"tp": t + 1 - 2 * lax.rem(t, 2)}
-    low_lane = sides[0]
-
-    def loads():
-        pairs = [(weights[2 + b], blocks.at[b]) for b in range(4)]
-        for s in range(2):
-            pairs.append((weights[s], vo_side.at[s]))
-        views = []
-        for n, ((ref, dst), k) in enumerate(zip(pairs, index[2:] + index[:2])):
-            src = ref if k is None else ref.at[k]
-            if n >= 4:
-                src = src.at[:, pl.ds(low_lane, vo_side.shape[2])]
-            views.append(pltpu.make_async_copy(src, dst, load.at[n]))
-        views.append(pltpu.make_async_copy(att_any, att, load.at[6]))
-        return views
-
+    return {"tp": t + 1 - 2 * lax.rem(t, 2)}
+
+
+def pushes(send, recv, core):
     def push(src, dst, slot):
         return pltpu.make_async_remote_copy(
             src_ref=src, dst_ref=dst, send_sem=send.at[slot], recv_sem=recv.at[slot],
             device_id=core, device_id_type=MESH,
         )
 
+    return push
+
+
+def greet(core):
+    barrier = pltpu.get_barrier_semaphore()
+    pl.semaphore_signal(barrier, inc=1, device_id=core, device_id_type=MESH)
+    pl.semaphore_wait(barrier, 1)
+
+
+def stack_index(weights):
+    return tuple(a[1] if isinstance(a, tuple) else None for a in weights)
+
+
+def entry(ref, k):
+    return ref if k is None else ref.at[k]
+
+
+def stages(steps):
+    starts = [sum(steps[:n]) for n in range(len(steps))]
+
+    def at(n, make):
+        return lambda i: make(jnp.clip(i - starts[n], 0, steps[n] - 1))
+
+    return at
+
+
+ANY = pl.BlockSpec(memory_space=pl.ANY)
+
+
+def project_kernel(w, low, steps, index, x_ref, gain_ref, scale_ref, *refs):
+    weights, refs = refs[:4], refs[4:]
+    own_ref, other_ref, q_ref, k_ref, v_ref = refs[:5]
+    own, other, qk, vo, load, send, recv = refs[5:]
+    i = pl.program_id(0)
+    rows_steps, half, _ = steps
+    bt, ba = x_ref.shape[0], q_ref.shape[1]
+    core = core_of()
+    push = pushes(send, recv, core)
+
+    def loads():
+        copies = [pltpu.make_async_copy(entry(weights[s], index[s]), qk.at[s], load.at[s]) for s in range(2)]
+        for s in range(2):
+            src = entry(weights[2 + s], index[2 + s]).at[:, pl.ds(0, low)]
+            copies.append(pltpu.make_async_copy(src, vo.at[s], load.at[2 + s]))
+        return copies
+
+    def push_rows(k):
+        part = pl.ds(pl.multiple_of(k * bt, bt), bt)
+        return push(own.at[part], other.at[part], k)
+
+    @pl.when(i == 0)
+    def _():
+        for c in loads():
+            c.start()
+        greet(core)
+
+    @pl.when(i < rows_steps)
+    def _():
+        x = x_ref[...]
+        h = (x * inverse_rms(x) * gain_ref[...]).astype(BF16)
+        own[pl.ds(pl.multiple_of(i * bt, bt), bt)] = h
+        own_ref[...] = h
+        push_rows(i).start()
+
+    at = i - rows_steps
+
+    @pl.when(at == 0)
+    def _():
+        for c in loads():
+            c.wait()
+
+    @pl.when(at == half)
+    def _():
+        for k in range(rows_steps):
+            push_rows(k).wait()
+
+    def project(h):
+        for s in range(2):
+            rows = slice(s * w, (s + 1) * w)
+            both = dot(qk[s], h, TT)
+            q_ref[rows] = (both[:w] * scale_ref[rows]).astype(BF16)
+            k_ref[rows] = both[w:].astype(BF16)
+            v_ref[rows] = dot(vo[s, :, :w], h, TT).astype(BF16)
+
+    @pl.when((at >= 0) & (at < half))
+    def _():
+        project(own[pl.ds(pl.multiple_of(at * ba, ba), ba)])
+
+    @pl.when(at >= half)
+    def _():
+        h = other[pl.ds(pl.multiple_of((at - half) * ba, ba), ba)]
+        other_ref[...] = h
+        project(h)
+
+
+def project(x, gain, qk, vo, scale, call):
+    rows, d = x.shape
+    w2 = plain(qk)[0].shape[-1]
+    w = w2 // 2
+    low = -(-w // 128) * 128
+    bt, ba = 256, 512
+    half = rows // ba
+    steps = (rows // bt, half, half)
+    row = pl.BlockSpec((bt, d), lambda i: (jnp.minimum(i, steps[0] - 1), 0))
+    wide = pl.BlockSpec((w2, ba), lambda i: (0, jnp.clip(i - steps[0], 0, 2 * half - 1)))
+    tall = pl.BlockSpec((ba, d), lambda i: (jnp.clip(i - steps[0] - half, 0, half - 1), 0))
+    weights = (*qk, *vo)
+    return pl.pallas_call(
+        functools.partial(project_kernel, w, low, steps, stack_index(weights)),
+        grid=(sum(steps),),
+        in_specs=[row, fixed((1, d)), fixed((w2, 1))] + [ANY] * 4,
+        out_specs=[row, tall] + [wide] * 3,
+        out_shape=[shape_of((rows, d))] * 2 + [shape_of((w2, 2 * rows))] * 3,
+        scratch_shapes=[
+            pltpu.VMEM((rows, d), BF16), pltpu.VMEM((rows, d), BF16),
+            pltpu.VMEM((2, d, w2), BF16), pltpu.VMEM((2, d, low), BF16),
+            pltpu.SemaphoreType.DMA((4,)), pltpu.SemaphoreType.DMA((steps[0],)), pltpu.SemaphoreType.DMA((steps[0],)),
+        ],
+        compiler_params=pltpu.CompilerParams(vmem_limit_bytes=VMEM_LIMIT, collective_id=call, has_side_effects=True),
+        cost_estimate=cost(4 * rows * d * 3 * w2, 12 * rows * d),
+        name="project",
+    )(x, gain, scale, *plain(weights))
+
+
+def middle_kernel(w, low, steps, index, x_ref, gm_ref, att_any, *refs):
+    weights, refs = refs[:4], refs[4:]
+    mid_ref, pre_ref, res_ref, up_out, down_out, out_out = refs[:6]
+    (up_mat, down_mat, out_mat, blocks, vo_side, att, part, got, load, store, send, recv) = refs[6:]
+    i = pl.program_id(0)
+    far, rows_steps = steps
+    bt = x_ref.shape[0]
+    ba = part.shape[0] // far
+    rows = part.shape[0]
+    core = core_of()
+    push = pushes(send, recv, core)
+
+    def loads():
+        copies = [pltpu.make_async_copy(att_any, att, load.at[0])]
+        for s in range(2):
+            src = entry(weights[s], index[s]).at[:, pl.ds(low, vo_side.shape[2])]
+            copies.append(pltpu.make_async_copy(src, vo_side.at[s], load.at[1 + s]))
+        for s in range(2):
+            copies.append(pltpu.make_async_copy(entry(weights[2 + s], index[2 + s]), blocks.at[s], load.at[3 + s]))
+        return copies
+
+    def stores():
+        pairs = ((up_mat, up_out), (down_mat, down_out), (out_mat, out_out))
+        return [pltpu.make_async_copy(src, dst, store.at[n]) for n, (src, dst) in enumerate(pairs)]
+
+    def push_block(s):
+        return push(blocks.at[s], blocks.at[2 + s], s)
+
+    def push_part(k):
+        here = pl.ds(pl.multiple_of(k * ba, ba), ba)
+        return push(part.at[here], got.at[here], 2 + k)
+
+    @pl.when(i == 0)
+    def _():
+        copies = loads()
+        for c in copies:
+            c.start()
+        greet(core)
+        for c in copies[:3]:
+            c.wait()
+        for s in range(2):
+            out_mat[:, s * w:(s + 1) * w] = vo_side[s, :, 2 * w - low - w:2 * w - low]
+        for s in range(2):
+            copies[3 + s].wait()
+            push_block(s).start()
+
+    @pl.when(i < far)
+    def _():
+        here = pl.ds(pl.multiple_of(i * ba, ba), ba)
+        cols = pl.ds(pl.multiple_of(rows + i * ba, ba), ba)
+        part[here] = dot(att[:, cols], out_mat[...], TT).astype(BF16)
+        push_part(i).start()
+
+    at = i - far
+
+    @pl.when(at == 0)
+    def _():
+        for s in range(2):
+            push_block(s).wait()
+        for b in range(4):
+            up_mat[:, b * w:(b + 1) * w] = blocks[b, :, 0:w]
+            down_mat[:, b * w:(b + 1) * w] = blocks[b, :, w:2 * w]
+        for c in stores():
+            c.start()
+
+    for k in range(far):
+        @pl.when(at == k * (ba // bt))
+        def _():
+            push_part(k).wait()
+
+    @pl.when(at >= 0)
+    def _():
+        here = pl.ds(pl.multiple_of(at * bt, bt), bt)
+        mid = x_ref[...] + got[here].astype(F32) + dot(att[:, here], out_mat[...], TT)
+        mid_ref[...] = mid
+        h_m = (mid * inverse_rms(mid) * gm_ref[...]).astype(BF16)
+        pre = dot(h_m, up_mat[...])
+        pre_ref[...] = pre
+        hidden = (pre / (1.0 + jnp.exp(-pre))).astype(BF16)
+        res_ref[...] = mid + dot(hidden, down_mat[...], NT)
+
+    @pl.when(at == rows_steps - 1)
+    def _():
+        for c in stores():
+            c.wait()
+
+
+def middle_call(x, att, gain_m, vo, un, call):
+    rows, d = x.shape
+    w2 = plain(vo)[0].shape[-1]
+    w, ff = w2 // 2, 2 * w2
+    low = w // 128 * 128
+    bt, ba = 256, 512
+    steps = (rows // ba, rows // bt)
+    row = pl.BlockSpec((bt, d), lambda i: (jnp.maximum(i - steps[0], 0), 0))
+    wide = pl.BlockSpec((bt, ff), lambda i: (jnp.maximum(i - steps[0], 0), 0))
+    weights = (*vo, *un)
+    mats = [(d, ff), (d, ff), (d, w2)]
+    slots = 2 + steps[0]
+    return pl.pallas_call(
+        functools.partial(middle_kernel, w, low, steps, stack_index(weights)),
+        grid=(sum(steps),),
+        in_specs=[row, fixed((1, d))] + [ANY] * 5,
+        out_specs=[row, wide, row] + [ANY] * 3,
+        out_shape=[shape_of((rows, d), F32), shape_of((rows, ff), F32), shape_of((rows, d), F32)] + [shape_of(m) for m in mats],
+        scratch_shapes=[pltpu.VMEM(m, BF16) for m in mats]
+        + [pltpu.VMEM((4, d, w2), BF16), pltpu.VMEM((2, d, w2 - low), BF16), pltpu.VMEM(att.shape, BF16)]
+        + [pltpu.VMEM((rows, d), BF16)] * 2
+        + [pltpu.SemaphoreType.DMA((5,)), pltpu.SemaphoreType.DMA((3,)), pltpu.SemaphoreType.DMA((slots,)), pltpu.SemaphoreType.DMA((slots,))],
+        compiler_params=pltpu.CompilerParams(vmem_limit_bytes=VMEM_LIMIT, collective_id=call, has_side_effects=True),
+        cost_estimate=cost(2 * rows * d * (2 * w2 + 2 * ff), 30 * rows * d),
+        name="middle",
+    )(x, gain_m, att, *plain(weights))
+
+
+def mlp_back_kernel(w, steps, g_ref, mid_ref, pre_ref, gm_ref, att_any, *refs):
+    mats, refs = refs[:3], refs[3:]
+    g_mid_ref, gain_ref, g_att_ref, o0, o1 = refs[:5]
+    (up_mat, down_mat, out_mat, g_all, hid_all, hm_all, gpre_all, low_own, low_other, blocks, got, att,
+     load, send, recv) = refs[5:]
+    i = pl.program_id(0)
+    rows_steps, grad_steps, att_steps, _ = steps
+    bt, bd, ba = g_ref.shape[0], o0.shape[0], g_att_ref.shape[1]
+    core = core_of()
+    push = pushes(send, recv, core)
+
+    def loads():
+        pairs = (*zip(mats, (up_mat, down_mat, out_mat)), (att_any, att))
+        return [pltpu.make_async_copy(src, dst, load.at[n]) for n, (src, dst) in enumerate(pairs)]
+
     def push_rows(k):
         part = pl.ds(pl.multiple_of(k * bt, bt), bt)
         return push(low_own.at[part], low_other.at[part], k)
@@ -684,14 +821,10 @@
         copies = loads()
         for c in copies:
             c.start()
-        barrier = pltpu.get_barrier_semaphore()
-        pl.semaphore_signal(barrier, inc=1, device_id=core, device_id_type=MESH)
         gain_ref[...] = jnp.zeros_like(gain_ref)
-        for b in range(4):
-            copies[b].wait()
-            up_mat[:, b * w:(b + 1) * w] = blocks[b, :, 0:w]
-            down_mat[:, b * w:(b + 1) * w] = blocks[b, :, w:2 * w]
-        pl.semaphore_wait(barrier, 1)
+        greet(core)
+        for c in copies[:2]:
+            c.wait()
 
     @pl.when(i < rows_steps)
     def _():
@@ -735,10 +868,7 @@
 
     @pl.when(to == 0)
     def _():
-        copies = loads()
-        for s in range(2):
-            copies[4 + s].wait()
-            out_mat[:, s * w:(s + 1) * w] = vo_side[s, :, sides[1]:sides[1] + w]
+        loads()[2].wait()
 
     half = att_steps // 2
 
@@ -761,7 +891,7 @@
 
     @pl.when(last == 0)
     def _():
-        loads()[6].wait()
+        loads()[3].wait()
 
     @pl.when(last >= 0)
     def _():
@@ -776,43 +906,35 @@
             out[:, 3 * w:] = jnp.zeros((bd, out.shape[1] - 3 * w), BF16)
 
 
-def mlp_back(g, mid, pre, gain, att, vo, un, width, call):
+def mlp_back(g, mid, pre, gain, att, mats, width, call):
     rows, d = g.shape
     ff = pre.shape[1]
-    w2 = plain(un)[0].shape[-1]
+    w2 = att.shape[0]
     w = w2 // 2
     bt, bd, ba = 256, 256, 512
     steps = (rows // bt, d // bd, 2 * rows // ba, d // bd)
-    starts = [sum(steps[:n]) for n in range(4)]
-    low = w // 128 * 128
-    sides = (low, w - low)
-
-    def at(n, make):
-        return lambda i: make(jnp.clip(i - starts[n], 0, steps[n] - 1))
-
+    at = stages(steps)
     row = pl.BlockSpec((bt, d), at(0, lambda k: (k, 0)))
     wide = pl.BlockSpec((bt, ff), at(0, lambda k: (k, 0)))
     block = pl.BlockSpec((bd, width), at(3, lambda k: (k, 0)))
-    any_spec = pl.BlockSpec(memory_space=pl.ANY)
-    index = tuple(a[1] if isinstance(a, tuple) else None for a in (*vo, *un))
     slots = steps[0] + 2 * steps[1]
     return pl.pallas_call(
-        functools.partial(mlp_back_kernel, w, sides, steps, index),
+        functools.partial(mlp_back_kernel, w, steps),
         grid=(sum(steps),),
-        in_specs=[row, row, wide, fixed((1, d))] + [any_spec] * 7,
+        in_specs=[row, row, wide, fixed((1, d))] + [ANY] * 4,
         out_specs=[row, fixed((8, d)), pl.BlockSpec((w2, ba), at(2, lambda k: (0, k))), block, block],
         out_shape=[shape_of((rows, d), F32), shape_of((8, d), F32), shape_of((w2, 2 * rows))] + [shape_of((d, width))] * 2,
         scratch_shapes=[pltpu.VMEM((d, ff), BF16)] * 2
         + [pltpu.VMEM((d, w2), BF16)]
         + [pltpu.VMEM((rows, d), BF16), pltpu.VMEM((rows, ff), BF16)] * 2
         + [pltpu.VMEM((rows, d), BF16)] * 2
-        + [pltpu.VMEM((4, d, w2), BF16), pltpu.VMEM((2, d, w2), BF16), pltpu.VMEM((2, d, w2 - low), BF16)]
+        + [pltpu.VMEM((4, d, w2), BF16), pltpu.VMEM((2, d, w2), BF16)]
         + [pltpu.VMEM(att.shape, BF16)]
-        + [pltpu.SemaphoreType.DMA((7,)), pltpu.SemaphoreType.DMA((slots,)), pltpu.SemaphoreType.DMA((slots,))],
+        + [pltpu.SemaphoreType.DMA((4,)), pltpu.SemaphoreType.DMA((slots,)), pltpu.SemaphoreType.DMA((slots,))],
         compiler_params=pltpu.CompilerParams(vmem_limit_bytes=62 * 2**20, collective_id=call, has_side_effects=True),
         cost_estimate=cost(8 * rows * d * ff + 8 * rows * d * w2, 40 * rows * d),
         name="mlp_back",
-    )(g, mid, pre, gain, att, *plain(vo), *plain(un))
+    )(g, mid, pre, gain, att, *mats)
 
 
 def weight_grad_kernel(w, own_ref, other_ref, dq_ref, dk_ref, dv_ref, *refs):
@@ -974,44 +1096,39 @@
     def both(rows):
         return rows, plan.across(rows)
 
-    def four(pair):
-        return (*pair, plan.core(pair[0]), plan.core(pair[1]))
-
     def stacked(rows):
         return (rows, 0), (rows, 1)
 
-    shards = jnp.stack([pairs[1, 1:], plan.across(pairs[1, 1:])], axis=1)
     un0_rows, qk1_rows = along(0, 2), along(1, 0)
-    vo1_rows, un1_rows = (lax.all_gather(shards[m], "fsdp", axis=1, tiled=True) for m in range(2))
     x = plan.order(plan.pick(inputs, plan.seq), other.astype(F32))
-    h = (x * inverse_rms(x) * norm_gain[0, 0]).astype(BF16)
-    h, un0_rows, qk1_rows, cotangent = after(h, un0_rows, qk1_rows, cotangent)
-    un0 = both(un0_rows)
+    x, un0_rows, cotangent, shards = after(x, un0_rows, cotangent, pairs[1, 1:])
+    shards_got, un0 = plan.across(shards), both(un0_rows)
     cot_block = plan.pick(cotangent, 1 - plan.seq).astype(BF16)
     kept, weights = [], []
     for l in range(layers):
         qk, vo = (qk0, vo0) if l == 0 else (qk1, vo1)
         scale = jnp.tile(factors[l] * LOG2E, 2 * w // dh)[:, None]
-        h_other = plan.core(h)
-        qkv = project(h, qk, vo, scale, 0)
-        q, k, v = project(h_other, qk, vo, scale, 1, qkv)
+        h, h_other, q, k, v = project(x, norm_gain[l, 0][None], qk, vo, scale, 3 + l)
+        if l == 0:
+            q, shards_got, qk1_rows = after(q, shards_got, qk1_rows)
+            shards = jnp.stack([shards, shards_got], axis=1)
+            vo1_rows, un1_rows = (lax.all_gather(shards[m], "fsdp", axis=1, tiled=True) for m in range(2))
+            qk1 = both(qk1_rows)
         att, lse = attention_forward(q, k, v, prefix, order, dh)
         if l == 0:
-            att, un0_got, qk1_rows = after(att, un0[1], qk1_rows)
-            un, qk1 = four((un0[0], un0_got)), both(qk1_rows)
+            att, un0_got = after(att, un0[1])
+            un = un0[0], un0_got
         else:
             att, un1_rows, cot_got = after(att, un1_rows, cot_got)
-            un = (*stacked(un1_rows), *stacked(plan.core(un1_rows)))
-        part = plan.core(out_project(att, vo, 1))
-        next_gain = norm_gain[(l + 1) % layers, 0][None]
-        mid, pre, res, h_next = middle_call(x, att, part, norm_gain[l, 1][None], next_gain, vo, un)
+            un = stacked(un1_rows)
+        mid, pre, res, *mats = middle_call(x, att, norm_gain[l, 1][None], vo, un, 5 + l)
         if l == 0:
-            h_next, qk1_got, vo1_rows, cot_block = after(h_next, qk1[1], vo1_rows, cot_block)
+            res, qk1_got, vo1_rows, cot_block = after(res, qk1[1], vo1_rows, cot_block)
             qk1, vo1 = (qk1[0], qk1_got), stacked(vo1_rows)
             cot_got = plan.across(cot_block)
         kept.append((x, h, h_other, q, k, v, att, lse, mid, pre))
-        weights.append((qk, vo, un))
-        x, h = res, h_next
+        weights.append((qk, vo, mats))
+        x = res
     g = plan.order(plan.pick(cotangent, plan.seq), cot_got.astype(F32))
     out_blocks = x.reshape(seqs, positions, d)
     out_send = plan.pick(out_blocks, 1 - plan.seq).astype(BF16)
@@ -1021,9 +1138,9 @@
     width = -(-3 * w // 128) * 128
     grads = [None] * layers
     for l in reversed(range(layers)):
-        qk, vo, un = weights[l]
+        qk, vo, mats = weights[l]
         x, h, h_other, q, k, v, att, lse, mid, pre = kept[l]
-        g_mid, gain_m, g_att, *early = mlp_back(g, mid, pre, norm_gain[l, 1][None], att, vo, un, width, 1 + l)
+        g_mid, gain_m, g_att, *early = mlp_back(g, mid, pre, norm_gain[l, 1][None], att, mats, width, 1 + l)
         early = [early[1], early[0]]
         if outputs is None:
             g_att, out_got = after(g_att, out_got)

time: 804 us -> 772 us (0.960)
  waiting for transfers between devices: 82.6 us -> 65.7 us
  Pallas kernels: 608 us -> 597 us
    ppermute x10, waiting for transfers between devices: 56 us -> 43.1 us  [across(): return lax.ppermute(a, 'tp', [(t, (t + self.ring) % n) for t in range(n)])]
    pallas_call x10 -> x6, Pallas kernels: 172 us -> 166 us  [the longest x2 77.3 us: mlp_back(): pl.pallas_call(functools.partial(mlp_back_kernel, w, steps), grid=(sum(st...]
  transfers between devices with their start and end apart: 32 -> 25, of which waited for: 14 -> 11; matrix products, arithmetic and copies ran while one was open for 6% -> 6% of each run, Pallas kernels for 74% -> 75%
where the time goes in v5:
time: 772 us; the launch traced here: 764 us
  Pallas kernels  597 us (77%)
  waiting for transfers between devices  65.7 us (9%)
  other arithmetic  43.9 us (6%)
  starting transfers between devices  22.7 us (3%)
  local copies, waits for them, and re-layouts  20.1 us (3%)
  between operations  15.2 us (2%)
    pallas_call x4, Pallas kernels, attention_backward(): pl.pallas_call(functools.partial(backward_kernel, pair=pair, dh=dh, bq=bq...  160 us
    pallas_call x1, Pallas kernels, gather_call(): pl.pallas_call(functools.partial(gather_kernel, pieces, pairs, outer, rin...  104 us
    pallas_call x2, Pallas kernels, mlp_back(): pl.pallas_call(functools.partial(mlp_back_kernel, w, steps), grid=(sum(st...  77.3 us
    pallas_call x2, Pallas kernels, attention_forward(): pl.pallas_call(functools.partial(forward_kernel, pair=pair, dh=dh, bq=bq,...  67 us
    pallas_call x2, Pallas kernels, middle_call(): pl.pallas_call(functools.partial(middle_kernel, w, low, steps, stack_inde...  50 us
    pallas_call x4, Pallas kernels, weight_grad(): pl.pallas_call(functools.partial(weight_grad_kernel, w), grid=(d // bd,),...  43.3 us
    ppermute x10, waiting for transfers between devices, across(): return lax.ppermute(a, 'tp', [(t, (t + self.ring) % n) for t in range(n)])  43.1 us
    pallas_call x2, Pallas kernels, project(): pl.pallas_call(functools.partial(project_kernel, w, low, steps, stack_ind...  39 us
  transfers between devices with their start and end apart: 25, of which 11 were waited for; matrix products, arithmetic and copies ran while one was open for 6% of the time, Pallas kernels for 75%

profile of v5, /device:TPU:0, one launch (start us, length us, event | category | flops | bytes accessed | tf_op | source)
XLA Modules:
  0.0 764.2 jit_solution(17118122650748551267)
XLA Ops:
  7.3 1.9 fusion.18
  9.2 1.3 slice_bitcast_fusion.2
  14.0 2.9 fusion.block_ref
  16.9 103.9 %gather_weights.1 = (bf16[4,2,160,640]{3,2,1,0:T(8,128)(2,1)}, bf16[4,2,160,640]{3,2,1,0:T(8,128)(2,1)}, bf16[4,2,160,640]{3,2,1,0:T(8,128)(2,1)}, bf16[4,2,160,640]{3,2,1,0:T(8,128)(2,1)}, bf16[512,1280]{1,0:T(8,128)(2,1)}) custom-call(bf16[2,160,640]{2,1,0:T(8,128)(2,1)} %get-tuple-element.265.shard_ref, bf16[512,1280]{1,0:T(8,128)(2,1)} %fusion.block_ref), custom_call_target="tpu_custom_call" | custom-call | tf_op jit(solution)/shard_map/gather_weights/pallas_call | solution.py:339
  120.9 2.5 convert_select_fusion.7
  123.4 2.7 pad_maximum_fusion.x_ref.refs_7_
  126.7 5.0 collective-permute-start
  131.7 19.3 %project.2 = (bf16[1024,1280]{1,0:T(8,128)(2,1)}, bf16[1024,1280]{1,0:T(8,128)(2,1)}, bf16[640,2048]{1,0:T(8,128)(2,1)}, bf16[640,2048]{1,0:T(8,128)(2,1)}, bf16[640,2048]{1,0:T(8,128)(2,1)}) custom-call(f32[1024,1280]{1,0:T(8,128)} %pad_maximum_fusion.x_ref.refs_7_, f32[1,1280]{1,0:T(1,128)} %get-tuple-element.269.gain_ref.refs_9_, ...), custom_call_target="tpu_custom_call" | custom-call | flops 10066329600 | bytes 15728640 | tf_op jit(solution)/shard_map/project/pallas_call | solution.py:664
  151.0 1.0 pad_maximum_fusion.9
  154.9 1.9 fusion.1
  156.8 2.0 collective-permute-start.2
  158.8 33.7 %attention_forward.2 = (bf16[640,2048]{1,0:T(8,128)(2,1)}, f32[8,1,2048]{2,1,0:T(1,128)}) custom-call(s32[1]{0:T(128)} %dynamic_slice.30.prefix_ref, s32[4]{0:T(128)} %fusion.22.order_ref, bf16[640,2048]{1,0:T(8,128)(2,1)} %get-tuple-element.126.q_ref, bf16[640,2048]{1,0:T(8,128)(2,1)} %get-tuple-element.127.k_ref, bf16[640,2048]{1,0:T(8,128)(2,1)} %get-tuple-element.128.v_ref), custom_call_target="tpu_custom_call" | custom-call | flops 20132659200 | bytes 10485760 | tf_op jit(solution)/shard_map/attention_forward/pallas_call | solution.py:95
  192.6 1.3 collective-permute-done.1.refs_3_
  193.8 24.9 %middle.2 = (f32[1024,1280]{1,0:T(8,128)}, f32[1024,1280]{1,0:T(8,128)}, f32[1024,1280]{1,0:T(8,128)}, bf16[1280,1280]{1,0:T(8,128)(2,1)}, bf16[1280,1280]{1,0:T(8,128)(2,1)}, /*index=5*/bf16[1280,640]{1,0:T(8,128)(2,1)}) custom-call(f32[1024,1280]{1,0:T(8,128)} %pad_maximum_fusion.x_ref.refs_7_, f32[1,1280]{1,0:T(1,128)} %get-tuple-element.270.gm_ref, ...), custom_call_target="tpu_custom_call" | custom-call | flops 10066329600 | bytes 39321600 | tf_op jit(solution)/shard_map/middle/pallas_call | solution.py:780
  218.8 8.4 %collective-permute-done.2.refs_1_.refs_7_.refs_11_ = bf16[1280,640]{1,0:T(8,128)(2,1)} collective-permute-done((bf16[1280,640]{1,0:T(8,128)(2,1)S(1)}, bf16[1280,640]{1,0:T(8,128)(2,1)}, u32[]{:S(2)}, u32[]{:S(2)}) %collective-permute-start.2) | collective-permute-done | bytes 1638432 | tf_op jit(solution)/shard_map/ppermute | solution.py:367
  227.4 19.8 %project.3 = (bf16[1024,1280]{1,0:T(8,128)(2,1)}, bf16[1024,1280]{1,0:T(8,128)(2,1)}, bf16[640,2048]{1,0:T(8,128)(2,1)}, bf16[640,2048]{1,0:T(8,128)(2,1)}, bf16[640,2048]{1,0:T(8,128)(2,1)}) custom-call(f32[1024,1280]{1,0:T(8,128)} %get-tuple-element.137.x_ref.refs_7_, f32[1,1280]{1,0:T(1,128)} %get-tuple-element.271.gain_ref.refs_9_, ...), custom_call_target="tpu_custom_call" | custom-call | flops 10066329600 | bytes 15728640 | tf_op jit(solution)/shard_map/project/pallas_call | solution.py:664
  247.2 33.3 %attention_forward.3 = (bf16[640,2048]{1,0:T(8,128)(2,1)}, f32[8,1,2048]{2,1,0:T(1,128)}) custom-call(s32[1]{0:T(128)} %dynamic_slice.30.prefix_ref, s32[4]{0:T(128)} %fusion.22.order_ref, bf16[640,2048]{1,0:T(8,128)(2,1)} %get-tuple-element.140.q_ref, bf16[640,2048]{1,0:T(8,128)(2,1)} %get-tuple-element.141.k_ref, bf16[640,2048]{1,0:T(8,128)(2,1)} %get-tuple-element.142.v_ref), custom_call_target="tpu_custom_call" | custom-call | flops 20132659200 | bytes 10485760 | tf_op jit(solution)/shard_map/attention_forward/pallas_call | solution.py:95
  280.5 25.0 %middle.3 = (f32[1024,1280]{1,0:T(8,128)}, f32[1024,1280]{1,0:T(8,128)}, f32[1024,1280]{1,0:T(8,128)}, bf16[1280,1280]{1,0:T(8,128)(2,1)}, bf16[1280,1280]{1,0:T(8,128)(2,1)}, /*index=5*/bf16[1280,640]{1,0:T(8,128)(2,1)}) custom-call(f32[1024,1280]{1,0:T(8,128)} %get-tuple-element.137.x_ref.refs_7_, f32[1,1280]{1,0:T(1,128)} %get-tuple-element.268.gm_ref, ...), custom_call_target="tpu_custom_call" | custom-call | flops 10066329600 | bytes 39321600 | tf_op jit(solution)/shard_map/middle/pallas_call | solution.py:780
  305.5 2.9 fusion.2
  308.4 2.1 convert_select_fusion.5
  310.6 2.7 pad_maximum_fusion.1.g_ref
  313.3 1.8 collective-permute-start.4
  315.0 38.5 %mlp_back.2 = (f32[1024,1280]{1,0:T(8,128)}, f32[8,1280]{1,0:T(8,128)}, bf16[640,2048]{1,0:T(8,128)(2,1)}, bf16[1280,1024]{1,0:T(8,128)(2,1)}, bf16[1280,1024]{1,0:T(8,128)(2,1)}) custom-call(f32[1024,1280]{1,0:T(8,128)} %pad_maximum_fusion.1.g_ref, f32[1024,1280]{1,0:T(8,128)} %get-tuple-element.150.mid_ref, f32[1024,1280]{1,0:T(8,128)} %get-tuple-element.151.pre_ref, ...), custom_call_target="tpu_custom_call" | custom-call | flops 20132659200 | bytes 52428800 | tf_op jit(solution)/shard_map/mlp_back/pallas_call | solution.py:921
  353.9 40.1 %attention_backward.4 = (bf16[320,2048]{1,0:T(8,128)(2,1)}, bf16[320,2048]{1,0:T(8,128)(2,1)}, bf16[320,2048]{1,0:T(8,128)(2,1)}, f32[80,128]{1,0:T(8,128)}) custom-call(s32[1]{0:T(128)} %dynamic_slice.30.prefix_ref, s32[4]{0:T(128)} %fusion.22.order_ref, bf16[640,2048]{1,0:T(8,128)(2,1)} %get-tuple-element.140.q_ref, ...), custom_call_target="tpu_custom_call" | custom-call | flops 26843545600 | bytes 10485760 | tf_op jit(solution)/shard_map/attention_backward/pallas_call | solution.py:205
  394.0 10.8 %weight_grad.4 = bf16[1280,1024]{1,0:T(8,128)(2,1)} custom-call(bf16[1024,1280]{1,0:T(8,128)(2,1)} %get-tuple-element.162.own_ref, bf16[1024,1280]{1,0:T(8,128)(2,1)} %get-tuple-element.163.other_ref, bf16[320,2048]{1,0:T(8,128)(2,1)} %get-tuple-element.165.dq_ref.refs_3_, bf16[320,2048]{1,0:T(8,128)(2,1)} %get-tuple-element.166.dk_ref.refs_4_, ...), custom_call_target="tpu_custom_call" | custom-call | flops 5033164800 | bytes 15728640 | tf_op jit(solution)/shard_map/weight_grad/pallas_call | solution.py:963
  404.8 8.0 %collective-permute-done.5 = bf16[1280,1024]{1,0:T(8,128)(2,1)} collective-permute-done((bf16[1280,1024]{1,0:T(8,128)(2,1)}, bf16[1280,1024]{1,0:T(8,128)(2,1)}, u32[]{:S(2)}, u32[]{:S(2)}) %collective-permute-start.5) | collective-permute-done | bytes 2621472 | tf_op jit(solution)/shard_map/ppermute | solution.py:367
  412.8 4.4 add_convert_fusion.1
  417.6 40.1 %attention_backward.5 = (bf16[320,2048]{1,0:T(8,128)(2,1)}, bf16[320,2048]{1,0:T(8,128)(2,1)}, bf16[320,2048]{1,0:T(8,128)(2,1)}, f32[80,128]{1,0:T(8,128)}) custom-call(s32[1]{0:T(128)} %dynamic_slice.30.prefix_ref, s32[4]{0:T(128)} %fusion.22.order_ref, bf16[640,2048]{1,0:T(8,128)(2,1)} %get-tuple-element.140.q_ref, ...), custom_call_target="tpu_custom_call" | custom-call | flops 26843545600 | bytes 10485760 | tf_op jit(solution)/shard_map/attention_backward/pallas_call | solution.py:205
  457.7 12.2 %input_other.2 = bf16[1024,1280]{1,0:T(8,128)(2,1)} custom-call(bf16[320,2048]{1,0:T(8,128)(2,1)} %get-tuple-element.176.refs_0_.dq_ref, bf16[320,2048]{1,0:T(8,128)(2,1)} %get-tuple-element.178.refs_1_.dk_ref, bf16[320,2048]{1,0:T(8,128)(2,1)} %get-tuple-element.174.refs_2_.dv_ref, bf16[320,2048]{1,0:T(8,128)(2,1)} %get-tuple-element.165.dq_ref.refs_3_, ...), custom_call_target="tpu_custom_call" | custom-call | flops 5033164800 | bytes 10485760 | tf_op jit(solution)/shard_map/input_other/pallas_call | solution.py:997
  469.9 5.7 collective-permute-done.6.refs_0_
  476.4 10.9 %weight_grad.5 = bf16[1280,1024]{1,0:T(8,128)(2,1)} custom-call(bf16[1024,1280]{1,0:T(8,128)(2,1)} %get-tuple-element.162.own_ref, bf16[1024,1280]{1,0:T(8,128)(2,1)} %get-tuple-element.163.other_ref, bf16[320,2048]{1,0:T(8,128)(2,1)} %get-tuple-element.176.refs_0_.dq_ref, bf16[320,2048]{1,0:T(8,128)(2,1)} %get-tuple-element.178.refs_1_.dk_ref, ...), custom_call_target="tpu_custom_call" | custom-call | flops 5033164800 | bytes 15728640 | tf_op jit(solution)/shard_map/weight_grad/pallas_call | solution.py:963
  487.4 2.2 reduce-scatter.5.cloned.1.call-done
  489.6 1.0 convert_element_type.74
  490.7 1.4 copy-done.1
  492.1 15.5 %input_own.2 = (f32[1024,1280]{1,0:T(8,128)}, f32[8,1280]{1,0:T(8,128)}) custom-call(bf16[320,2048]{1,0:T(8,128)(2,1)} %get-tuple-element.176.refs_0_.dq_ref, bf16[320,2048]{1,0:T(8,128)(2,1)} %get-tuple-element.178.refs_1_.dk_ref, bf16[320,2048]{1,0:T(8,128)(2,1)} %get-tuple-element.174.refs_2_.dv_ref, bf16[320,2048]{1,0:T(8,128)(2,1)} %get-tuple-element.165.dq_ref.refs_3_, ...), custom_call_target="tpu_custom_call" | custom-call | flops 5033164800 | bytes 31457280 | tf_op jit(solution)/shard_map/input_own/pallas_call | solution.py:1033
  507.6 38.8 %mlp_back.3 = (f32[1024,1280]{1,0:T(8,128)}, f32[8,1280]{1,0:T(8,128)}, bf16[640,2048]{1,0:T(8,128)(2,1)}, bf16[1280,1024]{1,0:T(8,128)(2,1)}, bf16[1280,1024]{1,0:T(8,128)(2,1)}) custom-call(f32[1024,1280]{1,0:T(8,128)} %get-tuple-element.183.g_ref, f32[1024,1280]{1,0:T(8,128)} %get-tuple-element.184.mid_ref, f32[1024,1280]{1,0:T(8,128)} %get-tuple-element.185.pre_ref, ...), custom_call_target="tpu_custom_call" | custom-call | flops 20132659200 | bytes 52428800 | tf_op jit(solution)/shard_map/mlp_back/pallas_call | solution.py:921
  546.4 1.6 collective-permute-start.8
  548.0 40.1 %attention_backward.6 = (bf16[320,2048]{1,0:T(8,128)(2,1)}, bf16[320,2048]{1,0:T(8,128)(2,1)}, bf16[320,2048]{1,0:T(8,128)(2,1)}, f32[80,128]{1,0:T(8,128)}) custom-call(s32[1]{0:T(128)} %dynamic_slice.30.prefix_ref, s32[4]{0:T(128)} %fusion.22.order_ref, bf16[640,2048]{1,0:T(8,128)(2,1)} %get-tuple-element.126.q_ref, ...), custom_call_target="tpu_custom_call" | custom-call | flops 26843545600 | bytes 10485760 | tf_op jit(solution)/shard_map/attention_backward/pallas_call | solution.py:205
  588.1 10.6 %weight_grad.6 = bf16[1280,1024]{1,0:T(8,128)(2,1)} custom-call(bf16[1024,1280]{1,0:T(8,128)(2,1)} %get-tuple-element.193.own_ref, bf16[1024,1280]{1,0:T(8,128)(2,1)} %get-tuple-element.194.other_ref, bf16[320,2048]{1,0:T(8,128)(2,1)} %get-tuple-element.196.dq_ref.refs_3_, bf16[320,2048]{1,0:T(8,128)(2,1)} %get-tuple-element.197.dk_ref.refs_4_, ...), custom_call_target="tpu_custom_call" | custom-call | flops 5033164800 | bytes 15728640 | tf_op jit(solution)/shard_map/weight_grad/pallas_call | solution.py:963
  598.7 5.8 collective-permute-done.8
  604.5 4.4 add_convert_fusion
  609.0 1.5 collective-permute-start.9
  610.6 40.1 %attention_backward.7 = (bf16[320,2048]{1,0:T(8,128)(2,1)}, bf16[320,2048]{1,0:T(8,128)(2,1)}, bf16[320,2048]{1,0:T(8,128)(2,1)}, f32[80,128]{1,0:T(8,128)}) custom-call(s32[1]{0:T(128)} %dynamic_slice.30.prefix_ref, s32[4]{0:T(128)} %fusion.22.order_ref, bf16[640,2048]{1,0:T(8,128)(2,1)} %get-tuple-element.126.q_ref, ...), custom_call_target="tpu_custom_call" | custom-call | flops 26843545600 | bytes 10485760 | tf_op jit(solution)/shard_map/attention_backward/pallas_call | solution.py:205
  650.7 1.9 convert_element_type.78
  652.7 12.2 %input_other.3 = bf16[1024,1280]{1,0:T(8,128)(2,1)} custom-call(bf16[320,2048]{1,0:T(8,128)(2,1)} %get-tuple-element.209.refs_0_.dq_ref, bf16[320,2048]{1,0:T(8,128)(2,1)} %get-tuple-element.211.refs_1_.dk_ref, bf16[320,2048]{1,0:T(8,128)(2,1)} %get-tuple-element.207.refs_2_.dv_ref, bf16[320,2048]{1,0:T(8,128)(2,1)} %get-tuple-element.196.dq_ref.refs_3_, ...), custom_call_target="tpu_custom_call" | custom-call | flops 5033164800 | bytes 10485760 | tf_op jit(solution)/shard_map/input_other/pallas_call | solution.py:997
  664.8 1.2 collective-permute-done.9.refs_0_
  667.3 10.9 %weight_grad.7 = bf16[1280,1024]{1,0:T(8,128)(2,1)} custom-call(bf16[1024,1280]{1,0:T(8,128)(2,1)} %get-tuple-element.193.own_ref, bf16[1024,1280]{1,0:T(8,128)(2,1)} %get-tuple-element.194.other_ref, bf16[320,2048]{1,0:T(8,128)(2,1)} %get-tuple-element.209.refs_0_.dq_ref, bf16[320,2048]{1,0:T(8,128)(2,1)} %get-tuple-element.211.refs_1_.dk_ref, ...), custom_call_target="tpu_custom_call" | custom-call | flops 5033164800 | bytes 15728640 | tf_op jit(solution)/shard_map/weight_grad/pallas_call | solution.py:963
  678.2 1.5 copy-done.2
  679.7 15.8 %input_own.3 = (f32[1024,1280]{1,0:T(8,128)}, f32[8,1280]{1,0:T(8,128)}) custom-call(bf16[320,2048]{1,0:T(8,128)(2,1)} %get-tuple-element.209.refs_0_.dq_ref, bf16[320,2048]{1,0:T(8,128)(2,1)} %get-tuple-element.211.refs_1_.dk_ref, bf16[320,2048]{1,0:T(8,128)(2,1)} %get-tuple-element.207.refs_2_.dv_ref, bf16[320,2048]{1,0:T(8,128)(2,1)} %get-tuple-element.196.dq_ref.refs_3_, ...), custom_call_target="tpu_custom_call" | custom-call | flops 5033164800 | bytes 31457280 | tf_op jit(solution)/shard_map/input_own/pallas_call | solution.py:1033
  696.9 2.5 convert_select_fusion.3
  699.5 1.7 collective-permute-start.13
  701.2 1.9 fusion.3
  703.6 2.1 collective-permute-start.14
  705.7 2.7 pad_maximum_fusion.2
  708.4 4.7 collective-permute-start.15
  713.1 1.0 bitcast_convert_fusion
  715.0 1.2 fusion.11
  716.3 3.4 collective-permute-done.16
  720.9 12.7 %collective-permute-done.11 = bf16[512,1280]{1,0:T(8,128)(2,1)S(1)} collective-permute-done((bf16[512,1280]{1,0:T(8,128)(2,1)S(1)}, bf16[512,1280]{1,0:T(8,128)(2,1)S(1)}, u32[]{:S(2)}, u32[]{:S(2)}) %collective-permute-start.11) | collective-permute-done | bytes 1310752 | tf_op jit(solution)/shard_map/ppermute | solution.py:367
  733.6 2.1 convert_select_fusion.1
  735.7 2.7 pad_maximum_fusion.3
  738.4 15.9 %reduce-scatter.9.cloned.1.call-done = bf16[160,1024]{1,0:T(8,128)(2,1)} async-done(((bf16[1280,1024]{1,0:T(8,128)(2,1)}), bf16[160,1024]{1,0:T(8,128)(2,1)}) %reduce-scatter.9.cloned.1.call-update) | async-done | bytes 327696 | tf_op jit(solution)/shard_map/reduce_scatter | solution.py:1064
  754.3 1.0 bitcast_convert_fusion.1
  755.7 1.2 copy.37
  (120 shorter events, 14.4 us)
Async XLA Ops:
  7.2 4.2 copy-start.7
  7.2 4.2 copy-start.8
  7.2 4.3 copy-start.19
  7.2 4.8 copy-start.9
  7.2 119.5 %all-gather.9.cloned.1.call-start = ((), (), s32[]{:S(2)}) async-start(), calls=%async_computation.8 | async-start | bytes 1843200 | tf_op jit(solution)/shard_map/all_gather | solution.py:1094
  9.2 141.9 %all-gather.11.cloned.1.call-start = ((), (), s32[]{:S(2)}) async-start(), calls=%async_computation.9 | async-start | bytes 1843200 | tf_op jit(solution)/shard_map/all_gather | solution.py:1094
  11.3 215.8 %all-gather.13.cloned.1.call-start = ((), (), s32[]{:S(2)}) async-start(), calls=%async_computation.10 | async-start | bytes 3686400 | tf_op jit(solution)/shard_map/all_gather | solution.py:1115
  11.5 5.4 copy-start.17
  123.4 2.7 copy-start.16
  126.7 24.3 %collective-permute-start = (bf16[2,160,640]{2,1,0:T(8,128)(2,1)S(1)}, bf16[2,160,640]{2,1,0:T(8,128)(2,1)S(1)}, u32[]{:S(2)}, u32[]{:S(2)}) collective-permute-start(bf16[2,160,640]{2,1,0:T(8,128)(2,1)S(1)} %get-tuple-element.125), channel_id=1, source_target_pairs={{0,2},{1,3},{2,0},{3,1},{4,6},{5,7},{6,4},{7,5},{8,10},{9,11},{10,... | collective-permute-start | bytes 1228808 | tf_op jit(solution)/shard_map/ppermute | solution.py:367
  131.7 20.4 %copy-start.22 = (s32[2]{0:T(128)S(1)}, s32[2]{0:T(128)}, u32[]{:S(2)}) copy-start(s32[2]{0:T(128)} %param.17) | copy-start | bytes 28
  151.0 5.7 copy-start
  152.0 128.4 %all-gather.15.cloned.1.call-start = ((), (), s32[]{:S(2)}) async-start(), calls=%async_computation.11 | async-start | bytes 3686400 | tf_op jit(solution)/shard_map/all_gather | solution.py:1115
  154.8 39.1 %collective-permute-start.1 = (bf16[1280,640]{1,0:T(8,128)(2,1)}, bf16[1280,640]{1,0:T(8,128)(2,1)}, u32[]{:S(2)}, u32[]{:S(2)}) collective-permute-start(bf16[1280,640]{1,0:T(8,128)(2,1)} %bitcast.139), channel_id=1, source_target_pairs={{0,2},{1,3},{2,0},{3,1},{4,6},{5,7},{6,4},{7,5},{8,10},{9,11},{10,... | collective-permute-start | bytes 4915208 | tf_op jit(solution)/shard_map/ppermute | solution.py:367
  154.8 334.8 %reduce-scatter.5.cloned.1.call-start = ((), (), s32[]{:S(2)}) async-start(), calls=%async_computation.4 | async-start | bytes 2949120 | tf_op jit(solution)/shard_map/reduce_scatter | solution.py:1064
  156.8 70.3 %collective-permute-start.2 = (bf16[1280,640]{1,0:T(8,128)(2,1)S(1)}, bf16[1280,640]{1,0:T(8,128)(2,1)}, u32[]{:S(2)}, u32[]{:S(2)}) collective-permute-start(bf16[1280,640]{1,0:T(8,128)(2,1)S(1)} %bitcast.109), channel_id=1, source_target_pairs={{0,2},{1,3},{2,0},{3,1},{4,6},{5,7},{6,4},{7,5},{8,10},{9,11},{10,... | collective-permute-start | bytes 4915208 | tf_op jit(solution)/shard_map/ppermute | solution.py:367
  227.1 53.4 %collective-permute-start.3 = (bf16[512,1280]{1,0:T(8,128)(2,1)S(1)}, bf16[512,1280]{1,0:T(8,128)(2,1)S(1)}, u32[]{:S(2)}, u32[]{:S(2)}) collective-permute-start(bf16[512,1280]{1,0:T(8,128)(2,1)S(1)} %fusion.1), channel_id=1, source_target_pairs={{0,2},{1,3},{2,0},{3,1},{4,6},{5,7},{6,4},{7,5},{8,10},{9,11},{10,... | collective-permute-start | bytes 3932168 | tf_op jit(solution)/shard_map/ppermute | solution.py:367
  313.3 40.7 %collective-permute-start.4 = (bf16[512,1280]{1,0:T(8,128)(2,1)}, bf16[512,1280]{1,0:T(8,128)(2,1)S(1)}, u32[]{:S(2)}, u32[]{:S(2)}) collective-permute-start(bf16[512,1280]{1,0:T(8,128)(2,1)} %fusion.2), channel_id=1, source_target_pairs={{0,2},{1,3},{2,0},{3,1},{4,6},{5,7},{6,4},{7,5},{8,10},{9,11},{10,... | collective-permute-start | bytes 3932168 | tf_op jit(solution)/shard_map/ppermute | solution.py:367
  353.6 59.3 %collective-permute-start.5 = (bf16[1280,1024]{1,0:T(8,128)(2,1)}, bf16[1280,1024]{1,0:T(8,128)(2,1)}, u32[]{:S(2)}, u32[]{:S(2)}) collective-permute-start(bf16[1280,1024]{1,0:T(8,128)(2,1)} %get-tuple-element.168), channel_id=1, source_target_pairs={{0,2},{1,3},{2,0},{3,1},{4,6},{5,7},{6,4},{7,5},{8,10},{9,11},{10,... | collective-permute-start | bytes 7864328 | tf_op jit(solution)/shard_map/ppermute | solution.py:367
  353.9 40.1 %copy-start.6 = (bf16[512,1280]{1,0:T(8,128)(2,1)}, bf16[512,1280]{1,0:T(8,128)(2,1)S(1)}, u32[]{:S(2)}) copy-start(bf16[512,1280]{1,0:T(8,128)(2,1)S(1)} %collective-permute-done.4) | copy-start | bytes 3932164
  394.0 18.8 %copy-start.3 = (bf16[1280,1024]{1,0:T(8,128)(2,1)S(1)}, bf16[1280,1024]{1,0:T(8,128)(2,1)}, u32[]{:S(2)}) copy-start(bf16[1280,1024]{1,0:T(8,128)(2,1)} %get-tuple-element.160) | copy-start | bytes 7864324
  417.3 58.4 %collective-permute-start.6 = (bf16[1280,1024]{1,0:T(8,128)(2,1)}, bf16[1280,1024]{1,0:T(8,128)(2,1)}, u32[]{:S(2)}, u32[]{:S(2)}) collective-permute-start(bf16[1280,1024]{1,0:T(8,128)(2,1)} %weight_grad.4), channel_id=1, source_target_pairs={{0,2},{1,3},{2,0},{3,1},{4,6},{5,7},{6,4},{7,5},{8,10},{9,11},{10,... | collective-permute-start | bytes 7864328 | tf_op jit(solution)/shard_map/ppermute | solution.py:367
  417.6 233.1 %reduce-scatter.7.cloned.1.call-start = ((), (), s32[]{:S(2)}) async-start(), calls=%async_computation.5 | async-start | bytes 2949120 | tf_op jit(solution)/shard_map/reduce_scatter | solution.py:1064
  457.7 17.9 %copy-start.21 = (f32[80,1]{0,1:T(1,128)S(1)}, f32[80,1]{0,1:T(1,128)}, u32[]{:S(2)}) copy-start(f32[80,1]{0,1:T(1,128)} %get-tuple-element.274) | copy-start | bytes 964
  475.6 15.0 %collective-permute-start.7 = (bf16[1024,1280]{1,0:T(8,128)(2,1)}, bf16[1024,1280]{1,0:T(8,128)(2,1)S(1)}, u32[]{:S(2)}, u32[]{:S(2)}) collective-permute-start(bf16[1024,1280]{1,0:T(8,128)(2,1)} %input_other.2), channel_id=1, source_target_pairs={{0,1},{1,0},{2,3},{3,2},{4,5},{5,4},{6,7},{7,6},{8,9},{9,8},{10,11... | collective-permute-start | bytes 7864328 | tf_op jit(solution)/shard_map/ppermute | solution.py:370
  487.3 225.8 %reduce-scatter.11.cloned.1.call-start = ((), (), s32[]{:S(2)}) async-start(), calls=%async_computation.7 | async-start | bytes 2949120 | tf_op jit(solution)/shard_map/reduce_scatter | solution.py:1064
  490.7 1.5 copy-start.1
  546.4 58.1 %collective-permute-start.8 = (bf16[1280,1024]{1,0:T(8,128)(2,1)}, bf16[1280,1024]{1,0:T(8,128)(2,1)}, u32[]{:S(2)}, u32[]{:S(2)}) collective-permute-start(bf16[1280,1024]{1,0:T(8,128)(2,1)} %get-tuple-element.199), channel_id=1, source_target_pairs={{0,2},{1,3},{2,0},{3,1},{4,6},{5,7},{6,4},{7,5},{8,10},{9,11},{10,... | collective-permute-start | bytes 7864328 | tf_op jit(solution)/shard_map/ppermute | solution.py:367
  588.1 16.4 %copy-start.4 = (bf16[1280,1024]{1,0:T(8,128)(2,1)S(1)}, bf16[1280,1024]{1,0:T(8,128)(2,1)}, u32[]{:S(2)}) copy-start(bf16[1280,1024]{1,0:T(8,128)(2,1)} %get-tuple-element.191) | copy-start | bytes 7864324
  609.0 57.1 %collective-permute-start.9 = (bf16[1280,1024]{1,0:T(8,128)(2,1)}, bf16[1280,1024]{1,0:T(8,128)(2,1)}, u32[]{:S(2)}, u32[]{:S(2)}) collective-permute-start(bf16[1280,1024]{1,0:T(8,128)(2,1)} %weight_grad.6), channel_id=1, source_target_pairs={{0,2},{1,3},{2,0},{3,1},{4,6},{5,7},{6,4},{7,5},{8,10},{9,11},{10,... | collective-permute-start | bytes 7864328 | tf_op jit(solution)/shard_map/ppermute | solution.py:367
  610.5 143.8 %reduce-scatter.9.cloned.1.call-start = ((), (), s32[]{:S(2)}) async-start(), calls=%async_computation.6 | async-start | bytes 2949120 | tf_op jit(solution)/shard_map/reduce_scatter | solution.py:1064
  652.6 13.5 %copy-start.14 = (f32[8,1280]{1,0:T(8,128)S(1)}, f32[8,1280]{1,0:T(8,128)}, u32[]{:S(2)}) copy-start(f32[8,1280]{1,0:T(8,128)} %get-tuple-element.224) | copy-start | bytes 122884
  652.6 13.5 %copy-start.10 = (f32[80,128]{1,0:T(8,128)S(1)}, f32[80,128]{1,0:T(8,128)}, u32[]{:S(2)}) copy-start(f32[80,128]{1,0:T(8,128)} %get-tuple-element.225) | copy-start | bytes 122884
  652.6 13.5 %copy-start.11 = (f32[80,128]{1,0:T(8,128)S(1)}, f32[80,128]{1,0:T(8,128)}, u32[]{:S(2)}) copy-start(f32[80,128]{1,0:T(8,128)} %get-tuple-element.226) | copy-start | bytes 122884
  652.6 14.4 %copy-start.15 = (f32[8,1280]{1,0:T(8,128)S(1)}, f32[8,1280]{1,0:T(8,128)}, u32[]{:S(2)}) copy-start(f32[8,1280]{1,0:T(8,128)} %get-tuple-element.223) | copy-start | bytes 122884
  652.6 14.5 %copy-start.12 = (f32[80,128]{1,0:T(8,128)S(1)}, f32[80,128]{1,0:T(8,128)}, u32[]{:S(2)}) copy-start(f32[80,128]{1,0:T(8,128)} %get-tuple-element.221) | copy-start | bytes 122884
  652.6 14.5 %copy-start.13 = (f32[80,128]{1,0:T(8,128)S(1)}, f32[80,128]{1,0:T(8,128)}, u32[]{:S(2)}) copy-start(f32[80,128]{1,0:T(8,128)} %get-tuple-element.222) | copy-start | bytes 122884
  652.6 14.6 %copy-start.18 = (f32[2,80]{1,0:T(2,128)S(1)}, f32[2,80]{1,0:T(2,128)}, u32[]{:S(2)}) copy-start(f32[2,80]{1,0:T(2,128)} %copy-done.17) | copy-start | bytes 1924
  666.1 12.1 %collective-permute-start.10 = (bf16[1024,1280]{1,0:T(8,128)(2,1)}, bf16[1024,1280]{1,0:T(8,128)(2,1)S(1)}, u32[]{:S(2)}, u32[]{:S(2)}) collective-permute-start(bf16[1024,1280]{1,0:T(8,128)(2,1)} %input_other.3), channel_id=1, source_target_pairs={{0,1},{1,0},{2,3},{3,2},{4,5},{5,4},{6,7},{7,6},{8,9},{9,8},{10,11... | collective-permute-start | bytes 7864328 | tf_op jit(solution)/shard_map/ppermute | solution.py:370
  678.2 1.5 copy-start.2
  696.4 3.1 collective-permute-start.12
  699.5 4.1 collective-permute-start.13
  703.1 30.5 %collective-permute-start.11 = (bf16[512,1280]{1,0:T(8,128)(2,1)S(1)}, bf16[512,1280]{1,0:T(8,128)(2,1)S(1)}, u32[]{:S(2)}, u32[]{:S(2)}) collective-permute-start(bf16[512,1280]{1,0:T(8,128)(2,1)S(1)} %fusion.3), channel_id=1, source_target_pairs={{0,2},{1,3},{2,0},{3,1},{4,6},{5,7},{6,4},{7,5},{8,10},{9,11},{10,... | collective-permute-start | bytes 3932168 | tf_op jit(solution)/shard_map/ppermute | solution.py:367
  703.6 4.8 collective-permute-start.14
  708.4 11.3 %copy-start.20 = (f32[2,80]{1,0:T(2,128)S(1)}, f32[2,80]{1,0:T(2,128)}, u32[]{:S(2)}) copy-start(f32[2,80]{1,0:T(2,128)} %param.16) | copy-start | bytes 1924
  708.4 6.5 collective-permute-start.15
  714.9 4.8 collective-permute-start.16
  735.7 19.7 %copy-start.5 = (f32[160,1024]{1,0:T(8,128)S(1)}, f32[160,1024]{1,0:T(8,128)}, u32[]{:S(2)}) copy-start(f32[160,1024]{1,0:T(8,128)} %convert_element_type.78) | copy-start | bytes 1966084
Sparse Core Ops, SparseCore 0:
  10.8 67.1 all-gather.8
  80.7 49.7 all-gather.10
  152.2 62.9 all-gather.12
  217.7 60.5 all-gather.14
  417.7 71.8 reduce-scatter.4
  493.0 69.2 reduce-scatter.6
  610.6 70.3 reduce-scatter.10
  684.6 69.6 reduce-scatter.8

commit v6 on v5

--- a/solution.py
+++ b/solution.py
@@ -583,13 +583,37 @@
 ANY = pl.BlockSpec(memory_space=pl.ANY)
 
 
-def project_kernel(w, low, steps, index, x_ref, gain_ref, scale_ref, *refs):
+class Halves:
+    def __init__(self, own_any, got_any, own, got, load, ring):
+        self.seq = lax.axis_index("tp") // ring
+        self.own, self.got = own, got
+        self.copies = [
+            pltpu.make_async_copy(own_any.at[self.seq], own, load.at[0]),
+            pltpu.make_async_copy(got_any, got, load.at[1]),
+        ]
+
+    def rows(self, k, size):
+        per = self.own.shape[0] // size
+        here = pl.ds(pl.multiple_of(lax.rem(k, per) * size, size), size)
+        return jnp.where(k // per == self.seq, self.own[here], self.got[here].astype(F32))
+
+
+def halves_scratch(rows, d):
+    return [pltpu.VMEM((rows // 2, d), F32), pltpu.VMEM((rows // 2, d), BF16), pltpu.SemaphoreType.DMA((2,))]
+
+
+def project_kernel(w, low, steps, index, bt, ring, gain_ref, scale_ref, *refs):
     weights, refs = refs[:4], refs[4:]
-    own_ref, other_ref, q_ref, k_ref, v_ref = refs[:5]
-    own, other, qk, vo, load, send, recv = refs[5:]
+    if ring:
+        own_any, got_any, own_ref, other_ref, q_ref, k_ref, v_ref, x_out = refs[:8]
+        own, other, qk, vo, load, send, recv, *rest = refs[8:]
+        halves = Halves(own_any, got_any, *rest, ring)
+    else:
+        x_ref, own_ref, other_ref, q_ref, k_ref, v_ref = refs[:6]
+        own, other, qk, vo, load, send, recv = refs[6:]
     i = pl.program_id(0)
     rows_steps, half, _ = steps
-    bt, ba = x_ref.shape[0], q_ref.shape[1]
+    ba = q_ref.shape[1]
     core = core_of()
     push = pushes(send, recv, core)
 
@@ -606,13 +630,23 @@
 
     @pl.when(i == 0)
     def _():
+        if ring:
+            for c in halves.copies:
+                c.start()
         for c in loads():
             c.start()
         greet(core)
+        if ring:
+            for c in halves.copies:
+                c.wait()
 
     @pl.when(i < rows_steps)
     def _():
-        x = x_ref[...]
+        if ring:
+            x = halves.rows(i, bt)
+            x_out[...] = x
+        else:
+            x = x_ref[...]
         h = (x * inverse_rms(x) * gain_ref[...]).astype(BF16)
         own[pl.ds(pl.multiple_of(i * bt, bt), bt)] = h
         own_ref[...] = h
@@ -649,8 +683,10 @@
         project(h)
 
 
-def project(x, gain, qk, vo, scale, call):
-    rows, d = x.shape
+def project(x, gain, qk, vo, scale, call, ring=0):
+    xs = x if ring else (x,)
+    d = xs[0].shape[-1]
+    rows = 2 * xs[1].shape[0] if ring else x.shape[0]
     w2 = plain(qk)[0].shape[-1]
     w = w2 // 2
     low = -(-w // 128) * 128
@@ -662,20 +698,21 @@
     tall = pl.BlockSpec((ba, d), lambda i: (jnp.clip(i - steps[0] - half, 0, half - 1), 0))
     weights = (*qk, *vo)
     return pl.pallas_call(
-        functools.partial(project_kernel, w, low, steps, stack_index(weights)),
+        functools.partial(project_kernel, w, low, steps, stack_index(weights), bt, ring),
         grid=(sum(steps),),
-        in_specs=[row, fixed((1, d)), fixed((w2, 1))] + [ANY] * 4,
-        out_specs=[row, tall] + [wide] * 3,
-        out_shape=[shape_of((rows, d))] * 2 + [shape_of((w2, 2 * rows))] * 3,
+        in_specs=[fixed((1, d)), fixed((w2, 1))] + [ANY] * 4 + ([ANY] * 2 if ring else [row]),
+        out_specs=[row, tall] + [wide] * 3 + ([row] if ring else []),
+        out_shape=[shape_of((rows, d))] * 2 + [shape_of((w2, 2 * rows))] * 3 + ([shape_of((rows, d), F32)] if ring else []),
         scratch_shapes=[
             pltpu.VMEM((rows, d), BF16), pltpu.VMEM((rows, d), BF16),
             pltpu.VMEM((2, d, w2), BF16), pltpu.VMEM((2, d, low), BF16),
             pltpu.SemaphoreType.DMA((4,)), pltpu.SemaphoreType.DMA((steps[0],)), pltpu.SemaphoreType.DMA((steps[0],)),
-        ],
+        ]
+        + (halves_scratch(rows, d) if ring else []),
         compiler_params=pltpu.CompilerParams(vmem_limit_bytes=VMEM_LIMIT, collective_id=call, has_side_effects=True),
         cost_estimate=cost(4 * rows * d * 3 * w2, 12 * rows * d),
         name="project",
-    )(x, gain, scale, *plain(weights))
+    )(gain, scale, *plain(weights), *xs)
 
 
 def middle_kernel(w, low, steps, index, x_ref, gm_ref, att_any, *refs):
@@ -793,14 +830,20 @@
     )(x, gain_m, att, *plain(weights))
 
 
-def mlp_back_kernel(w, steps, g_ref, mid_ref, pre_ref, gm_ref, att_any, *refs):
+def mlp_back_kernel(w, steps, ring, mid_ref, pre_ref, gm_ref, att_any, *refs):
     mats, refs = refs[:3], refs[3:]
+    if ring:
+        own_any, got_any, refs = refs[0], refs[1], refs[2:]
+        halves = Halves(own_any, got_any, *refs[-3:], ring)
+        refs = refs[:-3]
+    else:
+        g_ref, refs = refs[0], refs[1:]
     g_mid_ref, gain_ref, g_att_ref, o0, o1 = refs[:5]
     (up_mat, down_mat, out_mat, g_all, hid_all, hm_all, gpre_all, low_own, low_other, blocks, got, att,
      load, send, recv) = refs[5:]
     i = pl.program_id(0)
     rows_steps, grad_steps, att_steps, _ = steps
-    bt, bd, ba = g_ref.shape[0], o0.shape[0], g_att_ref.shape[1]
+    bt, bd, ba = mid_ref.shape[0], o0.shape[0], g_att_ref.shape[1]
     core = core_of()
     push = pushes(send, recv, core)
 
@@ -822,14 +865,17 @@
         for c in copies:
             c.start()
         gain_ref[...] = jnp.zeros_like(gain_ref)
+        if ring:
+            for c in halves.copies:
+                c.start()
         greet(core)
-        for c in copies[:2]:
+        for c in copies[:2] + (halves.copies if ring else []):
             c.wait()
 
     @pl.when(i < rows_steps)
     def _():
         here = pl.ds(pl.multiple_of(i * bt, bt), bt)
-        g = g_ref[...]
+        g = halves.rows(i, bt) if ring else g_ref[...]
         g_low = g.astype(BF16)
         g_all[here] = g_low
         pre = pre_ref[...]
@@ -906,8 +952,9 @@
             out[:, 3 * w:] = jnp.zeros((bd, out.shape[1] - 3 * w), BF16)
 
 
-def mlp_back(g, mid, pre, gain, att, mats, width, call):
-    rows, d = g.shape
+def mlp_back(g, mid, pre, gain, att, mats, width, call, ring=0):
+    rows, d = mid.shape
+    gs = g if ring else (g,)
     ff = pre.shape[1]
     w2 = att.shape[0]
     w = w2 // 2
@@ -919,9 +966,9 @@
     block = pl.BlockSpec((bd, width), at(3, lambda k: (k, 0)))
     slots = steps[0] + 2 * steps[1]
     return pl.pallas_call(
-        functools.partial(mlp_back_kernel, w, steps),
+        functools.partial(mlp_back_kernel, w, steps, ring),
         grid=(sum(steps),),
-        in_specs=[row, row, wide, fixed((1, d))] + [ANY] * 4,
+        in_specs=[row, wide, fixed((1, d))] + [ANY] * 4 + ([ANY] * 2 if ring else [row]),
         out_specs=[row, fixed((8, d)), pl.BlockSpec((w2, ba), at(2, lambda k: (0, k))), block, block],
         out_shape=[shape_of((rows, d), F32), shape_of((8, d), F32), shape_of((w2, 2 * rows))] + [shape_of((d, width))] * 2,
         scratch_shapes=[pltpu.VMEM((d, ff), BF16)] * 2
@@ -930,11 +977,12 @@
         + [pltpu.VMEM((rows, d), BF16)] * 2
         + [pltpu.VMEM((4, d, w2), BF16), pltpu.VMEM((2, d, w2), BF16)]
         + [pltpu.VMEM(att.shape, BF16)]
-        + [pltpu.SemaphoreType.DMA((4,)), pltpu.SemaphoreType.DMA((slots,)), pltpu.SemaphoreType.DMA((slots,))],
+        + [pltpu.SemaphoreType.DMA((4,)), pltpu.SemaphoreType.DMA((slots,)), pltpu.SemaphoreType.DMA((slots,))]
+        + (halves_scratch(rows, d) if ring else []),
         compiler_params=pltpu.CompilerParams(vmem_limit_bytes=62 * 2**20, collective_id=call, has_side_effects=True),
         cost_estimate=cost(8 * rows * d * ff + 8 * rows * d * w2, 40 * rows * d),
         name="mlp_back",
-    )(g, mid, pre, gain, att, *mats)
+    )(mid, pre, gain, att, *mats, *gs)
 
 
 def weight_grad_kernel(w, own_ref, other_ref, dq_ref, dk_ref, dv_ref, *refs):
@@ -973,74 +1021,122 @@
     )(own, other, dq, dk, dv, *extra)
 
 
-def input_sum(w, grads, qk, vo):
-    total = None
-    for s in range(2):
-        dq, dk, dv = grads[3 * s:3 * s + 3]
-        both = jnp.concatenate([dq[...], dk[...]], axis=0)
-        part = dot(both, qk[s][...], TT) + dot(dv[...], vo[s][:, :w], TT)
-        total = part if total is None else total + part
-    return total
-
-
-def input_other_kernel(w, *refs):
-    refs, out_ref = refs[:-1], refs[-1]
-    out_ref[...] = input_sum(w, refs[:6], refs[6:8], refs[8:10]).astype(BF16)
-
-
-def input_other(grads, qk, vo):
+def input_back_kernel(w, low, steps, index, x_ref, g_ref, gain_ref, *refs):
+    grads, weights, refs = refs[:6], refs[6:10], refs[10:]
+    stacked, qk, vo, part, got, load, send, recv = refs[-8:]
+    i = pl.program_id(0)
+    chunk_steps, far, _ = steps
+    if chunk_steps:
+        own_ref, other_ref, out_ref, sum_ref, piece_ref = refs[:-8]
+    else:
+        out_ref, sum_ref = refs[:-8]
+    bt, half = x_ref.shape[0], part.shape[0]
+    ba = half // far
+    push = pushes(send, recv, core_of())
+
+    def loads():
+        copies = [
+            pltpu.make_async_copy(grads[n], stacked.at[n // 3, pl.ds(n % 3 * w, w)], load.at[n]) for n in range(6)
+        ]
+        for s in range(2):
+            copies.append(pltpu.make_async_copy(entry(weights[s], index[s]), qk.at[s], load.at[6 + s]))
+        for s in range(2):
+            src = entry(weights[2 + s], index[2 + s]).at[:, pl.ds(0, low)]
+            copies.append(pltpu.make_async_copy(src, vo.at[s], load.at[8 + s]))
+        return copies
+
+    def push_part(k):
+        here = pl.ds(pl.multiple_of(k * ba, ba), ba)
+        return push(part.at[here], got.at[here], k)
+
+    def total(cols):
+        parts = [
+            dot(stacked[s, :2 * w, cols], qk[s], TT) + dot(stacked[s, 2 * w:, cols], vo[s, :, :w], TT) for s in range(2)
+        ]
+        return parts[0] + parts[1]
+
+    @pl.when(i == 0)
+    def _():
+        copies = loads()
+        for c in copies:
+            c.start()
+        sum_ref[...] = jnp.zeros_like(sum_ref)
+        greet(core_of())
+        for c in copies[:3]:
+            c.wait()
+
+    if chunk_steps:
+        @pl.when(i < chunk_steps)
+        def _():
+            grad = dot(own_ref[...], stacked[0, :, :half], TT) + dot(other_ref[...], stacked[0, :, half:], TT)
+            piece_ref[:, :3 * w] = grad.astype(BF16)
+            piece_ref[:, 3 * w:] = jnp.zeros((piece_ref.shape[0], piece_ref.shape[1] - 3 * w), BF16)
+
+    to = i - chunk_steps
+
+    @pl.when(to == 0)
+    def _():
+        for c in loads()[3:]:
+            c.wait()
+
+    @pl.when((to >= 0) & (to < far))
+    def _():
+        cols = pl.ds(pl.multiple_of(half + to * ba, ba), ba)
+        part[pl.ds(pl.multiple_of(to * ba, ba), ba)] = total(cols).astype(BF16)
+        push_part(to).start()
+
+    at = to - far
+    for k in range(far):
+        @pl.when(at == k * (ba // bt))
+        def _():
+            push_part(k).wait()
+
+    @pl.when(at >= 0)
+    def _():
+        here = pl.ds(pl.multiple_of(at * bt, bt), bt)
+        g_ha = total(here) + got[here].astype(F32)
+        x = x_ref[...]
+        inv = inverse_rms(x)
+        normed = x * inv
+        sum_ref[...] += eight(g_ha * normed)
+        scaled = g_ha * gain_ref[...]
+        out_ref[...] = g_ref[...] + inv * (scaled - normed * jnp.mean(scaled * normed, axis=-1, keepdims=True))
+
+
+def input_back(grads, x, g, gain, qk, vo, call, normed=(), width=0):
     w, length = grads[0].shape
-    d, w2 = plain(qk)[0].shape[-2:]
-    bt = 512
-    steps = length // 2 // bt
-    col = pl.BlockSpec((w, bt), lambda i: (0, i + steps))
+    rows, d = x.shape
+    low = -(-w // 128) * 128
+    bt, bd, ba = 256, 256, 512
+    chunks = d // bd if normed else 0
+    steps = (chunks, rows // ba, rows // bt)
+    row = pl.BlockSpec((bt, d), lambda i: (jnp.maximum(i - steps[0] - steps[1], 0), 0))
+
+    def chunk(k):
+        return jnp.minimum(k, chunks - 1)
+
+    weights = (*qk, *vo)
+    in_specs = [row, row, fixed((1, d))] + [ANY] * 10
+    out_specs, out_shape = [row, fixed((8, d))], [shape_of((rows, d), F32), shape_of((8, d), F32)]
+    if normed:
+        in_specs += [pl.BlockSpec((rows, bd), lambda i: (0, chunk(i)))] * 2
+        out_specs.append(pl.BlockSpec((bd, width), lambda i: (chunk(i), 0)))
+        out_shape.append(shape_of((d, width)))
     return pl.pallas_call(
-        functools.partial(input_other_kernel, w),
-        grid=(steps,),
-        in_specs=[col] * 6 + [weight(a) for a in (*qk, *vo)],
-        out_specs=pl.BlockSpec((bt, d), lambda i: (i, 0)),
-        out_shape=shape_of((length // 2, d)),
-        compiler_params=params(),
-        cost_estimate=cost(3 * length * d * w2, 4 * length * d),
-        name="input_other",
-    )(*grads, *plain(qk), *plain(vo))
-
-
-def input_own_kernel(w, *refs):
-    grads, refs = refs[:6], refs[6:]
-    got_ref, x_ref, g_ref, gain_ref, qk0, qk1, vo0, vo1, out_ref, sum_ref = refs
-
-    @pl.when(pl.program_id(0) == 0)
-    def _():
-        sum_ref[...] = jnp.zeros_like(sum_ref)
-
-    g_ha = input_sum(w, grads, (qk0, qk1), (vo0, vo1)) + got_ref[...].astype(F32)
-    x = x_ref[...]
-    inv = inverse_rms(x)
-    normed = x * inv
-    sum_ref[...] += eight(g_ha * normed)
-    scaled = g_ha * gain_ref[...]
-    out_ref[...] = g_ref[...] + inv * (scaled - normed * jnp.mean(scaled * normed, axis=-1, keepdims=True))
-
-
-def input_own(grads, got, x, g, gain, qk, vo):
-    w = grads[0].shape[0]
-    rows, d = x.shape
-    w2 = 2 * w
-    bt = 256
-    col = pl.BlockSpec((w, bt), lambda i: (0, i))
-    row = pl.BlockSpec((bt, d), lambda i: (i, 0))
-    return pl.pallas_call(
-        functools.partial(input_own_kernel, w),
-        grid=(rows // bt,),
-        in_specs=[col] * 6 + [row] * 3 + [fixed((1, d))]
-        + [weight(a) for a in (*qk, *vo)],
-        out_specs=[row, fixed((8, d))],
-        out_shape=[shape_of((rows, d), F32), shape_of((8, d), F32)],
-        compiler_params=params(),
-        cost_estimate=cost(6 * rows * d * w2, 24 * rows * d),
-        name="input_own",
-    )(*grads, got, x, g, gain, *plain(qk), *plain(vo))
+        functools.partial(input_back_kernel, w, low, steps, stack_index(weights)),
+        grid=(sum(steps),),
+        in_specs=in_specs,
+        out_specs=out_specs,
+        out_shape=out_shape,
+        scratch_shapes=[
+            pltpu.VMEM((2, 3 * w, length), BF16), pltpu.VMEM((2, d, 2 * w), BF16), pltpu.VMEM((2, d, low), BF16),
+            pltpu.VMEM((rows, d), BF16), pltpu.VMEM((rows, d), BF16),
+            pltpu.SemaphoreType.DMA((10,)), pltpu.SemaphoreType.DMA((steps[1],)), pltpu.SemaphoreType.DMA((steps[1],)),
+        ],
+        compiler_params=pltpu.CompilerParams(vmem_limit_bytes=VMEM_LIMIT, collective_id=call, has_side_effects=True),
+        cost_estimate=cost(9 * rows * d * 4 * w, 24 * rows * d),
+        name="input_back",
+    )(x, g, gain, *grads, *plain(weights), *normed)
 
 
 def total_over_all(plan, a):
@@ -1061,7 +1157,7 @@
 
 
 def scatter_rows(mine):
-    return lax.psum_scatter(mine, "fsdp", scatter_dimension=0, tiled=True).astype(F32)
+    return lax.psum_scatter(mine, "fsdp", scatter_dimension=0, tiled=True)
 
 
 def after(*arrays):
@@ -1100,15 +1196,18 @@
         return (rows, 0), (rows, 1)
 
     un0_rows, qk1_rows = along(0, 2), along(1, 0)
-    x = plan.order(plan.pick(inputs, plan.seq), other.astype(F32))
-    x, un0_rows, cotangent, shards = after(x, un0_rows, cotangent, pairs[1, 1:])
+    other, un0_rows, cotangent, shards = after(other, un0_rows, cotangent, pairs[1, 1:])
     shards_got, un0 = plan.across(shards), both(un0_rows)
     cot_block = plan.pick(cotangent, 1 - plan.seq).astype(BF16)
     kept, weights = [], []
     for l in range(layers):
         qk, vo = (qk0, vo0) if l == 0 else (qk1, vo1)
         scale = jnp.tile(factors[l] * LOG2E, 2 * w // dh)[:, None]
-        h, h_other, q, k, v = project(x, norm_gain[l, 0][None], qk, vo, scale, 3 + l)
+        gain = norm_gain[l, 0][None]
+        if l == 0:
+            h, h_other, q, k, v, x = project((inputs, other), gain, qk, vo, scale, 3, plan.ring)
+        else:
+            h, h_other, q, k, v = project(x, gain, qk, vo, scale, 3 + l)
         if l == 0:
             q, shards_got, qk1_rows = after(q, shards_got, qk1_rows)
             shards = jnp.stack([shards, shards_got], axis=1)
@@ -1129,10 +1228,11 @@
         kept.append((x, h, h_other, q, k, v, att, lse, mid, pre))
         weights.append((qk, vo, mats))
         x = res
-    g = plan.order(plan.pick(cotangent, plan.seq), cot_got.astype(F32))
+    g = cotangent, cot_got
     out_blocks = x.reshape(seqs, positions, d)
     out_send = plan.pick(out_blocks, 1 - plan.seq).astype(BF16)
-    g, out_send = after(g, out_send)
+    cot_got, out_send = after(cot_got, out_send)
+    g = cotangent, cot_got
     out_got = plan.across(out_send)
     outputs = None
     width = -(-3 * w // 128) * 128
@@ -1140,45 +1240,66 @@
     for l in reversed(range(layers)):
         qk, vo, mats = weights[l]
         x, h, h_other, q, k, v, att, lse, mid, pre = kept[l]
-        g_mid, gain_m, g_att, *early = mlp_back(g, mid, pre, norm_gain[l, 1][None], att, mats, width, 1 + l)
-        early = [early[1], early[0]]
-        if outputs is None:
-            g_att, out_got = after(g_att, out_got)
-            outputs = plan.order(plan.pick(out_blocks, plan.seq), out_got.astype(F32)).reshape(out_blocks.shape)
-        early_got = plan.across(early[0])
-        g_att, early[1] = after(g_att, early[1])
+        ring = plan.ring if l == layers - 1 else 0
+        g_mid, gain_m, g_att, *early = mlp_back(g, mid, pre, norm_gain[l, 1][None], att, mats, width, 1 + l, ring)
+        if l > 0:
+            early = [scatter_rows(a) for a in early]
+        else:
+            early_got = plan.across(early[1])
+        if l + 1 < layers:
+            g_att, grads[l + 1][0][1] = after(g_att, grads[l + 1][0][1])
         dgrads, fgs, pieces = [None] * 6, [], [None] * 2
         for s in (1, 0):
             dq, dk, dv, fg = attention_backward(
                 q, k, v, att, g_att, lse, factors[l], prefix, order, dh, s * w, w
             )
-            if s == 0 and l + 1 < layers:
-                dq, upper = after(dq, grads[l + 1][1])
-                grads[l + 1] = (grads[l + 1][0], upper, grads[l + 1][2])
             if s == 1:
                 pieces[1] = weight_grad(h, h_other, dq, dk, dv, width)
-                g_att, pieces[1], early_got = after(g_att, pieces[1], early_got)
+                if outputs is None:
+                    pieces[1], out_got = after(pieces[1], out_got)
+                    outputs = plan.order(plan.pick(out_blocks, plan.seq), out_got.astype(F32)).reshape(out_blocks.shape)
+                g_att, pieces[1] = after(g_att, pieces[1])
                 late_got = plan.across(pieces[1])
-                mine, g_att = after(add_low(early[1], early_got), g_att)
-                early = scatter_rows(mine)
+                if l + 1 < layers:
+                    g_att, grads[l + 1][1] = after(g_att, grads[l + 1][1])
+                if l == 0:
+                    g_att, early_got = after(g_att, early_got)
+                    mine, g_att = after(add_low(early[0], early_got), g_att)
+                    early = scatter_rows(mine)
+            elif l > 0:
+                dq, early[0] = after(dq, early[0])
             dgrads[3 * s:3 * s + 3] = [dq, dk, dv]
             fgs.append(fg)
         fg = fgs[0] + fgs[1]
-        part = input_other(dgrads, qk, vo)
-        part, dgrads[0], late_got = after(part, dgrads[0], late_got)
-        part = plan.core(part)
-        mine, dgrads[1] = after(weight_grad(h, h_other, *dgrads[:3], width, late_got), dgrads[1])
+        back = (dgrads, x, g_mid, norm_gain[l, 0][None], qk, vo, 7 + l)
+        if l > 0:
+            g, gain_a, pieces[0] = input_back(*back, (h, h_other), width)
+            pieces[0], late_got = after(pieces[0], late_got)
+            mine, g = after(add_low(pieces[0], late_got), g)
+        else:
+            pieces[0] = weight_grad(h, h_other, *dgrads[:3], width)
+            pieces[0], late_got, dgrads[3] = after(pieces[0], late_got, dgrads[3])
+            mine, dgrads[3] = after(add_low(pieces[0], late_got), dgrads[3])
+            g, gain_a = input_back(*back)
         late = scatter_rows(mine)
-        g, gain_a = input_own(dgrads, part, x, g_mid, norm_gain[l, 0][None], qk, vo)
-        if l > 0:
+        if l == 0:
             g, early = after(g, early)
         factor_grad = jnp.sum(fg, axis=1) / (factors[l] * LOG2E)
         small = jnp.concatenate([jnp.sum(gain_a, axis=0), jnp.sum(gain_m, axis=0), factor_grad])
-        grads[l] = (early, late, small)
-    input_grad = plan.unswap(g)
+        grads[l] = [early, late, small]
+    in_blocks = g.reshape(out_blocks.shape)
+    in_got = plan.across(plan.pick(in_blocks, 1 - plan.seq).astype(BF16))
+    input_grad = plan.order(plan.pick(in_blocks, plan.seq), in_got.astype(F32)).reshape(out_blocks.shape)
     small = jnp.stack([entry[2] for entry in grads])
     small = total_over_all(plan, small)
-    early, late = jnp.stack([e[0] for e in grads]), jnp.stack([e[1] for e in grads])
+    early = []
+    for entry, _, _ in grads:
+        if isinstance(entry, list):
+            early.append(entry[0].astype(F32) + plan.across(entry[1]).astype(F32))
+        else:
+            early.append(entry.astype(F32))
+    early = jnp.stack(early)
+    late = jnp.stack([entry[1].astype(F32) for entry in grads])
     qkv_g = jnp.stack([late[:, :, c * w:(c + 1) * w] for c in range(3)], axis=1)
     up_g, down_g, out_g = (early[:, :, c * w:(c + 1) * w] for c in range(3))
     scale_g = small[:, 2 * d:] * jax.nn.sigmoid(query_scale) * unit

time: 772 us -> 741 us (0.960)
  other arithmetic: 43.9 us -> 32.3 us
  Pallas kernels: 597 us -> 586 us
    ppermute x10, waiting for transfers between devices: 43.1 us -> 24.5 us  [across(): return lax.ppermute(a, 'tp', [(t, (t + self.ring) % n) for t in range(n)])]
    pallas_call x4 -> x3, Pallas kernels: 43.3 us -> 31.3 us  [weight_grad(): pl.pallas_call(functools.partial(weight_grad_kernel, w), grid=(d // bd,),...]
    reduce_scatter x4 -> x5, waiting for transfers between devices: 18.2 us -> 29.8 us  [scatter_rows(): return lax.psum_scatter(mine, 'fsdp', scatter_dimension=0, tiled=True)]
    pallas_call x6 -> x4, Pallas kernels: 133 us -> 134 us  [the longest x2 79.3 us: mlp_back(): pl.pallas_call(functools.partial(mlp_back_kernel, w, steps, ring), grid=(...]
  transfers between devices with their start and end apart: 25 -> 24, of which waited for: 11 -> 11; matrix products, arithmetic and copies ran while one was open for 6% -> 5% of each run, Pallas kernels for 75% -> 71%
where the time goes in v6:
time: 741 us; the launch traced here: 732 us
  Pallas kernels  586 us (79%)
  waiting for transfers between devices  60.1 us (8%)
  other arithmetic  32.3 us (4%)
  starting transfers between devices  22.1 us (3%)
  local copies, waits for them, and re-layouts  17.6 us (2%)
  between operations  14.6 us (2%)
    pallas_call x4, Pallas kernels, attention_backward(): pl.pallas_call(functools.partial(backward_kernel, pair=pair, dh=dh, bq=bq...  159 us
    pallas_call x1, Pallas kernels, gather_call(): pl.pallas_call(functools.partial(gather_kernel, pieces, pairs, outer, rin...  104 us
    pallas_call x2, Pallas kernels, mlp_back(): pl.pallas_call(functools.partial(mlp_back_kernel, w, steps, ring), grid=(...  79.3 us
    pallas_call x2, Pallas kernels, attention_forward(): pl.pallas_call(functools.partial(forward_kernel, pair=pair, dh=dh, bq=bq,...  66.5 us
    pallas_call x2, Pallas kernels, input_back(): pl.pallas_call(functools.partial(input_back_kernel, w, low, steps, stack_...  54.2 us
    pallas_call x2, Pallas kernels, middle_call(): pl.pallas_call(functools.partial(middle_kernel, w, low, steps, stack_inde...  50.3 us
    pallas_call x2, Pallas kernels, project(): pl.pallas_call(functools.partial(project_kernel, w, low, steps, stack_ind...  40.9 us
    pallas_call x3, Pallas kernels, weight_grad(): pl.pallas_call(functools.partial(weight_grad_kernel, w), grid=(d // bd,),...  31.3 us
  transfers between devices with their start and end apart: 24, of which 11 were waited for; matrix products, arithmetic and copies ran while one was open for 5% of the time, Pallas kernels for 71%

profile of v6, /device:TPU:0, one launch (start us, length us, event | category | flops | bytes accessed | tf_op | source)
XLA Modules:
  0.0 732.4 jit_solution(7474116415939516326)
XLA Ops:
  7.3 1.9 fusion.13
  9.2 1.3 slice_bitcast_fusion.5
  10.5 0.8 fusion.14
  12.0 0.9 broadcast_in_dim_tile.8.scale_ref
  13.3 0.8 fusion.11
  14.1 2.9 fusion.block_ref
  17.0 103.9 %gather_weights.1 = (bf16[4,2,160,640]{3,2,1,0:T(8,128)(2,1)}, bf16[4,2,160,640]{3,2,1,0:T(8,128)(2,1)}, bf16[4,2,160,640]{3,2,1,0:T(8,128)(2,1)}, bf16[4,2,160,640]{3,2,1,0:T(8,128)(2,1)}, bf16[512,1280]{1,0:T(8,128)(2,1)}) custom-call(bf16[2,160,640]{2,1,0:T(8,128)(2,1)} %get-tuple-element.259.shard_ref, bf16[512,1280]{1,0:T(8,128)(2,1)} %fusion.block_ref), custom_call_target="tpu_custom_call" | custom-call | tf_op jit(solution)/shard_map/gather_weights/pallas_call | solution.py:339
  121.0 0.6 slice_bitcast_fusion.7
  121.6 5.0 collective-permute-start
  126.6 21.5 %project.2 = (bf16[1024,1280]{1,0:T(8,128)(2,1)}, bf16[1024,1280]{1,0:T(8,128)(2,1)}, bf16[640,2048]{1,0:T(8,128)(2,1)}, bf16[640,2048]{1,0:T(8,128)(2,1)}, bf16...) custom-call(f32[1,1280]{1,0:T(1,128)} %get-tuple-element.264.gain_ref, f32[640,1]{1,0:T(8,128)} %broadcast_in_dim_tile.8.scale_ref, ...), custom_call_target="tpu_custom_call" | custom-call | flops 10066329600 | bytes 15728640 | tf_op jit(solution)/shard_map/project/pallas_call | solution.py:700
  148.2 1.0 pad_maximum_fusion.6
  149.2 0.9 broadcast_in_dim_tile.9.scale_ref
  151.4 1.9 fusion.1
  153.3 2.0 collective-permute-start.2
  155.2 33.5 %attention_forward.2 = (bf16[640,2048]{1,0:T(8,128)(2,1)}, f32[8,1,2048]{2,1,0:T(1,128)}) custom-call(s32[1]{0:T(128)} %dynamic_slice.23.prefix_ref, s32[4]{0:T(128)} %fusion.17.order_ref, bf16[640,2048]{1,0:T(8,128)(2,1)} %get-tuple-element.126.q_ref, bf16[640,2048]{1,0:T(8,128)(2,1)} %get-tuple-element.127.k_ref, bf16[640,2048]{1,0:T(8,128)(2,1)} %get-tuple-element.128.v_ref), custom_call_target="tpu_custom_call" | custom-call | flops 20132659200 | bytes 10485760 | tf_op jit(solution)/shard_map/attention_forward/pallas_call | solution.py:95
  188.8 1.5 collective-permute-done.1.refs_3_
  190.2 25.0 %middle.2 = (f32[1024,1280]{1,0:T(8,128)}, f32[1024,1280]{1,0:T(8,128)}, f32[1024,1280]{1,0:T(8,128)}, bf16[1280,1280]{1,0:T(8,128)(2,1)}, bf16[1280,1280]{1,0:T(8,128)(2,1)}, /*index=5*/bf16[1280,640]{1,0:T(8,128)(2,1)}) custom-call(f32[1024,1280]{1,0:T(8,128)} %get-tuple-element.123.x_ref, f32[1,1280]{1,0:T(1,128)} %get-tuple-element.263.gm_ref, ...), custom_call_target="tpu_custom_call" | custom-call | flops 10066329600 | bytes 39321600 | tf_op jit(solution)/shard_map/middle/pallas_call | solution.py:817
  215.2 7.2 collective-permute-done.2.refs_1_.refs_7_
  222.6 19.4 %project.3 = (bf16[1024,1280]{1,0:T(8,128)(2,1)}, bf16[1024,1280]{1,0:T(8,128)(2,1)}, bf16[640,2048]{1,0:T(8,128)(2,1)}, bf16[640,2048]{1,0:T(8,128)(2,1)}, bf16[640,2048]{1,0:T(8,128)(2,1)}) custom-call(f32[1,1280]{1,0:T(1,128)} %get-tuple-element.265.gain_ref, f32[640,1]{1,0:T(8,128)} %broadcast_in_dim_tile.9.scale_ref, bf16[1280,640]{1,0:T(8,128)(2,1)} %bitcast.125, ...), custom_call_target="tpu_custom_call" | custom-call | flops 10066329600 | bytes 15728640 | tf_op jit(solution)/shard_map/project/pallas_call | solution.py:700
  242.0 33.0 %attention_forward.3 = (bf16[640,2048]{1,0:T(8,128)(2,1)}, f32[8,1,2048]{2,1,0:T(1,128)}) custom-call(s32[1]{0:T(128)} %dynamic_slice.23.prefix_ref, s32[4]{0:T(128)} %fusion.17.order_ref, bf16[640,2048]{1,0:T(8,128)(2,1)} %get-tuple-element.140.q_ref, bf16[640,2048]{1,0:T(8,128)(2,1)} %get-tuple-element.141.k_ref, bf16[640,2048]{1,0:T(8,128)(2,1)} %get-tuple-element.142.v_ref), custom_call_target="tpu_custom_call" | custom-call | flops 20132659200 | bytes 10485760 | tf_op jit(solution)/shard_map/attention_forward/pallas_call | solution.py:95
  275.5 25.3 %middle.3 = (f32[1024,1280]{1,0:T(8,128)}, f32[1024,1280]{1,0:T(8,128)}, f32[1024,1280]{1,0:T(8,128)}, bf16[1280,1280]{1,0:T(8,128)(2,1)}, bf16[1280,1280]{1,0:T(8,128)(2,1)}, /*index=5*/bf16[1280,640]{1,0:T(8,128)(2,1)}) custom-call(f32[1024,1280]{1,0:T(8,128)} %get-tuple-element.137.refs_4_.x_ref, f32[1,1280]{1,0:T(1,128)} %get-tuple-element.262.gm_ref, ...), custom_call_target="tpu_custom_call" | custom-call | flops 10066329600 | bytes 39321600 | tf_op jit(solution)/shard_map/middle/pallas_call | solution.py:817
  300.8 1.9 fusion.2
  302.7 40.2 %mlp_back.2 = (f32[1024,1280]{1,0:T(8,128)}, f32[8,1280]{1,0:T(8,128)}, bf16[640,2048]{1,0:T(8,128)(2,1)}, bf16[1280,1024]{1,0:T(8,128)(2,1)}, bf16[1280,1024]{1,0:T(8,128)(2,1)}) custom-call(f32[1024,1280]{1,0:T(8,128)} %get-tuple-element.150.mid_ref, f32[1024,1280]{1,0:T(8,128)} %get-tuple-element.151.pre_ref, f32[1,1280]{1,0:T(1,128)} %get-tuple-element.262.gm_ref, ...), custom_call_target="tpu_custom_call" | custom-call | flops 20132659200 | bytes 52428800 | tf_op jit(solution)/shard_map/mlp_back/pallas_call | solution.py:968
  343.0 0.7 copy.33.scale_ref
  343.7 1.9 collective-permute-start.4
  345.6 39.7 %attention_backward.4 = (bf16[320,2048]{1,0:T(8,128)(2,1)}, bf16[320,2048]{1,0:T(8,128)(2,1)}, bf16[320,2048]{1,0:T(8,128)(2,1)}, f32[80,128]{1,0:T(8,128)}) custom-call(s32[1]{0:T(128)} %dynamic_slice.23.prefix_ref, s32[4]{0:T(128)} %fusion.17.order_ref, bf16[640,2048]{1,0:T(8,128)(2,1)} %get-tuple-element.140.q_ref, ...), custom_call_target="tpu_custom_call" | custom-call | flops 26843545600 | bytes 10485760 | tf_op jit(solution)/shard_map/attention_backward/pallas_call | solution.py:205
  385.3 10.3 %weight_grad.3 = bf16[1280,1024]{1,0:T(8,128)(2,1)} custom-call(bf16[1024,1280]{1,0:T(8,128)(2,1)} %get-tuple-element.148.own_ref.refs_10_, bf16[1024,1280]{1,0:T(8,128)(2,1)} %get-tuple-element.149.other_ref.refs_11_, bf16[320,2048]{1,0:T(8,128)(2,1)} %get-tuple-element.159.dq_ref.refs_3_, bf16[320,2048]{1,0:T(8,128)(2,1)} %get-tuple-element.160.dk_ref.refs_4_, ...), custom_call_target="tpu_custom_call" | custom-call | flops 5033164800 | bytes 15728640 | tf_op jit(solution)/shard_map/weight_grad/pallas_call | solution.py:1011
  396.2 40.0 %attention_backward.5 = (bf16[320,2048]{1,0:T(8,128)(2,1)}, bf16[320,2048]{1,0:T(8,128)(2,1)}, bf16[320,2048]{1,0:T(8,128)(2,1)}, f32[80,128]{1,0:T(8,128)}) custom-call(s32[1]{0:T(128)} %dynamic_slice.23.prefix_ref, s32[4]{0:T(128)} %fusion.17.order_ref, bf16[640,2048]{1,0:T(8,128)(2,1)} %get-tuple-element.140.q_ref, ...), custom_call_target="tpu_custom_call" | custom-call | flops 26843545600 | bytes 10485760 | tf_op jit(solution)/shard_map/attention_backward/pallas_call | solution.py:205
  436.2 29.9 %input_back.2 = (f32[1024,1280]{1,0:T(8,128)}, f32[8,1280]{1,0:T(8,128)}, bf16[1280,1024]{1,0:T(8,128)(2,1)}) custom-call(f32[1024,1280]{1,0:T(8,128)} %get-tuple-element.137.refs_4_.x_ref, f32[1024,1280]{1,0:T(8,128)} %get-tuple-element.169.g_ref, f32[1,1280]{1,0:T(1,128)} %get-tuple-element.265.gain_ref, bf16[320,2048]{1,0:T(8,128)(2,1)} %get-tuple-element.174.refs_0_, ...), custom_call_target="tpu_custom_call" | custom-call | flops 15099494400 | bytes 31457280 | tf_op jit(solution)/shard_map/input_back/pallas_call | solution.py:1125
  466.1 4.5 add_convert_fusion.2
  471.2 0.7 copy.35.scale_ref
  471.9 39.0 %mlp_back.3 = (f32[1024,1280]{1,0:T(8,128)}, f32[8,1280]{1,0:T(8,128)}, bf16[640,2048]{1,0:T(8,128)(2,1)}, bf16[1280,1024]{1,0:T(8,128)(2,1)}, bf16[1280,1024]{1,0:T(8,128)(2,1)}) custom-call(f32[1024,1280]{1,0:T(8,128)} %get-tuple-element.164.mid_ref, f32[1024,1280]{1,0:T(8,128)} %get-tuple-element.165.pre_ref, f32[1,1280]{1,0:T(1,128)} %get-tuple-element.263.gm_ref, ...), custom_call_target="tpu_custom_call" | custom-call | flops 20132659200 | bytes 52428800 | tf_op jit(solution)/shard_map/mlp_back/pallas_call | solution.py:968
  511.0 1.9 collective-permute-start.6
  512.9 39.9 %attention_backward.6 = (bf16[320,2048]{1,0:T(8,128)(2,1)}, bf16[320,2048]{1,0:T(8,128)(2,1)}, bf16[320,2048]{1,0:T(8,128)(2,1)}, f32[80,128]{1,0:T(8,128)}) custom-call(s32[1]{0:T(128)} %dynamic_slice.23.prefix_ref, s32[4]{0:T(128)} %fusion.17.order_ref, bf16[640,2048]{1,0:T(8,128)(2,1)} %get-tuple-element.126.q_ref, ...), custom_call_target="tpu_custom_call" | custom-call | flops 26843545600 | bytes 10485760 | tf_op jit(solution)/shard_map/attention_backward/pallas_call | solution.py:205
  552.8 10.6 %weight_grad.4 = bf16[1280,1024]{1,0:T(8,128)(2,1)} custom-call(bf16[1024,1280]{1,0:T(8,128)(2,1)} %get-tuple-element.188.own_ref, bf16[1024,1280]{1,0:T(8,128)(2,1)} %get-tuple-element.189.other_ref, bf16[320,2048]{1,0:T(8,128)(2,1)} %get-tuple-element.208.dq_ref.refs_3_, bf16[320,2048]{1,0:T(8,128)(2,1)} %get-tuple-element.192.dk_ref.refs_4_, ...), custom_call_target="tpu_custom_call" | custom-call | flops 5033164800 | bytes 15728640 | tf_op jit(solution)/shard_map/weight_grad/pallas_call | solution.py:1011
  563.4 6.6 collective-permute-done.6
  570.0 4.5 add_convert_fusion.1
  574.6 0.7 copy-done.10
  575.4 1.8 collective-permute-start.7
  577.3 39.8 %attention_backward.7 = (bf16[320,2048]{1,0:T(8,128)(2,1)}, bf16[320,2048]{1,0:T(8,128)(2,1)}, bf16[320,2048]{1,0:T(8,128)(2,1)}, f32[80,128]{1,0:T(8,128)}) custom-call(s32[1]{0:T(128)} %dynamic_slice.23.prefix_ref, s32[4]{0:T(128)} %fusion.17.order_ref, bf16[640,2048]{1,0:T(8,128)(2,1)} %get-tuple-element.126.q_ref, ...), custom_call_target="tpu_custom_call" | custom-call | flops 26843545600 | bytes 10485760 | tf_op jit(solution)/shard_map/attention_backward/pallas_call | solution.py:205
  617.0 10.3 %weight_grad.5 = bf16[1280,1024]{1,0:T(8,128)(2,1)} custom-call(bf16[1024,1280]{1,0:T(8,128)(2,1)} %get-tuple-element.188.own_ref, bf16[1024,1280]{1,0:T(8,128)(2,1)} %get-tuple-element.189.other_ref, bf16[320,2048]{1,0:T(8,128)(2,1)} %get-tuple-element.201.dq_ref.refs_0_, bf16[320,2048]{1,0:T(8,128)(2,1)} %get-tuple-element.202.dk_ref.refs_1_, ...), custom_call_target="tpu_custom_call" | custom-call | flops 5033164800 | bytes 15728640 | tf_op jit(solution)/shard_map/weight_grad/pallas_call | solution.py:1011
  627.4 6.1 collective-permute-done.7
  633.5 4.5 add_convert_fusion
  638.2 24.4 %input_back.3 = (f32[1024,1280]{1,0:T(8,128)}, f32[8,1280]{1,0:T(8,128)}) custom-call(f32[1024,1280]{1,0:T(8,128)} %get-tuple-element.123.x_ref, f32[1024,1280]{1,0:T(8,128)} %get-tuple-element.183.g_ref, f32[1,1280]{1,0:T(1,128)} %get-tuple-element.264.gain_ref, bf16[320,2048]{1,0:T(8,128)(2,1)} %get-tuple-element.201.dq_ref.refs_0_, ...), custom_call_target="tpu_custom_call" | custom-call | flops 15099494400 | bytes 31457280 | tf_op jit(solution)/shard_map/input_back/pallas_call | solution.py:1125
  662.6 0.8 reduce_sum.54
  663.5 1.2 collective-permute-done.10
  664.7 1.7 collective-permute-start.11
  666.4 2.2 collective-permute-done.11
  668.6 2.8 collective-permute-start.12
  671.4 2.5 convert_select_fusion.3
  674.0 1.5 collective-permute-start.9
  675.5 0.7 collective-permute-start.13
  676.2 2.7 pad_maximum_fusion
  679.7 3.1 collective-permute-done.9
  682.9 1.3 collective-permute-done.14
  684.2 0.6 fusion.16
  684.8 1.9 fusion.3
  686.6 1.3 collective-permute-start.8
  688.0 0.6 fusion.21
  688.6 29.8 %reduce-scatter.14.cloned.1.call-done = bf16[160,1024]{1,0:T(8,128)(2,1)} async-done(((bf16[1280,1024]{1,0:T(8,128)(2,1)}), bf16[160,1024]{1,0:T(8,128)(2,1)}) %reduce-scatter.14.cloned.1.call-update) | async-done | bytes 327696 | tf_op jit(solution)/shard_map/reduce_scatter | solution.py:1160
  718.4 1.3 maximum_convert_fusion
  720.0 1.2 copy.37
  721.3 1.2 fusion.7
  722.9 2.7 pad_maximum_fusion.1
  (115 shorter events, 6.6 us)
Async XLA Ops:
  7.2 5.7 copy-start.1
  7.2 5.6 copy-start.2
  7.2 4.2 copy-start.16
  7.2 5.8 copy-start.5
  7.2 114.4 %all-gather.9.cloned.1.call-start = ((), (), s32[]{:S(2)}) async-start(), calls=%async_computation.10 | async-start | bytes 1843200 | tf_op jit(solution)/shard_map/all_gather | solution.py:1190
  9.2 139.0 %all-gather.11.cloned.1.call-start = ((), (), s32[]{:S(2)}) async-start(), calls=%async_computation.11 | async-start | bytes 1843200 | tf_op jit(solution)/shard_map/all_gather | solution.py:1190
  11.3 211.2 %all-gather.13.cloned.1.call-start = ((), (), s32[]{:S(2)}) async-start(), calls=%async_computation.12 | async-start | bytes 3686400 | tf_op jit(solution)/shard_map/all_gather | solution.py:1214
  11.4 0.6 copy-start.14
  14.1 106.9 %copy-start.13 = (f32[2,2,1280]{2,1,0:T(2,128)S(1)}, f32[2,2,1280]{2,1,0:T(2,128)}, u32[]{:S(2)}) copy-start(f32[2,2,1280]{2,1,0:T(2,128)} %param.15) | copy-start | bytes 61444
  121.6 26.6 %collective-permute-start = (bf16[2,160,640]{2,1,0:T(8,128)(2,1)S(1)}, bf16[2,160,640]{2,1,0:T(8,128)(2,1)S(1)}, u32[]{:S(2)}, u32[]{:S(2)}) collective-permute-start(bf16[2,160,640]{2,1,0:T(8,128)(2,1)S(1)} %get-tuple-element.125), channel_id=1, source_target_pairs={{0,2},{1,3},{2,0},{3,1},{4,6},{5,7},{6,4},{7,5},{8,10},{9,11},{10,... | collective-permute-start | bytes 1228808 | tf_op jit(solution)/shard_map/ppermute | solution.py:367
  126.6 23.5 %copy-start.21 = (s32[2]{0:T(128)S(1)}, s32[2]{0:T(128)}, u32[]{:S(2)}) copy-start(s32[2]{0:T(128)} %param.17) | copy-start | bytes 28
  149.2 126.3 %all-gather.15.cloned.1.call-start = ((), (), s32[]{:S(2)}) async-start(), calls=%async_computation.13 | async-start | bytes 3686400 | tf_op jit(solution)/shard_map/all_gather | solution.py:1214
  151.2 39.1 %collective-permute-start.1 = (bf16[1280,640]{1,0:T(8,128)(2,1)}, bf16[1280,640]{1,0:T(8,128)(2,1)}, u32[]{:S(2)}, u32[]{:S(2)}) collective-permute-start(bf16[1280,640]{1,0:T(8,128)(2,1)} %bitcast.127), channel_id=1, source_target_pairs={{0,2},{1,3},{2,0},{3,1},{4,6},{5,7},{6,4},{7,5},{8,10},{9,11},{10,... | collective-permute-start | bytes 4915208 | tf_op jit(solution)/shard_map/ppermute | solution.py:367
  151.3 284.9 %reduce-scatter.6.cloned.1.call-start = ((), (), s32[]{:S(2)}) async-start(), calls=%async_computation.5 | async-start | bytes 2949120 | tf_op jit(solution)/shard_map/reduce_scatter | solution.py:1160
  153.3 69.2 %collective-permute-start.2 = (bf16[1280,640]{1,0:T(8,128)(2,1)}, bf16[1280,640]{1,0:T(8,128)(2,1)}, u32[]{:S(2)}, u32[]{:S(2)}) collective-permute-start(bf16[1280,640]{1,0:T(8,128)(2,1)} %bitcast.124), channel_id=1, source_target_pairs={{0,2},{1,3},{2,0},{3,1},{4,6},{5,7},{6,4},{7,5},{8,10},{9,11},{10,... | collective-permute-start | bytes 4915208 | tf_op jit(solution)/shard_map/ppermute | solution.py:367
  222.5 53.0 %collective-permute-start.3 = (bf16[512,1280]{1,0:T(8,128)(2,1)S(1)}, bf16[512,1280]{1,0:T(8,128)(2,1)S(1)}, u32[]{:S(2)}, u32[]{:S(2)}) collective-permute-start(bf16[512,1280]{1,0:T(8,128)(2,1)S(1)} %fusion.1), channel_id=1, source_target_pairs={{0,2},{1,3},{2,0},{3,1},{4,6},{5,7},{6,4},{7,5},{8,10},{9,11},{10,... | collective-permute-start | bytes 3932168 | tf_op jit(solution)/shard_map/ppermute | solution.py:367
  275.5 25.3 %copy-start.19 = (bf16[512,1280]{1,0:T(8,128)(2,1)}, bf16[512,1280]{1,0:T(8,128)(2,1)S(1)}, u32[]{:S(2)}) copy-start(bf16[512,1280]{1,0:T(8,128)(2,1)S(1)} %collective-permute-done.3.refs_4_) | copy-start | bytes 3932164
  342.9 168.1 %reduce-scatter.8.cloned.1.call-start = ((), (), s32[]{:S(2)}) async-start(), calls=%async_computation.6 | async-start | bytes 2949120 | tf_op jit(solution)/shard_map/reduce_scatter | solution.py:1160
  343.7 52.0 %collective-permute-start.4 = (bf16[512,1280]{1,0:T(8,128)(2,1)S(1)}, bf16[512,1280]{1,0:T(8,128)(2,1)}, u32[]{:S(2)}, u32[]{:S(2)}) collective-permute-start(bf16[512,1280]{1,0:T(8,128)(2,1)S(1)} %fusion.2), channel_id=1, source_target_pairs={{0,2},{1,3},{2,0},{3,1},{4,6},{5,7},{6,4},{7,5},{8,10},{9,11},{10,... | collective-permute-start | bytes 3932168 | tf_op jit(solution)/shard_map/ppermute | solution.py:367
  345.6 217.9 %reduce-scatter.10.cloned.1.call-start = ((), (), s32[]{:S(2)}) async-start(), calls=%async_computation.7 | async-start | bytes 2949120 | tf_op jit(solution)/shard_map/reduce_scatter | solution.py:1160
  395.7 70.4 %collective-permute-start.5 = (bf16[1280,1024]{1,0:T(8,128)(2,1)}, bf16[1280,1024]{1,0:T(8,128)(2,1)S(1)}, u32[]{:S(2)}, u32[]{:S(2)}) collective-permute-start(bf16[1280,1024]{1,0:T(8,128)(2,1)} %weight_grad.3), channel_id=1, source_target_pairs={{0,2},{1,3},{2,0},{3,1},{4,6},{5,7},{6,4},{7,5},{8,10},{9,11},{10,... | collective-permute-start | bytes 7864328 | tf_op jit(solution)/shard_map/ppermute | solution.py:367
  470.6 0.6 copy-start.18
  470.6 214.2 %reduce-scatter.12.cloned.1.call-start = ((), (), s32[]{:S(2)}) async-start(), calls=%async_computation.8 | async-start | bytes 2949120 | tf_op jit(solution)/shard_map/reduce_scatter | solution.py:1160
  511.0 59.0 %collective-permute-start.6 = (bf16[1280,1024]{1,0:T(8,128)(2,1)}, bf16[1280,1024]{1,0:T(8,128)(2,1)}, u32[]{:S(2)}, u32[]{:S(2)}) collective-permute-start(bf16[1280,1024]{1,0:T(8,128)(2,1)} %get-tuple-element.197), channel_id=1, source_target_pairs={{0,2},{1,3},{2,0},{3,1},{4,6},{5,7},{6,4},{7,5},{8,10},{9,11},{10,... | collective-permute-start | bytes 7864328 | tf_op jit(solution)/shard_map/ppermute | solution.py:367
  552.8 17.2 %copy-start = (bf16[1280,1024]{1,0:T(8,128)(2,1)S(1)}, bf16[1280,1024]{1,0:T(8,128)(2,1)}, u32[]{:S(2)}) copy-start(bf16[1280,1024]{1,0:T(8,128)(2,1)} %get-tuple-element.184) | copy-start | bytes 7864324
  574.5 0.8 copy-start.10
  574.5 0.8 copy-start.6
  574.5 0.8 copy-start.7
  574.5 2.7 copy-start.11
  574.5 2.7 copy-start.12
  574.5 143.8 %reduce-scatter.14.cloned.1.call-start = ((), (), s32[]{:S(2)}) async-start(), calls=%async_computation.9 | async-start | bytes 2949120 | tf_op jit(solution)/shard_map/reduce_scatter | solution.py:1160
  575.4 58.0 %collective-permute-start.7 = (bf16[1280,1024]{1,0:T(8,128)(2,1)}, bf16[1280,1024]{1,0:T(8,128)(2,1)S(1)}, u32[]{:S(2)}, u32[]{:S(2)}) collective-permute-start(bf16[1280,1024]{1,0:T(8,128)(2,1)} %weight_grad.4), channel_id=1, source_target_pairs={{0,2},{1,3},{2,0},{3,1},{4,6},{5,7},{6,4},{7,5},{8,10},{9,11},{10,... | collective-permute-start | bytes 7864328 | tf_op jit(solution)/shard_map/ppermute | solution.py:367
  627.3 10.6 %copy-start.8 = (f32[80,128]{1,0:T(8,128)S(1)}, f32[80,128]{1,0:T(8,128)}, u32[]{:S(2)}) copy-start(f32[80,128]{1,0:T(8,128)} %get-tuple-element.219) | copy-start | bytes 122884
  627.3 10.6 %copy-start.9 = (f32[80,128]{1,0:T(8,128)S(1)}, f32[80,128]{1,0:T(8,128)}, u32[]{:S(2)}) copy-start(f32[80,128]{1,0:T(8,128)} %get-tuple-element.220) | copy-start | bytes 122884
  627.4 10.7 %copy-start.15 = (f32[2,80]{1,0:T(2,128)S(1)}, f32[2,80]{1,0:T(2,128)}, u32[]{:S(2)}) copy-start(f32[2,80]{1,0:T(2,128)} %copy-done.14) | copy-start | bytes 1924
  663.4 1.3 collective-permute-start.10
  664.7 3.9 collective-permute-start.11
  668.6 5.4 copy-start.20
  668.6 6.9 collective-permute-start.12
  674.0 8.8 %collective-permute-start.9 = (bf16[160,1024]{1,0:T(8,128)(2,1)S(1)}, bf16[160,1024]{1,0:T(8,128)(2,1)S(1)}, u32[]{:S(2)}, u32[]{:S(2)}) collective-permute-start(bf16[160,1024]{1,0:T(8,128)(2,1)S(1)} %copy-done.20), channel_id=1, source_target_pairs={{0,2},{1,3},{2,0},{3,1},{4,6},{5,7},{6,4},{7,5},{8,10},{9,11},{10,... | collective-permute-start | bytes 983048 | tf_op jit(solution)/shard_map/ppermute | solution.py:367
  675.5 3.9 collective-permute-start.13
  676.2 6.6 copy-start.3
  676.2 8.0 %copy-start.17 = (f32[2,80]{1,0:T(2,128)S(1)}, f32[2,80]{1,0:T(2,128)}, u32[]{:S(2)}) copy-start(f32[2,80]{1,0:T(2,128)} %param.16) | copy-start | bytes 1924
  679.4 4.8 collective-permute-start.14
  686.6 35.9 %collective-permute-start.8 = (bf16[512,1280]{1,0:T(8,128)(2,1)S(1)}, bf16[512,1280]{1,0:T(8,128)(2,1)S(1)}, u32[]{:S(2)}, u32[]{:S(2)}) collective-permute-start(bf16[512,1280]{1,0:T(8,128)(2,1)S(1)} %fusion.3), channel_id=1, source_target_pairs={{0,2},{1,3},{2,0},{3,1},{4,6},{5,7},{6,4},{7,5},{8,10},{9,11},{10,... | collective-permute-start | bytes 3932168 | tf_op jit(solution)/shard_map/ppermute | solution.py:367
  718.4 4.2 slice-start
  719.9 1.3 copy-start.4
  719.9 2.6 slice-start.1
Sparse Core Ops, SparseCore 0:
  10.8 67.4 all-gather.8
  81.0 49.6 all-gather.10
  149.3 62.9 all-gather.12
  214.9 60.5 all-gather.14
  343.0 70.6 reduce-scatter.5
  417.1 69.2 reduce-scatter.7
  490.5 69.2 reduce-scatter.9
  574.7 70.2 reduce-scatter.11
  649.0 69.2 reduce-scatter.13

commit v7 on v6

--- a/solution.py
+++ b/solution.py
@@ -1137,6 +1137,194 @@
         cost_estimate=cost(9 * rows * d * 4 * w, 24 * rows * d),
         name="input_back",
     )(x, g, gain, *grads, *plain(weights), *normed)
+
+
+def finish_kernel(w, low, far, own_steps, outer, ring, index, gain_ref, small_ref, x_any, g_any, mine_any, *refs):
+    grads, weights, refs = refs[:6], refs[6:10], refs[10:]
+    own_any, got_any, late_ref, sums_ref = refs[:4]
+    (stacked, qk, vo, part, got, xs, gs, send_half, keep, near, hops, gain_sum, vec, vecs,
+     load, store, send, recv) = refs[4:]
+    i = pl.program_id(0)
+    half = part.shape[0]
+    ba, bt = half // far, half // own_steps
+    f, t = lax.axis_index("fsdp"), lax.axis_index("tp")
+    zz, yy, seq = f // 2, lax.rem(f, 2), t // ring
+    across = {"tp": lax.rem(t + ring, 2 * ring)}
+    beside = {"fsdp": zz * 2 + 1 - yy}
+    along = [{"fsdp": lax.rem(zz + k, outer) * 2 + yy} for k in range(1, outer)]
+    core = core_of()
+    chunk = keep.shape[1]
+    sends = far + outer + outer - 1
+    pushed = own_steps // 2
+
+    def push(src, dst, slot, peer):
+        return pltpu.make_async_remote_copy(
+            src_ref=src, dst_ref=dst, send_sem=send.at[slot], recv_sem=recv.at[slot],
+            device_id=peer, device_id_type=MESH,
+        )
+
+    def rows_of(j, side):
+        z = lax.rem(zz + 1 + j, outer)
+        return pl.ds(pl.multiple_of((z * 2 + side) * chunk, chunk), chunk)
+
+    def loads():
+        def columns(first):
+            cols = pl.ds(first, half)
+            return [(grads[n].at[:, cols], stacked.at[n // 3, pl.ds(n % 3 * w, w), cols]) for n in range(6)]
+
+        pairs = columns(half)
+        pairs += [(entry(weights[s], index[s]), qk.at[s]) for s in range(2)]
+        pairs += [(entry(weights[2 + s], index[2 + s]).at[:, pl.ds(0, low)], vo.at[s]) for s in range(2)]
+        pairs += columns(0)
+        pairs += [(x_any, xs), (g_any, gs)]
+        pairs += [(mine_any.at[rows_of(j, yy)], keep.at[j]) for j in range(outer)]
+        return [pltpu.make_async_copy(src, dst, load.at[n]) for n, (src, dst) in enumerate(pairs)]
+
+    def push_part(k):
+        here = pl.ds(pl.multiple_of(k * ba, ba), ba)
+        return push(part.at[here], got.at[here], k, core)
+
+    def push_near(j):
+        return push(mine_any.at[rows_of(j, 1 - yy)], near.at[j], far + j, beside)
+
+    def push_hop(j):
+        return push(keep.at[j], hops.at[j], far + outer + j, along[j])
+
+    def push_half(k):
+        here = pl.ds(pl.multiple_of(k * bt, bt), bt)
+        return push(send_half.at[here], got_any.at[here], sends + k, across)
+
+    def push_small(n):
+        peer = ([core, across, beside] + along)[n]
+        return push(vec.at[min(n, 3)], vecs.at[n], sends + pushed + n, peer)
+
+    def total(cols):
+        parts = [
+            dot(stacked[s, :2 * w, cols], qk[s], TT) + dot(stacked[s, 2 * w:, cols], vo[s, :, :w], TT) for s in range(2)
+        ]
+        return parts[0] + parts[1]
+
+    @pl.when(i == 0)
+    def _():
+        copies = loads()
+        for c in copies[:10]:
+            c.start()
+        gain_sum[...] = jnp.zeros_like(gain_sum)
+        barrier = pltpu.get_barrier_semaphore()
+        peers = [core, across, beside] + along
+        for peer in peers:
+            pl.semaphore_signal(barrier, inc=1, device_id=peer, device_id_type=MESH)
+        pl.semaphore_wait(barrier, len(peers))
+        for j in range(outer):
+            push_near(j).start()
+        for c in copies[:10]:
+            c.wait()
+        for c in copies[10:]:
+            c.start()
+
+    @pl.when(i < far)
+    def _():
+        cols = pl.ds(pl.multiple_of(half + i * ba, ba), ba)
+        part[pl.ds(pl.multiple_of(i * ba, ba), ba)] = total(cols).astype(BF16)
+        push_part(i).start()
+
+    at = i - far
+
+    @pl.when(at == 0)
+    def _():
+        for c in loads()[10:]:
+            c.wait()
+        for k in range(far):
+            push_part(k).wait()
+
+    for j in range(outer - 1):
+        @pl.when(at == j + 1)
+        def _():
+            push_near(j).wait_recv()
+            keep[j] = (keep[j].astype(F32) + near[j].astype(F32)).astype(BF16)
+            push_hop(j).start()
+
+    @pl.when((at >= 0) & (at < own_steps))
+    def _():
+        place = lax.rem(at + pushed * (1 - seq), own_steps)
+        here = pl.ds(pl.multiple_of(place * bt, bt), bt)
+        g_ha = total(here) + got[here].astype(F32)
+        x = xs[here]
+        inv = inverse_rms(x)
+        normed = x * inv
+        gain_sum[...] += eight(g_ha * normed)
+        scaled = g_ha * gain_ref[...]
+        gs[here] = gs[here] + inv * (scaled - normed * jnp.mean(scaled * normed, axis=-1, keepdims=True))
+
+    @pl.when((at >= 0) & (at < pushed))
+    def _():
+        place = at + pushed * (1 - seq)
+        send_half[pl.ds(pl.multiple_of(at * bt, bt), bt)] = gs[pl.ds(pl.multiple_of(place * bt, bt), bt)].astype(BF16)
+        push_half(at).start()
+
+    @pl.when(at == own_steps)
+    def _():
+        size = half // 2
+        mine = pl.ds(pl.multiple_of(seq * size, size), size)
+        out_own = pltpu.make_async_copy(gs.at[mine], own_any, store.at[0])
+        out_own.start()
+        first = lax.broadcasted_iota(jnp.int32, vec.shape[1:], 0) == 0
+        vec[0] = small_ref[...] + jnp.where(first, jnp.sum(gain_sum[...], axis=0, keepdims=True), 0.0)
+        for n in range(3):
+            push_small(n).start()
+            push_small(n).wait()
+            vec[n + 1] = vec[n] + vecs[n]
+        for n in range(3, 2 + outer):
+            push_small(n).start()
+        for n in range(3, 2 + outer):
+            push_small(n).wait()
+        sums = vec[3]
+        for n in range(3, 2 + outer):
+            sums = sums + vecs[n]
+        sums_ref[...] = sums
+        push_near(outer - 1).wait_recv()
+        late = keep[outer - 1].astype(F32) + near[outer - 1].astype(F32)
+        for j in range(outer - 1):
+            push_hop(j).wait()
+            late = late + hops[j].astype(F32)
+        late_ref[...] = late
+        for j in range(outer):
+            push_near(j).wait_send()
+        for k in range(pushed):
+            push_half(k).wait()
+        out_own.wait()
+
+
+def finish(grads, x, g, gain, small, mine, qk, vo, fsdp, ring, call):
+    w, length = grads[0].shape
+    rows, d = x.shape
+    width = mine.shape[1]
+    low = -(-w // 128) * 128
+    outer, chunk = fsdp // 2, mine.shape[0] // fsdp
+    far, own_steps = rows // 512, rows // 256
+    weights = (*qk, *vo)
+    slots = far + 2 * outer - 1 + own_steps // 2 + 2 + outer
+    dma = pltpu.SemaphoreType.DMA
+    return pl.pallas_call(
+        functools.partial(finish_kernel, w, low, far, own_steps, outer, ring, stack_index(weights)),
+        grid=(far + own_steps + 1,),
+        in_specs=[fixed((1, d)), fixed(small.shape)] + [ANY] * 13,
+        out_specs=[ANY, ANY, fixed((chunk, width)), fixed(small.shape)],
+        out_shape=[shape_of((rows // 2, d), F32), shape_of((rows // 2, d)), shape_of((chunk, width), F32), shape_of(small.shape, F32)],
+        scratch_shapes=[
+            pltpu.VMEM((2, 3 * w, length), BF16), pltpu.VMEM((2, d, 2 * w), BF16), pltpu.VMEM((2, d, low), BF16),
+            pltpu.VMEM((rows, d), BF16), pltpu.VMEM((rows, d), BF16),
+            pltpu.VMEM((rows, d), F32), pltpu.VMEM((rows, d), F32),
+            pltpu.VMEM((rows // 2, d), BF16),
+            pltpu.VMEM((outer, chunk, width), BF16), pltpu.VMEM((outer, chunk, width), BF16),
+            pltpu.VMEM((outer - 1, chunk, width), BF16),
+            pltpu.VMEM((8, d), F32), pltpu.VMEM((4,) + small.shape, F32), pltpu.VMEM((2 + outer,) + small.shape, F32),
+            dma((18 + outer,)), dma((1,)), dma((slots,)), dma((slots,)),
+        ],
+        compiler_params=pltpu.CompilerParams(vmem_limit_bytes=VMEM_LIMIT, collective_id=call, has_side_effects=True),
+        cost_estimate=cost(6 * rows * d * 4 * w, 24 * rows * d),
+        name="finish",
+    )(gain, small, x, g, mine, *grads, *plain(weights))
 
 
 def total_over_all(plan, a):
@@ -1255,10 +1443,13 @@
             )
             if s == 1:
                 pieces[1] = weight_grad(h, h_other, dq, dk, dv, width)
-                if outputs is None:
+                if l > 0:
                     pieces[1], out_got = after(pieces[1], out_got)
+                    g_att, pieces[1] = after(g_att, pieces[1])
+                else:
+                    g_att, pieces[1], out_got = after(g_att, pieces[1], out_got)
                     outputs = plan.order(plan.pick(out_blocks, plan.seq), out_got.astype(F32)).reshape(out_blocks.shape)
-                g_att, pieces[1] = after(g_att, pieces[1])
+                    pieces[1], early_got, outputs = after(pieces[1], early_got, outputs)
                 late_got = plan.across(pieces[1])
                 if l + 1 < layers:
                     g_att, grads[l + 1][1] = after(g_att, grads[l + 1][1])
@@ -1271,27 +1462,30 @@
             dgrads[3 * s:3 * s + 3] = [dq, dk, dv]
             fgs.append(fg)
         fg = fgs[0] + fgs[1]
-        back = (dgrads, x, g_mid, norm_gain[l, 0][None], qk, vo, 7 + l)
         if l > 0:
-            g, gain_a, pieces[0] = input_back(*back, (h, h_other), width)
+            g, gain_a, pieces[0] = input_back(
+                dgrads, x, g_mid, norm_gain[l, 0][None], qk, vo, 7 + l, (h, h_other), width
+            )
             pieces[0], late_got = after(pieces[0], late_got)
             mine, g = after(add_low(pieces[0], late_got), g)
         else:
             pieces[0] = weight_grad(h, h_other, *dgrads[:3], width)
             pieces[0], late_got, dgrads[3] = after(pieces[0], late_got, dgrads[3])
             mine, dgrads[3] = after(add_low(pieces[0], late_got), dgrads[3])
-            g, gain_a = input_back(*back)
-        late = scatter_rows(mine)
-        if l == 0:
-            g, early = after(g, early)
-        factor_grad = jnp.sum(fg, axis=1) / (factors[l] * LOG2E)
-        small = jnp.concatenate([jnp.sum(gain_a, axis=0), jnp.sum(gain_m, axis=0), factor_grad])
-        grads[l] = [early, late, small]
-    in_blocks = g.reshape(out_blocks.shape)
-    in_got = plan.across(plan.pick(in_blocks, 1 - plan.seq).astype(BF16))
-    input_grad = plan.order(plan.pick(in_blocks, plan.seq), in_got.astype(F32)).reshape(out_blocks.shape)
-    small = jnp.stack([entry[2] for entry in grads])
-    small = total_over_all(plan, small)
+        row = lambda a: jnp.pad(a, (0, d - a.shape[0]))[None]
+        small = [row(jnp.sum(gain_m, axis=0)), row(jnp.sum(fg, axis=1) / (factors[l] * LOG2E))]
+        if l > 0:
+            late = scatter_rows(mine)
+            small.append(row(jnp.sum(gain_a, axis=0)))
+            grads[l] = [early, late, small]
+    upper = grads[1][2]
+    zero = jnp.zeros((1, d), F32)
+    small = jnp.concatenate([zero, upper[2], small[0], upper[0], small[1], upper[1], zero, zero])
+    own_half, got_half, late, small = finish(
+        dgrads, x, g_mid, norm_gain[0, 0][None], small, mine, qk, vo, plan.fsdp, plan.ring, 9
+    )
+    grads[0] = [early, late, small]
+    input_grad = plan.order(own_half, got_half.astype(F32)).reshape(out_blocks.shape)
     early = []
     for entry, _, _ in grads:
         if isinstance(entry, list):
@@ -1302,10 +1496,10 @@
     late = jnp.stack([entry[1].astype(F32) for entry in grads])
     qkv_g = jnp.stack([late[:, :, c * w:(c + 1) * w] for c in range(3)], axis=1)
     up_g, down_g, out_g = (early[:, :, c * w:(c + 1) * w] for c in range(3))
-    scale_g = small[:, 2 * d:] * jax.nn.sigmoid(query_scale) * unit
+    scale_g = small[4:6, :dh] * jax.nn.sigmoid(query_scale) * unit
     return (
         outputs, input_grad, qkv_g, jnp.swapaxes(out_g, 1, 2), up_g, jnp.swapaxes(down_g, 1, 2),
-        small[:, :d], small[:, d:2 * d], scale_g,
+        small[:2], small[2:4], scale_g,
     )
 
 

time: 741 us -> 727 us (0.981)
  waiting for transfers between devices: 60.1 us -> 25.1 us
  Pallas kernels: 586 us -> 610 us
    pallas_call x0 -> x1, Pallas kernels: none -> 62.3 us  [finish(): pl.pallas_call(functools.partial(finish_kernel, w, low, far, own_steps, o...]
    reduce_scatter x5 -> x4, waiting for transfers between devices: 29.8 us -> 0.05 us  [scatter_rows(): return lax.psum_scatter(mine, 'fsdp', scatter_dimension=0, tiled=True)]
    pallas_call x2 -> x1, Pallas kernels: 54.2 us -> 29.9 us  [input_back(): pl.pallas_call(functools.partial(input_back_kernel, w, low, steps, stack_...]
    pallas_call x4, Pallas kernels: 159 us -> 149 us  [attention_backward(): pl.pallas_call(functools.partial(backward_kernel, pair=pair, dh=dh, bq=bq...]
    ppermute x10 -> x9, starting transfers between devices: 16.1 us -> 19.9 us  [across(): return lax.ppermute(a, 'tp', [(t, (t + self.ring) % n) for t in range(n)])]
    ppermute x10 -> x9, waiting for transfers between devices: 24.5 us -> 22.7 us  [across(): return lax.ppermute(a, 'tp', [(t, (t + self.ring) % n) for t in range(n)])]
  transfers between devices with their start and end apart: 24 -> 17, of which waited for: 11 -> 5; matrix products, arithmetic and copies ran while one was open for 5% -> 6% of each run, Pallas kernels for 71% -> 75%
where the time goes in v7:
time: 727 us; the launch traced here: 721 us
  Pallas kernels  610 us (84%)
  other arithmetic  34.4 us (5%)
  waiting for transfers between devices  25.1 us (3%)
  starting transfers between devices  20.2 us (3%)
  local copies, waits for them, and re-layouts  16.9 us (2%)
  between operations  14.9 us (2%)
    pallas_call x4, Pallas kernels, attention_backward(): pl.pallas_call(functools.partial(backward_kernel, pair=pair, dh=dh, bq=bq...  149 us
    pallas_call x1, Pallas kernels, gather_call(): pl.pallas_call(functools.partial(gather_kernel, pieces, pairs, outer, rin...  104 us
    pallas_call x2, Pallas kernels, mlp_back(): pl.pallas_call(functools.partial(mlp_back_kernel, w, steps, ring), grid=(...  79.2 us
    pallas_call x2, Pallas kernels, attention_forward(): pl.pallas_call(functools.partial(forward_kernel, pair=pair, dh=dh, bq=bq,...  62.7 us
    pallas_call x1, Pallas kernels, finish(): pl.pallas_call(functools.partial(finish_kernel, w, low, far, own_steps, o...  62.3 us
    pallas_call x2, Pallas kernels, middle_call(): pl.pallas_call(functools.partial(middle_kernel, w, low, steps, stack_inde...  50.3 us
    pallas_call x2, Pallas kernels, project(): pl.pallas_call(functools.partial(project_kernel, w, low, steps, stack_ind...  41 us
    pallas_call x3, Pallas kernels, weight_grad(): pl.pallas_call(functools.partial(weight_grad_kernel, w), grid=(d // bd,),...  31.3 us
  transfers between devices with their start and end apart: 17, of which 5 were waited for; matrix products, arithmetic and copies ran while one was open for 6% of the time, Pallas kernels for 75%

profile of v7, /device:TPU:0, one launch (start us, length us, event | category | flops | bytes accessed | tf_op | source)
XLA Modules:
  0.0 721.4 jit_solution(16750496336792093243)
XLA Ops:
  7.3 1.9 fusion.17
  9.2 1.3 slice_bitcast_fusion.2
  10.5 0.8 fusion.18
  11.4 0.5 copy-done.16
  12.0 0.9 broadcast_in_dim_tile.8.scale_ref
  13.3 0.8 fusion.15
  14.1 2.9 fusion.block_ref
  17.0 103.9 %gather_weights.1 = (bf16[4,2,160,640]{3,2,1,0:T(8,128)(2,1)}, bf16[4,2,160,640]{3,2,1,0:T(8,128)(2,1)}, bf16[4,2,160,640]{3,2,1,0:T(8,128)(2,1)}, bf16[4,2,160,640]{3,2,1,0:T(8,128)(2,1)}, bf16[512,1280]{1,0:T(8,128)(2,1)}) custom-call(bf16[2,160,640]{2,1,0:T(8,128)(2,1)} %get-tuple-element.267.shard_ref, bf16[512,1280]{1,0:T(8,128)(2,1)} %fusion.block_ref), custom_call_target="tpu_custom_call" | custom-call | tf_op jit(solution)/shard_map/gather_weights/pallas_call | solution.py:339
  121.0 0.6 slice_bitcast_fusion.3
  121.6 5.0 collective-permute-start
  126.6 21.6 %project.2 = (bf16[1024,1280]{1,0:T(8,128)(2,1)}, bf16[1024,1280]{1,0:T(8,128)(2,1)}, bf16[640,2048]{1,0:T(8,128)(2,1)}, bf16[640,2048]{1,0:T(8,128)(2,1)}, bf16...) custom-call(f32[1,1280]{1,0:T(1,128)} %get-tuple-element.272.gain_ref, f32[640,1]{1,0:T(8,128)} %broadcast_in_dim_tile.8.scale_ref, ...), custom_call_target="tpu_custom_call" | custom-call | flops 10066329600 | bytes 15728640 | tf_op jit(solution)/shard_map/project/pallas_call | solution.py:700
  148.2 1.0 pad_maximum_fusion.7
  149.3 0.9 broadcast_in_dim_tile.9.scale_ref
  150.1 0.6 dynamic_slice.17.prefix_ref
  150.8 0.6 fusion.21.order_ref
  151.5 1.9 fusion.1
  153.4 2.0 collective-permute-start.2
  155.4 31.7 %attention_forward.2 = (bf16[640,2048]{1,0:T(8,128)(2,1)}, f32[8,1,2048]{2,1,0:T(1,128)}) custom-call(s32[1]{0:T(128)} %dynamic_slice.17.prefix_ref, s32[4]{0:T(128)} %fusion.21.order_ref, bf16[640,2048]{1,0:T(8,128)(2,1)} %get-tuple-element.130.q_ref, bf16[640,2048]{1,0:T(8,128)(2,1)} %get-tuple-element.131.k_ref, bf16[640,2048]{1,0:T(8,128)(2,1)} %get-tuple-element.132.v_ref), custom_call_target="tpu_custom_call" | custom-call | flops 20132659200 | bytes 10485760 | tf_op jit(solution)/shard_map/attention_forward/pallas_call | solution.py:95
  187.0 3.4 collective-permute-done.1.refs_3_
  190.4 25.0 %middle.2 = (f32[1024,1280]{1,0:T(8,128)}, f32[1024,1280]{1,0:T(8,128)}, f32[1024,1280]{1,0:T(8,128)}, bf16[1280,1280]{1,0:T(8,128)(2,1)}, bf16[1280,1280]{1,0:T(8,128)(2,1)}, /*index=5*/bf16[1280,640]{1,0:T(8,128)(2,1)}) custom-call(f32[1024,1280]{1,0:T(8,128)} %get-tuple-element.127.x_ref.x_any, f32[1,1280]{1,0:T(1,128)} %get-tuple-element.271.gm_ref, ...), custom_call_target="tpu_custom_call" | custom-call | flops 10066329600 | bytes 39321600 | tf_op jit(solution)/shard_map/middle/pallas_call | solution.py:817
  215.4 7.3 %collective-permute-done.2.refs_1_.refs_7_ = bf16[1280,640]{1,0:T(8,128)(2,1)} collective-permute-done((bf16[1280,640]{1,0:T(8,128)(2,1)}, bf16[1280,640]{1,0:T(8,128)(2,1)}, u32[]{:S(2)}, u32[]{:S(2)}) %collective-permute-start.2) | collective-permute-done | bytes 1638432 | tf_op jit(solution)/shard_map/ppermute | solution.py:367
  222.7 19.4 %project.3 = (bf16[1024,1280]{1,0:T(8,128)(2,1)}, bf16[1024,1280]{1,0:T(8,128)(2,1)}, bf16[640,2048]{1,0:T(8,128)(2,1)}, bf16[640,2048]{1,0:T(8,128)(2,1)}, bf16[640,2048]{1,0:T(8,128)(2,1)}) custom-call(f32[1,1280]{1,0:T(1,128)} %get-tuple-element.270.gain_ref, f32[640,1]{1,0:T(8,128)} %broadcast_in_dim_tile.9.scale_ref, bf16[1280,640]{1,0:T(8,128)(2,1)} %bitcast.116, ...), custom_call_target="tpu_custom_call" | custom-call | flops 10066329600 | bytes 15728640 | tf_op jit(solution)/shard_map/project/pallas_call | solution.py:700
  242.2 31.1 %attention_forward.3 = (bf16[640,2048]{1,0:T(8,128)(2,1)}, f32[8,1,2048]{2,1,0:T(1,128)}) custom-call(s32[1]{0:T(128)} %dynamic_slice.17.prefix_ref, s32[4]{0:T(128)} %fusion.21.order_ref, bf16[640,2048]{1,0:T(8,128)(2,1)} %get-tuple-element.149.q_ref, bf16[640,2048]{1,0:T(8,128)(2,1)} %get-tuple-element.150.k_ref, bf16[640,2048]{1,0:T(8,128)(2,1)} %get-tuple-element.151.v_ref), custom_call_target="tpu_custom_call" | custom-call | flops 20132659200 | bytes 10485760 | tf_op jit(solution)/shard_map/attention_forward/pallas_call | solution.py:95
  273.3 2.2 all-gather.15.cloned.1.call-done
  275.5 25.3 %middle.3 = (f32[1024,1280]{1,0:T(8,128)}, f32[1024,1280]{1,0:T(8,128)}, f32[1024,1280]{1,0:T(8,128)}, bf16[1280,1280]{1,0:T(8,128)(2,1)}, bf16[1280,1280]{1,0:T(8,128)(2,1)}, /*index=5*/bf16[1280,640]{1,0:T(8,128)(2,1)}) custom-call(f32[1024,1280]{1,0:T(8,128)} %get-tuple-element.146.refs_4_.x_ref, f32[1,1280]{1,0:T(1,128)} %get-tuple-element.273.gm_ref, ...), custom_call_target="tpu_custom_call" | custom-call | flops 10066329600 | bytes 39321600 | tf_op jit(solution)/shard_map/middle/pallas_call | solution.py:817
  300.8 1.9 fusion.2
  302.7 40.2 %mlp_back.2 = (f32[1024,1280]{1,0:T(8,128)}, f32[8,1280]{1,0:T(8,128)}, bf16[640,2048]{1,0:T(8,128)(2,1)}, bf16[1280,1024]{1,0:T(8,128)(2,1)}, bf16[1280,1024]{1,0:T(8,128)(2,1)}) custom-call(f32[1024,1280]{1,0:T(8,128)} %get-tuple-element.156.mid_ref, f32[1024,1280]{1,0:T(8,128)} %get-tuple-element.157.pre_ref, f32[1,1280]{1,0:T(1,128)} %get-tuple-element.273.gm_ref, ...), custom_call_target="tpu_custom_call" | custom-call | flops 20132659200 | bytes 52428800 | tf_op jit(solution)/shard_map/mlp_back/pallas_call | solution.py:968
  343.0 0.7 copy.33.scale_ref
  343.7 0.7 copy.35.scale_ref
  344.4 2.0 collective-permute-start.4
  346.5 0.6 broadcast_in_dim.33
  347.1 37.3 %attention_backward.4 = (bf16[320,2048]{1,0:T(8,128)(2,1)}, bf16[320,2048]{1,0:T(8,128)(2,1)}, bf16[320,2048]{1,0:T(8,128)(2,1)}, f32[80,128]{1,0:T(8,128)}) custom-call(s32[1]{0:T(128)} %dynamic_slice.17.prefix_ref, s32[4]{0:T(128)} %fusion.21.order_ref, bf16[640,2048]{1,0:T(8,128)(2,1)} %get-tuple-element.149.q_ref, ...), custom_call_target="tpu_custom_call" | custom-call | flops 26843545600 | bytes 10485760 | tf_op jit(solution)/shard_map/attention_backward/pallas_call | solution.py:205
  384.4 10.3 %weight_grad.3 = bf16[1280,1024]{1,0:T(8,128)(2,1)} custom-call(bf16[1024,1280]{1,0:T(8,128)(2,1)} %get-tuple-element.166.own_ref.refs_10_, bf16[1024,1280]{1,0:T(8,128)(2,1)} %get-tuple-element.167.other_ref.refs_11_, bf16[320,2048]{1,0:T(8,128)(2,1)} %get-tuple-element.169.dq_ref.refs_3_, bf16[320,2048]{1,0:T(8,128)(2,1)} %get-tuple-element.170.dk_ref.refs_4_, ...), custom_call_target="tpu_custom_call" | custom-call | flops 5033164800 | bytes 15728640 | tf_op jit(solution)/shard_map/weight_grad/pallas_call | solution.py:1011
  394.7 3.0 collective-permute-start.5
  397.7 37.3 %attention_backward.5 = (bf16[320,2048]{1,0:T(8,128)(2,1)}, bf16[320,2048]{1,0:T(8,128)(2,1)}, bf16[320,2048]{1,0:T(8,128)(2,1)}, f32[80,128]{1,0:T(8,128)}) custom-call(s32[1]{0:T(128)} %dynamic_slice.17.prefix_ref, s32[4]{0:T(128)} %fusion.21.order_ref, bf16[640,2048]{1,0:T(8,128)(2,1)} %get-tuple-element.149.q_ref, ...), custom_call_target="tpu_custom_call" | custom-call | flops 26843545600 | bytes 10485760 | tf_op jit(solution)/shard_map/attention_backward/pallas_call | solution.py:205
  435.0 0.9 add_reduce_fusion
  435.9 29.9 %input_back.1 = (f32[1024,1280]{1,0:T(8,128)}, f32[8,1280]{1,0:T(8,128)}, bf16[1280,1024]{1,0:T(8,128)(2,1)}) custom-call(f32[1024,1280]{1,0:T(8,128)} %get-tuple-element.146.refs_4_.x_ref, f32[1024,1280]{1,0:T(8,128)} %get-tuple-element.164.g_ref, f32[1,1280]{1,0:T(1,128)} %get-tuple-element.270.gain_ref, bf16[320,2048]{1,0:T(8,128)(2,1)} %get-tuple-element.177.refs_0_, ...), custom_call_target="tpu_custom_call" | custom-call | flops 15099494400 | bytes 31457280 | tf_op jit(solution)/shard_map/input_back/pallas_call | solution.py:1125
  465.8 4.5 add_convert_fusion.2
  470.4 39.0 %mlp_back.3 = (f32[1024,1280]{1,0:T(8,128)}, f32[8,1280]{1,0:T(8,128)}, bf16[640,2048]{1,0:T(8,128)(2,1)}, bf16[1280,1024]{1,0:T(8,128)(2,1)}, bf16[1280,1024]{1,0:T(8,128)(2,1)}) custom-call(f32[1024,1280]{1,0:T(8,128)} %get-tuple-element.137.mid_ref, f32[1024,1280]{1,0:T(8,128)} %get-tuple-element.138.pre_ref, f32[1,1280]{1,0:T(1,128)} %get-tuple-element.271.gm_ref, ...), custom_call_target="tpu_custom_call" | custom-call | flops 20132659200 | bytes 52428800 | tf_op jit(solution)/shard_map/mlp_back/pallas_call | solution.py:968
  509.4 3.0 collective-permute-start.6
  512.5 37.4 %attention_backward.6 = (bf16[320,2048]{1,0:T(8,128)(2,1)}, bf16[320,2048]{1,0:T(8,128)(2,1)}, bf16[320,2048]{1,0:T(8,128)(2,1)}, f32[80,128]{1,0:T(8,128)}) custom-call(s32[1]{0:T(128)} %dynamic_slice.17.prefix_ref, s32[4]{0:T(128)} %fusion.21.order_ref, bf16[640,2048]{1,0:T(8,128)(2,1)} %get-tuple-element.130.q_ref, ...), custom_call_target="tpu_custom_call" | custom-call | flops 26843545600 | bytes 10485760 | tf_op jit(solution)/shard_map/attention_backward/pallas_call | solution.py:205
  549.9 10.7 %weight_grad.4 = bf16[1280,1024]{1,0:T(8,128)(2,1)} custom-call(bf16[1024,1280]{1,0:T(8,128)(2,1)} %get-tuple-element.189.own_ref, bf16[1024,1280]{1,0:T(8,128)(2,1)} %get-tuple-element.190.other_ref, bf16[320,2048]{1,0:T(8,128)(2,1)} %get-tuple-element.224.dq_ref.refs_3_, bf16[320,2048]{1,0:T(8,128)(2,1)} %get-tuple-element.193.dk_ref.refs_4_, ...), custom_call_target="tpu_custom_call" | custom-call | flops 5033164800 | bytes 15728640 | tf_op jit(solution)/shard_map/weight_grad/pallas_call | solution.py:1011
  560.7 2.9 collective-permute-start.8
  563.6 2.5 convert_select_fusion.3
  566.1 2.7 pad_maximum_fusion
  568.8 8.1 %collective-permute-done.8 = bf16[160,1024]{1,0:T(8,128)(2,1)S(1)} collective-permute-done((bf16[160,1024]{1,0:T(8,128)(2,1)S(1)}, bf16[160,1024]{1,0:T(8,128)(2,1)S(1)}, u32[]{:S(2)}, u32[]{:S(2)}) %collective-permute-start.8) | collective-permute-done | bytes 327712 | tf_op jit(solution)/shard_map/ppermute | solution.py:367
  577.0 1.8 collective-permute-start.7
  578.9 4.5 add_convert_fusion.1
  583.4 37.3 %attention_backward.7 = (bf16[320,2048]{1,0:T(8,128)(2,1)}, bf16[320,2048]{1,0:T(8,128)(2,1)}, bf16[320,2048]{1,0:T(8,128)(2,1)}, f32[80,128]{1,0:T(8,128)}) custom-call(s32[1]{0:T(128)} %dynamic_slice.17.prefix_ref, s32[4]{0:T(128)} %fusion.21.order_ref, bf16[640,2048]{1,0:T(8,128)(2,1)} %get-tuple-element.130.q_ref, ...), custom_call_target="tpu_custom_call" | custom-call | flops 26843545600 | bytes 10485760 | tf_op jit(solution)/shard_map/attention_backward/pallas_call | solution.py:205
  620.7 0.9 add_reduce_fusion.1
  621.7 10.3 %weight_grad.5 = bf16[1280,1024]{1,0:T(8,128)(2,1)} custom-call(bf16[1024,1280]{1,0:T(8,128)(2,1)} %get-tuple-element.189.own_ref, bf16[1024,1280]{1,0:T(8,128)(2,1)} %get-tuple-element.190.other_ref, bf16[320,2048]{1,0:T(8,128)(2,1)} %get-tuple-element.216.dq_ref.refs_0_, bf16[320,2048]{1,0:T(8,128)(2,1)} %get-tuple-element.217.dk_ref.refs_1_, ...), custom_call_target="tpu_custom_call" | custom-call | flops 5033164800 | bytes 15728640 | tf_op jit(solution)/shard_map/weight_grad/pallas_call | solution.py:1011
  632.0 3.9 collective-permute-done.7
  635.9 5.3 add_convert_fusion.mine_any
  641.2 0.7 concatenate.35.small_ref
  642.0 62.3 %finish.1 = (f32[512,1280]{1,0:T(8,128)}, bf16[512,1280]{1,0:T(8,128)(2,1)}, f32[160,1024]{1,0:T(8,128)}, f32[8,1280]{1,0:T(8,128)}) custom-call(f32[1,1280]{1,0:T(1,128)} %get-tuple-element.272.gain_ref, f32[8,1280]{1,0:T(8,128)} %concatenate.35.small_ref, f32[1024,1280]{1,0:T(8,128)} %get-tuple-element.127.x_ref.x_any, ...), custom_call_target="tpu_custom_call" | custom-call | flops 10066329600 | bytes 31457280 | tf_op jit(solution)/shard_map/finish/pallas_call | solution.py:1308
  704.3 1.4 fusion.9
  705.8 1.2 copy.37
  707.0 0.6 fusion.20
  707.6 0.4 copy-done
  708.0 0.4 copy-done.2
  708.7 2.7 pad_maximum_fusion.1
  711.4 0.6 fusion.24
  712.0 1.0 bitcast_convert_fusion
  713.1 1.2 fusion.10
  (95 shorter events, 2.0 us)
Async XLA Ops:
  7.2 5.7 copy-start.3
  7.2 5.6 copy-start.4
  7.2 4.2 copy-start.18
  7.2 5.8 copy-start.7
  7.2 114.4 %all-gather.9.cloned.1.call-start = ((), (), s32[]{:S(2)}) async-start(), calls=%async_computation.8 | async-start | bytes 1843200 | tf_op jit(solution)/shard_map/all_gather | solution.py:1378
  9.2 139.0 %all-gather.11.cloned.1.call-start = ((), (), s32[]{:S(2)}) async-start(), calls=%async_computation.9 | async-start | bytes 1843200 | tf_op jit(solution)/shard_map/all_gather | solution.py:1378
  11.3 211.3 %all-gather.13.cloned.1.call-start = ((), (), s32[]{:S(2)}) async-start(), calls=%async_computation.10 | async-start | bytes 3686400 | tf_op jit(solution)/shard_map/all_gather | solution.py:1402
  11.4 0.6 copy-start.16
  14.1 106.9 %copy-start.14 = (f32[2,2,1280]{2,1,0:T(2,128)S(1)}, f32[2,2,1280]{2,1,0:T(2,128)}, u32[]{:S(2)}) copy-start(f32[2,2,1280]{2,1,0:T(2,128)} %param.15) | copy-start | bytes 61444
  121.6 26.6 %collective-permute-start = (bf16[2,160,640]{2,1,0:T(8,128)(2,1)S(1)}, bf16[2,160,640]{2,1,0:T(8,128)(2,1)S(1)}, u32[]{:S(2)}, u32[]{:S(2)}) collective-permute-start(bf16[2,160,640]{2,1,0:T(8,128)(2,1)S(1)} %get-tuple-element.129), channel_id=1, source_target_pairs={{0,2},{1,3},{2,0},{3,1},{4,6},{5,7},{6,4},{7,5},{8,10},{9,11},{10,... | collective-permute-start | bytes 1228808 | tf_op jit(solution)/shard_map/ppermute | solution.py:367
  126.6 23.5 %copy-start.22 = (s32[2]{0:T(128)S(1)}, s32[2]{0:T(128)}, u32[]{:S(2)}) copy-start(s32[2]{0:T(128)} %param.17) | copy-start | bytes 28
  149.2 126.3 %all-gather.15.cloned.1.call-start = ((), (), s32[]{:S(2)}) async-start(), calls=%async_computation.11 | async-start | bytes 3686400 | tf_op jit(solution)/shard_map/all_gather | solution.py:1402
  151.3 39.1 %collective-permute-start.1 = (bf16[1280,640]{1,0:T(8,128)(2,1)}, bf16[1280,640]{1,0:T(8,128)(2,1)}, u32[]{:S(2)}, u32[]{:S(2)}) collective-permute-start(bf16[1280,640]{1,0:T(8,128)(2,1)} %bitcast.118), channel_id=1, source_target_pairs={{0,2},{1,3},{2,0},{3,1},{4,6},{5,7},{6,4},{7,5},{8,10},{9,11},{10,... | collective-permute-start | bytes 4915208 | tf_op jit(solution)/shard_map/ppermute | solution.py:367
  151.5 284.4 %reduce-scatter.5.cloned.1.call-start = ((), (), s32[]{:S(2)}) async-start(), calls=%async_computation.4 | async-start | bytes 2949120 | tf_op jit(solution)/shard_map/reduce_scatter | solution.py:1348
  153.4 69.2 %collective-permute-start.2 = (bf16[1280,640]{1,0:T(8,128)(2,1)}, bf16[1280,640]{1,0:T(8,128)(2,1)}, u32[]{:S(2)}, u32[]{:S(2)}) collective-permute-start(bf16[1280,640]{1,0:T(8,128)(2,1)} %bitcast.115), channel_id=1, source_target_pairs={{0,2},{1,3},{2,0},{3,1},{4,6},{5,7},{6,4},{7,5},{8,10},{9,11},{10,... | collective-permute-start | bytes 4915208 | tf_op jit(solution)/shard_map/ppermute | solution.py:367
  222.6 52.9 %collective-permute-start.3 = (bf16[512,1280]{1,0:T(8,128)(2,1)S(1)}, bf16[512,1280]{1,0:T(8,128)(2,1)S(1)}, u32[]{:S(2)}, u32[]{:S(2)}) collective-permute-start(bf16[512,1280]{1,0:T(8,128)(2,1)S(1)} %fusion.1), channel_id=1, source_target_pairs={{0,2},{1,3},{2,0},{3,1},{4,6},{5,7},{6,4},{7,5},{8,10},{9,11},{10,... | collective-permute-start | bytes 3932168 | tf_op jit(solution)/shard_map/ppermute | solution.py:367
  275.5 25.3 %copy-start.20 = (bf16[512,1280]{1,0:T(8,128)(2,1)}, bf16[512,1280]{1,0:T(8,128)(2,1)S(1)}, u32[]{:S(2)}) copy-start(bf16[512,1280]{1,0:T(8,128)(2,1)S(1)} %collective-permute-done.3.refs_4_) | copy-start | bytes 3932164
  342.9 3.5 copy-start.11
  343.0 166.4 %reduce-scatter.7.cloned.1.call-start = ((), (), s32[]{:S(2)}) async-start(), calls=%async_computation.5 | async-start | bytes 2949120 | tf_op jit(solution)/shard_map/reduce_scatter | solution.py:1348
  344.4 50.2 %collective-permute-start.4 = (bf16[512,1280]{1,0:T(8,128)(2,1)S(1)}, bf16[512,1280]{1,0:T(8,128)(2,1)}, u32[]{:S(2)}, u32[]{:S(2)}) collective-permute-start(bf16[512,1280]{1,0:T(8,128)(2,1)S(1)} %fusion.2), channel_id=1, source_target_pairs={{0,2},{1,3},{2,0},{3,1},{4,6},{5,7},{6,4},{7,5},{8,10},{9,11},{10,... | collective-permute-start | bytes 3932168 | tf_op jit(solution)/shard_map/ppermute | solution.py:367
  347.1 231.8 %reduce-scatter.9.cloned.1.call-start = ((), (), s32[]{:S(2)}) async-start(), calls=%async_computation.6 | async-start | bytes 2949120 | tf_op jit(solution)/shard_map/reduce_scatter | solution.py:1348
  394.7 40.3 %copy-start.9 = (f32[80,128]{1,0:T(8,128)S(1)}, f32[80,128]{1,0:T(8,128)}, u32[]{:S(2)}) copy-start(f32[80,128]{1,0:T(8,128)} %get-tuple-element.213) | copy-start | bytes 122884
  394.7 71.1 %collective-permute-start.5 = (bf16[1280,1024]{1,0:T(8,128)(2,1)}, bf16[1280,1024]{1,0:T(8,128)(2,1)S(1)}, u32[]{:S(2)}, u32[]{:S(2)}) collective-permute-start(bf16[1280,1024]{1,0:T(8,128)(2,1)} %weight_grad.3), channel_id=1, source_target_pairs={{0,2},{1,3},{2,0},{3,1},{4,6},{5,7},{6,4},{7,5},{8,10},{9,11},{10,... | collective-permute-start | bytes 7864328 | tf_op jit(solution)/shard_map/ppermute | solution.py:367
  470.3 241.7 %reduce-scatter.11.cloned.1.call-start = ((), (), s32[]{:S(2)}) async-start(), calls=%async_computation.7 | async-start | bytes 2949120 | tf_op jit(solution)/shard_map/reduce_scatter | solution.py:1348
  509.4 67.6 %collective-permute-start.6 = (bf16[1280,1024]{1,0:T(8,128)(2,1)}, bf16[1280,1024]{1,0:T(8,128)(2,1)}, u32[]{:S(2)}, u32[]{:S(2)}) collective-permute-start(bf16[1280,1024]{1,0:T(8,128)(2,1)} %get-tuple-element.197), channel_id=1, source_target_pairs={{0,2},{1,3},{2,0},{3,1},{4,6},{5,7},{6,4},{7,5},{8,10},{9,11},{10,... | collective-permute-start | bytes 7864328 | tf_op jit(solution)/shard_map/ppermute | solution.py:367
  549.9 10.7 %copy-start.10 = (f32[8,1280]{1,0:T(8,128)S(1)}, f32[8,1280]{1,0:T(8,128)}, u32[]{:S(2)}) copy-start(f32[8,1280]{1,0:T(8,128)} %get-tuple-element.200) | copy-start | bytes 122884
  549.9 10.8 %copy-start.12 = (f32[8,1280]{1,0:T(8,128)S(1)}, f32[8,1280]{1,0:T(8,128)}, u32[]{:S(2)}) copy-start(f32[8,1280]{1,0:T(8,128)} %get-tuple-element.201) | copy-start | bytes 122884
  549.9 10.8 %copy-start.21 = (bf16[160,1024]{1,0:T(8,128)(2,1)S(1)}, bf16[160,1024]{1,0:T(8,128)(2,1)}, u32[]{:S(2)}) copy-start(bf16[160,1024]{1,0:T(8,128)(2,1)} %reduce-scatter.7.cloned.1.call-done) | copy-start | bytes 983044
  560.7 16.2 %collective-permute-start.8 = (bf16[160,1024]{1,0:T(8,128)(2,1)S(1)}, bf16[160,1024]{1,0:T(8,128)(2,1)S(1)}, u32[]{:S(2)}, u32[]{:S(2)}) collective-permute-start(bf16[160,1024]{1,0:T(8,128)(2,1)S(1)} %copy-done.21), channel_id=1, source_target_pairs={{0,2},{1,3},{2,0},{3,1},{4,6},{5,7},{6,4},{7,5},{8,10},{9,11},{10,... | collective-permute-start | bytes 983048 | tf_op jit(solution)/shard_map/ppermute | solution.py:367
  566.1 10.9 %copy-start.5 = (bf16[160,1024]{1,0:T(8,128)(2,1)S(1)}, bf16[160,1024]{1,0:T(8,128)(2,1)}, u32[]{:S(2)}) copy-start(bf16[160,1024]{1,0:T(8,128)(2,1)} %reduce-scatter.5.cloned.1.call-done) | copy-start | bytes 983044
  566.1 12.8 %copy-start.1 = (bf16[1280,1024]{1,0:T(8,128)(2,1)S(1)}, bf16[1280,1024]{1,0:T(8,128)(2,1)}, u32[]{:S(2)}) copy-start(bf16[1280,1024]{1,0:T(8,128)(2,1)} %get-tuple-element.204) | copy-start | bytes 7864324
  577.0 58.9 %collective-permute-start.7 = (bf16[1280,1024]{1,0:T(8,128)(2,1)}, bf16[1280,1024]{1,0:T(8,128)(2,1)}, u32[]{:S(2)}, u32[]{:S(2)}) collective-permute-start(bf16[1280,1024]{1,0:T(8,128)(2,1)} %weight_grad.4), channel_id=1, source_target_pairs={{0,2},{1,3},{2,0},{3,1},{4,6},{5,7},{6,4},{7,5},{8,10},{9,11},{10,... | collective-permute-start | bytes 7864328 | tf_op jit(solution)/shard_map/ppermute | solution.py:367
  583.4 37.3 %copy-start.8 = (f32[80,128]{1,0:T(8,128)S(1)}, f32[80,128]{1,0:T(8,128)}, u32[]{:S(2)}) copy-start(f32[80,128]{1,0:T(8,128)} %get-tuple-element.203) | copy-start | bytes 122884
  583.4 38.2 %copy-start.17 = (f32[2,80]{1,0:T(2,128)S(1)}, f32[2,80]{1,0:T(2,128)}, u32[]{:S(2)}) copy-start(f32[2,80]{1,0:T(2,128)} %copy-done.16) | copy-start | bytes 1924
  632.0 9.2 %copy-start.13 = (f32[1,1280]{1,0:T(1,128)S(1)}, f32[1,1280]{1,0:T(1,128)}, u32[]{:S(2)}) copy-start(f32[1,1280]{1,0:T(1,128)} %broadcast_in_dim.33) | copy-start | bytes 15364
  632.0 9.9 %copy-start.6 = (bf16[160,1024]{1,0:T(8,128)(2,1)S(1)}, bf16[160,1024]{1,0:T(8,128)(2,1)}, u32[]{:S(2)}) copy-start(bf16[160,1024]{1,0:T(8,128)(2,1)} %reduce-scatter.9.cloned.1.call-done) | copy-start | bytes 983044
  705.7 1.4 copy-start.15
  705.7 1.3 copy-start.19
  705.7 2.3 copy-start
  705.7 2.7 copy-start.2
Sparse Core Ops, SparseCore 0:
  10.8 67.4 all-gather.8
  81.0 49.7 all-gather.10
  149.3 62.9 all-gather.12
  214.9 60.5 all-gather.14
  343.1 75.0 reduce-scatter.4
  421.6 69.3 reduce-scatter.6
  494.4 69.1 reduce-scatter.8
  583.5 76.3 reduce-scatter.10

commit v8 on v7

--- a/solution.py
+++ b/solution.py
@@ -1139,10 +1139,10 @@
     )(x, g, gain, *grads, *plain(weights), *normed)
 
 
-def finish_kernel(w, low, far, own_steps, outer, ring, index, gain_ref, small_ref, x_any, g_any, mine_any, *refs):
+def finish_kernel(w, low, far, own_steps, outer, ring, index, gain_ref, small_ref, x_any, g_any, piece_any, came_any, *refs):
     grads, weights, refs = refs[:6], refs[6:10], refs[10:]
     own_any, got_any, late_ref, sums_ref = refs[:4]
-    (stacked, qk, vo, part, got, xs, gs, send_half, keep, near, hops, gain_sum, vec, vecs,
+    (stacked, qk, vo, part, got, xs, gs, send_half, keep, away, came, near, hops, gain_sum, vec, vecs,
      load, store, send, recv) = refs[4:]
     i = pl.program_id(0)
     half = part.shape[0]
@@ -1177,15 +1177,20 @@
         pairs += [(entry(weights[2 + s], index[2 + s]).at[:, pl.ds(0, low)], vo.at[s]) for s in range(2)]
         pairs += columns(0)
         pairs += [(x_any, xs), (g_any, gs)]
-        pairs += [(mine_any.at[rows_of(j, yy)], keep.at[j]) for j in range(outer)]
+        for j in range(outer):
+            for n, (side, dst) in enumerate(((1 - yy, away), (yy, keep))):
+                pairs += [(piece_any.at[rows_of(j, side)], dst.at[j]), (came_any.at[rows_of(j, side)], came.at[n, j])]
         return [pltpu.make_async_copy(src, dst, load.at[n]) for n, (src, dst) in enumerate(pairs)]
 
+    def chunk_of(k):
+        return 1 - seq if k == 0 else seq
+
     def push_part(k):
-        here = pl.ds(pl.multiple_of(k * ba, ba), ba)
+        here = pl.ds(pl.multiple_of(chunk_of(k) * ba, ba), ba)
         return push(part.at[here], got.at[here], k, core)
 
     def push_near(j):
-        return push(mine_any.at[rows_of(j, 1 - yy)], near.at[j], far + j, beside)
+        return push(away.at[j], near.at[j], far + j, beside)
 
     def push_hop(j):
         return push(keep.at[j], hops.at[j], far + outer + j, along[j])
@@ -1207,7 +1212,7 @@
     @pl.when(i == 0)
     def _():
         copies = loads()
-        for c in copies[:10]:
+        for c in copies[18:] + copies[:10]:
             c.start()
         gain_sum[...] = jnp.zeros_like(gain_sum)
         barrier = pltpu.get_barrier_semaphore()
@@ -1215,33 +1220,43 @@
         for peer in peers:
             pl.semaphore_signal(barrier, inc=1, device_id=peer, device_id_type=MESH)
         pl.semaphore_wait(barrier, len(peers))
+        for c in copies[18:]:
+            c.wait()
         for j in range(outer):
+            away[j] = (away[j].astype(F32) + came[0, j].astype(F32)).astype(BF16)
             push_near(j).start()
         for c in copies[:10]:
             c.wait()
-        for c in copies[10:]:
+        for c in copies[10:18]:
             c.start()
 
-    @pl.when(i < far)
-    def _():
-        cols = pl.ds(pl.multiple_of(half + i * ba, ba), ba)
-        part[pl.ds(pl.multiple_of(i * ba, ba), ba)] = total(cols).astype(BF16)
-        push_part(i).start()
-
-    at = i - far
+    run = 1 + pushed
+    for k in range(far):
+        @pl.when(i == k * run)
+        def _():
+            cols = pl.ds(pl.multiple_of(half + chunk_of(k) * ba, ba), ba)
+            part[pl.ds(pl.multiple_of(chunk_of(k) * ba, ba), ba)] = total(cols).astype(BF16)
+            push_part(k).start()
+
+    place_in_run = lax.rem(i, run)
+    at = jnp.where(place_in_run == 0, -1, i // run * pushed + place_in_run - 1)
+    at = jnp.where(i == far + own_steps, own_steps, at)
 
     @pl.when(at == 0)
     def _():
-        for c in loads()[10:]:
+        for c in loads()[10:18]:
             c.wait()
-        for k in range(far):
+
+    for k in range(far):
+        @pl.when(at == k * pushed)
+        def _():
             push_part(k).wait()
 
     for j in range(outer - 1):
         @pl.when(at == j + 1)
         def _():
             push_near(j).wait_recv()
-            keep[j] = (keep[j].astype(F32) + near[j].astype(F32)).astype(BF16)
+            keep[j] = (keep[j].astype(F32) + came[1, j].astype(F32) + near[j].astype(F32)).astype(BF16)
             push_hop(j).start()
 
     @pl.when((at >= 0) & (at < own_steps))
@@ -1283,7 +1298,7 @@
             sums = sums + vecs[n]
         sums_ref[...] = sums
         push_near(outer - 1).wait_recv()
-        late = keep[outer - 1].astype(F32) + near[outer - 1].astype(F32)
+        late = keep[outer - 1].astype(F32) + came[1, outer - 1].astype(F32) + near[outer - 1].astype(F32)
         for j in range(outer - 1):
             push_hop(j).wait()
             late = late + hops[j].astype(F32)
@@ -1295,12 +1310,12 @@
         out_own.wait()
 
 
-def finish(grads, x, g, gain, small, mine, qk, vo, fsdp, ring, call):
+def finish(grads, x, g, gain, small, piece, came, qk, vo, fsdp, ring, call):
     w, length = grads[0].shape
     rows, d = x.shape
-    width = mine.shape[1]
+    width = piece.shape[1]
     low = -(-w // 128) * 128
-    outer, chunk = fsdp // 2, mine.shape[0] // fsdp
+    outer, chunk = fsdp // 2, piece.shape[0] // fsdp
     far, own_steps = rows // 512, rows // 256
     weights = (*qk, *vo)
     slots = far + 2 * outer - 1 + own_steps // 2 + 2 + outer
@@ -1308,7 +1323,7 @@
     return pl.pallas_call(
         functools.partial(finish_kernel, w, low, far, own_steps, outer, ring, stack_index(weights)),
         grid=(far + own_steps + 1,),
-        in_specs=[fixed((1, d)), fixed(small.shape)] + [ANY] * 13,
+        in_specs=[fixed((1, d)), fixed(small.shape)] + [ANY] * 14,
         out_specs=[ANY, ANY, fixed((chunk, width)), fixed(small.shape)],
         out_shape=[shape_of((rows // 2, d), F32), shape_of((rows // 2, d)), shape_of((chunk, width), F32), shape_of(small.shape, F32)],
         scratch_shapes=[
@@ -1317,14 +1332,15 @@
             pltpu.VMEM((rows, d), F32), pltpu.VMEM((rows, d), F32),
             pltpu.VMEM((rows // 2, d), BF16),
             pltpu.VMEM((outer, chunk, width), BF16), pltpu.VMEM((outer, chunk, width), BF16),
+            pltpu.VMEM((2, outer, chunk, width), BF16), pltpu.VMEM((outer, chunk, width), BF16),
             pltpu.VMEM((outer - 1, chunk, width), BF16),
             pltpu.VMEM((8, d), F32), pltpu.VMEM((4,) + small.shape, F32), pltpu.VMEM((2 + outer,) + small.shape, F32),
-            dma((18 + outer,)), dma((1,)), dma((slots,)), dma((slots,)),
+            dma((18 + 4 * outer,)), dma((1,)), dma((slots,)), dma((slots,)),
         ],
         compiler_params=pltpu.CompilerParams(vmem_limit_bytes=VMEM_LIMIT, collective_id=call, has_side_effects=True),
         cost_estimate=cost(6 * rows * d * 4 * w, 24 * rows * d),
         name="finish",
-    )(gain, small, x, g, mine, *grads, *plain(weights))
+    )(gain, small, x, g, piece, came, *grads, *plain(weights))
 
 
 def total_over_all(plan, a):
@@ -1384,9 +1400,8 @@
         return (rows, 0), (rows, 1)
 
     un0_rows, qk1_rows = along(0, 2), along(1, 0)
-    other, un0_rows, cotangent, shards = after(other, un0_rows, cotangent, pairs[1, 1:])
+    other, un0_rows, shards = after(other, un0_rows, pairs[1, 1:])
     shards_got, un0 = plan.across(shards), both(un0_rows)
-    cot_block = plan.pick(cotangent, 1 - plan.seq).astype(BF16)
     kept, weights = [], []
     for l in range(layers):
         qk, vo = (qk0, vo0) if l == 0 else (qk1, vo1)
@@ -1410,6 +1425,8 @@
             un = stacked(un1_rows)
         mid, pre, res, *mats = middle_call(x, att, norm_gain[l, 1][None], vo, un, 5 + l)
         if l == 0:
+            res, cotangent = after(res, cotangent)
+            cot_block = plan.pick(cotangent, 1 - plan.seq).astype(BF16)
             res, qk1_got, vo1_rows, cot_block = after(res, qk1[1], vo1_rows, cot_block)
             qk1, vo1 = (qk1[0], qk1_got), stacked(vo1_rows)
             cot_got = plan.across(cot_block)
@@ -1470,8 +1487,6 @@
             mine, g = after(add_low(pieces[0], late_got), g)
         else:
             pieces[0] = weight_grad(h, h_other, *dgrads[:3], width)
-            pieces[0], late_got, dgrads[3] = after(pieces[0], late_got, dgrads[3])
-            mine, dgrads[3] = after(add_low(pieces[0], late_got), dgrads[3])
         row = lambda a: jnp.pad(a, (0, d - a.shape[0]))[None]
         small = [row(jnp.sum(gain_m, axis=0)), row(jnp.sum(fg, axis=1) / (factors[l] * LOG2E))]
         if l > 0:
@@ -1482,7 +1497,7 @@
     zero = jnp.zeros((1, d), F32)
     small = jnp.concatenate([zero, upper[2], small[0], upper[0], small[1], upper[1], zero, zero])
     own_half, got_half, late, small = finish(
-        dgrads, x, g_mid, norm_gain[0, 0][None], small, mine, qk, vo, plan.fsdp, plan.ring, 9
+        dgrads, x, g_mid, norm_gain[0, 0][None], small, pieces[0], late_got, qk, vo, plan.fsdp, plan.ring, 9
     )
     grads[0] = [early, late, small]
     input_grad = plan.order(own_half, got_half.astype(F32)).reshape(out_blocks.shape)

time: 727 us -> 718 us (0.988)
  transfers between devices with their start and end apart: 17 -> 17, of which waited for: 5 -> 5; matrix products, arithmetic and copies ran while one was open for 6% -> 5% of each run, Pallas kernels for 75% -> 76%
where the time goes in v8:
time: 718 us; the launch traced here: 711 us
  Pallas kernels  606 us (84%)
  other arithmetic  29 us (4%)
  waiting for transfers between devices  22.7 us (3%)
  starting transfers between devices  20.2 us (3%)
  local copies, waits for them, and re-layouts  18.1 us (3%)
  between operations  15.2 us (2%)
    pallas_call x4, Pallas kernels, attention_backward(): pl.pallas_call(functools.partial(backward_kernel, pair=pair, dh=dh, bq=bq...  150 us
    pallas_call x1, Pallas kernels, gather_call(): pl.pallas_call(functools.partial(gather_kernel, pieces, pairs, outer, rin...  104 us
    pallas_call x2, Pallas kernels, mlp_back(): pl.pallas_call(functools.partial(mlp_back_kernel, w, steps, ring), grid=(...  79.5 us
    pallas_call x2, Pallas kernels, attention_forward(): pl.pallas_call(functools.partial(forward_kernel, pair=pair, dh=dh, bq=bq,...  62.4 us
    pallas_call x1, Pallas kernels, finish(): pl.pallas_call(functools.partial(finish_kernel, w, low, far, own_steps, o...  58.3 us
    pallas_call x2, Pallas kernels, middle_call(): pl.pallas_call(functools.partial(middle_kernel, w, low, steps, stack_inde...  50.3 us
    pallas_call x2, Pallas kernels, project(): pl.pallas_call(functools.partial(project_kernel, w, low, steps, stack_ind...  41.3 us
    pallas_call x3, Pallas kernels, weight_grad(): pl.pallas_call(functools.partial(weight_grad_kernel, w), grid=(d // bd,),...  31.1 us
  transfers between devices with their start and end apart: 17, of which 5 were waited for; matrix products, arithmetic and copies ran while one was open for 5% of the time, Pallas kernels for 76%

profile of v8, /device:TPU:0, one launch (start us, length us, event | category | flops | bytes accessed | tf_op | source)
XLA Modules:
  0.0 711.5 jit_solution(2735126240497801025)
XLA Ops:
  7.3 1.9 fusion.17
  9.2 1.3 slice_bitcast_fusion.2
  10.5 0.8 fusion.18
  11.4 0.5 copy-done.16
  12.0 0.9 broadcast_in_dim_tile.8.scale_ref
  13.3 0.8 fusion.15
  14.1 2.9 fusion.block_ref
  17.0 103.9 %gather_weights.1 = (bf16[4,2,160,640]{3,2,1,0:T(8,128)(2,1)}, bf16[4,2,160,640]{3,2,1,0:T(8,128)(2,1)}, bf16[4,2,160,640]{3,2,1,0:T(8,128)(2,1)}, bf16[4,2,160,640]{3,2,1,0:T(8,128)(2,1)}, bf16[512,1280]{1,0:T(8,128)(2,1)}) custom-call(bf16[2,160,640]{2,1,0:T(8,128)(2,1)} %get-tuple-element.259.shard_ref, bf16[512,1280]{1,0:T(8,128)(2,1)} %fusion.block_ref), custom_call_target="tpu_custom_call" | custom-call | tf_op jit(solution)/shard_map/gather_weights/pallas_call | solution.py:339
  121.0 0.6 slice_bitcast_fusion.3
  121.6 5.0 collective-permute-start
  126.6 21.5 %project.2 = (bf16[1024,1280]{1,0:T(8,128)(2,1)}, bf16[1024,1280]{1,0:T(8,128)(2,1)}, bf16[640,2048]{1,0:T(8,128)(2,1)}, bf16[640,2048]{1,0:T(8,128)(2,1)}, bf16...) custom-call(f32[1,1280]{1,0:T(1,128)} %get-tuple-element.264.gain_ref, f32[640,1]{1,0:T(8,128)} %broadcast_in_dim_tile.8.scale_ref, ...), custom_call_target="tpu_custom_call" | custom-call | flops 10066329600 | bytes 15728640 | tf_op jit(solution)/shard_map/project/pallas_call | solution.py:700
  148.2 1.0 pad_maximum_fusion.7
  149.2 0.9 broadcast_in_dim_tile.9.scale_ref
  150.1 0.7 dynamic_slice.17.prefix_ref
  150.8 0.5 fusion.21.order_ref
  151.4 1.9 collective-permute-start.2
  153.6 31.1 %attention_forward.2 = (bf16[640,2048]{1,0:T(8,128)(2,1)}, f32[8,1,2048]{2,1,0:T(1,128)}) custom-call(s32[1]{0:T(128)} %dynamic_slice.17.prefix_ref, s32[4]{0:T(128)} %fusion.21.order_ref, bf16[640,2048]{1,0:T(8,128)(2,1)} %get-tuple-element.126.q_ref, bf16[640,2048]{1,0:T(8,128)(2,1)} %get-tuple-element.127.k_ref, bf16[640,2048]{1,0:T(8,128)(2,1)} %get-tuple-element.128.v_ref), custom_call_target="tpu_custom_call" | custom-call | flops 20132659200 | bytes 10485760 | tf_op jit(solution)/shard_map/attention_forward/pallas_call | solution.py:95
  184.7 5.6 collective-permute-done.1.refs_3_
  190.2 1.2 copy-done.20
  191.4 24.9 %middle.2 = (f32[1024,1280]{1,0:T(8,128)}, f32[1024,1280]{1,0:T(8,128)}, f32[1024,1280]{1,0:T(8,128)}, bf16[1280,1280]{1,0:T(8,128)(2,1)}, bf16[1280,1280]{1,0:T(8,128)(2,1)}, /*index=5*/bf16[1280,640]{1,0:T(8,128)(2,1)}) custom-call(f32[1024,1280]{1,0:T(8,128)} %get-tuple-element.123.x_ref.x_any, f32[1,1280]{1,0:T(1,128)} %get-tuple-element.263.gm_ref, ...), custom_call_target="tpu_custom_call" | custom-call | flops 10066329600 | bytes 39321600 | tf_op jit(solution)/shard_map/middle/pallas_call | solution.py:817
  216.3 1.9 fusion.1
  218.2 3.5 collective-permute-done.2.refs_1_.refs_7_
  222.0 19.7 %project.3 = (bf16[1024,1280]{1,0:T(8,128)(2,1)}, bf16[1024,1280]{1,0:T(8,128)(2,1)}, bf16[640,2048]{1,0:T(8,128)(2,1)}, bf16[640,2048]{1,0:T(8,128)(2,1)}, bf16[640,2048]{1,0:T(8,128)(2,1)}) custom-call(f32[1,1280]{1,0:T(1,128)} %get-tuple-element.262.gain_ref, f32[640,1]{1,0:T(8,128)} %broadcast_in_dim_tile.9.scale_ref, bf16[1280,640]{1,0:T(8,128)(2,1)} %bitcast.116, ...), custom_call_target="tpu_custom_call" | custom-call | flops 10066329600 | bytes 15728640 | tf_op jit(solution)/shard_map/project/pallas_call | solution.py:700
  241.8 31.3 %attention_forward.3 = (bf16[640,2048]{1,0:T(8,128)(2,1)}, f32[8,1,2048]{2,1,0:T(1,128)}) custom-call(s32[1]{0:T(128)} %dynamic_slice.17.prefix_ref, s32[4]{0:T(128)} %fusion.21.order_ref, bf16[640,2048]{1,0:T(8,128)(2,1)} %get-tuple-element.146.q_ref, bf16[640,2048]{1,0:T(8,128)(2,1)} %get-tuple-element.147.k_ref, bf16[640,2048]{1,0:T(8,128)(2,1)} %get-tuple-element.148.v_ref), custom_call_target="tpu_custom_call" | custom-call | flops 20132659200 | bytes 10485760 | tf_op jit(solution)/shard_map/attention_forward/pallas_call | solution.py:95
  273.0 2.5 all-gather.15.cloned.1.call-done
  275.5 25.4 %middle.3 = (f32[1024,1280]{1,0:T(8,128)}, f32[1024,1280]{1,0:T(8,128)}, f32[1024,1280]{1,0:T(8,128)}, bf16[1280,1280]{1,0:T(8,128)(2,1)}, bf16[1280,1280]{1,0:T(8,128)(2,1)}, /*index=5*/bf16[1280,640]{1,0:T(8,128)(2,1)}) custom-call(f32[1024,1280]{1,0:T(8,128)} %get-tuple-element.143.refs_4_.x_ref, f32[1,1280]{1,0:T(1,128)} %get-tuple-element.265.gm_ref, ...), custom_call_target="tpu_custom_call" | custom-call | flops 10066329600 | bytes 39321600 | tf_op jit(solution)/shard_map/middle/pallas_call | solution.py:817
  300.9 1.9 fusion.2
  302.8 40.4 %mlp_back.2 = (f32[1024,1280]{1,0:T(8,128)}, f32[8,1280]{1,0:T(8,128)}, bf16[640,2048]{1,0:T(8,128)(2,1)}, bf16[1280,1024]{1,0:T(8,128)(2,1)}, bf16[1280,1024]{1,0:T(8,128)(2,1)}) custom-call(f32[1024,1280]{1,0:T(8,128)} %get-tuple-element.153.mid_ref, f32[1024,1280]{1,0:T(8,128)} %get-tuple-element.154.pre_ref, f32[1,1280]{1,0:T(1,128)} %get-tuple-element.265.gm_ref, ...), custom_call_target="tpu_custom_call" | custom-call | flops 20132659200 | bytes 52428800 | tf_op jit(solution)/shard_map/mlp_back/pallas_call | solution.py:968
  343.3 0.7 copy.33.scale_ref
  344.0 0.7 copy.35.scale_ref
  344.7 1.7 collective-permute-start.4
  346.4 0.6 broadcast_in_dim.33
  347.1 37.3 %attention_backward.4 = (bf16[320,2048]{1,0:T(8,128)(2,1)}, bf16[320,2048]{1,0:T(8,128)(2,1)}, bf16[320,2048]{1,0:T(8,128)(2,1)}, f32[80,128]{1,0:T(8,128)}) custom-call(s32[1]{0:T(128)} %dynamic_slice.17.prefix_ref, s32[4]{0:T(128)} %fusion.21.order_ref, bf16[640,2048]{1,0:T(8,128)(2,1)} %get-tuple-element.146.q_ref, ...), custom_call_target="tpu_custom_call" | custom-call | flops 26843545600 | bytes 10485760 | tf_op jit(solution)/shard_map/attention_backward/pallas_call | solution.py:205
  384.4 10.3 %weight_grad.3 = bf16[1280,1024]{1,0:T(8,128)(2,1)} custom-call(bf16[1024,1280]{1,0:T(8,128)(2,1)} %get-tuple-element.163.own_ref.refs_10_, bf16[1024,1280]{1,0:T(8,128)(2,1)} %get-tuple-element.164.other_ref.refs_11_, bf16[320,2048]{1,0:T(8,128)(2,1)} %get-tuple-element.166.dq_ref.refs_3_, bf16[320,2048]{1,0:T(8,128)(2,1)} %get-tuple-element.167.dk_ref.refs_4_, ...), custom_call_target="tpu_custom_call" | custom-call | flops 5033164800 | bytes 15728640 | tf_op jit(solution)/shard_map/weight_grad/pallas_call | solution.py:1011
  394.7 3.3 collective-permute-start.5
  398.1 37.6 %attention_backward.5 = (bf16[320,2048]{1,0:T(8,128)(2,1)}, bf16[320,2048]{1,0:T(8,128)(2,1)}, bf16[320,2048]{1,0:T(8,128)(2,1)}, f32[80,128]{1,0:T(8,128)}) custom-call(s32[1]{0:T(128)} %dynamic_slice.17.prefix_ref, s32[4]{0:T(128)} %fusion.21.order_ref, bf16[640,2048]{1,0:T(8,128)(2,1)} %get-tuple-element.146.q_ref, ...), custom_call_target="tpu_custom_call" | custom-call | flops 26843545600 | bytes 10485760 | tf_op jit(solution)/shard_map/attention_backward/pallas_call | solution.py:205
  435.6 0.9 add_reduce_fusion
  436.5 29.9 %input_back.1 = (f32[1024,1280]{1,0:T(8,128)}, f32[8,1280]{1,0:T(8,128)}, bf16[1280,1024]{1,0:T(8,128)(2,1)}) custom-call(f32[1024,1280]{1,0:T(8,128)} %get-tuple-element.143.refs_4_.x_ref, f32[1024,1280]{1,0:T(8,128)} %get-tuple-element.161.g_ref, f32[1,1280]{1,0:T(1,128)} %get-tuple-element.262.gain_ref, bf16[320,2048]{1,0:T(8,128)(2,1)} %get-tuple-element.174.refs_0_, ...), custom_call_target="tpu_custom_call" | custom-call | flops 15099494400 | bytes 31457280 | tf_op jit(solution)/shard_map/input_back/pallas_call | solution.py:1125
  466.4 4.5 add_convert_fusion.1
  471.0 39.0 %mlp_back.3 = (f32[1024,1280]{1,0:T(8,128)}, f32[8,1280]{1,0:T(8,128)}, bf16[640,2048]{1,0:T(8,128)(2,1)}, bf16[1280,1024]{1,0:T(8,128)(2,1)}, bf16[1280,1024]{1,0:T(8,128)(2,1)}) custom-call(f32[1024,1280]{1,0:T(8,128)} %get-tuple-element.133.mid_ref, f32[1024,1280]{1,0:T(8,128)} %get-tuple-element.134.pre_ref, f32[1,1280]{1,0:T(1,128)} %get-tuple-element.263.gm_ref, ...), custom_call_target="tpu_custom_call" | custom-call | flops 20132659200 | bytes 52428800 | tf_op jit(solution)/shard_map/mlp_back/pallas_call | solution.py:968
  510.1 2.6 collective-permute-start.6
  512.6 37.4 %attention_backward.6 = (bf16[320,2048]{1,0:T(8,128)(2,1)}, bf16[320,2048]{1,0:T(8,128)(2,1)}, bf16[320,2048]{1,0:T(8,128)(2,1)}, f32[80,128]{1,0:T(8,128)}) custom-call(s32[1]{0:T(128)} %dynamic_slice.17.prefix_ref, s32[4]{0:T(128)} %fusion.21.order_ref, bf16[640,2048]{1,0:T(8,128)(2,1)} %get-tuple-element.126.q_ref, ...), custom_call_target="tpu_custom_call" | custom-call | flops 26843545600 | bytes 10485760 | tf_op jit(solution)/shard_map/attention_backward/pallas_call | solution.py:205
  550.1 10.5 %weight_grad.4 = bf16[1280,1024]{1,0:T(8,128)(2,1)} custom-call(bf16[1024,1280]{1,0:T(8,128)(2,1)} %get-tuple-element.186.own_ref, bf16[1024,1280]{1,0:T(8,128)(2,1)} %get-tuple-element.187.other_ref, bf16[320,2048]{1,0:T(8,128)(2,1)} %get-tuple-element.189.dq_ref.refs_3_, bf16[320,2048]{1,0:T(8,128)(2,1)} %get-tuple-element.190.dk_ref.refs_4_, ...), custom_call_target="tpu_custom_call" | custom-call | flops 5033164800 | bytes 15728640 | tf_op jit(solution)/shard_map/weight_grad/pallas_call | solution.py:1011
  560.7 3.0 collective-permute-start.8
  563.7 2.5 convert_select_fusion.3
  566.2 2.7 pad_maximum_fusion
  569.0 8.0 %collective-permute-done.8 = bf16[160,1024]{1,0:T(8,128)(2,1)S(1)} collective-permute-done((bf16[160,1024]{1,0:T(8,128)(2,1)S(1)}, bf16[160,1024]{1,0:T(8,128)(2,1)S(1)}, u32[]{:S(2)}, u32[]{:S(2)}) %collective-permute-start.8) | collective-permute-done | bytes 327712 | tf_op jit(solution)/shard_map/ppermute | solution.py:367
  577.1 1.8 collective-permute-start.7
  578.9 4.5 add_convert_fusion
  583.5 37.4 %attention_backward.7 = (bf16[320,2048]{1,0:T(8,128)(2,1)}, bf16[320,2048]{1,0:T(8,128)(2,1)}, bf16[320,2048]{1,0:T(8,128)(2,1)}, f32[80,128]{1,0:T(8,128)}) custom-call(s32[1]{0:T(128)} %dynamic_slice.17.prefix_ref, s32[4]{0:T(128)} %fusion.21.order_ref, bf16[640,2048]{1,0:T(8,128)(2,1)} %get-tuple-element.126.q_ref, ...), custom_call_target="tpu_custom_call" | custom-call | flops 26843545600 | bytes 10485760 | tf_op jit(solution)/shard_map/attention_backward/pallas_call | solution.py:205
  620.9 0.9 add_reduce_fusion.1
  621.9 0.7 concatenate.35.small_ref
  622.7 10.3 %weight_grad.5.piece_any = bf16[1280,1024]{1,0:T(8,128)(2,1)} custom-call(bf16[1024,1280]{1,0:T(8,128)(2,1)} %get-tuple-element.186.own_ref, bf16[1024,1280]{1,0:T(8,128)(2,1)} %get-tuple-element.187.other_ref, bf16[320,2048]{1,0:T(8,128)(2,1)} %get-tuple-element.213.dq_ref.refs_0_, bf16[320,2048]{1,0:T(8,128)(2,1)} %get-tuple-element.214.dk_ref.refs_1_, ...), custom_call_target="tpu_custom_call" | custom-call | flops 5033164800 | bytes 15728640 | tf_op jit(solution)/shard_map/weight_grad/pallas_call | solution.py:1011
  633.0 2.9 collective-permute-done.7.came_any
  635.8 58.3 %finish.1 = (f32[512,1280]{1,0:T(8,128)}, bf16[512,1280]{1,0:T(8,128)(2,1)}, f32[160,1024]{1,0:T(8,128)}, f32[8,1280]{1,0:T(8,128)}) custom-call(f32[1,1280]{1,0:T(1,128)} %get-tuple-element.264.gain_ref, f32[8,1280]{1,0:T(8,128)} %concatenate.35.small_ref, f32[1024,1280]{1,0:T(8,128)} %get-tuple-element.123.x_ref.x_any, ...), custom_call_target="tpu_custom_call" | custom-call | flops 10066329600 | bytes 31457280 | tf_op jit(solution)/shard_map/finish/pallas_call | solution.py:1323
  694.1 1.4 fusion.9
  695.7 1.2 copy.37
  696.9 0.6 fusion.20
  697.5 0.4 copy-done
  697.9 0.4 copy-done.2
  698.6 2.7 pad_maximum_fusion.1
  701.3 0.6 fusion.24
  701.9 1.0 bitcast_convert_fusion
  703.0 1.2 fusion.10
  (96 shorter events, 2.4 us)
Async XLA Ops:
  7.2 5.7 copy-start.3
  7.2 5.6 copy-start.4
  7.2 4.2 copy-start.18
  7.2 5.8 copy-start.7
  7.2 114.4 %all-gather.9.cloned.1.call-start = ((), (), s32[]{:S(2)}) async-start(), calls=%async_computation.8 | async-start | bytes 1843200 | tf_op jit(solution)/shard_map/all_gather | solution.py:1394
  9.2 139.0 %all-gather.11.cloned.1.call-start = ((), (), s32[]{:S(2)}) async-start(), calls=%async_computation.9 | async-start | bytes 1843200 | tf_op jit(solution)/shard_map/all_gather | solution.py:1394
  11.3 210.4 %all-gather.13.cloned.1.call-start = ((), (), s32[]{:S(2)}) async-start(), calls=%async_computation.10 | async-start | bytes 3686400 | tf_op jit(solution)/shard_map/all_gather | solution.py:1417
  11.4 0.6 copy-start.16
  14.1 106.9 %copy-start.14 = (f32[2,2,1280]{2,1,0:T(2,128)S(1)}, f32[2,2,1280]{2,1,0:T(2,128)}, u32[]{:S(2)}) copy-start(f32[2,2,1280]{2,1,0:T(2,128)} %param.15) | copy-start | bytes 61444
  121.6 26.6 %collective-permute-start = (bf16[2,160,640]{2,1,0:T(8,128)(2,1)S(1)}, bf16[2,160,640]{2,1,0:T(8,128)(2,1)S(1)}, u32[]{:S(2)}, u32[]{:S(2)}) collective-permute-start(bf16[2,160,640]{2,1,0:T(8,128)(2,1)S(1)} %get-tuple-element.125), channel_id=1, source_target_pairs={{0,2},{1,3},{2,0},{3,1},{4,6},{5,7},{6,4},{7,5},{8,10},{9,11},{10,... | collective-permute-start | bytes 1228808 | tf_op jit(solution)/shard_map/ppermute | solution.py:367
  126.6 23.5 %copy-start.23 = (s32[2]{0:T(128)S(1)}, s32[2]{0:T(128)}, u32[]{:S(2)}) copy-start(s32[2]{0:T(128)} %param.17) | copy-start | bytes 28
  149.2 126.3 %all-gather.15.cloned.1.call-start = ((), (), s32[]{:S(2)}) async-start(), calls=%async_computation.11 | async-start | bytes 3686400 | tf_op jit(solution)/shard_map/all_gather | solution.py:1417
  151.3 38.9 %collective-permute-start.1 = (bf16[1280,640]{1,0:T(8,128)(2,1)}, bf16[1280,640]{1,0:T(8,128)(2,1)S(1)}, u32[]{:S(2)}, u32[]{:S(2)}) collective-permute-start(bf16[1280,640]{1,0:T(8,128)(2,1)} %bitcast.118), channel_id=1, source_target_pairs={{0,2},{1,3},{2,0},{3,1},{4,6},{5,7},{6,4},{7,5},{8,10},{9,11},{10,... | collective-permute-start | bytes 4915208 | tf_op jit(solution)/shard_map/ppermute | solution.py:367
  151.4 70.3 %collective-permute-start.2 = (bf16[1280,640]{1,0:T(8,128)(2,1)}, bf16[1280,640]{1,0:T(8,128)(2,1)}, u32[]{:S(2)}, u32[]{:S(2)}) collective-permute-start(bf16[1280,640]{1,0:T(8,128)(2,1)} %bitcast.115), channel_id=1, source_target_pairs={{0,2},{1,3},{2,0},{3,1},{4,6},{5,7},{6,4},{7,5},{8,10},{9,11},{10,... | collective-permute-start | bytes 4915208 | tf_op jit(solution)/shard_map/ppermute | solution.py:367
  153.3 283.2 %reduce-scatter.5.cloned.1.call-start = ((), (), s32[]{:S(2)}) async-start(), calls=%async_computation.4 | async-start | bytes 2949120 | tf_op jit(solution)/shard_map/reduce_scatter | solution.py:1364
  190.2 1.2 copy-start.20
  221.7 53.8 %collective-permute-start.3 = (bf16[512,1280]{1,0:T(8,128)(2,1)S(1)}, bf16[512,1280]{1,0:T(8,128)(2,1)S(1)}, u32[]{:S(2)}, u32[]{:S(2)}) collective-permute-start(bf16[512,1280]{1,0:T(8,128)(2,1)S(1)} %fusion.1), channel_id=1, source_target_pairs={{0,2},{1,3},{2,0},{3,1},{4,6},{5,7},{6,4},{7,5},{8,10},{9,11},{10,... | collective-permute-start | bytes 3932168 | tf_op jit(solution)/shard_map/ppermute | solution.py:367
  275.5 25.4 %copy-start.21 = (bf16[512,1280]{1,0:T(8,128)(2,1)}, bf16[512,1280]{1,0:T(8,128)(2,1)S(1)}, u32[]{:S(2)}) copy-start(bf16[512,1280]{1,0:T(8,128)(2,1)S(1)} %collective-permute-done.3.refs_4_) | copy-start | bytes 3932164
  343.2 3.2 copy-start.11
  343.2 166.8 %reduce-scatter.7.cloned.1.call-start = ((), (), s32[]{:S(2)}) async-start(), calls=%async_computation.5 | async-start | bytes 2949120 | tf_op jit(solution)/shard_map/reduce_scatter | solution.py:1364
  344.7 50.0 %collective-permute-start.4 = (bf16[512,1280]{1,0:T(8,128)(2,1)S(1)}, bf16[512,1280]{1,0:T(8,128)(2,1)}, u32[]{:S(2)}, u32[]{:S(2)}) collective-permute-start(bf16[512,1280]{1,0:T(8,128)(2,1)S(1)} %fusion.2), channel_id=1, source_target_pairs={{0,2},{1,3},{2,0},{3,1},{4,6},{5,7},{6,4},{7,5},{8,10},{9,11},{10,... | collective-permute-start | bytes 3932168 | tf_op jit(solution)/shard_map/ppermute | solution.py:367
  347.0 231.9 %reduce-scatter.9.cloned.1.call-start = ((), (), s32[]{:S(2)}) async-start(), calls=%async_computation.6 | async-start | bytes 2949120 | tf_op jit(solution)/shard_map/reduce_scatter | solution.py:1364
  394.7 40.9 %copy-start.9 = (f32[80,128]{1,0:T(8,128)S(1)}, f32[80,128]{1,0:T(8,128)}, u32[]{:S(2)}) copy-start(f32[80,128]{1,0:T(8,128)} %get-tuple-element.210) | copy-start | bytes 122884
  394.7 71.7 %collective-permute-start.5 = (bf16[1280,1024]{1,0:T(8,128)(2,1)}, bf16[1280,1024]{1,0:T(8,128)(2,1)S(1)}, u32[]{:S(2)}, u32[]{:S(2)}) collective-permute-start(bf16[1280,1024]{1,0:T(8,128)(2,1)} %weight_grad.3), channel_id=1, source_target_pairs={{0,2},{1,3},{2,0},{3,1},{4,6},{5,7},{6,4},{7,5},{8,10},{9,11},{10,... | collective-permute-start | bytes 7864328 | tf_op jit(solution)/shard_map/ppermute | solution.py:367
  470.9 231.0 %reduce-scatter.11.cloned.1.call-start = ((), (), s32[]{:S(2)}) async-start(), calls=%async_computation.7 | async-start | bytes 2949120 | tf_op jit(solution)/shard_map/reduce_scatter | solution.py:1364
  510.1 67.0 %collective-permute-start.6 = (bf16[1280,1024]{1,0:T(8,128)(2,1)}, bf16[1280,1024]{1,0:T(8,128)(2,1)}, u32[]{:S(2)}, u32[]{:S(2)}) collective-permute-start(bf16[1280,1024]{1,0:T(8,128)(2,1)} %get-tuple-element.194), channel_id=1, source_target_pairs={{0,2},{1,3},{2,0},{3,1},{4,6},{5,7},{6,4},{7,5},{8,10},{9,11},{10,... | collective-permute-start | bytes 7864328 | tf_op jit(solution)/shard_map/ppermute | solution.py:367
  550.0 10.6 %copy-start.10 = (f32[8,1280]{1,0:T(8,128)S(1)}, f32[8,1280]{1,0:T(8,128)}, u32[]{:S(2)}) copy-start(f32[8,1280]{1,0:T(8,128)} %get-tuple-element.197) | copy-start | bytes 122884
  550.0 10.6 %copy-start.12 = (f32[8,1280]{1,0:T(8,128)S(1)}, f32[8,1280]{1,0:T(8,128)}, u32[]{:S(2)}) copy-start(f32[8,1280]{1,0:T(8,128)} %get-tuple-element.198) | copy-start | bytes 122884
  550.0 10.6 %copy-start.22 = (bf16[160,1024]{1,0:T(8,128)(2,1)S(1)}, bf16[160,1024]{1,0:T(8,128)(2,1)}, u32[]{:S(2)}) copy-start(bf16[160,1024]{1,0:T(8,128)(2,1)} %reduce-scatter.7.cloned.1.call-done) | copy-start | bytes 983044
  560.7 16.3 %collective-permute-start.8 = (bf16[160,1024]{1,0:T(8,128)(2,1)S(1)}, bf16[160,1024]{1,0:T(8,128)(2,1)S(1)}, u32[]{:S(2)}, u32[]{:S(2)}) collective-permute-start(bf16[160,1024]{1,0:T(8,128)(2,1)S(1)} %copy-done.22), channel_id=1, source_target_pairs={{0,2},{1,3},{2,0},{3,1},{4,6},{5,7},{6,4},{7,5},{8,10},{9,11},{10,... | collective-permute-start | bytes 983048 | tf_op jit(solution)/shard_map/ppermute | solution.py:367
  566.2 10.8 %copy-start.5 = (bf16[160,1024]{1,0:T(8,128)(2,1)S(1)}, bf16[160,1024]{1,0:T(8,128)(2,1)}, u32[]{:S(2)}) copy-start(bf16[160,1024]{1,0:T(8,128)(2,1)} %reduce-scatter.5.cloned.1.call-done) | copy-start | bytes 983044
  566.2 12.7 %copy-start.1 = (bf16[1280,1024]{1,0:T(8,128)(2,1)S(1)}, bf16[1280,1024]{1,0:T(8,128)(2,1)}, u32[]{:S(2)}) copy-start(bf16[1280,1024]{1,0:T(8,128)(2,1)} %get-tuple-element.201) | copy-start | bytes 7864324
  577.1 58.7 %collective-permute-start.7 = (bf16[1280,1024]{1,0:T(8,128)(2,1)}, bf16[1280,1024]{1,0:T(8,128)(2,1)}, u32[]{:S(2)}, u32[]{:S(2)}) collective-permute-start(bf16[1280,1024]{1,0:T(8,128)(2,1)} %weight_grad.4), channel_id=1, source_target_pairs={{0,2},{1,3},{2,0},{3,1},{4,6},{5,7},{6,4},{7,5},{8,10},{9,11},{10,... | collective-permute-start | bytes 7864328 | tf_op jit(solution)/shard_map/ppermute | solution.py:367
  583.5 37.5 %copy-start.8 = (f32[80,128]{1,0:T(8,128)S(1)}, f32[80,128]{1,0:T(8,128)}, u32[]{:S(2)}) copy-start(f32[80,128]{1,0:T(8,128)} %get-tuple-element.200) | copy-start | bytes 122884
  583.5 38.3 %copy-start.17 = (f32[2,80]{1,0:T(2,128)S(1)}, f32[2,80]{1,0:T(2,128)}, u32[]{:S(2)}) copy-start(f32[2,80]{1,0:T(2,128)} %copy-done.16) | copy-start | bytes 1924
  583.5 38.4 %copy-start.13 = (f32[1,1280]{1,0:T(1,128)S(1)}, f32[1,1280]{1,0:T(1,128)}, u32[]{:S(2)}) copy-start(f32[1,1280]{1,0:T(1,128)} %broadcast_in_dim.33) | copy-start | bytes 15364
  583.5 39.1 %copy-start.6 = (bf16[160,1024]{1,0:T(8,128)(2,1)S(1)}, bf16[160,1024]{1,0:T(8,128)(2,1)}, u32[]{:S(2)}) copy-start(bf16[160,1024]{1,0:T(8,128)(2,1)} %reduce-scatter.9.cloned.1.call-done) | copy-start | bytes 983044
  695.5 1.4 copy-start.15
  695.6 1.3 copy-start.19
  695.6 2.3 copy-start
  695.6 2.7 copy-start.2
Sparse Core Ops, SparseCore 0:
  10.8 67.4 all-gather.8
  81.0 49.6 all-gather.10
  149.3 62.9 all-gather.12
  214.9 60.5 all-gather.14
  343.4 72.0 reduce-scatter.4
  418.8 69.1 reduce-scatter.6
  491.5 69.3 reduce-scatter.8
  583.6 74.5 reduce-scatter.10

commit v9 on v8

--- a/solution.py
+++ b/solution.py
@@ -238,10 +238,10 @@
     return jnp.einsum(spec, *args, preferred_element_type=F32)
 
 
-def gather_kernel(pieces, pairs, outer, ring, shard_ref, block_ref, *refs):
+def gather_kernel(pieces, pairs, outer, ring, shard_ref, input_ref, *refs):
     outs = [refs[2 * m:2 * m + 2] for m in range(pairs)]
     got_ref = refs[2 * pairs]
-    send, recv, local = refs[2 * pairs + 1:]
+    wide_ref, block_ref, send, recv, local = refs[2 * pairs + 1:]
     f, t = lax.axis_index("fsdp"), lax.axis_index("tp")
     zz, yy = f // 2, f % 2
     across = {"tp": lax.rem(t + ring, 2 * ring)}
@@ -253,6 +253,8 @@
         pl.semaphore_signal(barrier, inc=1, device_id=peer, device_id_type=MESH)
     pl.semaphore_wait(barrier, len(peers))
     used = [0]
+    wide = pltpu.make_async_copy(input_ref.at[1 - t // ring], wide_ref, local.at[len(pieces)])
+    wide.start()
 
     def copy(src, dst, peer):
         slot = used[0]
@@ -291,7 +293,8 @@
     ahead = 3
     for i in range(min(ahead, count)):
         begin(i)
-    started = 0
+    wide.wait()
+    block_ref[...] = wide_ref[...].astype(BF16)
     for b in blocks[:2]:
         b.start()
     started = 2
@@ -331,7 +334,7 @@
     )
 
 
-def gather_call(shards, block, pieces, fsdp, ring):
+def gather_call(shards, inputs, pieces, fsdp, ring):
     pairs, rows, w = shards.shape
     outer = fsdp // 2
     slots = 4 + len(pieces) * (outer + 2)
@@ -339,17 +342,19 @@
     got = pl.pallas_call(
         functools.partial(gather_kernel, pieces, pairs, outer, ring),
         out_shape=[jax.ShapeDtypeStruct((outer, 2, rows, w), BF16)] * (2 * pairs)
-        + [jax.ShapeDtypeStruct(block.shape, block.dtype)],
+        + [jax.ShapeDtypeStruct(inputs.shape[1:], BF16)],
         in_specs=[any_spec] * 2,
         out_specs=[any_spec] * (2 * pairs + 1),
         scratch_shapes=[
+            pltpu.VMEM(inputs.shape[1:], F32),
+            pltpu.VMEM(inputs.shape[1:], BF16),
             pltpu.SemaphoreType.DMA((slots,)),
             pltpu.SemaphoreType.DMA((slots,)),
-            pltpu.SemaphoreType.DMA((len(pieces),)),
+            pltpu.SemaphoreType.DMA((len(pieces) + 1,)),
         ],
-        compiler_params=pltpu.CompilerParams(collective_id=0, has_side_effects=True),
+        compiler_params=pltpu.CompilerParams(vmem_limit_bytes=VMEM_LIMIT, collective_id=0, has_side_effects=True),
         name="gather_weights",
-    )(shards, block)
+    )(shards, inputs)
     return [a.reshape(outer * 2 * rows, w) for a in got[:-1]], got[-1]
 
 
@@ -715,9 +720,12 @@
     )(gain, scale, *plain(weights), *xs)
 
 
-def middle_kernel(w, low, steps, index, x_ref, gm_ref, att_any, *refs):
+def middle_kernel(w, low, steps, index, ring, x_ref, gm_ref, att_any, *refs):
     weights, refs = refs[:4], refs[4:]
     mid_ref, pre_ref, res_ref, up_out, down_out, out_out = refs[:6]
+    if ring:
+        half_out, half = refs[6], refs[-1]
+        refs = refs[:6] + refs[7:-1]
     (up_mat, down_mat, out_mat, blocks, vo_side, att, part, got, load, store, send, recv) = refs[6:]
     i = pl.program_id(0)
     far, rows_steps = steps
@@ -737,7 +745,7 @@
         return copies
 
     def stores():
-        pairs = ((up_mat, up_out), (down_mat, down_out), (out_mat, out_out))
+        pairs = [(up_mat, up_out), (down_mat, down_out), (out_mat, out_out)]
         return [pltpu.make_async_copy(src, dst, store.at[n]) for n, (src, dst) in enumerate(pairs)]
 
     def push_block(s):
@@ -794,15 +802,26 @@
         pre = dot(h_m, up_mat[...])
         pre_ref[...] = pre
         hidden = (pre / (1.0 + jnp.exp(-pre))).astype(BF16)
-        res_ref[...] = mid + dot(hidden, down_mat[...], NT)
+        res = mid + dot(hidden, down_mat[...], NT)
+        res_ref[...] = res
+        if ring:
+            per = rows_steps // 2
+
+            @pl.when(at // per == 1 - lax.axis_index("tp") // ring)
+            def _():
+                half[pl.ds(pl.multiple_of(lax.rem(at, per) * bt, bt), bt)] = res.astype(BF16)
 
     @pl.when(at == rows_steps - 1)
     def _():
+        if ring:
+            leave = pltpu.make_async_copy(half, half_out, store.at[3])
+            leave.start()
+            leave.wait()
         for c in stores():
             c.wait()
 
 
-def middle_call(x, att, gain_m, vo, un, call):
+def middle_call(x, att, gain_m, vo, un, call, ring=0):
     rows, d = x.shape
     w2 = plain(vo)[0].shape[-1]
     w, ff = w2 // 2, 2 * w2
@@ -815,15 +834,17 @@
     mats = [(d, ff), (d, ff), (d, w2)]
     slots = 2 + steps[0]
     return pl.pallas_call(
-        functools.partial(middle_kernel, w, low, steps, stack_index(weights)),
+        functools.partial(middle_kernel, w, low, steps, stack_index(weights), ring),
         grid=(sum(steps),),
         in_specs=[row, fixed((1, d))] + [ANY] * 5,
-        out_specs=[row, wide, row] + [ANY] * 3,
-        out_shape=[shape_of((rows, d), F32), shape_of((rows, ff), F32), shape_of((rows, d), F32)] + [shape_of(m) for m in mats],
+        out_specs=[row, wide, row] + [ANY] * (4 if ring else 3),
+        out_shape=[shape_of((rows, d), F32), shape_of((rows, ff), F32), shape_of((rows, d), F32)] + [shape_of(m) for m in mats]
+        + ([shape_of((rows // 2, d))] if ring else []),
         scratch_shapes=[pltpu.VMEM(m, BF16) for m in mats]
         + [pltpu.VMEM((4, d, w2), BF16), pltpu.VMEM((2, d, w2 - low), BF16), pltpu.VMEM(att.shape, BF16)]
         + [pltpu.VMEM((rows, d), BF16)] * 2
-        + [pltpu.SemaphoreType.DMA((5,)), pltpu.SemaphoreType.DMA((3,)), pltpu.SemaphoreType.DMA((slots,)), pltpu.SemaphoreType.DMA((slots,))],
+        + [pltpu.SemaphoreType.DMA((5,)), pltpu.SemaphoreType.DMA((4,)), pltpu.SemaphoreType.DMA((slots,)), pltpu.SemaphoreType.DMA((slots,))]
+        + ([pltpu.VMEM((rows // 2, d), BF16)] if ring else []),
         compiler_params=pltpu.CompilerParams(vmem_limit_bytes=VMEM_LIMIT, collective_id=call, has_side_effects=True),
         cost_estimate=cost(2 * rows * d * (2 * w2 + 2 * ff), 30 * rows * d),
         name="middle",
@@ -1386,8 +1407,7 @@
         axis=1,
     )
 
-    block = plan.pick(inputs, 1 - plan.seq).astype(BF16)
-    got, other = gather_call(pairs[0, :2], block, pieces_of(2, pairs.shape[2]), plan.fsdp, plan.ring)
+    got, other = gather_call(pairs[0, :2], inputs, pieces_of(2, pairs.shape[2]), plan.fsdp, plan.ring)
     qk0, vo0 = got[0:2], got[2:4]
 
     def along(l, m):
@@ -1423,7 +1443,10 @@
         else:
             att, un1_rows, cot_got = after(att, un1_rows, cot_got)
             un = stacked(un1_rows)
-        mid, pre, res, *mats = middle_call(x, att, norm_gain[l, 1][None], vo, un, 5 + l)
+        last = plan.ring if l == layers - 1 else 0
+        mid, pre, res, *mats = middle_call(x, att, norm_gain[l, 1][None], vo, un, 5 + l, last)
+        if last:
+            *mats, out_send = mats
         if l == 0:
             res, cotangent = after(res, cotangent)
             cot_block = plan.pick(cotangent, 1 - plan.seq).astype(BF16)
@@ -1435,7 +1458,6 @@
         x = res
     g = cotangent, cot_got
     out_blocks = x.reshape(seqs, positions, d)
-    out_send = plan.pick(out_blocks, 1 - plan.seq).astype(BF16)
     cot_got, out_send = after(cot_got, out_send)
     g = cotangent, cot_got
     out_got = plan.across(out_send)

time: 718 us -> 717 us (level)
  Pallas kernels: 606 us -> 628 us
  starting transfers between devices: 20.2 us -> 8.12 us
    ppermute x9, starting transfers between devices: 19.7 us -> 7.17 us  [across(): return lax.ppermute(a, 'tp', [(t, (t + self.ring) % n) for t in range(n)])]
    pallas_call x4, Pallas kernels: 150 us -> 161 us  [attention_backward(): pl.pallas_call(functools.partial(backward_kernel, pair=pair, dh=dh, bq=bq...]
  transfers between devices with their start and end apart: 17 -> 17, of which waited for: 5 -> 4; matrix products, arithmetic and copies ran while one was open for 5% -> 5% of each run, Pallas kernels for 76% -> 78%
where the time goes in v9:
time: 717 us; the launch traced here: 712 us
  Pallas kernels  628 us (88%)
  other arithmetic  29.1 us (4%)
  waiting for transfers between devices  19.7 us (3%)
  between operations  15.2 us (2%)
  local copies, waits for them, and re-layouts  12.1 us (2%)
  starting transfers between devices  8.12 us (1%)
    pallas_call x4, Pallas kernels, attention_backward(): pl.pallas_call(functools.partial(backward_kernel, pair=pair, dh=dh, bq=bq...  161 us
    pallas_call x1, Pallas kernels, gather_call(): pl.pallas_call(functools.partial(gather_kernel, pieces, pairs, outer, rin...  105 us
    pallas_call x2, Pallas kernels, mlp_back(): pl.pallas_call(functools.partial(mlp_back_kernel, w, steps, ring), grid=(...  78.9 us
    pallas_call x2, Pallas kernels, attention_forward(): pl.pallas_call(functools.partial(forward_kernel, pair=pair, dh=dh, bq=bq,...  66.9 us
    pallas_call x1, Pallas kernels, finish(): pl.pallas_call(functools.partial(finish_kernel, w, low, far, own_steps, o...  57.6 us
    pallas_call x2, Pallas kernels, middle_call(): pl.pallas_call(functools.partial(middle_kernel, w, low, steps, stack_inde...  55.9 us
    pallas_call x2, Pallas kernels, project(): pl.pallas_call(functools.partial(project_kernel, w, low, steps, stack_ind...  41.4 us
    pallas_call x3, Pallas kernels, weight_grad(): pl.pallas_call(functools.partial(weight_grad_kernel, w), grid=(d // bd,),...  31.2 us
  transfers between devices with their start and end apart: 17, of which 4 were waited for; matrix products, arithmetic and copies ran while one was open for 5% of the time, Pallas kernels for 78%

profile of v9, /device:TPU:0, one launch (start us, length us, event | category | flops | bytes accessed | tf_op | source)
XLA Modules:
  0.0 712.2 jit_solution(11671723841605657567)
XLA Ops:
  7.3 1.9 fusion.15
  9.2 1.3 slice_bitcast_fusion.2
  10.5 0.8 fusion.16
  11.4 0.5 copy-done.16
  11.9 0.9 broadcast_in_dim_tile.8.scale_ref
  12.8 0.1 fusion.10
  13.0 0.3 fusion.11
  13.2 0.8 fusion.13
  14.1 105.4 %gather_weights.1 = (bf16[4,2,160,640]{3,2,1,0:T(8,128)(2,1)}, bf16[4,2,160,640]{3,2,1,0:T(8,128)(2,1)}, bf16[4,2,160,640]{3,2,1,0:T(8,128)(2,1)}, bf16[4,2,160,640]{3,2,1,0:T(8,128)(2,1)}, bf16[512,1280]{1,0:T(8,128)(2,1)}) custom-call(bf16[2,160,640]{2,1,0:T(8,128)(2,1)} %get-tuple-element.261.shard_ref, f32[2,512,1280]{2,1,0:T(8,128)} %refs_4_.1), custom_call_target="tpu_custom_call" | custom-call | tf_op jit(solution)/shard_map/gather_weights/pallas_call | solution.py:342
  119.5 0.6 slice_bitcast_fusion.3
  120.1 4.5 collective-permute-start
  124.7 21.7 %project.2 = (bf16[1024,1280]{1,0:T(8,128)(2,1)}, bf16[1024,1280]{1,0:T(8,128)(2,1)}, bf16[640,2048]{1,0:T(8,128)(2,1)}, bf16[640,2048]{1,0:T(8,128)(2,1)}, bf16...) custom-call(f32[1,1280]{1,0:T(1,128)} %get-tuple-element.266.gain_ref, f32[640,1]{1,0:T(8,128)} %broadcast_in_dim_tile.8.scale_ref, ...), custom_call_target="tpu_custom_call" | custom-call | flops 10066329600 | bytes 15728640 | tf_op jit(solution)/shard_map/project/pallas_call | solution.py:705
  146.4 1.0 pad_maximum_fusion.7
  147.5 0.9 broadcast_in_dim_tile.9.scale_ref
  148.4 0.6 dynamic_slice.10.prefix_ref
  149.0 0.5 fusion.19.order_ref
  149.5 2.0 collective-permute-start.2
  151.5 0.3 reduce-scatter.5.cloned.1.call-start
  151.8 33.5 %attention_forward.2 = (bf16[640,2048]{1,0:T(8,128)(2,1)}, f32[8,1,2048]{2,1,0:T(1,128)}) custom-call(s32[1]{0:T(128)} %dynamic_slice.10.prefix_ref, s32[4]{0:T(128)} %fusion.19.order_ref, bf16[640,2048]{1,0:T(8,128)(2,1)} %get-tuple-element.127.q_ref, bf16[640,2048]{1,0:T(8,128)(2,1)} %get-tuple-element.128.k_ref, bf16[640,2048]{1,0:T(8,128)(2,1)} %get-tuple-element.129.v_ref), custom_call_target="tpu_custom_call" | custom-call | flops 20132659200 | bytes 10485760 | tf_op jit(solution)/shard_map/attention_forward/pallas_call | solution.py:95
  185.3 3.0 collective-permute-done.1.refs_3_
  188.3 25.0 %middle.2 = (f32[1024,1280]{1,0:T(8,128)}, f32[1024,1280]{1,0:T(8,128)}, f32[1024,1280]{1,0:T(8,128)}, bf16[1280,1280]{1,0:T(8,128)(2,1)}, bf16[1280,1280]{1,0:T(8,128)(2,1)}, /*index=5*/bf16[1280,640]{1,0:T(8,128)(2,1)}) custom-call(f32[1024,1280]{1,0:T(8,128)} %get-tuple-element.124.x_ref.x_any, f32[1,1280]{1,0:T(1,128)} %get-tuple-element.265.gm_ref, ...), custom_call_target="tpu_custom_call" | custom-call | flops 10066329600 | bytes 39321600 | tf_op jit(solution)/shard_map/middle/pallas_call | solution.py:836
  213.3 1.9 fusion
  215.2 5.4 collective-permute-done.2.refs_1_.refs_7_
  220.6 19.7 %project.3 = (bf16[1024,1280]{1,0:T(8,128)(2,1)}, bf16[1024,1280]{1,0:T(8,128)(2,1)}, bf16[640,2048]{1,0:T(8,128)(2,1)}, bf16[640,2048]{1,0:T(8,128)(2,1)}, bf16[640,2048]{1,0:T(8,128)(2,1)}) custom-call(f32[1,1280]{1,0:T(1,128)} %get-tuple-element.264.gain_ref, f32[640,1]{1,0:T(8,128)} %broadcast_in_dim_tile.9.scale_ref, bf16[1280,640]{1,0:T(8,128)(2,1)} %bitcast.111, ...), custom_call_target="tpu_custom_call" | custom-call | flops 10066329600 | bytes 15728640 | tf_op jit(solution)/shard_map/project/pallas_call | solution.py:705
  240.4 33.3 %attention_forward.3 = (bf16[640,2048]{1,0:T(8,128)(2,1)}, f32[8,1,2048]{2,1,0:T(1,128)}) custom-call(s32[1]{0:T(128)} %dynamic_slice.10.prefix_ref, s32[4]{0:T(128)} %fusion.19.order_ref, bf16[640,2048]{1,0:T(8,128)(2,1)} %get-tuple-element.147.q_ref, bf16[640,2048]{1,0:T(8,128)(2,1)} %get-tuple-element.148.k_ref, bf16[640,2048]{1,0:T(8,128)(2,1)} %get-tuple-element.149.v_ref), custom_call_target="tpu_custom_call" | custom-call | flops 20132659200 | bytes 10485760 | tf_op jit(solution)/shard_map/attention_forward/pallas_call | solution.py:95
  273.7 31.0 %middle.3 = (f32[1024,1280]{1,0:T(8,128)}, f32[1024,1280]{1,0:T(8,128)}, f32[1024,1280]{1,0:T(8,128)}, bf16[1280,1280]{1,0:T(8,128)(2,1)}, bf16[1280,1280]{1,0:T...) custom-call(f32[1024,1280]{1,0:T(8,128)} %get-tuple-element.144.refs_4_.x_ref, ...), custom_call_target="tpu_custom_call" | custom-call | flops 10066329600 | bytes 39321600 | tf_op jit(solution)/shard_map/middle/pallas_call | solution.py:836
  304.7 40.1 %mlp_back.2 = (f32[1024,1280]{1,0:T(8,128)}, f32[8,1280]{1,0:T(8,128)}, bf16[640,2048]{1,0:T(8,128)(2,1)}, bf16[1280,1024]{1,0:T(8,128)(2,1)}, bf16[1280,1024]{1,0:T(8,128)(2,1)}) custom-call(f32[1024,1280]{1,0:T(8,128)} %get-tuple-element.154.mid_ref, f32[1024,1280]{1,0:T(8,128)} %get-tuple-element.155.pre_ref, f32[1,1280]{1,0:T(1,128)} %get-tuple-element.267.gm_ref, ...), custom_call_target="tpu_custom_call" | custom-call | flops 20132659200 | bytes 52428800 | tf_op jit(solution)/shard_map/mlp_back/pallas_call | solution.py:989
  344.8 0.4 reduce-scatter.7.cloned.1.call-start
  345.2 0.7 copy.33.scale_ref
  346.0 0.7 copy.35.scale_ref
  346.7 0.6 broadcast_in_dim.33
  347.4 40.2 %attention_backward.4 = (bf16[320,2048]{1,0:T(8,128)(2,1)}, bf16[320,2048]{1,0:T(8,128)(2,1)}, bf16[320,2048]{1,0:T(8,128)(2,1)}, f32[80,128]{1,0:T(8,128)}) custom-call(s32[1]{0:T(128)} %dynamic_slice.10.prefix_ref, s32[4]{0:T(128)} %fusion.19.order_ref, bf16[640,2048]{1,0:T(8,128)(2,1)} %get-tuple-element.147.q_ref, ...), custom_call_target="tpu_custom_call" | custom-call | flops 26843545600 | bytes 10485760 | tf_op jit(solution)/shard_map/attention_backward/pallas_call | solution.py:205
  387.5 10.3 %weight_grad.3 = bf16[1280,1024]{1,0:T(8,128)(2,1)} custom-call(bf16[1024,1280]{1,0:T(8,128)(2,1)} %get-tuple-element.164.own_ref.refs_10_, bf16[1024,1280]{1,0:T(8,128)(2,1)} %get-tuple-element.165.other_ref.refs_11_, bf16[320,2048]{1,0:T(8,128)(2,1)} %get-tuple-element.167.dq_ref.refs_3_, bf16[320,2048]{1,0:T(8,128)(2,1)} %get-tuple-element.168.dk_ref.refs_4_, ...), custom_call_target="tpu_custom_call" | custom-call | flops 5033164800 | bytes 15728640 | tf_op jit(solution)/shard_map/weight_grad/pallas_call | solution.py:1032
  398.0 40.4 %attention_backward.5 = (bf16[320,2048]{1,0:T(8,128)(2,1)}, bf16[320,2048]{1,0:T(8,128)(2,1)}, bf16[320,2048]{1,0:T(8,128)(2,1)}, f32[80,128]{1,0:T(8,128)}) custom-call(s32[1]{0:T(128)} %dynamic_slice.10.prefix_ref, s32[4]{0:T(128)} %fusion.19.order_ref, bf16[640,2048]{1,0:T(8,128)(2,1)} %get-tuple-element.147.q_ref, ...), custom_call_target="tpu_custom_call" | custom-call | flops 26843545600 | bytes 10485760 | tf_op jit(solution)/shard_map/attention_backward/pallas_call | solution.py:205
  438.4 0.9 add_reduce_fusion
  439.3 29.8 %input_back.1 = (f32[1024,1280]{1,0:T(8,128)}, f32[8,1280]{1,0:T(8,128)}, bf16[1280,1024]{1,0:T(8,128)(2,1)}) custom-call(f32[1024,1280]{1,0:T(8,128)} %get-tuple-element.144.refs_4_.x_ref, f32[1024,1280]{1,0:T(8,128)} %get-tuple-element.162.g_ref, f32[1,1280]{1,0:T(1,128)} %get-tuple-element.264.gain_ref, bf16[320,2048]{1,0:T(8,128)(2,1)} %get-tuple-element.175.refs_0_, ...), custom_call_target="tpu_custom_call" | custom-call | flops 15099494400 | bytes 31457280 | tf_op jit(solution)/shard_map/input_back/pallas_call | solution.py:1146
  469.1 4.5 add_convert_fusion.1
  473.6 38.9 %mlp_back.3 = (f32[1024,1280]{1,0:T(8,128)}, f32[8,1280]{1,0:T(8,128)}, bf16[640,2048]{1,0:T(8,128)(2,1)}, bf16[1280,1024]{1,0:T(8,128)(2,1)}, bf16[1280,1024]{1,0:T(8,128)(2,1)}) custom-call(f32[1024,1280]{1,0:T(8,128)} %get-tuple-element.134.mid_ref, f32[1024,1280]{1,0:T(8,128)} %get-tuple-element.135.pre_ref, f32[1,1280]{1,0:T(1,128)} %get-tuple-element.265.gm_ref, ...), custom_call_target="tpu_custom_call" | custom-call | flops 20132659200 | bytes 52428800 | tf_op jit(solution)/shard_map/mlp_back/pallas_call | solution.py:989
  512.5 0.1 collective-permute-start.6
  512.6 40.2 %attention_backward.6 = (bf16[320,2048]{1,0:T(8,128)(2,1)}, bf16[320,2048]{1,0:T(8,128)(2,1)}, bf16[320,2048]{1,0:T(8,128)(2,1)}, f32[80,128]{1,0:T(8,128)}) custom-call(s32[1]{0:T(128)} %dynamic_slice.10.prefix_ref, s32[4]{0:T(128)} %fusion.19.order_ref, bf16[640,2048]{1,0:T(8,128)(2,1)} %get-tuple-element.127.q_ref, ...), custom_call_target="tpu_custom_call" | custom-call | flops 26843545600 | bytes 10485760 | tf_op jit(solution)/shard_map/attention_backward/pallas_call | solution.py:205
  552.8 10.5 %weight_grad.4 = bf16[1280,1024]{1,0:T(8,128)(2,1)} custom-call(bf16[1024,1280]{1,0:T(8,128)(2,1)} %get-tuple-element.187.own_ref, bf16[1024,1280]{1,0:T(8,128)(2,1)} %get-tuple-element.188.other_ref, bf16[320,2048]{1,0:T(8,128)(2,1)} %get-tuple-element.190.dq_ref.refs_3_, bf16[320,2048]{1,0:T(8,128)(2,1)} %get-tuple-element.191.dk_ref.refs_4_, ...), custom_call_target="tpu_custom_call" | custom-call | flops 5033164800 | bytes 15728640 | tf_op jit(solution)/shard_map/weight_grad/pallas_call | solution.py:1032
  563.5 2.5 convert_select_fusion.3
  566.1 2.7 pad_maximum_fusion
  568.8 9.9 %collective-permute-done.8 = bf16[160,1024]{1,0:T(8,128)(2,1)S(1)} collective-permute-done((bf16[160,1024]{1,0:T(8,128)(2,1)S(1)}, bf16[160,1024]{1,0:T(8,128)(2,1)S(1)}, u32[]{:S(2)}, u32[]{:S(2)}) %collective-permute-start.8) | collective-permute-done | bytes 327712 | tf_op jit(solution)/shard_map/ppermute | solution.py:372
  578.7 0.1 add_bitcast_fusion
  578.8 0.4 collective-permute-start.7
  579.2 4.5 add_convert_fusion
  583.8 40.2 %attention_backward.7 = (bf16[320,2048]{1,0:T(8,128)(2,1)}, bf16[320,2048]{1,0:T(8,128)(2,1)}, bf16[320,2048]{1,0:T(8,128)(2,1)}, f32[80,128]{1,0:T(8,128)}) custom-call(s32[1]{0:T(128)} %dynamic_slice.10.prefix_ref, s32[4]{0:T(128)} %fusion.19.order_ref, bf16[640,2048]{1,0:T(8,128)(2,1)} %get-tuple-element.127.q_ref, ...), custom_call_target="tpu_custom_call" | custom-call | flops 26843545600 | bytes 10485760 | tf_op jit(solution)/shard_map/attention_backward/pallas_call | solution.py:205
  624.0 0.9 add_reduce_fusion.1
  625.0 0.7 concatenate.35.small_ref
  625.7 10.3 %weight_grad.5.piece_any = bf16[1280,1024]{1,0:T(8,128)(2,1)} custom-call(bf16[1024,1280]{1,0:T(8,128)(2,1)} %get-tuple-element.187.own_ref, bf16[1024,1280]{1,0:T(8,128)(2,1)} %get-tuple-element.188.other_ref, bf16[320,2048]{1,0:T(8,128)(2,1)} %get-tuple-element.215.dq_ref.refs_0_, bf16[320,2048]{1,0:T(8,128)(2,1)} %get-tuple-element.216.dk_ref.refs_1_, ...), custom_call_target="tpu_custom_call" | custom-call | flops 5033164800 | bytes 15728640 | tf_op jit(solution)/shard_map/weight_grad/pallas_call | solution.py:1032
  636.0 1.2 collective-permute-done.7.came_any
  637.2 57.6 %finish.1 = (f32[512,1280]{1,0:T(8,128)}, bf16[512,1280]{1,0:T(8,128)(2,1)}, f32[160,1024]{1,0:T(8,128)}, f32[8,1280]{1,0:T(8,128)}) custom-call(f32[1,1280]{1,0:T(1,128)} %get-tuple-element.266.gain_ref, f32[8,1280]{1,0:T(8,128)} %concatenate.35.small_ref, f32[1024,1280]{1,0:T(8,128)} %get-tuple-element.124.x_ref.x_any, ...), custom_call_target="tpu_custom_call" | custom-call | flops 10066329600 | bytes 31457280 | tf_op jit(solution)/shard_map/finish/pallas_call | solution.py:1344
  694.9 1.4 fusion.7
  696.4 0.1 pad_maximum_fusion.2
  696.5 1.2 copy.37
  697.7 0.6 fusion.18
  698.3 0.4 copy-done
  698.6 0.4 copy-done.2
  699.0 0.4 convert_select_fusion.1
  699.4 2.7 pad_maximum_fusion.1
  702.1 0.6 fusion.22
  702.7 1.0 bitcast_convert_fusion
  703.7 1.2 fusion.8
  (96 shorter events, 1.0 us)
Async XLA Ops:
  7.2 5.6 copy-start.3
  7.2 5.6 copy-start.4
  7.2 4.2 copy-start.18
  7.2 5.8 copy-start.7
  7.2 112.9 %all-gather.9.cloned.1.call-start = ((), (), s32[]{:S(2)}) async-start(), calls=%async_computation.8 | async-start | bytes 1843200 | tf_op jit(solution)/shard_map/all_gather | solution.py:1414
  9.2 137.2 %all-gather.11.cloned.1.call-start = ((), (), s32[]{:S(2)}) async-start(), calls=%async_computation.9 | async-start | bytes 1843200 | tf_op jit(solution)/shard_map/all_gather | solution.py:1414
  11.3 209.3 %all-gather.13.cloned.1.call-start = ((), (), s32[]{:S(2)}) async-start(), calls=%async_computation.10 | async-start | bytes 3686400 | tf_op jit(solution)/shard_map/all_gather | solution.py:1437
  11.4 0.6 copy-start.16
  14.1 105.4 %copy-start.14 = (f32[2,2,1280]{2,1,0:T(2,128)S(1)}, f32[2,2,1280]{2,1,0:T(2,128)}, u32[]{:S(2)}) copy-start(f32[2,2,1280]{2,1,0:T(2,128)} %param.15) | copy-start | bytes 61444
  120.1 26.3 %collective-permute-start = (bf16[2,160,640]{2,1,0:T(8,128)(2,1)S(1)}, bf16[2,160,640]{2,1,0:T(8,128)(2,1)S(1)}, u32[]{:S(2)}, u32[]{:S(2)}) collective-permute-start(bf16[2,160,640]{2,1,0:T(8,128)(2,1)S(1)} %get-tuple-element.126), channel_id=1, source_target_pairs={{0,2},{1,3},{2,0},{3,1},{4,6},{5,7},{6,4},{7,5},{8,10},{9,11},{10,... | collective-permute-start | bytes 1228808 | tf_op jit(solution)/shard_map/ppermute | solution.py:372
  124.7 23.7 %copy-start.24 = (s32[2]{0:T(128)S(1)}, s32[2]{0:T(128)}, u32[]{:S(2)}) copy-start(s32[2]{0:T(128)} %param.17) | copy-start | bytes 28
  124.7 24.8 %copy-start.20 = (bf16[1,1280,640]{2,1,0:T(8,128)(2,1)S(1)}, bf16[1,1280,640]{2,1,0:T(8,128)(2,1)}, u32[]{:S(2)}) copy-start(bf16[1,1280,640]{2,1,0:T(8,128)(2,1)} %all-gather.9.cloned.1.call-done) | copy-start | bytes 4915204
  147.4 126.3 %all-gather.15.cloned.1.call-start = ((), (), s32[]{:S(2)}) async-start(), calls=%async_computation.11 | async-start | bytes 3686400 | tf_op jit(solution)/shard_map/all_gather | solution.py:1437
  149.5 38.8 %collective-permute-start.1 = (bf16[1280,640]{1,0:T(8,128)(2,1)S(1)}, bf16[1280,640]{1,0:T(8,128)(2,1)}, u32[]{:S(2)}, u32[]{:S(2)}) collective-permute-start(bf16[1280,640]{1,0:T(8,128)(2,1)S(1)} %bitcast.114), channel_id=1, source_target_pairs={{0,2},{1,3},{2,0},{3,1},{4,6},{5,7},{6,4},{7,5},{8,10},{9,11},{10,... | collective-permute-start | bytes 4915208 | tf_op jit(solution)/shard_map/ppermute | solution.py:372
  149.5 71.0 %collective-permute-start.2 = (bf16[1280,640]{1,0:T(8,128)(2,1)}, bf16[1280,640]{1,0:T(8,128)(2,1)}, u32[]{:S(2)}, u32[]{:S(2)}) collective-permute-start(bf16[1280,640]{1,0:T(8,128)(2,1)} %bitcast.110), channel_id=1, source_target_pairs={{0,2},{1,3},{2,0},{3,1},{4,6},{5,7},{6,4},{7,5},{8,10},{9,11},{10,... | collective-permute-start | bytes 4915208 | tf_op jit(solution)/shard_map/ppermute | solution.py:372
  151.5 287.7 %reduce-scatter.5.cloned.1.call-start = ((), (), s32[]{:S(2)}) async-start(), calls=%async_computation.4 | async-start | bytes 2949120 | tf_op jit(solution)/shard_map/reduce_scatter | solution.py:1385
  220.6 53.1 %collective-permute-start.3 = (bf16[512,1280]{1,0:T(8,128)(2,1)S(1)}, bf16[512,1280]{1,0:T(8,128)(2,1)S(1)}, u32[]{:S(2)}, u32[]{:S(2)}) collective-permute-start(bf16[512,1280]{1,0:T(8,128)(2,1)S(1)} %fusion), channel_id=1, source_target_pairs={{0,2},{1,3},{2,0},{3,1},{4,6},{5,7},{6,4},{7,5},{8,10},{9,11},{10,... | collective-permute-start | bytes 3932168 | tf_op jit(solution)/shard_map/ppermute | solution.py:372
  273.7 31.0 %copy-start.22 = (bf16[512,1280]{1,0:T(8,128)(2,1)}, bf16[512,1280]{1,0:T(8,128)(2,1)S(1)}, u32[]{:S(2)}) copy-start(bf16[512,1280]{1,0:T(8,128)(2,1)S(1)} %collective-permute-done.3.refs_4_) | copy-start | bytes 3932164
  344.7 1.9 copy-start.21
  344.8 1.9 copy-start.11
  344.8 167.7 %reduce-scatter.7.cloned.1.call-start = ((), (), s32[]{:S(2)}) async-start(), calls=%async_computation.5 | async-start | bytes 2949120 | tf_op jit(solution)/shard_map/reduce_scatter | solution.py:1385
  346.7 51.2 %collective-permute-start.4 = (bf16[512,1280]{1,0:T(8,128)(2,1)S(1)}, bf16[512,1280]{1,0:T(8,128)(2,1)}, u32[]{:S(2)}, u32[]{:S(2)}) collective-permute-start(bf16[512,1280]{1,0:T(8,128)(2,1)S(1)} %copy-done.21), channel_id=1, source_target_pairs={{0,2},{1,3},{2,0},{3,1},{4,6},{5,7},{6,4},{7,5},{8,10},{9,11},{10,... | collective-permute-start | bytes 3932168 | tf_op jit(solution)/shard_map/ppermute | solution.py:372
  347.3 231.8 %reduce-scatter.9.cloned.1.call-start = ((), (), s32[]{:S(2)}) async-start(), calls=%async_computation.6 | async-start | bytes 2949120 | tf_op jit(solution)/shard_map/reduce_scatter | solution.py:1385
  397.9 40.5 %copy-start.9 = (f32[80,128]{1,0:T(8,128)S(1)}, f32[80,128]{1,0:T(8,128)}, u32[]{:S(2)}) copy-start(f32[80,128]{1,0:T(8,128)} %get-tuple-element.212) | copy-start | bytes 122884
  397.9 71.2 %collective-permute-start.5 = (bf16[1280,1024]{1,0:T(8,128)(2,1)}, bf16[1280,1024]{1,0:T(8,128)(2,1)S(1)}, u32[]{:S(2)}, u32[]{:S(2)}) collective-permute-start(bf16[1280,1024]{1,0:T(8,128)(2,1)} %weight_grad.3), channel_id=1, source_target_pairs={{0,2},{1,3},{2,0},{3,1},{4,6},{5,7},{6,4},{7,5},{8,10},{9,11},{10,... | collective-permute-start | bytes 7864328 | tf_op jit(solution)/shard_map/ppermute | solution.py:372
  473.6 229.1 %reduce-scatter.11.cloned.1.call-start = ((), (), s32[]{:S(2)}) async-start(), calls=%async_computation.7 | async-start | bytes 2949120 | tf_op jit(solution)/shard_map/reduce_scatter | solution.py:1385
  512.5 66.3 %collective-permute-start.6 = (bf16[1280,1024]{1,0:T(8,128)(2,1)}, bf16[1280,1024]{1,0:T(8,128)(2,1)}, u32[]{:S(2)}, u32[]{:S(2)}) collective-permute-start(bf16[1280,1024]{1,0:T(8,128)(2,1)} %get-tuple-element.195), channel_id=1, source_target_pairs={{0,2},{1,3},{2,0},{3,1},{4,6},{5,7},{6,4},{7,5},{8,10},{9,11},{10,... | collective-permute-start | bytes 7864328 | tf_op jit(solution)/shard_map/ppermute | solution.py:372
  552.8 10.6 %copy-start.10 = (f32[8,1280]{1,0:T(8,128)S(1)}, f32[8,1280]{1,0:T(8,128)}, u32[]{:S(2)}) copy-start(f32[8,1280]{1,0:T(8,128)} %get-tuple-element.199) | copy-start | bytes 122884
  552.8 10.6 %copy-start.12 = (f32[8,1280]{1,0:T(8,128)S(1)}, f32[8,1280]{1,0:T(8,128)}, u32[]{:S(2)}) copy-start(f32[8,1280]{1,0:T(8,128)} %get-tuple-element.200) | copy-start | bytes 122884
  552.8 10.6 %copy-start.23 = (bf16[160,1024]{1,0:T(8,128)(2,1)S(1)}, bf16[160,1024]{1,0:T(8,128)(2,1)}, u32[]{:S(2)}) copy-start(bf16[160,1024]{1,0:T(8,128)(2,1)} %reduce-scatter.7.cloned.1.call-done) | copy-start | bytes 983044
  563.4 15.3 %collective-permute-start.8 = (bf16[160,1024]{1,0:T(8,128)(2,1)S(1)}, bf16[160,1024]{1,0:T(8,128)(2,1)S(1)}, u32[]{:S(2)}, u32[]{:S(2)}) collective-permute-start(bf16[160,1024]{1,0:T(8,128)(2,1)S(1)} %copy-done.23), channel_id=1, source_target_pairs={{0,2},{1,3},{2,0},{3,1},{4,6},{5,7},{6,4},{7,5},{8,10},{9,11},{10,... | collective-permute-start | bytes 983048 | tf_op jit(solution)/shard_map/ppermute | solution.py:372
  566.0 12.7 %copy-start.5 = (bf16[160,1024]{1,0:T(8,128)(2,1)S(1)}, bf16[160,1024]{1,0:T(8,128)(2,1)}, u32[]{:S(2)}) copy-start(bf16[160,1024]{1,0:T(8,128)(2,1)} %reduce-scatter.5.cloned.1.call-done) | copy-start | bytes 983044
  566.1 13.1 %copy-start.1 = (bf16[1280,1024]{1,0:T(8,128)(2,1)S(1)}, bf16[1280,1024]{1,0:T(8,128)(2,1)}, u32[]{:S(2)}) copy-start(bf16[1280,1024]{1,0:T(8,128)(2,1)} %get-tuple-element.203) | copy-start | bytes 7864324
  578.8 58.4 %collective-permute-start.7 = (bf16[1280,1024]{1,0:T(8,128)(2,1)}, bf16[1280,1024]{1,0:T(8,128)(2,1)}, u32[]{:S(2)}, u32[]{:S(2)}) collective-permute-start(bf16[1280,1024]{1,0:T(8,128)(2,1)} %weight_grad.4), channel_id=1, source_target_pairs={{0,2},{1,3},{2,0},{3,1},{4,6},{5,7},{6,4},{7,5},{8,10},{9,11},{10,... | collective-permute-start | bytes 7864328 | tf_op jit(solution)/shard_map/ppermute | solution.py:372
  583.7 40.2 %copy-start.8 = (f32[80,128]{1,0:T(8,128)S(1)}, f32[80,128]{1,0:T(8,128)}, u32[]{:S(2)}) copy-start(f32[80,128]{1,0:T(8,128)} %get-tuple-element.202) | copy-start | bytes 122884
  583.7 41.1 %copy-start.17 = (f32[2,80]{1,0:T(2,128)S(1)}, f32[2,80]{1,0:T(2,128)}, u32[]{:S(2)}) copy-start(f32[2,80]{1,0:T(2,128)} %copy-done.16) | copy-start | bytes 1924
  583.8 41.2 %copy-start.13 = (f32[1,1280]{1,0:T(1,128)S(1)}, f32[1,1280]{1,0:T(1,128)}, u32[]{:S(2)}) copy-start(f32[1,1280]{1,0:T(1,128)} %broadcast_in_dim.33) | copy-start | bytes 15364
  583.8 41.9 %copy-start.6 = (bf16[160,1024]{1,0:T(8,128)(2,1)S(1)}, bf16[160,1024]{1,0:T(8,128)(2,1)}, u32[]{:S(2)}) copy-start(bf16[160,1024]{1,0:T(8,128)(2,1)} %reduce-scatter.9.cloned.1.call-done) | copy-start | bytes 983044
  696.3 1.4 copy-start.15
  696.3 1.3 copy-start.19
  696.3 2.3 copy-start
  696.3 2.7 copy-start.2
Sparse Core Ops, SparseCore 0:
  10.8 64.9 all-gather.8
  78.5 49.5 all-gather.10
  147.5 61.0 all-gather.12
  211.3 60.5 all-gather.14
  344.9 70.9 reduce-scatter.4
  419.3 69.2 reduce-scatter.6
  492.1 69.1 reduce-scatter.8
  583.8 75.5 reduce-scatter.10

commit v10 on v9

--- a/solution.py
+++ b/solution.py
@@ -170,9 +170,36 @@
                 fresh.append(state[h] + dot(ds, k_ref[rows, there], ((1,), (1,))))
             return tuple(fresh)
 
+        def corner(_, state):
+            cut, base = bk // 2, order_ref[qi] * bk
+            fresh = []
+            for low in (0, cut):
+                size = bq - low
+                keys = pl.ds(pl.multiple_of(base + low, cut), cut)
+                queries = pl.ds(pl.multiple_of(base + low, cut), size)
+                rows = low + lax.broadcasted_iota(jnp.int32, (size, cut), 0)
+                cols = low + lax.broadcasted_iota(jnp.int32, (size, cut), 1)
+                allowed = cols <= jnp.maximum(rows, prefix - 1 - start)
+                s = [dot(query_ext[h, :, queries], key_ext[h, :, keys], ((0,), (0,))) for h in range(pair)]
+                gp = [dot(grad_ext[h, :, queries], value_ext[h, :, keys], ((0,), (0,))) for h in range(pair)]
+                parts = []
+                for h in range(pair):
+                    p = jnp.exp2(jnp.where(allowed, s[h], MASKED))
+                    ds = (p * gp[h]).astype(BF16)
+                    rows_h = slice(h * dh, (h + 1) * dh)
+                    dv_acc[h, :, keys] += dot(g_ref[rows_h, queries], p.astype(BF16))
+                    dk_acc[h, :, keys] += dot(q_ref[rows_h, queries], ds)
+                    parts.append(dot(ds, k_ref[rows_h, keys], ((1,), (1,))))
+                fresh.append(parts)
+            upper = [state[h][:bk // 2] + fresh[0][h][:bk // 2] for h in range(pair)]
+            lower = [state[h][bk // 2:] + fresh[0][h][bk // 2:] + fresh[1][h] for h in range(pair)]
+            return tuple(jnp.concatenate([a, b], axis=0) for a, b in zip(upper, lower))
+
         state = tuple(jnp.zeros((bq, dh), F32) for _ in range(pair))
         state = lax.fori_loop(0, full, functools.partial(step, False), state)
-        state = lax.fori_loop(full, stop, functools.partial(step, True), state)
+        plain_corner = prefix <= start + bq // 2
+        state = lax.fori_loop(full, jnp.where(plain_corner, full, stop), functools.partial(step, True), state)
+        state = lax.fori_loop(0, plain_corner.astype(jnp.int32), corner, state)
         for h in range(pair):
             rows = slice(h * dh, (h + 1) * dh)
             dq = state[h].T

time: 717 us -> 714 us (level)
  no operation moved by 1% of the time
where the time goes in v10:
time: 714 us; the launch traced here: 708 us
  Pallas kernels  622 us (87%)
  other arithmetic  29.1 us (4%)
  waiting for transfers between devices  21.8 us (3%)
  between operations  15.2 us (2%)
  local copies, waits for them, and re-layouts  12.1 us (2%)
  starting transfers between devices  7.93 us (1%)
    pallas_call x4, Pallas kernels, attention_backward(): pl.pallas_call(functools.partial(backward_kernel, pair=pair, dh=dh, bq=bq...  158 us
    pallas_call x1, Pallas kernels, gather_call(): pl.pallas_call(functools.partial(gather_kernel, pieces, pairs, outer, rin...  105 us
    pallas_call x2, Pallas kernels, mlp_back(): pl.pallas_call(functools.partial(mlp_back_kernel, w, steps, ring), grid=(...  78.9 us
    pallas_call x2, Pallas kernels, attention_forward(): pl.pallas_call(functools.partial(forward_kernel, pair=pair, dh=dh, bq=bq,...  66.9 us
    pallas_call x1, Pallas kernels, finish(): pl.pallas_call(functools.partial(finish_kernel, w, low, far, own_steps, o...  58.4 us
    pallas_call x2, Pallas kernels, middle_call(): pl.pallas_call(functools.partial(middle_kernel, w, low, steps, stack_inde...  51.5 us
    pallas_call x2, Pallas kernels, project(): pl.pallas_call(functools.partial(project_kernel, w, low, steps, stack_ind...  41.4 us
    pallas_call x3, Pallas kernels, weight_grad(): pl.pallas_call(functools.partial(weight_grad_kernel, w), grid=(d // bd,),...  31.1 us
  transfers between devices with their start and end apart: 17, of which 4 were waited for; matrix products, arithmetic and copies ran while one was open for 5% of the time, Pallas kernels for 78%

profile of v10, /device:TPU:0, one launch (start us, length us, event | category | flops | bytes accessed | tf_op | source)
XLA Modules:
  0.0 708.1 jit_solution(1006800821216695517)
XLA Ops:
  7.3 1.9 fusion.15
  9.2 1.3 slice_bitcast_fusion.2
  10.5 0.8 fusion.16
  11.4 0.5 copy-done.16
  11.9 0.9 broadcast_in_dim_tile.8.scale_ref
  12.8 0.1 fusion.10
  13.0 0.3 fusion.11
  13.2 0.8 fusion.13
  14.1 105.4 %gather_weights.1 = (bf16[4,2,160,640]{3,2,1,0:T(8,128)(2,1)}, bf16[4,2,160,640]{3,2,1,0:T(8,128)(2,1)}, bf16[4,2,160,640]{3,2,1,0:T(8,128)(2,1)}, bf16[4,2,160,640]{3,2,1,0:T(8,128)(2,1)}, bf16[512,1280]{1,0:T(8,128)(2,1)}) custom-call(bf16[2,160,640]{2,1,0:T(8,128)(2,1)} %get-tuple-element.261.shard_ref, f32[2,512,1280]{2,1,0:T(8,128)} %refs_4_.1), custom_call_target="tpu_custom_call" | custom-call | tf_op jit(solution)/shard_map/gather_weights/pallas_call | solution.py:369
  119.5 0.6 slice_bitcast_fusion.3
  120.1 4.5 collective-permute-start
  124.7 21.7 %project.2 = (bf16[1024,1280]{1,0:T(8,128)(2,1)}, bf16[1024,1280]{1,0:T(8,128)(2,1)}, bf16[640,2048]{1,0:T(8,128)(2,1)}, bf16[640,2048]{1,0:T(8,128)(2,1)}, bf16...) custom-call(f32[1,1280]{1,0:T(1,128)} %get-tuple-element.266.gain_ref, f32[640,1]{1,0:T(8,128)} %broadcast_in_dim_tile.8.scale_ref, ...), custom_call_target="tpu_custom_call" | custom-call | flops 10066329600 | bytes 15728640 | tf_op jit(solution)/shard_map/project/pallas_call | solution.py:732
  146.4 1.0 pad_maximum_fusion.7
  147.5 0.9 broadcast_in_dim_tile.9.scale_ref
  148.4 0.6 dynamic_slice.10.prefix_ref
  149.0 0.5 fusion.19.order_ref
  149.5 2.0 collective-permute-start.2
  151.5 0.3 reduce-scatter.5.cloned.1.call-start
  151.8 33.5 %attention_forward.2 = (bf16[640,2048]{1,0:T(8,128)(2,1)}, f32[8,1,2048]{2,1,0:T(1,128)}) custom-call(s32[1]{0:T(128)} %dynamic_slice.10.prefix_ref, s32[4]{0:T(128)} %fusion.19.order_ref, bf16[640,2048]{1,0:T(8,128)(2,1)} %get-tuple-element.127.q_ref, bf16[640,2048]{1,0:T(8,128)(2,1)} %get-tuple-element.128.k_ref, bf16[640,2048]{1,0:T(8,128)(2,1)} %get-tuple-element.129.v_ref), custom_call_target="tpu_custom_call" | custom-call | flops 20132659200 | bytes 10485760 | tf_op jit(solution)/shard_map/attention_forward/pallas_call | solution.py:95
  185.3 3.0 collective-permute-done.1.refs_3_
  188.3 25.0 %middle.2 = (f32[1024,1280]{1,0:T(8,128)}, f32[1024,1280]{1,0:T(8,128)}, f32[1024,1280]{1,0:T(8,128)}, bf16[1280,1280]{1,0:T(8,128)(2,1)}, bf16[1280,1280]{1,0:T(8,128)(2,1)}, /*index=5*/bf16[1280,640]{1,0:T(8,128)(2,1)}) custom-call(f32[1024,1280]{1,0:T(8,128)} %get-tuple-element.124.x_ref.x_any, f32[1,1280]{1,0:T(1,128)} %get-tuple-element.265.gm_ref, ...), custom_call_target="tpu_custom_call" | custom-call | flops 10066329600 | bytes 39321600 | tf_op jit(solution)/shard_map/middle/pallas_call | solution.py:863
  213.3 1.9 fusion
  215.2 5.4 collective-permute-done.2.refs_1_.refs_7_
  220.6 19.7 %project.3 = (bf16[1024,1280]{1,0:T(8,128)(2,1)}, bf16[1024,1280]{1,0:T(8,128)(2,1)}, bf16[640,2048]{1,0:T(8,128)(2,1)}, bf16[640,2048]{1,0:T(8,128)(2,1)}, bf16[640,2048]{1,0:T(8,128)(2,1)}) custom-call(f32[1,1280]{1,0:T(1,128)} %get-tuple-element.264.gain_ref, f32[640,1]{1,0:T(8,128)} %broadcast_in_dim_tile.9.scale_ref, bf16[1280,640]{1,0:T(8,128)(2,1)} %bitcast.111, ...), custom_call_target="tpu_custom_call" | custom-call | flops 10066329600 | bytes 15728640 | tf_op jit(solution)/shard_map/project/pallas_call | solution.py:732
  240.4 33.3 %attention_forward.3 = (bf16[640,2048]{1,0:T(8,128)(2,1)}, f32[8,1,2048]{2,1,0:T(1,128)}) custom-call(s32[1]{0:T(128)} %dynamic_slice.10.prefix_ref, s32[4]{0:T(128)} %fusion.19.order_ref, bf16[640,2048]{1,0:T(8,128)(2,1)} %get-tuple-element.147.q_ref, bf16[640,2048]{1,0:T(8,128)(2,1)} %get-tuple-element.148.k_ref, bf16[640,2048]{1,0:T(8,128)(2,1)} %get-tuple-element.149.v_ref), custom_call_target="tpu_custom_call" | custom-call | flops 20132659200 | bytes 10485760 | tf_op jit(solution)/shard_map/attention_forward/pallas_call | solution.py:95
  273.7 26.5 %middle.3 = (f32[1024,1280]{1,0:T(8,128)}, f32[1024,1280]{1,0:T(8,128)}, f32[1024,1280]{1,0:T(8,128)}, bf16[1280,1280]{1,0:T(8,128)(2,1)}, bf16[1280,1280]{1,0:T...) custom-call(f32[1024,1280]{1,0:T(8,128)} %get-tuple-element.144.refs_4_.x_ref, ...), custom_call_target="tpu_custom_call" | custom-call | flops 10066329600 | bytes 39321600 | tf_op jit(solution)/shard_map/middle/pallas_call | solution.py:863
  300.2 40.1 %mlp_back.2 = (f32[1024,1280]{1,0:T(8,128)}, f32[8,1280]{1,0:T(8,128)}, bf16[640,2048]{1,0:T(8,128)(2,1)}, bf16[1280,1024]{1,0:T(8,128)(2,1)}, bf16[1280,1024]{1,0:T(8,128)(2,1)}) custom-call(f32[1024,1280]{1,0:T(8,128)} %get-tuple-element.154.mid_ref, f32[1024,1280]{1,0:T(8,128)} %get-tuple-element.155.pre_ref, f32[1,1280]{1,0:T(1,128)} %get-tuple-element.267.gm_ref, ...), custom_call_target="tpu_custom_call" | custom-call | flops 20132659200 | bytes 52428800 | tf_op jit(solution)/shard_map/mlp_back/pallas_call | solution.py:1016
  340.3 0.3 reduce-scatter.7.cloned.1.call-start
  340.6 0.7 copy.33.scale_ref
  341.3 0.7 copy.35.scale_ref
  342.1 0.6 broadcast_in_dim.33
  342.8 39.5 %attention_backward.4 = (bf16[320,2048]{1,0:T(8,128)(2,1)}, bf16[320,2048]{1,0:T(8,128)(2,1)}, bf16[320,2048]{1,0:T(8,128)(2,1)}, f32[80,128]{1,0:T(8,128)}) custom-call(s32[1]{0:T(128)} %dynamic_slice.10.prefix_ref, s32[4]{0:T(128)} %fusion.19.order_ref, bf16[640,2048]{1,0:T(8,128)(2,1)} %get-tuple-element.147.q_ref, ...), custom_call_target="tpu_custom_call" | custom-call | flops 26843545600 | bytes 10485760 | tf_op jit(solution)/shard_map/attention_backward/pallas_call | solution.py:232
  382.2 10.3 %weight_grad.3 = bf16[1280,1024]{1,0:T(8,128)(2,1)} custom-call(bf16[1024,1280]{1,0:T(8,128)(2,1)} %get-tuple-element.164.own_ref.refs_10_, bf16[1024,1280]{1,0:T(8,128)(2,1)} %get-tuple-element.165.other_ref.refs_11_, bf16[320,2048]{1,0:T(8,128)(2,1)} %get-tuple-element.167.dq_ref.refs_3_, bf16[320,2048]{1,0:T(8,128)(2,1)} %get-tuple-element.168.dk_ref.refs_4_, ...), custom_call_target="tpu_custom_call" | custom-call | flops 5033164800 | bytes 15728640 | tf_op jit(solution)/shard_map/weight_grad/pallas_call | solution.py:1059
  392.6 39.6 %attention_backward.5 = (bf16[320,2048]{1,0:T(8,128)(2,1)}, bf16[320,2048]{1,0:T(8,128)(2,1)}, bf16[320,2048]{1,0:T(8,128)(2,1)}, f32[80,128]{1,0:T(8,128)}) custom-call(s32[1]{0:T(128)} %dynamic_slice.10.prefix_ref, s32[4]{0:T(128)} %fusion.19.order_ref, bf16[640,2048]{1,0:T(8,128)(2,1)} %get-tuple-element.147.q_ref, ...), custom_call_target="tpu_custom_call" | custom-call | flops 26843545600 | bytes 10485760 | tf_op jit(solution)/shard_map/attention_backward/pallas_call | solution.py:232
  432.2 0.9 add_reduce_fusion
  433.2 30.2 %input_back.1 = (f32[1024,1280]{1,0:T(8,128)}, f32[8,1280]{1,0:T(8,128)}, bf16[1280,1024]{1,0:T(8,128)(2,1)}) custom-call(f32[1024,1280]{1,0:T(8,128)} %get-tuple-element.144.refs_4_.x_ref, f32[1024,1280]{1,0:T(8,128)} %get-tuple-element.162.g_ref, f32[1,1280]{1,0:T(1,128)} %get-tuple-element.264.gain_ref, bf16[320,2048]{1,0:T(8,128)(2,1)} %get-tuple-element.175.refs_0_, ...), custom_call_target="tpu_custom_call" | custom-call | flops 15099494400 | bytes 31457280 | tf_op jit(solution)/shard_map/input_back/pallas_call | solution.py:1173
  463.4 4.5 add_convert_fusion.1
  468.0 38.9 %mlp_back.3 = (f32[1024,1280]{1,0:T(8,128)}, f32[8,1280]{1,0:T(8,128)}, bf16[640,2048]{1,0:T(8,128)(2,1)}, bf16[1280,1024]{1,0:T(8,128)(2,1)}, bf16[1280,1024]{1,0:T(8,128)(2,1)}) custom-call(f32[1024,1280]{1,0:T(8,128)} %get-tuple-element.134.mid_ref, f32[1024,1280]{1,0:T(8,128)} %get-tuple-element.135.pre_ref, f32[1,1280]{1,0:T(1,128)} %get-tuple-element.265.gm_ref, ...), custom_call_target="tpu_custom_call" | custom-call | flops 20132659200 | bytes 52428800 | tf_op jit(solution)/shard_map/mlp_back/pallas_call | solution.py:1016
  506.9 0.1 collective-permute-start.6
  506.9 39.6 %attention_backward.6 = (bf16[320,2048]{1,0:T(8,128)(2,1)}, bf16[320,2048]{1,0:T(8,128)(2,1)}, bf16[320,2048]{1,0:T(8,128)(2,1)}, f32[80,128]{1,0:T(8,128)}) custom-call(s32[1]{0:T(128)} %dynamic_slice.10.prefix_ref, s32[4]{0:T(128)} %fusion.19.order_ref, bf16[640,2048]{1,0:T(8,128)(2,1)} %get-tuple-element.127.q_ref, ...), custom_call_target="tpu_custom_call" | custom-call | flops 26843545600 | bytes 10485760 | tf_op jit(solution)/shard_map/attention_backward/pallas_call | solution.py:232
  546.5 10.5 %weight_grad.4 = bf16[1280,1024]{1,0:T(8,128)(2,1)} custom-call(bf16[1024,1280]{1,0:T(8,128)(2,1)} %get-tuple-element.187.own_ref, bf16[1024,1280]{1,0:T(8,128)(2,1)} %get-tuple-element.188.other_ref, bf16[320,2048]{1,0:T(8,128)(2,1)} %get-tuple-element.190.dq_ref.refs_3_, bf16[320,2048]{1,0:T(8,128)(2,1)} %get-tuple-element.191.dk_ref.refs_4_, ...), custom_call_target="tpu_custom_call" | custom-call | flops 5033164800 | bytes 15728640 | tf_op jit(solution)/shard_map/weight_grad/pallas_call | solution.py:1059
  557.2 2.5 convert_select_fusion.3
  559.8 2.7 pad_maximum_fusion
  562.5 10.9 %collective-permute-done.8 = bf16[160,1024]{1,0:T(8,128)(2,1)S(1)} collective-permute-done((bf16[160,1024]{1,0:T(8,128)(2,1)S(1)}, bf16[160,1024]{1,0:T(8,128)(2,1)S(1)}, u32[]{:S(2)}, u32[]{:S(2)}) %collective-permute-start.8) | collective-permute-done | bytes 327712 | tf_op jit(solution)/shard_map/ppermute | solution.py:399
  573.4 0.1 add_bitcast_fusion
  573.5 0.4 collective-permute-start.7
  573.9 4.5 add_convert_fusion
  578.5 39.5 %attention_backward.7 = (bf16[320,2048]{1,0:T(8,128)(2,1)}, bf16[320,2048]{1,0:T(8,128)(2,1)}, bf16[320,2048]{1,0:T(8,128)(2,1)}, f32[80,128]{1,0:T(8,128)}) custom-call(s32[1]{0:T(128)} %dynamic_slice.10.prefix_ref, s32[4]{0:T(128)} %fusion.19.order_ref, bf16[640,2048]{1,0:T(8,128)(2,1)} %get-tuple-element.127.q_ref, ...), custom_call_target="tpu_custom_call" | custom-call | flops 26843545600 | bytes 10485760 | tf_op jit(solution)/shard_map/attention_backward/pallas_call | solution.py:232
  618.0 0.9 add_reduce_fusion.1
  619.0 0.7 concatenate.35.small_ref
  619.7 10.3 %weight_grad.5.piece_any = bf16[1280,1024]{1,0:T(8,128)(2,1)} custom-call(bf16[1024,1280]{1,0:T(8,128)(2,1)} %get-tuple-element.187.own_ref, bf16[1024,1280]{1,0:T(8,128)(2,1)} %get-tuple-element.188.other_ref, bf16[320,2048]{1,0:T(8,128)(2,1)} %get-tuple-element.215.dq_ref.refs_0_, bf16[320,2048]{1,0:T(8,128)(2,1)} %get-tuple-element.216.dk_ref.refs_1_, ...), custom_call_target="tpu_custom_call" | custom-call | flops 5033164800 | bytes 15728640 | tf_op jit(solution)/shard_map/weight_grad/pallas_call | solution.py:1059
  630.0 2.3 collective-permute-done.7.came_any
  632.4 58.4 %finish.1 = (f32[512,1280]{1,0:T(8,128)}, bf16[512,1280]{1,0:T(8,128)(2,1)}, f32[160,1024]{1,0:T(8,128)}, f32[8,1280]{1,0:T(8,128)}) custom-call(f32[1,1280]{1,0:T(1,128)} %get-tuple-element.266.gain_ref, f32[8,1280]{1,0:T(8,128)} %concatenate.35.small_ref, f32[1024,1280]{1,0:T(8,128)} %get-tuple-element.124.x_ref.x_any, ...), custom_call_target="tpu_custom_call" | custom-call | flops 10066329600 | bytes 31457280 | tf_op jit(solution)/shard_map/finish/pallas_call | solution.py:1371
  690.7 1.4 fusion.7
  692.2 0.1 pad_maximum_fusion.2
  692.3 1.2 copy.37
  693.5 0.6 fusion.18
  694.1 0.4 copy-done
  694.5 0.4 copy-done.2
  694.8 0.4 convert_select_fusion.1
  695.2 2.7 pad_maximum_fusion.1
  697.9 0.6 fusion.22
  698.5 1.0 bitcast_convert_fusion
  699.6 1.2 fusion.8
  (96 shorter events, 1.0 us)
Async XLA Ops:
  7.2 5.6 copy-start.3
  7.2 5.6 copy-start.4
  7.2 4.2 copy-start.18
  7.2 5.8 copy-start.7
  7.2 112.9 %all-gather.9.cloned.1.call-start = ((), (), s32[]{:S(2)}) async-start(), calls=%async_computation.8 | async-start | bytes 1843200 | tf_op jit(solution)/shard_map/all_gather | solution.py:1441
  9.2 137.2 %all-gather.11.cloned.1.call-start = ((), (), s32[]{:S(2)}) async-start(), calls=%async_computation.9 | async-start | bytes 1843200 | tf_op jit(solution)/shard_map/all_gather | solution.py:1441
  11.3 209.3 %all-gather.13.cloned.1.call-start = ((), (), s32[]{:S(2)}) async-start(), calls=%async_computation.10 | async-start | bytes 3686400 | tf_op jit(solution)/shard_map/all_gather | solution.py:1464
  11.4 0.6 copy-start.16
  14.1 105.4 %copy-start.14 = (f32[2,2,1280]{2,1,0:T(2,128)S(1)}, f32[2,2,1280]{2,1,0:T(2,128)}, u32[]{:S(2)}) copy-start(f32[2,2,1280]{2,1,0:T(2,128)} %param.15) | copy-start | bytes 61444
  120.1 26.3 %collective-permute-start = (bf16[2,160,640]{2,1,0:T(8,128)(2,1)S(1)}, bf16[2,160,640]{2,1,0:T(8,128)(2,1)S(1)}, u32[]{:S(2)}, u32[]{:S(2)}) collective-permute-start(bf16[2,160,640]{2,1,0:T(8,128)(2,1)S(1)} %get-tuple-element.126), channel_id=1, source_target_pairs={{0,2},{1,3},{2,0},{3,1},{4,6},{5,7},{6,4},{7,5},{8,10},{9,11},{10,... | collective-permute-start | bytes 1228808 | tf_op jit(solution)/shard_map/ppermute | solution.py:399
  124.7 23.7 %copy-start.24 = (s32[2]{0:T(128)S(1)}, s32[2]{0:T(128)}, u32[]{:S(2)}) copy-start(s32[2]{0:T(128)} %param.17) | copy-start | bytes 28
  124.7 24.8 %copy-start.20 = (bf16[1,1280,640]{2,1,0:T(8,128)(2,1)S(1)}, bf16[1,1280,640]{2,1,0:T(8,128)(2,1)}, u32[]{:S(2)}) copy-start(bf16[1,1280,640]{2,1,0:T(8,128)(2,1)} %all-gather.9.cloned.1.call-done) | copy-start | bytes 4915204
  147.4 126.3 %all-gather.15.cloned.1.call-start = ((), (), s32[]{:S(2)}) async-start(), calls=%async_computation.11 | async-start | bytes 3686400 | tf_op jit(solution)/shard_map/all_gather | solution.py:1464
  149.5 38.8 %collective-permute-start.1 = (bf16[1280,640]{1,0:T(8,128)(2,1)S(1)}, bf16[1280,640]{1,0:T(8,128)(2,1)}, u32[]{:S(2)}, u32[]{:S(2)}) collective-permute-start(bf16[1280,640]{1,0:T(8,128)(2,1)S(1)} %bitcast.114), channel_id=1, source_target_pairs={{0,2},{1,3},{2,0},{3,1},{4,6},{5,7},{6,4},{7,5},{8,10},{9,11},{10,... | collective-permute-start | bytes 4915208 | tf_op jit(solution)/shard_map/ppermute | solution.py:399
  149.5 71.0 %collective-permute-start.2 = (bf16[1280,640]{1,0:T(8,128)(2,1)}, bf16[1280,640]{1,0:T(8,128)(2,1)}, u32[]{:S(2)}, u32[]{:S(2)}) collective-permute-start(bf16[1280,640]{1,0:T(8,128)(2,1)} %bitcast.110), channel_id=1, source_target_pairs={{0,2},{1,3},{2,0},{3,1},{4,6},{5,7},{6,4},{7,5},{8,10},{9,11},{10,... | collective-permute-start | bytes 4915208 | tf_op jit(solution)/shard_map/ppermute | solution.py:399
  151.5 281.6 %reduce-scatter.5.cloned.1.call-start = ((), (), s32[]{:S(2)}) async-start(), calls=%async_computation.4 | async-start | bytes 2949120 | tf_op jit(solution)/shard_map/reduce_scatter | solution.py:1412
  220.6 53.1 %collective-permute-start.3 = (bf16[512,1280]{1,0:T(8,128)(2,1)S(1)}, bf16[512,1280]{1,0:T(8,128)(2,1)S(1)}, u32[]{:S(2)}, u32[]{:S(2)}) collective-permute-start(bf16[512,1280]{1,0:T(8,128)(2,1)S(1)} %fusion), channel_id=1, source_target_pairs={{0,2},{1,3},{2,0},{3,1},{4,6},{5,7},{6,4},{7,5},{8,10},{9,11},{10,... | collective-permute-start | bytes 3932168 | tf_op jit(solution)/shard_map/ppermute | solution.py:399
  273.7 26.5 %copy-start.22 = (bf16[512,1280]{1,0:T(8,128)(2,1)}, bf16[512,1280]{1,0:T(8,128)(2,1)S(1)}, u32[]{:S(2)}) copy-start(bf16[512,1280]{1,0:T(8,128)(2,1)S(1)} %collective-permute-done.3.refs_4_) | copy-start | bytes 3932164
  340.3 1.7 copy-start.21
  340.3 1.7 copy-start.11
  340.3 166.5 %reduce-scatter.7.cloned.1.call-start = ((), (), s32[]{:S(2)}) async-start(), calls=%async_computation.5 | async-start | bytes 2949120 | tf_op jit(solution)/shard_map/reduce_scatter | solution.py:1412
  342.0 50.5 %collective-permute-start.4 = (bf16[512,1280]{1,0:T(8,128)(2,1)S(1)}, bf16[512,1280]{1,0:T(8,128)(2,1)}, u32[]{:S(2)}, u32[]{:S(2)}) collective-permute-start(bf16[512,1280]{1,0:T(8,128)(2,1)S(1)} %copy-done.21), channel_id=1, source_target_pairs={{0,2},{1,3},{2,0},{3,1},{4,6},{5,7},{6,4},{7,5},{8,10},{9,11},{10,... | collective-permute-start | bytes 3932168 | tf_op jit(solution)/shard_map/ppermute | solution.py:399
  342.7 231.2 %reduce-scatter.9.cloned.1.call-start = ((), (), s32[]{:S(2)}) async-start(), calls=%async_computation.6 | async-start | bytes 2949120 | tf_op jit(solution)/shard_map/reduce_scatter | solution.py:1412
  392.6 39.7 %copy-start.9 = (f32[80,128]{1,0:T(8,128)S(1)}, f32[80,128]{1,0:T(8,128)}, u32[]{:S(2)}) copy-start(f32[80,128]{1,0:T(8,128)} %get-tuple-element.212) | copy-start | bytes 122884
  392.6 70.8 %collective-permute-start.5 = (bf16[1280,1024]{1,0:T(8,128)(2,1)}, bf16[1280,1024]{1,0:T(8,128)(2,1)S(1)}, u32[]{:S(2)}, u32[]{:S(2)}) collective-permute-start(bf16[1280,1024]{1,0:T(8,128)(2,1)} %weight_grad.3), channel_id=1, source_target_pairs={{0,2},{1,3},{2,0},{3,1},{4,6},{5,7},{6,4},{7,5},{8,10},{9,11},{10,... | collective-permute-start | bytes 7864328 | tf_op jit(solution)/shard_map/ppermute | solution.py:399
  467.9 230.6 %reduce-scatter.11.cloned.1.call-start = ((), (), s32[]{:S(2)}) async-start(), calls=%async_computation.7 | async-start | bytes 2949120 | tf_op jit(solution)/shard_map/reduce_scatter | solution.py:1412
  506.9 66.6 %collective-permute-start.6 = (bf16[1280,1024]{1,0:T(8,128)(2,1)}, bf16[1280,1024]{1,0:T(8,128)(2,1)}, u32[]{:S(2)}, u32[]{:S(2)}) collective-permute-start(bf16[1280,1024]{1,0:T(8,128)(2,1)} %get-tuple-element.195), channel_id=1, source_target_pairs={{0,2},{1,3},{2,0},{3,1},{4,6},{5,7},{6,4},{7,5},{8,10},{9,11},{10,... | collective-permute-start | bytes 7864328 | tf_op jit(solution)/shard_map/ppermute | solution.py:399
  546.5 10.5 %copy-start.10 = (f32[8,1280]{1,0:T(8,128)S(1)}, f32[8,1280]{1,0:T(8,128)}, u32[]{:S(2)}) copy-start(f32[8,1280]{1,0:T(8,128)} %get-tuple-element.199) | copy-start | bytes 122884
  546.5 10.6 %copy-start.12 = (f32[8,1280]{1,0:T(8,128)S(1)}, f32[8,1280]{1,0:T(8,128)}, u32[]{:S(2)}) copy-start(f32[8,1280]{1,0:T(8,128)} %get-tuple-element.200) | copy-start | bytes 122884
  546.5 10.6 %copy-start.23 = (bf16[160,1024]{1,0:T(8,128)(2,1)S(1)}, bf16[160,1024]{1,0:T(8,128)(2,1)}, u32[]{:S(2)}) copy-start(bf16[160,1024]{1,0:T(8,128)(2,1)} %reduce-scatter.7.cloned.1.call-done) | copy-start | bytes 983044
  557.2 16.2 %collective-permute-start.8 = (bf16[160,1024]{1,0:T(8,128)(2,1)S(1)}, bf16[160,1024]{1,0:T(8,128)(2,1)S(1)}, u32[]{:S(2)}, u32[]{:S(2)}) collective-permute-start(bf16[160,1024]{1,0:T(8,128)(2,1)S(1)} %copy-done.23), channel_id=1, source_target_pairs={{0,2},{1,3},{2,0},{3,1},{4,6},{5,7},{6,4},{7,5},{8,10},{9,11},{10,... | collective-permute-start | bytes 983048 | tf_op jit(solution)/shard_map/ppermute | solution.py:399
  559.8 13.6 %copy-start.5 = (bf16[160,1024]{1,0:T(8,128)(2,1)S(1)}, bf16[160,1024]{1,0:T(8,128)(2,1)}, u32[]{:S(2)}) copy-start(bf16[160,1024]{1,0:T(8,128)(2,1)} %reduce-scatter.5.cloned.1.call-done) | copy-start | bytes 983044
  559.8 14.1 %copy-start.1 = (bf16[1280,1024]{1,0:T(8,128)(2,1)S(1)}, bf16[1280,1024]{1,0:T(8,128)(2,1)}, u32[]{:S(2)}) copy-start(bf16[1280,1024]{1,0:T(8,128)(2,1)} %get-tuple-element.203) | copy-start | bytes 7864324
  573.5 58.8 %collective-permute-start.7 = (bf16[1280,1024]{1,0:T(8,128)(2,1)}, bf16[1280,1024]{1,0:T(8,128)(2,1)}, u32[]{:S(2)}, u32[]{:S(2)}) collective-permute-start(bf16[1280,1024]{1,0:T(8,128)(2,1)} %weight_grad.4), channel_id=1, source_target_pairs={{0,2},{1,3},{2,0},{3,1},{4,6},{5,7},{6,4},{7,5},{8,10},{9,11},{10,... | collective-permute-start | bytes 7864328 | tf_op jit(solution)/shard_map/ppermute | solution.py:399
  578.4 39.6 %copy-start.8 = (f32[80,128]{1,0:T(8,128)S(1)}, f32[80,128]{1,0:T(8,128)}, u32[]{:S(2)}) copy-start(f32[80,128]{1,0:T(8,128)} %get-tuple-element.202) | copy-start | bytes 122884
  578.4 40.4 %copy-start.17 = (f32[2,80]{1,0:T(2,128)S(1)}, f32[2,80]{1,0:T(2,128)}, u32[]{:S(2)}) copy-start(f32[2,80]{1,0:T(2,128)} %copy-done.16) | copy-start | bytes 1924
  578.5 40.5 %copy-start.13 = (f32[1,1280]{1,0:T(1,128)S(1)}, f32[1,1280]{1,0:T(1,128)}, u32[]{:S(2)}) copy-start(f32[1,1280]{1,0:T(1,128)} %broadcast_in_dim.33) | copy-start | bytes 15364
  578.5 41.2 %copy-start.6 = (bf16[160,1024]{1,0:T(8,128)(2,1)S(1)}, bf16[160,1024]{1,0:T(8,128)(2,1)}, u32[]{:S(2)}) copy-start(bf16[160,1024]{1,0:T(8,128)(2,1)} %reduce-scatter.9.cloned.1.call-done) | copy-start | bytes 983044
  692.1 1.4 copy-start.15
  692.2 1.3 copy-start.19
  692.2 2.3 copy-start
  692.2 2.7 copy-start.2
Sparse Core Ops, SparseCore 0:
  10.8 64.9 all-gather.8
  78.5 49.5 all-gather.10
  147.5 61.0 all-gather.12
  211.3 60.5 all-gather.14
  340.5 70.9 reduce-scatter.4
  414.8 69.1 reduce-scatter.6
  487.6 69.1 reduce-scatter.8
  578.6 77.3 reduce-scatter.10
